TPU v7x, 32 devices: a whole 2x2x4 slice. The times are simulated.
32 devices in a mesh: groups: 2 (over y), ep: 4 (over z), tp: 4 (over x, core).
Axes of the slice: x: 2, y: 2, z: 4, core: 2. Of those that a mesh axis runs over, the one named last changes fastest.
Arguments:
- tokens: bfloat16 [1024, 3584], P(('groups', 'ep'), 'tp'), parts along dimension 0, may hold values from -6 to 6
- expert_ids: int32 [1024, 8], P(('groups', 'ep')), parts along dimension 0, may hold values from 0 to 255, as said below
- route_scores: float32 [1024, 8], P(('groups', 'ep')), parts along dimension 0, may hold values from -6 to 6
- w_gate: bfloat16 [4, 3584, 512], P('ep', None, 'tp'), may hold values from -0.09375 to 0.09375
- w_up: bfloat16 [4, 3584, 512], P('ep', None, 'tp'), may hold values from -0.09375 to 0.09375
- w_down: bfloat16 [4, 512, 3584], P('ep', 'tp'), may hold values from -0.1875 to 0.1875
Outputs:
- routed_out: bfloat16 [1024, 3584], P(('groups', 'ep'), 'tp'), parts along dimension 0
There are 2 independent parts, one for each index of `groups`. A program takes and returns all parts, laid end to end along the dimension named above; an argument that names none is the same for every part. Nothing has to cross between parts.
Inputs may be any that keep to these rules, and one draw needn't show every extreme that they name: `expert_ids`: each token names 8 different experts, one from each range k * 32 to (k + 1) * 32 - 1 in some order. Among the 128 tokens of one index of ep no expert is named by more than 8 tokens.
All inputs are finite; a program needn't handle non-finite values.
Results may differ from a plain program's by a relative error of at most 0.013.
Values may be sent and summed in bfloat16 or wider, within the bound.
No kernel may reach another device: no remote copies, remote signals or barrier semaphores. Data moves between devices by JAX's collectives and lax.ppermute only.
A program may use at most 64 MiB of HBM per device.

v0:
```python
import jax
import jax.numpy as jnp
from jax import lax
from jax.sharding import PartitionSpec as P

CAP = 8


def combine_rows(returned, first, second, weights, row_count, top_count):
    running = jnp.zeros((row_count, returned.shape[1]), jnp.float32)
    first_cols = first.reshape(row_count, top_count)
    second_cols = second.reshape(row_count, top_count)
    for column in range(top_count):
        inside = first_cols[:, column] >= 0
        upper = jnp.take(returned, jnp.maximum(first_cols[:, column], 0), axis=0).astype(
            jnp.float32
        )
        lower = jnp.take(returned, jnp.maximum(second_cols[:, column], 0), axis=0).astype(
            jnp.float32
        )
        running = running + jnp.where(
            inside[:, None], weights[:, column : column + 1] * (upper + lower), 0.0
        )
    return running


def shards(tokens, expert_ids, route_scores, w_gate, w_up, w_down):
    row_count, features_dev = tokens.shape
    top_count = expert_ids.shape[1]
    ep_count = lax.axis_size("ep")
    slot_count = ep_count * CAP
    resident_count = ep_count // 2
    squashed = jax.nn.sigmoid(route_scores)
    weights = 2.5 * squashed / jnp.sum(squashed, axis=1, keepdims=True)
    flat_ids = expert_ids.reshape(row_count * top_count)
    onehot = (flat_ids[:, None] == jnp.arange(resident_count, dtype=jnp.int32)[None, :]).astype(
        jnp.int32
    )
    slot_index = jnp.sum((jnp.cumsum(onehot, axis=0) - 1) * onehot, axis=1)
    resident = jnp.sum(onehot, axis=1)
    first = jnp.where(resident > 0, 2 * flat_ids * CAP + slot_index, -1)
    second = jnp.where(resident > 0, first + CAP, -1)
    slot_ids = jnp.arange(slot_count, dtype=jnp.int32)[None, :]
    matches = ((first[:, None] == slot_ids) | (second[:, None] == slot_ids)).astype(jnp.int32)
    dispatch_matrix = jnp.sum(matches.reshape(row_count, top_count, slot_count), axis=1).astype(
        jnp.bfloat16
    )
    gate_rows = w_gate[0]
    up_rows = w_up[0]
    outgoing = jnp.einsum(
        "rs,rf->sf", dispatch_matrix, tokens, preferred_element_type=jnp.float32
    ).astype(jnp.bfloat16)
    incoming = lax.all_to_all(
        outgoing.reshape(ep_count, CAP, features_dev), "ep", split_axis=0, concat_axis=0, tiled=True
    )
    local_slots = incoming.reshape(slot_count, features_dev)
    block_cols = lax.all_gather(local_slots, "tp", axis=1, tiled=True)
    gate_act = jnp.dot(block_cols, gate_rows, preferred_element_type=jnp.float32)
    up_act = jnp.dot(block_cols, up_rows, preferred_element_type=jnp.float32)
    hidden = (jax.nn.silu(gate_act) * up_act).astype(jnp.bfloat16)
    partial_value = jnp.dot(hidden, w_down[0], preferred_element_type=jnp.float32)
    expert_out = lax.psum_scatter(
        partial_value.astype(jnp.bfloat16), "tp", scatter_dimension=1, tiled=True
    ).astype(jnp.float32)
    returned = lax.all_to_all(
        expert_out.reshape(ep_count, CAP, features_dev).astype(jnp.bfloat16),
        "ep",
        split_axis=0,
        concat_axis=0,
        tiled=True,
    ).astype(jnp.float32)
    mixed = combine_rows(
        returned.reshape(slot_count, features_dev), first, second, weights, row_count, top_count
    )
    return mixed.astype(jnp.bfloat16)


def solution(mesh):
    placed = (
        P(("groups", "ep"), "tp"),
        P(("groups", "ep"), None),
        P(("groups", "ep"), None),
        P("ep", None, "tp"),
        P("ep", None, "tp"),
        P("ep", "tp", None),
    )
    return jax.shard_map(
        shards, mesh=mesh, in_specs=placed, out_specs=P(("groups", "ep"), "tp"), check_vma=False
    )
```

profile of v0, /device:TPU:0, one launch (start us, length us, event | category | flops | bytes accessed | tf_op | source)
XLA Modules:
  0.0 97.4 jit_solution(8637383760074348672)
XLA Ops:
  6.5 0.0 copy-start
  6.5 0.9 copy.27
  7.5 0.1 eq.57
  7.6 0.1 eq.53
  7.7 0.6 reduce-window.6
  8.3 0.2 slice_reduce_fusion
  8.5 0.2 reduce-window.9
  8.7 0.1 add_bitcast_fusion
  8.8 0.1 gt.17
  8.9 0.1 copy.30
  8.9 0.1 reduce_sum.40
  9.1 0.7 add_select_fusion
  9.9 0.0 copy-done.3
  9.9 0.8 fusion
  10.7 6.4 %all-to-all-start = ((bf16[4,8,896]{2,1,0:T(8,128)(2,1)}), bf16[4,8,896]{2,1,0:T(8,128)(2,1)S(1)}, u32[]{:S(2)}, u32[]{:S(2)}) async-start(bf16[4,8,896]{2,1,0:T(8,128)(2,1)} %fusion), calls=%async_computation | async-start | bytes 114688 | tf_op jit(solution)/shard_map/all_to_all | solution.py:53
  17.1 0.0 reduce-scatter.4.cloned.1.call-start
  17.1 0.1 compare_and_fusion.14
  17.2 0.7 fusion.42
  18.1 4.7 %all-to-all-done = bf16[4,8,896]{2,1,0:T(8,128)(2,1)S(1)} async-done(((bf16[4,8,896]{2,1,0:T(8,128)(2,1)}), bf16[4,8,896]{2,1,0:T(8,128)(2,1)S(1)}, u32[]{:S(2)}, u32[]{:S(2)}) %all-to-all-start) | async-done | bytes 57376 | tf_op jit(solution)/shard_map/all_to_all | solution.py:53
  22.8 5.7 %all_gather.3 = bf16[32,3584]{1,0:T(8,128)(2,1)S(1)} all-gather(bf16[32,896]{1,0:T(8,128)(2,1)S(1)} %bitcast.119), channel_id=1, replica_groups=mesh['groups'=2,'ep'=4,'tp'=4] {'tp'}, dimensions={1}, use_global_device_ids=true | all-gather | bytes 286720 | tf_op jit(solution)/shard_map/all_gather | solution.py:57
  28.5 0.2 fusion.5
  28.8 0.0 copy-done
  28.8 0.5 convolution_convert_fusion
  29.3 1.2 %copy.32 = bf16[32,3584]{0,1:T(8,128)(2,1)} copy(bf16[32,3584]{1,0:T(8,128)(2,1)S(1)} %convolution_convert_fusion) | data formatting | bytes 458752
  30.5 0.0 reduce-scatter.4.cloned.1.call-update
  30.5 0.0 copy-start.4
  30.6 0.7 copy-done.4
  31.3 22.1 %reduce-scatter.4.cloned.1.call-done = bf16[896,32]{1,0:T(8,128)(2,1)} async-done(((bf16[3584,32]{1,0:T(8,128)(2,1)}), bf16[896,32]{1,0:T(8,128)(2,1)}) %reduce-scatter.4.cloned.1.call-update) | async-done | bytes 57360
  53.3 1.7 %copy.33 = bf16[32,896]{1,0:T(8,128)(2,1)} copy(bf16[32,896]{0,1:T(8,128)(2,1)} %bitcast.118) | data formatting | bytes 114688
  55.0 4.6 %all-to-all-start.1 = ((bf16[4,8,896]{2,1,0:T(8,128)(2,1)}), bf16[4,8,896]{2,1,0:T(8,128)(2,1)S(1)}, u32[]{:S(2)}, u32[]{:S(2)}) async-start(bf16[4,8,896]{2,1,0:T(8,128)(2,1)} %bitcast.9), calls=%async_computation.1 | async-start | bytes 114688 | tf_op jit(solution)/shard_map/all_to_all | solution.py:65
  59.6 5.7 %all-to-all-done.1 = bf16[4,8,896]{2,1,0:T(8,128)(2,1)S(1)} async-done(((bf16[4,8,896]{2,1,0:T(8,128)(2,1)}), bf16[4,8,896]{2,1,0:T(8,128)(2,1)S(1)}, u32[]{:S(2)}, u32[]{:S(2)}) %all-to-all-start.1) | async-done | bytes 57376 | tf_op jit(solution)/shard_map/all_to_all | solution.py:65
  65.3 0.8 gather_fusion.15
  66.1 0.8 gather_fusion.14
  66.9 0.8 gather_fusion.13
  67.8 0.8 gather_fusion.12
  68.6 0.8 gather_fusion.11
  69.4 1.6 %gather_fusion.10 = f32[128,896]{1,0:T(8,128)} fusion(f32[32,896]{1,0:T(8,128)S(1)} %bitcast_convert_fusion, s32[1024]{0:T(1024)S(1)} %pad_clamp_fusion.5), kind=kCustom, calls=%fused_computation.10.clone | custom fusion | bytes 918016 | tf_op jit(solution)/shard_map/jit(_take)/gather | solution.py:15
  71.0 1.6 %gather_fusion.9 = f32[128,896]{1,0:T(8,128)} fusion(f32[32,896]{1,0:T(8,128)S(1)} %bitcast_convert_fusion, s32[1024]{0:T(1024)S(1)} %pad_clamp_fusion.6), kind=kCustom, calls=%fused_computation.9.clone | custom fusion | bytes 918016 | tf_op jit(solution)/shard_map/jit(_take)/gather | solution.py:18
  72.6 1.6 %gather_fusion.8 = f32[128,896]{1,0:T(8,128)} fusion(f32[32,896]{1,0:T(8,128)S(1)} %bitcast_convert_fusion, s32[1024]{0:T(1024)S(1)} %pad_clamp_fusion.7), kind=kCustom, calls=%fused_computation.8.clone | custom fusion | bytes 918016 | tf_op jit(solution)/shard_map/jit(_take)/gather | solution.py:15
  74.2 1.6 %gather_fusion.7 = f32[128,896]{1,0:T(8,128)} fusion(f32[32,896]{1,0:T(8,128)S(1)} %bitcast_convert_fusion, s32[1024]{0:T(1024)S(1)} %pad_clamp_fusion.8), kind=kCustom, calls=%fused_computation.7.clone | custom fusion | bytes 918016 | tf_op jit(solution)/shard_map/jit(_take)/gather | solution.py:18
  75.8 1.6 %gather_fusion.6 = f32[128,896]{1,0:T(8,128)} fusion(f32[32,896]{1,0:T(8,128)S(1)} %bitcast_convert_fusion, s32[1024]{0:T(1024)S(1)} %pad_clamp_fusion.9), kind=kCustom, calls=%fused_computation.6.clone | custom fusion | bytes 918016 | tf_op jit(solution)/shard_map/jit(_take)/gather | solution.py:15
  77.4 1.6 %gather_fusion.5 = f32[128,896]{1,0:T(8,128)} fusion(f32[32,896]{1,0:T(8,128)S(1)} %bitcast_convert_fusion, s32[1024]{0:T(1024)S(1)} %pad_clamp_fusion.10), kind=kCustom, calls=%fused_computation.5.clone | custom fusion | bytes 918016 | tf_op jit(solution)/shard_map/jit(_take)/gather | solution.py:18
  78.9 1.6 %gather_fusion.4 = f32[128,896]{1,0:T(8,128)} fusion(f32[32,896]{1,0:T(8,128)S(1)} %bitcast_convert_fusion, s32[1024]{0:T(1024)S(1)} %pad_clamp_fusion.11), kind=kCustom, calls=%fused_computation.4.clone | custom fusion | bytes 918016 | tf_op jit(solution)/shard_map/jit(_take)/gather | solution.py:15
  80.5 1.6 %gather_fusion.3 = f32[128,896]{1,0:T(8,128)} fusion(f32[32,896]{1,0:T(8,128)S(1)} %bitcast_convert_fusion, s32[1024]{0:T(1024)S(1)} %pad_clamp_fusion.12), kind=kCustom, calls=%fused_computation.3.clone | custom fusion | bytes 918016 | tf_op jit(solution)/shard_map/jit(_take)/gather | solution.py:18
  82.1 1.6 %gather_fusion.2 = f32[128,896]{1,0:T(8,128)} fusion(f32[32,896]{1,0:T(8,128)S(1)} %bitcast_convert_fusion, s32[1024]{0:T(1024)S(1)} %pad_clamp_fusion.13), kind=kCustom, calls=%fused_computation.2.clone | custom fusion | bytes 918016 | tf_op jit(solution)/shard_map/jit(_take)/gather | solution.py:15
  83.7 1.6 %gather_fusion.1 = f32[128,896]{1,0:T(8,128)} fusion(f32[32,896]{1,0:T(8,128)S(1)} %bitcast_convert_fusion, s32[1024]{0:T(1024)S(1)} %pad_clamp_fusion.14), kind=kCustom, calls=%fused_computation.1.clone | custom fusion | bytes 918016 | tf_op jit(solution)/shard_map/jit(_take)/gather | solution.py:18
  85.3 1.6 %gather_fusion = f32[128,896]{1,0:T(8,128)} fusion(f32[32,896]{1,0:T(8,128)S(1)} %bitcast_convert_fusion, s32[1024]{0:T(1024)S(1)} %pad_clamp_fusion.15), kind=kCustom, calls=%fused_computation.clone | custom fusion | bytes 918016 | tf_op jit(solution)/shard_map/jit(_take)/gather | solution.py:15
  86.8 3.7 %fusion.10 = bf16[128,896]{1,0:T(8,128)(2,1)} fusion(f32[128,896]{1,0:T(8,128)S(1)} %gather_fusion.15, f32[128,896]{1,0:T(8,128)S(1)} %gather_fusion.14, f32[128,896]{1,0:T(8,128)S(1)} %gather_fusion.13, f32[128,896]{1,0:T(8,128)S(1)} %gather_fusion.12, f32[128,896]{1,0:T(8,128)S(1)} %gather_fusion.11, f32[128,896]{1,0:T(8,128)} %gather_fusion.10, ...), kind=kLoop, calls=%fused_computation.29 | loop fusion | flops 5505024 | bytes 7576576 | tf_op jit(solution)/shard_map/convert_element_type | solution.py:75
  (30 shorter events, 0.3 us)
Async XLA Ops:
  6.5 22.2 %copy-start = (bf16[1,128,3584]{2,1,0:T(8,128)(2,1)S(1)}, bf16[1,128,3584]{2,1,0:T(8,128)(2,1)}, u32[]{:S(2)}) copy-start(bf16[1,128,3584]{2,1,0:T(8,128)(2,1)} %param.13) | copy-start | bytes 2752516
  6.5 3.3 %copy-start.3 = (bf16[128,896]{1,0:T(8,128)(2,1)S(1)}, bf16[128,896]{1,0:T(8,128)(2,1)}, u32[]{:S(2)}) copy-start(bf16[128,896]{1,0:T(8,128)(2,1)} %param.8) | copy-start | bytes 688132
  6.5 22.0 %copy-start.2 = (bf16[1,3584,128]{2,1,0:T(8,128)(2,1)S(1)}, bf16[1,3584,128]{2,1,0:T(8,128)(2,1)}, u32[]{:S(2)}) copy-start(bf16[1,3584,128]{2,1,0:T(8,128)(2,1)} %param.11) | copy-start | bytes 2752516
  10.7 18.1 %copy-start.1 = (bf16[1,3584,128]{2,1,0:T(8,128)(2,1)S(1)}, bf16[1,3584,128]{2,1,0:T(8,128)(2,1)}, u32[]{:S(2)}) copy-start(bf16[1,3584,128]{2,1,0:T(8,128)(2,1)} %param.12) | copy-start | bytes 2752516
  10.7 12.2 %all-to-all-start = ((bf16[4,8,896]{2,1,0:T(8,128)(2,1)}), bf16[4,8,896]{2,1,0:T(8,128)(2,1)S(1)}, u32[]{:S(2)}, u32[]{:S(2)}) async-start(bf16[4,8,896]{2,1,0:T(8,128)(2,1)} %fusion), calls=%async_computation | async-start | bytes 114688 | tf_op jit(solution)/shard_map/all_to_all | solution.py:53
  17.1 36.2 %reduce-scatter.4.cloned.1.call-start = ((), (), s32[]{:S(2)}) async-start(), calls=%async_computation.3 | async-start | bytes 1146880
  30.5 0.7 copy-start.4
  55.0 10.3 %all-to-all-start.1 = ((bf16[4,8,896]{2,1,0:T(8,128)(2,1)}), bf16[4,8,896]{2,1,0:T(8,128)(2,1)S(1)}, u32[]{:S(2)}, u32[]{:S(2)}) async-start(bf16[4,8,896]{2,1,0:T(8,128)(2,1)} %bitcast.9), calls=%async_computation.1 | async-start | bytes 114688 | tf_op jit(solution)/shard_map/all_to_all | solution.py:65
Sparse Core Ops, SparseCore 0:
  30.7 22.5 reduce-scatter.3
where the time goes:
time: 97.9 us; the launch traced here: 97.4 us
  waiting for transfers between devices  32.5 us (33%)
  local copies, waits for them, and re-layouts  26.8 us (27%)
  between operations  13.6 us (14%)
  starting transfers between devices  11 us (11%)
  other arithmetic  6.22 us (6%)
  blocking collectives  5.68 us (6%)
  matrix products  1.51 us (2%)
    unnamed x2, waiting for transfers between devices  22.1 us
    gather x8, local copies, waits for them, and re-layouts, combine_rows(): jnp.take(returned, jnp.maximum(first_cols[:, column], 0), axis=0)  11.1 us
    gather x8, local copies, waits for them, and re-layouts, combine_rows(): jnp.take(returned, jnp.maximum(second_cols[:, column], 0), axis=0)  10.4 us
    all_to_all x1, starting transfers between devices, shards(): lax.all_to_all(outgoing.reshape(ep_count, CAP, features_dev), 'ep', split...  6.45 us
    all_to_all x1, waiting for transfers between devices, shards(): lax.all_to_all(expert_out.reshape(ep_count, CAP, features_dev).astype(jnp...  5.71 us
    all_gather x1, blocking collectives, shards(): block_cols = lax.all_gather(local_slots, 'tp', axis=1, tiled=True)  5.68 us
    all_to_all x1, waiting for transfers between devices, shards(): lax.all_to_all(outgoing.reshape(ep_count, CAP, features_dev), 'ep', split...  4.75 us
    all_to_all x1, starting transfers between devices, shards(): lax.all_to_all(expert_out.reshape(ep_count, CAP, features_dev).astype(jnp...  4.59 us
  transfers between devices with their start and end apart: 3, of which 3 were waited for; matrix products, arithmetic and copies ran while one was open for 1% of the time, Pallas kernels for 0%

commit v1 on v0

v1 whole, which is shorter than its diff:
```python
import jax
import jax.numpy as jnp
from jax import lax
from jax.experimental import pallas as pl
from jax.experimental.pallas import tpu as pltpu
from jax.sharding import PartitionSpec as P

CAP = 8


def route(ep_count, ids_ref, scores_ref, tokens_ref, outgoing_ref, match_ref, weight_ref):
    row_count = ids_ref.shape[0]
    slot_rows = outgoing_ref.shape[0]
    ids = ids_ref[...].astype(jnp.float32)
    expert = jnp.min(ids, axis=1, keepdims=True)
    squashed = jax.nn.sigmoid(scores_ref[...])
    chosen = jnp.sum(jnp.where(ids == expert, squashed, 0.0), axis=1, keepdims=True)
    weight_ref[...] = 2.5 * chosen / jnp.sum(squashed, axis=1, keepdims=True)
    lanes = lax.broadcasted_iota(jnp.int32, (row_count, 128), 1).astype(jnp.float32)
    onehot = jnp.where(expert == lanes, 1.0, 0.0)
    earlier = jnp.where(
        lax.broadcasted_iota(jnp.int32, (row_count, row_count), 1)
        < lax.broadcasted_iota(jnp.int32, (row_count, row_count), 0),
        1.0,
        0.0,
    ).astype(jnp.bfloat16)
    counts = jnp.dot(earlier, onehot.astype(jnp.bfloat16), preferred_element_type=jnp.float32)
    slot = jnp.sum(counts * onehot, axis=1, keepdims=True)
    code = expert * CAP + slot
    column = lax.broadcasted_iota(jnp.int32, (row_count, slot_rows), 1)
    index = lax.rem(column, ep_count * CAP)
    wanted = (index // (2 * CAP)) * CAP + lax.rem(index, CAP)
    match = jnp.where(code == wanted.astype(jnp.float32), 1.0, 0.0).astype(jnp.bfloat16)
    match_ref[...] = match
    outgoing_ref[...] = lax.dot_general(
        match, tokens_ref[...], (((0,), (0,)), ((), ())), preferred_element_type=jnp.float32
    ).astype(jnp.bfloat16)


def experts(tp_count, rows_ref, gate_ref, up_ref, down_ref, out_ref):
    slot_count = rows_ref.shape[0] // tp_count
    features = rows_ref.shape[1]
    gate_act = jnp.zeros((slot_count, gate_ref.shape[2]), jnp.float32)
    up_act = jnp.zeros((slot_count, up_ref.shape[2]), jnp.float32)
    for part in range(tp_count):
        rows = rows_ref[part * slot_count : (part + 1) * slot_count, :]
        columns = slice(part * features, (part + 1) * features)
        gate_act += jnp.dot(rows, gate_ref[0, columns, :], preferred_element_type=jnp.float32)
        up_act += jnp.dot(rows, up_ref[0, columns, :], preferred_element_type=jnp.float32)
    hidden = (gate_act / (1.0 + jnp.exp(-gate_act)) * up_act).astype(jnp.bfloat16)
    for part in range(tp_count):
        columns = slice(part * features, (part + 1) * features)
        out_ref[part * slot_count : (part + 1) * slot_count, :] = jnp.dot(
            hidden, down_ref[0, :, columns], preferred_element_type=jnp.float32
        ).astype(jnp.bfloat16)


def combine(match_ref, weight_ref, returned_ref, out_ref):
    summed = jnp.dot(match_ref[...], returned_ref[...], preferred_element_type=jnp.float32)
    out_ref[...] = (weight_ref[...] * summed).astype(jnp.bfloat16)


def shards(tokens, expert_ids, route_scores, w_gate, w_up, w_down):
    row_count, features = tokens.shape
    ep_count, tp_count = lax.axis_size("ep"), lax.axis_size("tp")
    slot_rows = ep_count * tp_count * CAP
    limit = pltpu.CompilerParams(vmem_limit_bytes=32 * 1024 * 1024)
    outgoing, match, weight = pl.pallas_call(
        lambda *refs: route(ep_count, *refs),
        out_shape=(
            jax.ShapeDtypeStruct((slot_rows, features), jnp.bfloat16),
            jax.ShapeDtypeStruct((row_count, slot_rows), jnp.bfloat16),
            jax.ShapeDtypeStruct((row_count, 1), jnp.float32),
        ),
        compiler_params=limit,
        name="route",
    )(expert_ids, route_scores, tokens)
    incoming = lax.all_to_all(outgoing, ("tp", "ep"), split_axis=0, concat_axis=0, tiled=True)
    partial_value = pl.pallas_call(
        lambda *refs: experts(tp_count, *refs),
        out_shape=jax.ShapeDtypeStruct((slot_rows, features), jnp.bfloat16),
        compiler_params=limit,
        name="experts",
    )(incoming, w_gate, w_up, w_down)
    returned = lax.all_to_all(partial_value, ("tp", "ep"), split_axis=0, concat_axis=0, tiled=True)
    return pl.pallas_call(
        combine,
        out_shape=jax.ShapeDtypeStruct((row_count, features), jnp.bfloat16),
        compiler_params=limit,
        name="combine",
    )(match, weight, returned)


def solution(mesh):
    placed = (
        P(("groups", "ep"), "tp"),
        P(("groups", "ep"), None),
        P(("groups", "ep"), None),
        P("ep", None, "tp"),
        P("ep", None, "tp"),
        P("ep", "tp", None),
    )
    return jax.shard_map(
        shards, mesh=mesh, in_specs=placed, out_specs=P(("groups", "ep"), "tp"), check_vma=False
    )
```

time: 97.9 us -> 36.2 us (0.37)
  waiting for transfers between devices: 32.5 us -> 0 us
  blocking collectives: 5.68 us -> 28.9 us
  local copies, waits for them, and re-layouts: 26.8 us -> 4.95 us
  between operations: 13.6 us -> 0.02 us
  starting transfers between devices: 11 us -> 0 us
  other arithmetic: 6.22 us -> 0 us
  Pallas kernels: 0 us -> 2.08 us
  matrix products: 1.51 us -> 0 us
    all_to_all x0 -> x2, blocking collectives: none -> 28.9 us  [the longest x1 16.4 us: shards(): lax.all_to_all(outgoing, ('tp', 'ep'), split_axis=0, concat_axis=0, tiled...]
    unnamed x2 -> x0, waiting for transfers between devices: 22.1 us -> none
    gather x16 -> x0, local copies, waits for them, and re-layouts: 21.5 us -> none  [the longest x8 11.1 us: combine_rows(): jnp.take(returned, jnp.maximum(first_cols[:, column], 0), axis=0)]
    all_to_all x2 -> x0, starting transfers between devices: 11 us -> none  [the longest x1 6.45 us: shards(): lax.all_to_all(outgoing.reshape(ep_count, CAP, features_dev), 'ep', split...]
    all_to_all x2 -> x0, waiting for transfers between devices: 10.5 us -> none  [the longest x1 5.71 us: shards(): lax.all_to_all(expert_out.reshape(ep_count, CAP, features_dev).astype(jnp...]
    all_gather x1 -> x0, blocking collectives: 5.68 us -> none  [shards(): block_cols = lax.all_gather(local_slots, 'tp', axis=1, tiled=True)]
    convert_element_type x2 -> x0, other arithmetic: 3.71 us -> none  [the longest x1 3.71 us: shards(): return mixed.astype(jnp.bfloat16)]
    pallas_call x0 -> x3, Pallas kernels: none -> 2.08 us  [the longest x1 0.9 us: shards(): pl.pallas_call(combine, out_shape=jax.ShapeDtypeStruct((row_count, featur...]
  transfers between devices with their start and end apart: 3 -> 0, of which waited for: 3 -> 0; matrix products, arithmetic and copies ran while one was open for 1% -> 0% of each run, Pallas kernels for 0% -> 0%
where the time goes in v1:
time: 36.2 us; the launch traced here: 35.9 us
  blocking collectives  28.9 us (80%)
  local copies, waits for them, and re-layouts  4.95 us (14%)
  Pallas kernels  2.08 us (6%)
    all_to_all x1, blocking collectives, shards(): lax.all_to_all(outgoing, ('tp', 'ep'), split_axis=0, concat_axis=0, tiled...  16.4 us
    all_to_all x1, blocking collectives, shards(): lax.all_to_all(partial_value, ('tp', 'ep'), split_axis=0, concat_axis=0,...  12.5 us
    unnamed x10, local copies, waits for them, and re-layouts  4.95 us
    pallas_call x1, Pallas kernels, shards(): pl.pallas_call(combine, out_shape=jax.ShapeDtypeStruct((row_count, featur...  0.9 us

profile of v1, /device:TPU:0, one launch (start us, length us, event | category | flops | bytes accessed | tf_op | source)
XLA Modules:
  0.0 35.9 jit_solution(8642456097981560393)
XLA Ops:
  0.0 0.0 copy-start
  0.0 0.9 %copy.7.refs_0_ = s32[128,8]{1,0:T(8,128)S(1)} copy(s32[128,8]{0,1:T(8,128)} %param.7) | data formatting | bytes 8192 | tf_op args[1]
  0.9 0.8 %copy.8.refs_1_ = f32[128,8]{1,0:T(8,128)S(1)} copy(f32[128,8]{0,1:T(8,128)} %param.8) | data formatting | bytes 8192 | tf_op args[2]
  1.7 0.0 copy-start.3
  1.7 0.9 %copy-done.3 = bf16[128,896]{1,0:T(8,128)(2,1)S(1)} copy-done((bf16[128,896]{1,0:T(8,128)(2,1)S(1)}, bf16[128,896]{1,0:T(8,128)(2,1)}, u32[]{:S(2)}) %copy-start.3) | copy-done | bytes 229400
  2.6 0.5 %route.1 = (bf16[128,896]{1,0:T(8,128)(2,1)S(1)}, bf16[128,128]{1,0:T(8,128)(2,1)S(1)}, f32[128,1]{1,0:T(8,128)S(1)}) custom-call(s32[128,8]{1,0:T(8,128)S(1)} %copy.7.refs_0_, f32[128,8]{1,0:T(8,128)S(1)} %copy.8.refs_1_, bf16[128,896]{1,0:T(8,128)(2,1)S(1)} %copy-done.3), custom_call_target="tpu_custom_call" | custom-call | tf_op jit(solution)/shard_map/route/pallas_call | solution.py:68
  3.1 16.4 %all_to_all.22 = bf16[16,8,896]{2,1,0:T(8,128)(2,1)S(1)} all-to-all(bf16[16,8,896]{2,1,0:T(8,128)(2,1)S(1)} %bitcast.7), channel_id=1, replica_groups=mesh['groups'=2,'ep'=4,'tp'=4] {'tp','ep'}, dimensions={0} | all-to-all | bytes 458752 | tf_op jit(solution)/shard_map/all_to_all | solution.py:78
  19.5 0.0 copy-done
  19.5 0.0 copy-start.1
  19.5 1.2 %copy-done.1 = bf16[1,3584,128]{2,1,0:T(8,128)(2,1)S(1)} copy-done((bf16[1,3584,128]{2,1,0:T(8,128)(2,1)S(1)}, bf16[1,3584,128]{2,1,0:T(8,128)(2,1)}, u32[]{:S(2)}) %copy-start.1) | copy-done | bytes 917528
  20.7 0.0 copy-start.2
  20.7 1.2 %copy-done.2 = bf16[1,128,3584]{2,1,0:T(8,128)(2,1)S(1)} copy-done((bf16[1,128,3584]{2,1,0:T(8,128)(2,1)S(1)}, bf16[1,128,3584]{2,1,0:T(8,128)(2,1)}, u32[]{:S(2)}) %copy-start.2) | copy-done | bytes 917528
  21.9 0.6 %experts.1 = bf16[128,896]{1,0:T(8,128)(2,1)S(1)} custom-call(bf16[128,896]{1,0:T(8,128)(2,1)S(1)} %bitcast.4, bf16[1,3584,128]{2,1,0:T(8,128)(2,1)S(1)} %copy-done, bf16[1,3584,128]{2,1,0:T(8,128)(2,1)S(1)} %copy-done.1, bf16[1,128,3584]{2,1,0:T(8,128)(2,1)S(1)} %copy-done.2), custom_call_target="tpu_custom_call" | custom-call | tf_op jit(solution)/shard_map/experts/pallas_call | solution.py:79
  22.5 12.5 %all_to_all.23 = bf16[16,8,896]{2,1,0:T(8,128)(2,1)S(1)} all-to-all(bf16[16,8,896]{2,1,0:T(8,128)(2,1)S(1)} %bitcast.5), channel_id=1, replica_groups=mesh['groups'=2,'ep'=4,'tp'=4] {'tp','ep'}, dimensions={0} | all-to-all | bytes 458752 | tf_op jit(solution)/shard_map/all_to_all | solution.py:85
  35.0 0.9 %combine.1 = bf16[128,896]{1,0:T(8,128)(2,1)} custom-call(bf16[128,128]{1,0:T(8,128)(2,1)S(1)} %get-tuple-element.8.match_ref, f32[128,1]{1,0:T(8,128)S(1)} %get-tuple-element.9.weight_ref, bf16[128,896]{1,0:T(8,128)(2,1)S(1)} %bitcast.6), custom_call_target="tpu_custom_call" | custom-call | tf_op jit(solution)/shard_map/combine/pallas_call | solution.py:86
Async XLA Ops:
  0.0 19.5 %copy-start = (bf16[1,3584,128]{2,1,0:T(8,128)(2,1)S(1)}, bf16[1,3584,128]{2,1,0:T(8,128)(2,1)}, u32[]{:S(2)}) copy-start(bf16[1,3584,128]{2,1,0:T(8,128)(2,1)} %refs_1_.2) | copy-start | bytes 2752516
  1.7 0.9 %copy-start.3 = (bf16[128,896]{1,0:T(8,128)(2,1)S(1)}, bf16[128,896]{1,0:T(8,128)(2,1)}, u32[]{:S(2)}) copy-start(bf16[128,896]{1,0:T(8,128)(2,1)} %refs_2_.2) | copy-start | bytes 688132
  19.5 1.2 %copy-start.1 = (bf16[1,3584,128]{2,1,0:T(8,128)(2,1)S(1)}, bf16[1,3584,128]{2,1,0:T(8,128)(2,1)}, u32[]{:S(2)}) copy-start(bf16[1,3584,128]{2,1,0:T(8,128)(2,1)} %refs_2_.3) | copy-start | bytes 2752516
  20.7 1.2 %copy-start.2 = (bf16[1,128,3584]{2,1,0:T(8,128)(2,1)S(1)}, bf16[1,128,3584]{2,1,0:T(8,128)(2,1)}, u32[]{:S(2)}) copy-start(bf16[1,128,3584]{2,1,0:T(8,128)(2,1)} %refs_3_.1) | copy-start | bytes 2752516

commit v2 on v1

v2 whole, which is shorter than its diff:
```python
import jax
import jax.numpy as jnp
from jax import lax
from jax.experimental import pallas as pl
from jax.experimental.pallas import tpu as pltpu
from jax.sharding import PartitionSpec as P

CAP = 8
AXES = ("tp", "ep")
LIMIT = pltpu.CompilerParams(vmem_limit_bytes=16 * 1024 * 1024)


def iota(shape, dim):
    return lax.broadcasted_iota(jnp.int32, shape, dim)


def to_column(row):
    size = row.shape[1]
    square = (size, size)
    return jnp.sum(jnp.where(iota(square, 0) == iota(square, 1), row, 0.0), axis=1, keepdims=True)


def route(ep_count, resident, gathered, ids_ref, scores_ref, tokens_ref, outgoing_ref, match_ref, weight_ref):
    row_count = ids_ref.shape[1]
    slot_rows = match_ref.shape[1]
    ids = ids_ref[...].astype(jnp.float32)
    expert = jnp.min(ids, axis=0, keepdims=True)
    squashed = jax.nn.sigmoid(scores_ref[...])
    chosen = jnp.sum(jnp.where(ids == expert, squashed, 0.0), axis=0, keepdims=True)
    weight = 2.5 * chosen / jnp.sum(squashed, axis=0, keepdims=True)
    onehot_shape = (-(-resident // 16) * 16, row_count)
    onehot = jnp.where(expert == iota(onehot_shape, 0).astype(jnp.float32), 1.0, 0.0)
    square = (row_count, row_count)
    earlier = jnp.where(iota(square, 0) < iota(square, 1), 1.0, 0.0).astype(jnp.bfloat16)
    counts = jnp.dot(onehot.astype(jnp.bfloat16), earlier, preferred_element_type=jnp.float32)
    code = expert * CAP + jnp.sum(counts * onehot, axis=0, keepdims=True)
    send_rows = outgoing_ref.shape[0]
    row = iota((send_rows, row_count), 0)
    if gathered:
        wanted = row
    else:
        index = lax.rem(row, ep_count * CAP)
        wanted = (index // (2 * CAP)) * CAP + lax.rem(index, CAP)
    dispatch = jnp.where(code == wanted.astype(jnp.float32), 1.0, 0.0).astype(jnp.bfloat16)
    outgoing_ref[...] = jnp.dot(
        dispatch, tokens_ref[...], preferred_element_type=jnp.float32
    ).astype(jnp.bfloat16)
    column = iota((row_count, slot_rows), 1)
    source = lax.rem(column // CAP, ep_count)
    if gathered:
        source = lax.rem(lax.axis_index("ep") + ep_count - source, ep_count)
    returned = (source // 2) * CAP + lax.rem(column, CAP)
    match_ref[...] = jnp.where(to_column(code) == returned.astype(jnp.float32), 1.0, 0.0).astype(
        jnp.bfloat16
    )
    weight_ref[...] = to_column(weight)


def experts(ep_count, tp_count, resident, gathered, rows_ref, gate_ref, up_ref, down_ref, *out_refs):
    features = down_ref.shape[2] // tp_count
    part_rows = resident * ep_count * CAP if gathered else rows_ref.shape[0] // tp_count
    gate_act = jnp.zeros((part_rows, gate_ref.shape[2]), jnp.float32)
    up_act = jnp.zeros((part_rows, up_ref.shape[2]), jnp.float32)
    for part in range(tp_count):
        columns = slice(part * features, (part + 1) * features)
        if gathered:
            offsets = [(block * tp_count + part) * features for block in range(ep_count)]
            rows = jnp.concatenate([rows_ref[:, at : at + features] for at in offsets], axis=0)
        else:
            rows = rows_ref[part * part_rows : (part + 1) * part_rows, :]
        gate_act += jnp.dot(rows, gate_ref[0, columns, :], preferred_element_type=jnp.float32)
        up_act += jnp.dot(rows, up_ref[0, columns, :], preferred_element_type=jnp.float32)
    hidden = (gate_act / (1.0 + jnp.exp(-gate_act)) * up_act).astype(jnp.bfloat16)
    if not gathered:
        for part in range(tp_count):
            columns = slice(part * features, (part + 1) * features)
            out_refs[0][part * part_rows : (part + 1) * part_rows, :] = jnp.dot(
                hidden, down_ref[0, :, columns], preferred_element_type=jnp.float32
            ).astype(jnp.bfloat16)
        return
    here, lane = lax.axis_index("ep"), lax.axis_index("tp")
    picked_shape = (ep_count * CAP, part_rows)
    picked_row, held_row = iota(picked_shape, 0), iota(picked_shape, 1)
    block = lax.rem(here + picked_row // CAP, ep_count)
    origin = (block * resident + here // 2) * CAP + lax.rem(picked_row, CAP)
    pick = jnp.where(held_row == origin, 1.0, 0.0).astype(jnp.bfloat16)
    picked = jnp.dot(pick, hidden, preferred_element_type=jnp.float32).astype(jnp.bfloat16)
    for part in range(tp_count):
        start = pl.multiple_of(lax.rem(lane + part, tp_count) * features, features)
        values = jnp.dot(
            picked, down_ref[0, :, pl.ds(start, features)], preferred_element_type=jnp.float32
        ).astype(jnp.bfloat16)
        for block in range(ep_count):
            out_refs[part * ep_count + block][...] = values[block * CAP : (block + 1) * CAP, :]


def combine(match_ref, weight_ref, *refs):
    returned = jnp.concatenate([ref[...] for ref in refs[:-1]], axis=0)
    summed = jnp.dot(match_ref[...], returned, preferred_element_type=jnp.float32)
    refs[-1][...] = (weight_ref[...] * summed).astype(jnp.bfloat16)


def shards(tokens, expert_ids, route_scores, w_gate, w_up, w_down):
    row_count, features = tokens.shape
    ep_count, tp_count = lax.axis_size("ep"), lax.axis_size("tp")
    resident = ep_count // 2
    peers = ep_count * tp_count
    gathered = peers <= 16
    slot_rows = peers * CAP
    outgoing, match, weight = pl.pallas_call(
        lambda *refs: route(ep_count, resident, gathered, *refs),
        out_shape=(
            jax.ShapeDtypeStruct((resident * CAP if gathered else slot_rows, features), jnp.bfloat16),
            jax.ShapeDtypeStruct((row_count, slot_rows), jnp.bfloat16),
            jax.ShapeDtypeStruct((row_count, 1), jnp.float32),
        ),
        compiler_params=LIMIT,
        name="route",
    )(expert_ids.T, route_scores.T, tokens)
    if gathered:
        incoming = lax.all_gather(outgoing, ("ep", "tp"), axis=1, tiled=True)
        chunk = jax.ShapeDtypeStruct((CAP, features), jnp.bfloat16)
        partial_shape = (chunk,) * peers
    else:
        incoming = lax.all_to_all(outgoing, AXES, split_axis=0, concat_axis=0, tiled=True)
        partial_shape = (jax.ShapeDtypeStruct((slot_rows, features), jnp.bfloat16),)
    partial_values = pl.pallas_call(
        lambda *refs: experts(ep_count, tp_count, resident, gathered, *refs),
        out_shape=partial_shape,
        compiler_params=LIMIT,
        name="experts",
    )(incoming, w_gate, w_up, w_down)
    if gathered:
        returned = list(partial_values)
        for part in range(tp_count):
            for block in range(ep_count):
                which = part * ep_count + block
                if which:
                    pairs = [
                        (z * tp_count + f, (z + block) % ep_count * tp_count + (f + part) % tp_count)
                        for f in range(tp_count)
                        for z in range(ep_count)
                    ]
                    returned[which] = lax.ppermute(partial_values[which], ("ep", "tp"), pairs)
    else:
        returned = [
            lax.all_to_all(partial_values[0], AXES, split_axis=0, concat_axis=0, tiled=True)
        ]
    return pl.pallas_call(
        combine,
        out_shape=jax.ShapeDtypeStruct((row_count, features), jnp.bfloat16),
        compiler_params=LIMIT,
        name="combine",
    )(match, weight, *returned)


def solution(mesh):
    placed = (
        P(("groups", "ep"), "tp"),
        P(("groups", "ep"), None),
        P(("groups", "ep"), None),
        P("ep", None, "tp"),
        P("ep", None, "tp"),
        P("ep", "tp", None),
    )
    return jax.shard_map(
        shards, mesh=mesh, in_specs=placed, out_specs=P(("groups", "ep"), "tp"), check_vma=False
    )
```

time: 36.2 us -> 55.5 us (1.53)
  starting transfers between devices: 0 us -> 19.9 us
  blocking collectives: 28.9 us -> 24.3 us
  waiting for transfers between devices: 0 us -> 3.15 us
  local copies, waits for them, and re-layouts: 4.95 us -> 5.85 us
    all_to_all x2 -> x0, blocking collectives: 28.9 us -> none  [the longest x1 16.4 us: shards(): lax.all_to_all(outgoing, ('tp', 'ep'), split_axis=0, concat_axis=0, tiled...]
    all_gather x0 -> x1, blocking collectives: none -> 24.3 us  [shards(): incoming = lax.all_gather(outgoing, ('ep', 'tp'), axis=1, tiled=True)]
    ppermute x0 -> x15, starting transfers between devices: none -> 19.9 us  [shards(): returned[which] = lax.ppermute(partial_values[which], ('ep', 'tp'), pairs)]
    ppermute x0 -> x15, waiting for transfers between devices: none -> 3.15 us  [shards(): returned[which] = lax.ppermute(partial_values[which], ('ep', 'tp'), pairs)]
    unnamed x10 -> x12, local copies, waits for them, and re-layouts: 4.95 us -> 5.85 us
  transfers between devices with their start and end apart: 0 -> 15, of which waited for: 0 -> 2; matrix products, arithmetic and copies ran while one was open for 0% -> 0% of each run, Pallas kernels for 0% -> 0%
where the time goes in v2:
time: 55.5 us; the launch traced here: 55.2 us
  blocking collectives  24.3 us (44%)
  starting transfers between devices  19.9 us (36%)
  local copies, waits for them, and re-layouts  5.85 us (11%)
  waiting for transfers between devices  3.15 us (6%)
  Pallas kernels  1.98 us (4%)
    all_gather x1, blocking collectives, shards(): incoming = lax.all_gather(outgoing, ('ep', 'tp'), axis=1, tiled=True)  24.3 us
    ppermute x15, starting transfers between devices, shards(): returned[which] = lax.ppermute(partial_values[which], ('ep', 'tp'), pairs)  19.9 us
    unnamed x12, local copies, waits for them, and re-layouts  5.85 us
    ppermute x15, waiting for transfers between devices, shards(): returned[which] = lax.ppermute(partial_values[which], ('ep', 'tp'), pairs)  3.15 us
  transfers between devices with their start and end apart: 15, of which 2 were waited for; matrix products, arithmetic and copies ran while one was open for 0% of the time, Pallas kernels for 0%

profile of v2, /device:TPU:0, one launch (start us, length us, event | category | flops | bytes accessed | tf_op | source)
XLA Modules:
  0.0 55.2 jit_solution(12203519504109591521)
XLA Ops:
  0.0 0.0 copy-start.3
  0.0 0.9 %copy-done.3 = bf16[128,896]{1,0:T(8,128)(2,1)S(1)} copy-done((bf16[128,896]{1,0:T(8,128)(2,1)S(1)}, bf16[128,896]{1,0:T(8,128)(2,1)}, u32[]{:S(2)}) %copy-start.3) | copy-done | bytes 229400
  0.9 0.0 copy-start.4
  0.9 0.7 %copy-done.4 = s32[128,8]{0,1:T(8,128)S(1)} copy-done((s32[128,8]{0,1:T(8,128)S(1)}, s32[128,8]{0,1:T(8,128)}, u32[]{:S(2)}) %copy-start.4) | copy-done | bytes 4120
  1.6 0.0 copy-start.5
  1.6 0.7 %copy-done.5 = f32[128,8]{0,1:T(8,128)S(1)} copy-done((f32[128,8]{0,1:T(8,128)S(1)}, f32[128,8]{0,1:T(8,128)}, u32[]{:S(2)}) %copy-start.5) | copy-done | bytes 4120
  2.3 0.3 route.1
  2.6 24.3 %all_gather.3.refs_0_ = bf16[16,14336]{1,0:T(8,128)(2,1)S(1)} all-gather(bf16[16,896]{1,0:T(8,128)(2,1)S(1)} %get-tuple-element.26), channel_id=1, replica_groups=mesh['groups'=2,'ep'=4,'tp'=4] {'ep','tp'}, dimensions={1}, use_global_device_ids=true | all-gather | bytes 487424 | tf_op jit(solution)/shard_map/all_gather | solution.py:121
  26.9 0.0 copy-start
  26.9 1.2 %copy-done = bf16[1,3584,128]{2,1,0:T(8,128)(2,1)S(1)} copy-done((bf16[1,3584,128]{2,1,0:T(8,128)(2,1)S(1)}, bf16[1,3584,128]{2,1,0:T(8,128)(2,1)}, u32[]{:S(2)}) %copy-start) | copy-done | bytes 917528
  28.1 0.0 copy-start.1
  28.1 1.2 %copy-done.1 = bf16[1,3584,128]{2,1,0:T(8,128)(2,1)S(1)} copy-done((bf16[1,3584,128]{2,1,0:T(8,128)(2,1)S(1)}, bf16[1,3584,128]{2,1,0:T(8,128)(2,1)}, u32[]{:S(2)}) %copy-start.1) | copy-done | bytes 917528
  29.3 0.0 copy-start.2
  29.3 1.2 %copy-done.2 = bf16[1,128,3584]{2,1,0:T(8,128)(2,1)S(1)} copy-done((bf16[1,128,3584]{2,1,0:T(8,128)(2,1)S(1)}, bf16[1,128,3584]{2,1,0:T(8,128)(2,1)}, u32[]{:S(2)}) %copy-start.2) | copy-done | bytes 917528
  30.4 0.8 %experts.1 = (bf16[8,896]{1,0:T(8,128)(2,1)S(1)}, bf16[8,896]{1,0:T(8,128)(2,1)S(1)}, bf16[8,896]{1,0:T(8,128)(2,1)S(1)}, bf16[8,896]{1,0:T(8,128)(2,1)S(1)}, bf...) custom-call(bf16[16,14336]{1,0:T(8,128)(2,1)S(1)} %all_gather.3.refs, ...), custom_call_target="tpu_custom_call" | custom-call | tf_op jit(solution)/shard_map/experts/pallas_call | solution.py:127
  31.2 0.1 collective-permute-start
  31.3 0.1 collective-permute-start.1
  31.4 3.7 %collective-permute-start.2 = (bf16[8,896]{1,0:T(8,128)(2,1)S(1)}, bf16[8,896]{1,0:T(8,128)(2,1)S(1)}, u32[]{:S(2)}, u32[]{:S(2)}) collective-permute-start(bf16[8,896]{1,0:T(8,128)(2,1)S(1)} %get-tuple-element.30), channel_id=1, source_target_pairs={{0,12},{4,0},{8,4},{12,8},{1,13},{5,1},{9,5},{13,9},{2,14},{6,2},{... | collective-permute-start | bytes 43016 | tf_op jit(solution)/shard_map/ppermute | solution.py:144
  35.1 0.0 collective-permute-start.3
  35.1 0.0 collective-permute-start.4
  35.1 1.7 %collective-permute-done.refs_1_ = bf16[8,896]{1,0:T(8,128)(2,1)S(1)} collective-permute-done((bf16[8,896]{1,0:T(8,128)(2,1)S(1)}, bf16[8,896]{1,0:T(8,128)(2,1)S(1)}, u32[]{:S(2)}, u32[]{:S(2)}) %collective-permute-start) | collective-permute-done | bytes 14368 | tf_op jit(solution)/shard_map/ppermute | solution.py:144
  36.8 0.0 collective-permute-start.5
  36.8 0.0 collective-permute-done.1.refs_2_
  36.8 4.2 %collective-permute-start.6 = (bf16[8,896]{1,0:T(8,128)(2,1)S(1)}, bf16[8,896]{1,0:T(8,128)(2,1)S(1)}, u32[]{:S(2)}, u32[]{:S(2)}) collective-permute-start(bf16[8,896]{1,0:T(8,128)(2,1)S(1)} %get-tuple-element.34), channel_id=1, source_target_pairs={{0,13},{4,1},{8,5},{12,9},{1,14},{5,2},{9,6},{13,10},{2,15},{6,3},... | collective-permute-start | bytes 43016 | tf_op jit(solution)/shard_map/ppermute | solution.py:144
  41.0 0.0 collective-permute-done.2.refs_3_
  41.0 0.0 collective-permute-start.7
  41.0 0.0 collective-permute-done.3.refs_4_
  41.0 0.1 collective-permute-start.8
  41.1 0.0 collective-permute-done.4.refs_5_
  41.1 2.8 %collective-permute-start.9 = (bf16[8,896]{1,0:T(8,128)(2,1)S(1)}, bf16[8,896]{1,0:T(8,128)(2,1)S(1)}, u32[]{:S(2)}, u32[]{:S(2)}) collective-permute-start(bf16[8,896]{1,0:T(8,128)(2,1)S(1)} %get-tuple-element.37), channel_id=1, source_target_pairs={{0,10},{4,14},{8,2},{12,6},{1,11},{5,15},{9,3},{13,7},{2,8},{6,12}... | collective-permute-start | bytes 43016 | tf_op jit(solution)/shard_map/ppermute | solution.py:144
  43.9 0.0 collective-permute-done.5.refs_6_
  43.9 3.3 %collective-permute-start.10 = (bf16[8,896]{1,0:T(8,128)(2,1)S(1)}, bf16[8,896]{1,0:T(8,128)(2,1)S(1)}, u32[]{:S(2)}, u32[]{:S(2)}) collective-permute-start(bf16[8,896]{1,0:T(8,128)(2,1)S(1)} %get-tuple-element.38), channel_id=1, source_target_pairs={{0,14},{4,2},{8,6},{12,10},{1,15},{5,3},{9,7},{13,11},{2,12},{6,0}... | collective-permute-start | bytes 43016 | tf_op jit(solution)/shard_map/ppermute | solution.py:144
  47.2 0.0 collective-permute-done.6.refs_7_
  47.2 0.0 collective-permute-start.11
  47.2 0.0 collective-permute-done.7.refs_8_
  47.2 0.7 %collective-permute-start.12 = (bf16[8,896]{1,0:T(8,128)(2,1)S(1)}, bf16[8,896]{1,0:T(8,128)(2,1)S(1)}, u32[]{:S(2)}, u32[]{:S(2)}) collective-permute-start(bf16[8,896]{1,0:T(8,128)(2,1)S(1)} %get-tuple-element.40), channel_id=1, source_target_pairs={{0,7},{4,11},{8,15},{12,3},{1,4},{5,8},{9,12},{13,0},{2,5},{6,9},{... | collective-permute-start | bytes 43016 | tf_op jit(solution)/shard_map/ppermute | solution.py:144
  47.9 0.0 collective-permute-done.8.refs_9_
  47.9 1.0 %collective-permute-start.13 = (bf16[8,896]{1,0:T(8,128)(2,1)S(1)}, bf16[8,896]{1,0:T(8,128)(2,1)S(1)}, u32[]{:S(2)}, u32[]{:S(2)}) collective-permute-start(bf16[8,896]{1,0:T(8,128)(2,1)S(1)} %get-tuple-element.41), channel_id=1, source_target_pairs={{0,11},{4,15},{8,3},{12,7},{1,8},{5,12},{9,0},{13,4},{2,9},{6,13},... | collective-permute-start | bytes 43016 | tf_op jit(solution)/shard_map/ppermute | solution.py:144
  48.9 0.0 collective-permute-done.9.refs_10_
  48.9 4.0 %collective-permute-start.14 = (bf16[8,896]{1,0:T(8,128)(2,1)S(1)}, bf16[8,896]{1,0:T(8,128)(2,1)S(1)}, u32[]{:S(2)}, u32[]{:S(2)}) collective-permute-start(bf16[8,896]{1,0:T(8,128)(2,1)S(1)} %get-tuple-element.42), channel_id=1, source_target_pairs={{0,15},{4,3},{8,7},{12,11},{1,12},{5,0},{9,4},{13,8},{2,13},{6,1},... | collective-permute-start | bytes 43016 | tf_op jit(solution)/shard_map/ppermute | solution.py:144
  52.9 0.0 collective-permute-done.10.refs_11_
  52.9 0.0 collective-permute-done.11.refs_12_
  52.9 0.0 collective-permute-done.12.refs_13_
  52.9 0.0 collective-permute-done.13.refs_14_
  52.9 1.4 %collective-permute-done.14.refs_15_ = bf16[8,896]{1,0:T(8,128)(2,1)S(1)} collective-permute-done((bf16[8,896]{1,0:T(8,128)(2,1)S(1)}, bf16[8,896]{1,0:T(8,128)(2,1)S(1)}, u32[]{:S(2)}, u32[]{:S(2)}) %collective-permute-start.14) | collective-permute-done | bytes 14368 | tf_op jit(solution)/shard_map/ppermute | solution.py:144
  54.3 0.9 %combine.1 = bf16[128,896]{1,0:T(8,128)(2,1)} custom-call(bf16[128,128]{1,0:T(8,128)(2,1)S(1)} %get-tuple-element.24.match_ref, f32[128,1]{1,0:T(8,128)S(1)} %get-tuple-element.25.weight_ref, bf16[8,896]{1,0:T(8,128)(2,1)S(1)} %get-tuple-element.27.refs_0_, bf16[8,896]{1,0:T(8,128)(2,1)S(1)} %collective-permute-done.refs_1_, ...), custom_call_target="tpu_custom_call" | custom-call | tf_op jit(solution)/shard_map/combine/pallas_call | solution.py:149
Async XLA Ops:
  0.0 0.9 %copy-start.3 = (bf16[128,896]{1,0:T(8,128)(2,1)S(1)}, bf16[128,896]{1,0:T(8,128)(2,1)}, u32[]{:S(2)}) copy-start(bf16[128,896]{1,0:T(8,128)(2,1)} %refs_2_.2) | copy-start | bytes 688132
  0.9 0.7 %copy-start.4 = (s32[128,8]{0,1:T(8,128)S(1)}, s32[128,8]{0,1:T(8,128)}, u32[]{:S(2)}) copy-start(s32[128,8]{0,1:T(8,128)} %param.7) | copy-start | bytes 12292
  1.6 0.7 %copy-start.5 = (f32[128,8]{0,1:T(8,128)S(1)}, f32[128,8]{0,1:T(8,128)}, u32[]{:S(2)}) copy-start(f32[128,8]{0,1:T(8,128)} %param.8) | copy-start | bytes 12292
  26.9 1.2 %copy-start = (bf16[1,3584,128]{2,1,0:T(8,128)(2,1)S(1)}, bf16[1,3584,128]{2,1,0:T(8,128)(2,1)}, u32[]{:S(2)}) copy-start(bf16[1,3584,128]{2,1,0:T(8,128)(2,1)} %refs_1_.1) | copy-start | bytes 2752516
  28.1 1.2 %copy-start.1 = (bf16[1,3584,128]{2,1,0:T(8,128)(2,1)S(1)}, bf16[1,3584,128]{2,1,0:T(8,128)(2,1)}, u32[]{:S(2)}) copy-start(bf16[1,3584,128]{2,1,0:T(8,128)(2,1)} %refs_2_.3) | copy-start | bytes 2752516
  29.3 1.2 %copy-start.2 = (bf16[1,128,3584]{2,1,0:T(8,128)(2,1)S(1)}, bf16[1,128,3584]{2,1,0:T(8,128)(2,1)}, u32[]{:S(2)}) copy-start(bf16[1,128,3584]{2,1,0:T(8,128)(2,1)} %refs_3_.1) | copy-start | bytes 2752516
  31.2 5.6 %collective-permute-start = (bf16[8,896]{1,0:T(8,128)(2,1)S(1)}, bf16[8,896]{1,0:T(8,128)(2,1)S(1)}, u32[]{:S(2)}, u32[]{:S(2)}) collective-permute-start(bf16[8,896]{1,0:T(8,128)(2,1)S(1)} %get-tuple-element.28), channel_id=1, source_target_pairs={{0,4},{4,8},{8,12},{12,0},{1,5},{5,9},{9,13},{13,1},{2,6},{6,10},{... | collective-permute-start | bytes 43016 | tf_op jit(solution)/shard_map/ppermute | solution.py:144
  31.3 5.5 %collective-permute-start.1 = (bf16[8,896]{1,0:T(8,128)(2,1)S(1)}, bf16[8,896]{1,0:T(8,128)(2,1)S(1)}, u32[]{:S(2)}, u32[]{:S(2)}) collective-permute-start(bf16[8,896]{1,0:T(8,128)(2,1)S(1)} %get-tuple-element.29), channel_id=1, source_target_pairs={{0,8},{4,12},{8,0},{12,4},{1,9},{5,13},{9,1},{13,5},{2,10},{6,14},... | collective-permute-start | bytes 43016 | tf_op jit(solution)/shard_map/ppermute | solution.py:144
  31.4 9.6 %collective-permute-start.2 = (bf16[8,896]{1,0:T(8,128)(2,1)S(1)}, bf16[8,896]{1,0:T(8,128)(2,1)S(1)}, u32[]{:S(2)}, u32[]{:S(2)}) collective-permute-start(bf16[8,896]{1,0:T(8,128)(2,1)S(1)} %get-tuple-element.30), channel_id=1, source_target_pairs={{0,12},{4,0},{8,4},{12,8},{1,13},{5,1},{9,5},{13,9},{2,14},{6,2},{... | collective-permute-start | bytes 43016 | tf_op jit(solution)/shard_map/ppermute | solution.py:144
  35.1 5.9 %collective-permute-start.3 = (bf16[8,896]{1,0:T(8,128)(2,1)S(1)}, bf16[8,896]{1,0:T(8,128)(2,1)S(1)}, u32[]{:S(2)}, u32[]{:S(2)}) collective-permute-start(bf16[8,896]{1,0:T(8,128)(2,1)S(1)} %get-tuple-element.31), channel_id=1, source_target_pairs={{0,1},{4,5},{8,9},{12,13},{1,2},{5,6},{9,10},{13,14},{2,3},{6,7},{... | collective-permute-start | bytes 43016 | tf_op jit(solution)/shard_map/ppermute | solution.py:144
  35.1 6.0 %collective-permute-start.4 = (bf16[8,896]{1,0:T(8,128)(2,1)S(1)}, bf16[8,896]{1,0:T(8,128)(2,1)S(1)}, u32[]{:S(2)}, u32[]{:S(2)}) collective-permute-start(bf16[8,896]{1,0:T(8,128)(2,1)S(1)} %get-tuple-element.32), channel_id=1, source_target_pairs={{0,5},{4,9},{8,13},{12,1},{1,6},{5,10},{9,14},{13,2},{2,7},{6,11},... | collective-permute-start | bytes 43016 | tf_op jit(solution)/shard_map/ppermute | solution.py:144
  36.8 7.1 %collective-permute-start.5 = (bf16[8,896]{1,0:T(8,128)(2,1)S(1)}, bf16[8,896]{1,0:T(8,128)(2,1)S(1)}, u32[]{:S(2)}, u32[]{:S(2)}) collective-permute-start(bf16[8,896]{1,0:T(8,128)(2,1)S(1)} %get-tuple-element.33), channel_id=1, source_target_pairs={{0,9},{4,13},{8,1},{12,5},{1,10},{5,14},{9,2},{13,6},{2,11},{6,15}... | collective-permute-start | bytes 43016 | tf_op jit(solution)/shard_map/ppermute | solution.py:144
  36.8 10.4 %collective-permute-start.6 = (bf16[8,896]{1,0:T(8,128)(2,1)S(1)}, bf16[8,896]{1,0:T(8,128)(2,1)S(1)}, u32[]{:S(2)}, u32[]{:S(2)}) collective-permute-start(bf16[8,896]{1,0:T(8,128)(2,1)S(1)} %get-tuple-element.34), channel_id=1, source_target_pairs={{0,13},{4,1},{8,5},{12,9},{1,14},{5,2},{9,6},{13,10},{2,15},{6,3},... | collective-permute-start | bytes 43016 | tf_op jit(solution)/shard_map/ppermute | solution.py:144
  41.0 6.2 %collective-permute-start.7 = (bf16[8,896]{1,0:T(8,128)(2,1)S(1)}, bf16[8,896]{1,0:T(8,128)(2,1)S(1)}, u32[]{:S(2)}, u32[]{:S(2)}) collective-permute-start(bf16[8,896]{1,0:T(8,128)(2,1)S(1)} %get-tuple-element.35), channel_id=1, source_target_pairs={{0,2},{4,6},{8,10},{12,14},{1,3},{5,7},{9,11},{13,15},{2,0},{6,4},... | collective-permute-start | bytes 43016 | tf_op jit(solution)/shard_map/ppermute | solution.py:144
  41.0 6.9 %collective-permute-start.8 = (bf16[8,896]{1,0:T(8,128)(2,1)S(1)}, bf16[8,896]{1,0:T(8,128)(2,1)S(1)}, u32[]{:S(2)}, u32[]{:S(2)}) collective-permute-start(bf16[8,896]{1,0:T(8,128)(2,1)S(1)} %get-tuple-element.36), channel_id=1, source_target_pairs={{0,6},{4,10},{8,14},{12,2},{1,7},{5,11},{9,15},{13,3},{2,4},{6,8},... | collective-permute-start | bytes 43016 | tf_op jit(solution)/shard_map/ppermute | solution.py:144
  41.1 7.8 %collective-permute-start.9 = (bf16[8,896]{1,0:T(8,128)(2,1)S(1)}, bf16[8,896]{1,0:T(8,128)(2,1)S(1)}, u32[]{:S(2)}, u32[]{:S(2)}) collective-permute-start(bf16[8,896]{1,0:T(8,128)(2,1)S(1)} %get-tuple-element.37), channel_id=1, source_target_pairs={{0,10},{4,14},{8,2},{12,6},{1,11},{5,15},{9,3},{13,7},{2,8},{6,12}... | collective-permute-start | bytes 43016 | tf_op jit(solution)/shard_map/ppermute | solution.py:144
  43.9 9.0 %collective-permute-start.10 = (bf16[8,896]{1,0:T(8,128)(2,1)S(1)}, bf16[8,896]{1,0:T(8,128)(2,1)S(1)}, u32[]{:S(2)}, u32[]{:S(2)}) collective-permute-start(bf16[8,896]{1,0:T(8,128)(2,1)S(1)} %get-tuple-element.38), channel_id=1, source_target_pairs={{0,14},{4,2},{8,6},{12,10},{1,15},{5,3},{9,7},{13,11},{2,12},{6,0}... | collective-permute-start | bytes 43016 | tf_op jit(solution)/shard_map/ppermute | solution.py:144
  47.2 5.7 %collective-permute-start.11 = (bf16[8,896]{1,0:T(8,128)(2,1)S(1)}, bf16[8,896]{1,0:T(8,128)(2,1)S(1)}, u32[]{:S(2)}, u32[]{:S(2)}) collective-permute-start(bf16[8,896]{1,0:T(8,128)(2,1)S(1)} %get-tuple-element.39), channel_id=1, source_target_pairs={{0,3},{4,7},{8,11},{12,15},{1,0},{5,4},{9,8},{13,12},{2,1},{6,5},{... | collective-permute-start | bytes 43016 | tf_op jit(solution)/shard_map/ppermute | solution.py:144
  47.2 5.7 %collective-permute-start.12 = (bf16[8,896]{1,0:T(8,128)(2,1)S(1)}, bf16[8,896]{1,0:T(8,128)(2,1)S(1)}, u32[]{:S(2)}, u32[]{:S(2)}) collective-permute-start(bf16[8,896]{1,0:T(8,128)(2,1)S(1)} %get-tuple-element.40), channel_id=1, source_target_pairs={{0,7},{4,11},{8,15},{12,3},{1,4},{5,8},{9,12},{13,0},{2,5},{6,9},{... | collective-permute-start | bytes 43016 | tf_op jit(solution)/shard_map/ppermute | solution.py:144
  47.9 5.0 %collective-permute-start.13 = (bf16[8,896]{1,0:T(8,128)(2,1)S(1)}, bf16[8,896]{1,0:T(8,128)(2,1)S(1)}, u32[]{:S(2)}, u32[]{:S(2)}) collective-permute-start(bf16[8,896]{1,0:T(8,128)(2,1)S(1)} %get-tuple-element.41), channel_id=1, source_target_pairs={{0,11},{4,15},{8,3},{12,7},{1,8},{5,12},{9,0},{13,4},{2,9},{6,13},... | collective-permute-start | bytes 43016 | tf_op jit(solution)/shard_map/ppermute | solution.py:144
  48.9 5.4 %collective-permute-start.14 = (bf16[8,896]{1,0:T(8,128)(2,1)S(1)}, bf16[8,896]{1,0:T(8,128)(2,1)S(1)}, u32[]{:S(2)}, u32[]{:S(2)}) collective-permute-start(bf16[8,896]{1,0:T(8,128)(2,1)S(1)} %get-tuple-element.42), channel_id=1, source_target_pairs={{0,15},{4,3},{8,7},{12,11},{1,12},{5,0},{9,4},{13,8},{2,13},{6,1},... | collective-permute-start | bytes 43016 | tf_op jit(solution)/shard_map/ppermute | solution.py:144

commit v3 on v1

v3 whole, which is shorter than its diff:
```python
import jax
import jax.numpy as jnp
from jax import lax
from jax.experimental import pallas as pl
from jax.experimental.pallas import tpu as pltpu
from jax.sharding import PartitionSpec as P

CAP = 8
PIECE = 32
WEIGHT_PARTS = 4
AXES = ("tp", "ep")
LIMIT = pltpu.CompilerParams(vmem_limit_bytes=16 * 1024 * 1024)


def iota(shape, dim):
    return lax.broadcasted_iota(jnp.int32, shape, dim)


def to_column(row):
    size = row.shape[1]
    square = (size, size)
    return jnp.sum(jnp.where(iota(square, 0) == iota(square, 1), row, 0.0), axis=1, keepdims=True)


def route(ep_count, resident, *refs):
    ids_hbm, scores_hbm, tokens_hbm, outgoing_ref, match_ref, weight_ref = refs[:3] + refs[6:9]
    ids_ref, scores_ref, tokens_ref, sems, weight_sems = refs[12:]
    row_count = ids_ref.shape[1]
    slot_rows = match_ref.shape[1]
    parts = row_count // PIECE
    copies = [
        pltpu.make_async_copy(ids_hbm, ids_ref, sems.at[parts]),
        pltpu.make_async_copy(scores_hbm, scores_ref, sems.at[parts + 1]),
    ] + [
        pltpu.make_async_copy(
            tokens_hbm.at[pl.ds(part * PIECE, PIECE), :],
            tokens_ref.at[pl.ds(part * PIECE, PIECE), :],
            sems.at[part],
        )
        for part in range(parts)
    ]
    pieces = [
        pltpu.make_async_copy(
            source.at[:, pl.ds(part * size, size), :],
            target.at[:, pl.ds(part * size, size), :],
            weight_sems.at[which * WEIGHT_PARTS + part],
        )
        for which, (source, target) in enumerate(zip(refs[3:6], refs[9:12]))
        for size in [source.shape[1] // WEIGHT_PARTS]
        for part in range(WEIGHT_PARTS)
    ]
    for copy in copies + pieces:
        copy.start()
    square = (row_count, row_count)
    earlier = jnp.where(iota(square, 0) < iota(square, 1), 1.0, 0.0).astype(jnp.bfloat16)
    copies[0].wait()
    ids = ids_ref[...].astype(jnp.float32)
    expert = jnp.min(ids, axis=0, keepdims=True)
    onehot_shape = (-(-resident // 16) * 16, row_count)
    onehot = jnp.where(expert == iota(onehot_shape, 0).astype(jnp.float32), 1.0, 0.0)
    counts = jnp.dot(onehot.astype(jnp.bfloat16), earlier, preferred_element_type=jnp.float32)
    code = expert * CAP + jnp.sum(counts * onehot, axis=0, keepdims=True)
    index = lax.rem(iota((slot_rows, row_count), 0), ep_count * CAP)
    wanted = (index // (2 * CAP)) * CAP + lax.rem(index, CAP)
    dispatch = jnp.where(code == wanted.astype(jnp.float32), 1.0, 0.0).astype(jnp.bfloat16)
    index = lax.rem(iota((row_count, slot_rows), 1), ep_count * CAP)
    wanted = (index // (2 * CAP)) * CAP + lax.rem(index, CAP)
    match_ref[...] = jnp.where(to_column(code) == wanted.astype(jnp.float32), 1.0, 0.0).astype(
        jnp.bfloat16
    )
    copies[1].wait()
    squashed = jax.nn.sigmoid(scores_ref[...])
    chosen = jnp.sum(jnp.where(ids == expert, squashed, 0.0), axis=0, keepdims=True)
    weight_ref[...] = to_column(2.5 * chosen / jnp.sum(squashed, axis=0, keepdims=True))
    for copy in copies[2:]:
        copy.wait()
    outgoing_ref[...] = jnp.dot(
        dispatch, tokens_ref[...], preferred_element_type=jnp.float32
    ).astype(jnp.bfloat16)
    for piece in pieces:
        piece.wait()


def experts(tp_count, rows_ref, gate_ref, up_ref, down_ref, out_ref):
    part_rows, features = rows_ref.shape[0] // tp_count, rows_ref.shape[1]
    gate_act = jnp.zeros((part_rows, gate_ref.shape[2]), jnp.float32)
    up_act = jnp.zeros((part_rows, up_ref.shape[2]), jnp.float32)
    for part in range(tp_count):
        rows = rows_ref[part * part_rows : (part + 1) * part_rows, :]
        columns = slice(part * features, (part + 1) * features)
        gate_act += jnp.dot(rows, gate_ref[0, columns, :], preferred_element_type=jnp.float32)
        up_act += jnp.dot(rows, up_ref[0, columns, :], preferred_element_type=jnp.float32)
    hidden = (gate_act / (1.0 + jnp.exp(-gate_act)) * up_act).astype(jnp.bfloat16)
    for part in range(tp_count):
        columns = slice(part * features, (part + 1) * features)
        out_ref[part * part_rows : (part + 1) * part_rows, :] = jnp.dot(
            hidden, down_ref[0, :, columns], preferred_element_type=jnp.float32
        ).astype(jnp.bfloat16)


def combine(match_ref, weight_ref, returned_ref, out_ref):
    summed = jnp.dot(match_ref[...], returned_ref[...], preferred_element_type=jnp.float32)
    out_ref[...] = (weight_ref[...] * summed).astype(jnp.bfloat16)


def shards(tokens, expert_ids, route_scores, w_gate, w_up, w_down):
    row_count, features = tokens.shape
    ep_count, tp_count = lax.axis_size("ep"), lax.axis_size("tp")
    slot_rows = ep_count * tp_count * CAP
    top_count = expert_ids.shape[1]
    inputs = (expert_ids.T, route_scores.T, tokens, w_gate, w_up, w_down)
    inputs = [pltpu.with_memory_space_constraint(value, pltpu.HBM) for value in inputs]
    outgoing, match, weight, *held = pl.pallas_call(
        lambda *refs: route(ep_count, ep_count // 2, *refs),
        in_specs=[pl.BlockSpec(memory_space=pltpu.HBM)] * 6,
        out_shape=(
            jax.ShapeDtypeStruct((slot_rows, features), jnp.bfloat16),
            jax.ShapeDtypeStruct((row_count, slot_rows), jnp.bfloat16),
            jax.ShapeDtypeStruct((row_count, 1), jnp.float32),
        )
        + tuple(jax.ShapeDtypeStruct(value.shape, value.dtype) for value in (w_gate, w_up, w_down)),
        scratch_shapes=[
            pltpu.VMEM((top_count, row_count), jnp.int32),
            pltpu.VMEM((top_count, row_count), jnp.float32),
            pltpu.VMEM((row_count, features), jnp.bfloat16),
            pltpu.SemaphoreType.DMA((row_count // PIECE + 2,)),
            pltpu.SemaphoreType.DMA((3 * WEIGHT_PARTS,)),
        ],
        compiler_params=LIMIT,
        name="route",
    )(*inputs)
    incoming = lax.all_to_all(outgoing, AXES, split_axis=0, concat_axis=0, tiled=True)
    partial_value = pl.pallas_call(
        lambda *refs: experts(tp_count, *refs),
        out_shape=jax.ShapeDtypeStruct((slot_rows, features), jnp.bfloat16),
        compiler_params=LIMIT,
        name="experts",
    )(incoming, *held)
    returned = lax.all_to_all(partial_value, AXES, split_axis=0, concat_axis=0, tiled=True)
    return pl.pallas_call(
        combine,
        out_shape=jax.ShapeDtypeStruct((row_count, features), jnp.bfloat16),
        compiler_params=LIMIT,
        name="combine",
    )(match, weight, returned)


def solution(mesh):
    placed = (
        P(("groups", "ep"), "tp"),
        P(("groups", "ep"), None),
        P(("groups", "ep"), None),
        P("ep", None, "tp"),
        P("ep", None, "tp"),
        P("ep", "tp", None),
    )
    return jax.shard_map(
        shards, mesh=mesh, in_specs=placed, out_specs=P(("groups", "ep"), "tp"), check_vma=False
    )
```

time: 36.2 us -> 32.8 us (0.906)
  local copies, waits for them, and re-layouts: 4.95 us -> 0 us
  Pallas kernels: 2.08 us -> 3.71 us
    unnamed x10 -> x0, local copies, waits for them, and re-layouts: 4.95 us -> none
    pallas_call x1, Pallas kernels: 0.54 us -> 2.16 us  [shards(): pl.pallas_call(lambda *refs: route(ep_count, ep_count // 2, *refs), in_sp...]
where the time goes in v3:
time: 32.8 us; the launch traced here: 32.6 us
  blocking collectives  28.9 us (88%)
  Pallas kernels  3.71 us (11%)
    all_to_all x1, blocking collectives, shards(): lax.all_to_all(outgoing, AXES, split_axis=0, concat_axis=0, tiled=True)  16.4 us
    all_to_all x1, blocking collectives, shards(): lax.all_to_all(partial_value, AXES, split_axis=0, concat_axis=0, tiled=True)  12.5 us
    pallas_call x1, Pallas kernels, shards(): pl.pallas_call(lambda *refs: route(ep_count, ep_count // 2, *refs), in_sp...  2.16 us
    pallas_call x1, Pallas kernels, shards(): pl.pallas_call(combine, out_shape=jax.ShapeDtypeStruct((row_count, featur...  0.9 us

profile of v3, /device:TPU:0, one launch (start us, length us, event | category | flops | bytes accessed | tf_op | source)
XLA Modules:
  0.0 32.6 jit_solution(1630631843754471822)
XLA Ops:
  0.0 2.2 %route.1 = (bf16[128,896]{1,0:T(8,128)(2,1)S(1)}, bf16[128,128]{1,0:T(8,128)(2,1)S(1)}, f32[128,1]{1,0:T(8,128)S(1)}, bf16[1,3584,128]{2,1,0:T(8,128)(2,1)S(1)},...) custom-call(s32[8,128]{1,0:T(8,128)} %bitcast.10, f32[8,128]{1,0:T(8,128)} %bitcast.11, ...), custom_call_target="tpu_custom_call" | custom-call | tf_op jit(solution)/shard_map/route/pallas_call | solution.py:113
  2.2 16.4 %all_to_all.22 = bf16[16,8,896]{2,1,0:T(8,128)(2,1)S(1)} all-to-all(bf16[16,8,896]{2,1,0:T(8,128)(2,1)S(1)} %bitcast.9), channel_id=1, replica_groups=mesh['groups'=2,'ep'=4,'tp'=4] {'tp','ep'}, dimensions={0} | all-to-all | bytes 458752 | tf_op jit(solution)/shard_map/all_to_all | solution.py:132
  18.5 0.6 %experts.1 = bf16[128,896]{1,0:T(8,128)(2,1)S(1)} custom-call(bf16[128,896]{1,0:T(8,128)(2,1)S(1)} %bitcast.6, bf16[1,3584,128]{2,1,0:T(8,128)(2,1)S(1)} %get-tuple-element.14.refs_1_, bf16[1,3584,128]{2,1,0:T(8,128)(2,1)S(1)} %get-tuple-element.15.refs_2_, bf16[1,128,3584]{2,1,0:T(8,128)(2,1)S(1)} %get-tuple-element.16.refs_3_), custom_call_target="tpu_custom_call" | custom-call | tf_op jit(solution)/shard_map/experts/pallas_call | solution.py:133
  19.2 12.5 %all_to_all.23 = bf16[16,8,896]{2,1,0:T(8,128)(2,1)S(1)} all-to-all(bf16[16,8,896]{2,1,0:T(8,128)(2,1)S(1)} %bitcast.7), channel_id=1, replica_groups=mesh['groups'=2,'ep'=4,'tp'=4] {'tp','ep'}, dimensions={0} | all-to-all | bytes 458752 | tf_op jit(solution)/shard_map/all_to_all | solution.py:139
  31.7 0.9 %combine.1 = bf16[128,896]{1,0:T(8,128)(2,1)} custom-call(bf16[128,128]{1,0:T(8,128)(2,1)S(1)} %get-tuple-element.11.match_ref, f32[128,1]{1,0:T(8,128)S(1)} %get-tuple-element.12.weight_ref, bf16[128,896]{1,0:T(8,128)(2,1)S(1)} %bitcast.8), custom_call_target="tpu_custom_call" | custom-call | tf_op jit(solution)/shard_map/combine/pallas_call | solution.py:140

commit v4 on v3

--- a/solution.py
+++ b/solution.py
@@ -8,7 +8,7 @@
 CAP = 8
 PIECE = 32
 WEIGHT_PARTS = 4
-AXES = ("tp", "ep")
+AXES = ("chip", "ep")
 LIMIT = pltpu.CompilerParams(vmem_limit_bytes=16 * 1024 * 1024)
 
 
@@ -81,21 +81,44 @@
         piece.wait()
 
 
-def experts(tp_count, rows_ref, gate_ref, up_ref, down_ref, out_ref):
-    part_rows, features = rows_ref.shape[0] // tp_count, rows_ref.shape[1]
+def lift(tp_count, ep_count, own, rows_ref, gate_ref, up_ref):
+    part_rows, features = ep_count * CAP, rows_ref.shape[1]
+    core = lax.axis_index("core")
+    core = core if own else 1 - core
     gate_act = jnp.zeros((part_rows, gate_ref.shape[2]), jnp.float32)
     up_act = jnp.zeros((part_rows, up_ref.shape[2]), jnp.float32)
-    for part in range(tp_count):
-        rows = rows_ref[part * part_rows : (part + 1) * part_rows, :]
-        columns = slice(part * features, (part + 1) * features)
+    for chip in range(tp_count // 2):
+        rows = rows_ref[chip * part_rows : (chip + 1) * part_rows, :]
+        start = pl.multiple_of((2 * chip + core) * features, features)
+        columns = pl.ds(start, features)
         gate_act += jnp.dot(rows, gate_ref[0, columns, :], preferred_element_type=jnp.float32)
         up_act += jnp.dot(rows, up_ref[0, columns, :], preferred_element_type=jnp.float32)
+    return gate_act, up_act
+
+
+def begin(tp_count, ep_count, rows_ref, gate_ref, up_ref, gate_act_ref, up_act_ref):
+    gate_act_ref[...], up_act_ref[...] = lift(tp_count, ep_count, True, rows_ref, gate_ref, up_ref)
+
+
+def finish(tp_count, ep_count, *refs):
+    rows_ref, gate_act_ref, up_act_ref, gate_ref, up_ref, down_ref, mine_ref, other_ref = refs
+    part_rows, features = ep_count * CAP, rows_ref.shape[1]
+    gate_act, up_act = lift(tp_count, ep_count, False, rows_ref, gate_ref, up_ref)
+    gate_act += gate_act_ref[...]
+    up_act += up_act_ref[...]
     hidden = (gate_act / (1.0 + jnp.exp(-gate_act)) * up_act).astype(jnp.bfloat16)
-    for part in range(tp_count):
-        columns = slice(part * features, (part + 1) * features)
-        out_ref[part * part_rows : (part + 1) * part_rows, :] = jnp.dot(
-            hidden, down_ref[0, :, columns], preferred_element_type=jnp.float32
-        ).astype(jnp.bfloat16)
+    core = lax.axis_index("core")
+    for out_ref, target in ((other_ref, 1 - core), (mine_ref, core)):
+        for chip in range(tp_count // 2):
+            start = pl.multiple_of((2 * chip + target) * features, features)
+            out_ref[chip * part_rows : (chip + 1) * part_rows, :] = jnp.dot(
+                hidden, down_ref[0, :, pl.ds(start, features)], preferred_element_type=jnp.float32
+            ).astype(jnp.bfloat16)
+
+
+def add(mine_ref, other_ref, out_ref):
+    total = mine_ref[...].astype(jnp.float32) + other_ref[...].astype(jnp.float32)
+    out_ref[...] = total.astype(jnp.bfloat16)
 
 
 def combine(match_ref, weight_ref, returned_ref, out_ref):
@@ -105,9 +128,10 @@
 
 def shards(tokens, expert_ids, route_scores, w_gate, w_up, w_down):
     row_count, features = tokens.shape
-    ep_count, tp_count = lax.axis_size("ep"), lax.axis_size("tp")
-    slot_rows = ep_count * tp_count * CAP
+    ep_count, tp_count = lax.axis_size("ep"), 2 * lax.axis_size("chip")
+    slot_rows = ep_count * tp_count // 2 * CAP
     top_count = expert_ids.shape[1]
+    hidden_count = w_gate.shape[2]
     inputs = (expert_ids.T, route_scores.T, tokens, w_gate, w_up, w_down)
     inputs = [pltpu.with_memory_space_constraint(value, pltpu.HBM) for value in inputs]
     outgoing, match, weight, *held = pl.pallas_call(
@@ -129,14 +153,27 @@
         compiler_params=LIMIT,
         name="route",
     )(*inputs)
+    swap = [(0, 1), (1, 0)]
     incoming = lax.all_to_all(outgoing, AXES, split_axis=0, concat_axis=0, tiled=True)
-    partial_value = pl.pallas_call(
-        lambda *refs: experts(tp_count, *refs),
-        out_shape=jax.ShapeDtypeStruct((slot_rows, features), jnp.bfloat16),
-        compiler_params=LIMIT,
-        name="experts",
-    )(incoming, *held)
-    returned = lax.all_to_all(partial_value, AXES, split_axis=0, concat_axis=0, tiled=True)
+    across = lax.ppermute(incoming, "core", swap)
+    acts = (jax.ShapeDtypeStruct((ep_count * CAP, hidden_count), jnp.float32),) * 2
+    begun = pl.pallas_call(
+        lambda *refs: begin(tp_count, ep_count, *refs),
+        out_shape=acts,
+        compiler_params=LIMIT,
+        name="begin",
+    )(incoming, held[0], held[1])
+    half = jax.ShapeDtypeStruct((slot_rows, features), jnp.bfloat16)
+    mine, other = pl.pallas_call(
+        lambda *refs: finish(tp_count, ep_count, *refs),
+        out_shape=(half, half),
+        compiler_params=LIMIT,
+        name="finish",
+    )(across, *begun, *held)
+    summed = pl.pallas_call(add, out_shape=half, compiler_params=LIMIT, name="add")(
+        mine, lax.ppermute(other, "core", swap)
+    )
+    returned = lax.all_to_all(summed, AXES, split_axis=0, concat_axis=0, tiled=True)
     return pl.pallas_call(
         combine,
         out_shape=jax.ShapeDtypeStruct((row_count, features), jnp.bfloat16),
@@ -146,14 +183,19 @@
 
 
 def solution(mesh):
+    groups, ep_count, tp_count = (mesh.shape[name] for name in ("groups", "ep", "tp"))
+    split = jax.sharding.Mesh(
+        mesh.devices.reshape(groups, ep_count, tp_count // 2, 2), ("groups", "ep", "chip", "core")
+    )
+    tp = ("chip", "core")
     placed = (
-        P(("groups", "ep"), "tp"),
+        P(("groups", "ep"), tp),
         P(("groups", "ep"), None),
         P(("groups", "ep"), None),
-        P("ep", None, "tp"),
-        P("ep", None, "tp"),
-        P("ep", "tp", None),
+        P("ep", None, tp),
+        P("ep", None, tp),
+        P("ep", tp, None),
     )
     return jax.shard_map(
-        shards, mesh=mesh, in_specs=placed, out_specs=P(("groups", "ep"), "tp"), check_vma=False
-    )
+        shards, mesh=split, in_specs=placed, out_specs=P(("groups", "ep"), tp), check_vma=False
+    )

time: 32.8 us -> 30.8 us (0.939)
  blocking collectives: 28.9 us -> 24.3 us
  waiting for transfers between devices: 0 us -> 2.23 us
    all_to_all x1, blocking collectives: 12.5 us -> 9.88 us  [shards(): lax.all_to_all(summed, AXES, split_axis=0, concat_axis=0, tiled=True)]
    ppermute x0 -> x2, waiting for transfers between devices: none -> 2.23 us  [the longest x1 1.17 us: shards(): lax.ppermute(other, 'core', swap)]
    all_to_all x1, blocking collectives: 16.4 us -> 14.4 us  [shards(): lax.all_to_all(outgoing, AXES, split_axis=0, concat_axis=0, tiled=True)]
    pallas_call x1 -> x3, Pallas kernels: 0.64 us -> 0.79 us  [the longest x1 0.51 us: shards(): pl.pallas_call(lambda *refs: finish(tp_count, ep_count, *refs), out_shape...]
  transfers between devices with their start and end apart: 0 -> 2, of which waited for: 0 -> 2; matrix products, arithmetic and copies ran while one was open for 0% -> 0% of each run, Pallas kernels for 0% -> 1%
where the time goes in v4:
time: 30.8 us; the launch traced here: 30.6 us
  blocking collectives  24.3 us (79%)
  Pallas kernels  3.81 us (12%)
  waiting for transfers between devices  2.23 us (7%)
    all_to_all x1, blocking collectives, shards(): lax.all_to_all(outgoing, AXES, split_axis=0, concat_axis=0, tiled=True)  14.4 us
    all_to_all x1, blocking collectives, shards(): lax.all_to_all(summed, AXES, split_axis=0, concat_axis=0, tiled=True)  9.88 us
    pallas_call x1, Pallas kernels, shards(): pl.pallas_call(lambda *refs: route(ep_count, ep_count // 2, *refs), in_sp...  2.13 us
    ppermute x1, waiting for transfers between devices, shards(): lax.ppermute(other, 'core', swap)  1.17 us
    ppermute x1, waiting for transfers between devices, shards(): across = lax.ppermute(incoming, 'core', swap)  1.06 us
    pallas_call x1, Pallas kernels, shards(): pl.pallas_call(combine, out_shape=jax.ShapeDtypeStruct((row_count, featur...  0.89 us
  transfers between devices with their start and end apart: 2, of which 2 were waited for; matrix products, arithmetic and copies ran while one was open for 0% of the time, Pallas kernels for 1%

profile of v4, /device:TPU:0, one launch (start us, length us, event | category | flops | bytes accessed | tf_op | source)
XLA Modules:
  0.0 30.6 jit_solution(9743374203164055658)
XLA Ops:
  0.0 2.1 %route.1 = (bf16[64,896]{1,0:T(8,128)(2,1)S(1)}, bf16[128,64]{1,0:T(8,128)(2,1)S(1)}, f32[128,1]{1,0:T(8,128)S(1)}, bf16[1,3584,128]{2,1,0:T(8,128)(2,1)S(1)}, b...) custom-call(s32[8,128]{1,0:T(8,128)} %bitcast.11, f32[8,128]{1,0:T(8,128)} %bitcast.12, ...), custom_call_target="tpu_custom_call" | custom-call | tf_op jit(solution)/shard_map/route/pallas_call | solution.py:137
  2.1 14.4 %all_to_all.22 = bf16[8,8,896]{2,1,0:T(8,128)(2,1)S(1)} all-to-all(bf16[8,8,896]{2,1,0:T(8,128)(2,1)S(1)} %bitcast.10), channel_id=1, replica_groups=mesh['groups'=2,'ep'=4,'chip'=2,'core'=2] {'chip','ep'}, dimensions={0} | all-to-all | bytes 229376 | tf_op jit(solution)/shard_map/all_to_all | solution.py:157
  16.6 0.0 collective-permute-start
  16.6 0.3 begin.1
  16.8 1.1 %collective-permute-done.refs_0_ = bf16[64,896]{1,0:T(8,128)(2,1)S(1)} collective-permute-done((bf16[64,896]{1,0:T(8,128)(2,1)S(1)}, bf16[64,896]{1,0:T(8,128)(2,1)S(1)}, u32[]{:S(2)}, u32[]{:S(2)}) %collective-permute-start) | collective-permute-done | bytes 114720 | tf_op jit(solution)/shard_map/ppermute | solution.py:158
  17.9 0.5 %finish.1 = (bf16[64,896]{1,0:T(8,128)(2,1)S(1)}, bf16[64,896]{1,0:T(8,128)(2,1)S(1)}) custom-call(bf16[64,896]{1,0:T(8,128)(2,1)S(1)} %collective-permute-done.refs_0_, f32[32,128]{1,0:T(8,128)S(1)} %get-tuple-element.20.refs_1_, f32[32,128]{1,0:T(8,128)S(1)} %get-tuple-element.21.refs_2_, bf16[1,3584,128]{2,1,0:T(8,128)(2,1)S(1)} %get-tuple-element.18.refs_1_.refs_3_, ...), custom_call_target="tpu_custom_call" | custom-call | tf_op jit(solution)/shard_map/finish/pallas_call | solution.py:167
  18.4 0.2 collective-permute-start.1
  18.6 1.2 %collective-permute-done.1.other_ref = bf16[64,896]{1,0:T(8,128)(2,1)S(1)} collective-permute-done((bf16[64,896]{1,0:T(8,128)(2,1)S(1)}, bf16[64,896]{1,0:T(8,128)(2,1)S(1)}, u32[]{:S(2)}, u32[]{:S(2)}) %collective-permute-start.1) | collective-permute-done | bytes 114720 | tf_op jit(solution)/shard_map/ppermute | solution.py:174
  19.8 9.9 %all_to_all.23 = bf16[8,8,896]{2,1,0:T(8,128)(2,1)S(1)} all-to-all(bf16[8,8,896]{2,1,0:T(8,128)(2,1)S(1)} %bitcast.7), channel_id=1, replica_groups=mesh['groups'=2,'ep'=4,'chip'=2,'core'=2] {'chip','ep'}, dimensions={0} | all-to-all | bytes 229376 | tf_op jit(solution)/shard_map/all_to_all | solution.py:176
  29.7 0.9 %combine.1 = bf16[128,896]{1,0:T(8,128)(2,1)} custom-call(bf16[128,64]{1,0:T(8,128)(2,1)S(1)} %get-tuple-element.15.match_ref, f32[128,1]{1,0:T(8,128)S(1)} %get-tuple-element.16.weight_ref, bf16[64,896]{1,0:T(8,128)(2,1)S(1)} %bitcast.6), custom_call_target="tpu_custom_call" | custom-call | tf_op jit(solution)/shard_map/combine/pallas_call | solution.py:177
  (1 shorter events, 0.0 us)
Async XLA Ops:
  16.6 1.3 %collective-permute-start = (bf16[64,896]{1,0:T(8,128)(2,1)S(1)}, bf16[64,896]{1,0:T(8,128)(2,1)S(1)}, u32[]{:S(2)}, u32[]{:S(2)}) collective-permute-start(bf16[64,896]{1,0:T(8,128)(2,1)S(1)} %bitcast.8), channel_id=1, source_target_pairs={{0,1},{1,0},{2,3},{3,2},{4,5},{5,4},{6,7},{7,6},{8,9},{9,8},{10,11... | collective-permute-start | bytes 344072 | tf_op jit(solution)/shard_map/ppermute | solution.py:158
  18.4 1.4 %collective-permute-start.1 = (bf16[64,896]{1,0:T(8,128)(2,1)S(1)}, bf16[64,896]{1,0:T(8,128)(2,1)S(1)}, u32[]{:S(2)}, u32[]{:S(2)}) collective-permute-start(bf16[64,896]{1,0:T(8,128)(2,1)S(1)} %get-tuple-element.24), channel_id=1, source_target_pairs={{0,1},{1,0},{2,3},{3,2},{4,5},{5,4},{6,7},{7,6},{8,9},{9,8},{10,11... | collective-permute-start | bytes 344072 | tf_op jit(solution)/shard_map/ppermute | solution.py:174

commit v5 on v4

v5 whole, which is shorter than its diff:
```python
import jax
import jax.numpy as jnp
from jax import lax
from jax.experimental import pallas as pl
from jax.experimental.pallas import tpu as pltpu
from jax.sharding import PartitionSpec as P

CAP = 8
PIECE = 32
WEIGHT_PARTS = 4
NEAR = ("chip", "half")
SWAP = [(0, 1), (1, 0)]
LIMIT = pltpu.CompilerParams(vmem_limit_bytes=16 * 1024 * 1024)


def iota(shape, dim):
    return lax.broadcasted_iota(jnp.int32, shape, dim)


def to_column(row):
    size = row.shape[1]
    square = (size, size)
    return jnp.sum(jnp.where(iota(square, 0) == iota(square, 1), row, 0.0), axis=1, keepdims=True)


def slot_codes(ids, resident):
    row_count = ids.shape[1]
    expert = jnp.min(ids, axis=0, keepdims=True)
    onehot_shape = (-(-resident // 16) * 16, row_count)
    onehot = jnp.where(expert == iota(onehot_shape, 0).astype(jnp.float32), 1.0, 0.0)
    square = (row_count, row_count)
    earlier = jnp.where(iota(square, 0) < iota(square, 1), 1.0, 0.0).astype(jnp.bfloat16)
    counts = jnp.dot(onehot.astype(jnp.bfloat16), earlier, preferred_element_type=jnp.float32)
    return expert * CAP + jnp.sum(counts * onehot, axis=0, keepdims=True), expert


def block_codes(index, resident):
    if resident == 2:
        index = lax.rem(index + lax.axis_index("expert") * CAP, resident * CAP)
    return index.astype(jnp.float32)


def route(resident, ids_hbm, tokens_hbm, *refs):
    out_refs, (ids_ref, tokens_ref, sems) = refs[:-3], refs[-3:]
    row_count = ids_ref.shape[1]
    parts = row_count // PIECE
    copies = [pltpu.make_async_copy(ids_hbm, ids_ref, sems.at[parts])] + [
        pltpu.make_async_copy(
            tokens_hbm.at[pl.ds(part * PIECE, PIECE), :],
            tokens_ref.at[pl.ds(part * PIECE, PIECE), :],
            sems.at[part],
        )
        for part in range(parts)
    ]
    for copy in copies:
        copy.start()
    copies[0].wait()
    code, _ = slot_codes(ids_ref[...].astype(jnp.float32), resident)
    rows = iota((resident * CAP, row_count), 0)
    dispatch = jnp.where(code == block_codes(rows, resident), 1.0, 0.0).astype(jnp.bfloat16)
    for copy in copies[1:]:
        copy.wait()
    outgoing = jnp.dot(dispatch, tokens_ref[...], preferred_element_type=jnp.float32).astype(
        jnp.bfloat16
    )
    size = resident * CAP // len(out_refs)
    for which, out_ref in enumerate(out_refs):
        out_ref[...] = outgoing[which * size : (which + 1) * size, :]


def prepare(resident, ids_ref, scores_ref, _, *refs):
    weights, (match_ref, weight_ref), held, sems = refs[:3], refs[3:5], refs[5:8], refs[8]
    pieces = [
        pltpu.make_async_copy(
            source.at[:, pl.ds(part * size, size), :],
            target.at[:, pl.ds(part * size, size), :],
            sems.at[which * WEIGHT_PARTS + part],
        )
        for which, (source, target) in enumerate(zip(weights, held))
        for size in [source.shape[1] // WEIGHT_PARTS]
        for part in range(WEIGHT_PARTS)
    ]
    for piece in pieces:
        piece.start()
    ids = ids_ref[...].astype(jnp.float32)
    code, expert = slot_codes(ids, resident)
    wanted = block_codes(iota(match_ref.shape, 1), resident)
    match_ref[...] = jnp.where(to_column(code) == wanted, 1.0, 0.0).astype(jnp.bfloat16)
    squashed = jax.nn.sigmoid(scores_ref[...])
    chosen = jnp.sum(jnp.where(ids == expert, squashed, 0.0), axis=0, keepdims=True)
    weight_ref[...] = to_column(2.5 * chosen / jnp.sum(squashed, axis=0, keepdims=True))
    for piece in pieces:
        piece.wait()


def pack(_, *refs):
    rows = jnp.concatenate([ref[...] for ref in refs[:-1]], axis=0)
    size = rows.shape[0]
    for member in range(refs[-1].shape[0] // size):
        refs[-1][member * size : (member + 1) * size, :] = rows


def lift(chips, own, rows_ref, gate_ref, up_ref):
    part_rows, features = rows_ref.shape[0] // chips, rows_ref.shape[1]
    core = lax.axis_index("core")
    core = core if own else 1 - core
    gate_act = jnp.zeros((part_rows, gate_ref.shape[2]), jnp.float32)
    up_act = jnp.zeros((part_rows, up_ref.shape[2]), jnp.float32)
    for chip in range(chips):
        rows = rows_ref[chip * part_rows : (chip + 1) * part_rows, :]
        columns = pl.ds(pl.multiple_of((2 * chip + core) * features, features), features)
        gate_act += jnp.dot(rows, gate_ref[0, columns, :], preferred_element_type=jnp.float32)
        up_act += jnp.dot(rows, up_ref[0, columns, :], preferred_element_type=jnp.float32)
    return gate_act, up_act


def begin(chips, rows_ref, gate_ref, up_ref, gate_act_ref, up_act_ref):
    gate_act_ref[...], up_act_ref[...] = lift(chips, True, rows_ref, gate_ref, up_ref)


def finish(chips, *refs):
    rows_ref, gate_act_ref, up_act_ref, gate_ref, up_ref, down_ref, mine_ref, other_ref = refs
    part_rows, features = rows_ref.shape[0] // chips, rows_ref.shape[1]
    gate_act, up_act = lift(chips, False, rows_ref, gate_ref, up_ref)
    gate_act += gate_act_ref[...]
    up_act += up_act_ref[...]
    hidden = (gate_act / (1.0 + jnp.exp(-gate_act)) * up_act).astype(jnp.bfloat16)
    core = lax.axis_index("core")
    for out_ref, target in ((other_ref, 1 - core), (mine_ref, core)):
        for chip in range(chips):
            start = pl.multiple_of((2 * chip + target) * features, features)
            out_ref[chip * part_rows : (chip + 1) * part_rows, :] = jnp.dot(
                hidden, down_ref[0, :, pl.ds(start, features)], preferred_element_type=jnp.float32
            ).astype(jnp.bfloat16)


def add(mine_ref, other_ref, out_ref):
    total = mine_ref[...].astype(jnp.float32) + other_ref[...].astype(jnp.float32)
    out_ref[...] = total.astype(jnp.bfloat16)


def total(rows_ref, *out_refs):
    size = out_refs[0].shape[0]
    count = rows_ref.shape[0] // (size * len(out_refs))
    for which, out_ref in enumerate(out_refs):
        summed = jnp.zeros(out_ref.shape, jnp.float32)
        for member in range(count):
            start = (member * len(out_refs) + which) * size
            summed += rows_ref[start : start + size, :].astype(jnp.float32)
        out_ref[...] = summed.astype(jnp.bfloat16)


def combine(match_ref, weight_ref, *refs):
    returned = jnp.concatenate([ref[...] for ref in refs[:-1]], axis=0)
    summed = jnp.dot(match_ref[...], returned, preferred_element_type=jnp.float32)
    refs[-1][...] = (weight_ref[...] * summed).astype(jnp.bfloat16)


def across_experts(blocks, resident):
    if resident == 2:
        return [blocks[0], lax.ppermute(blocks[1], "expert", SWAP)]
    return [lax.all_to_all(blocks[0], "expert", split_axis=0, concat_axis=0, tiled=True)]


def shards(tokens, expert_ids, route_scores, w_gate, w_up, w_down):
    row_count, features = tokens.shape
    top_count, hidden_count = expert_ids.shape[1], w_gate.shape[2]
    resident, chips = lax.axis_size("expert"), lax.axis_size("chip")
    kept = resident * CAP
    members = 2 * chips
    call = lambda kernel, name, out_shape, **rest: pl.pallas_call(
        kernel, out_shape=out_shape, name=name, compiler_params=LIMIT, **rest
    )
    rows_of = lambda count: jax.ShapeDtypeStruct((count, features), jnp.bfloat16)
    blocks_shape = (rows_of(CAP),) * 2 if resident == 2 else (rows_of(kept),)
    ids, scores = expert_ids.T, route_scores.T
    far = lambda value: pltpu.with_memory_space_constraint(value, pltpu.HBM)
    hbm = pl.BlockSpec(memory_space=pltpu.HBM)

    outgoing = call(
        lambda *refs: route(resident, *refs),
        "route",
        blocks_shape,
        in_specs=[hbm] * 2,
        scratch_shapes=[
            pltpu.VMEM((top_count, row_count), jnp.int32),
            pltpu.VMEM((row_count, features), jnp.bfloat16),
            pltpu.SemaphoreType.DMA((row_count // PIECE + 1,)),
        ],
    )(far(ids), far(tokens))
    weights = (w_gate, w_up, w_down)
    vmem = pl.BlockSpec(memory_space=pltpu.VMEM)
    match, weight, *held = call(
        lambda *refs: prepare(resident, *refs),
        "prepare",
        (
            jax.ShapeDtypeStruct((row_count, kept), jnp.bfloat16),
            jax.ShapeDtypeStruct((row_count, 1), jnp.float32),
        )
        + tuple(jax.ShapeDtypeStruct(value.shape, value.dtype) for value in weights),
        in_specs=[vmem] * 2 + [pl.BlockSpec(memory_space=pl.ANY)] + [hbm] * 3,
        scratch_shapes=[pltpu.SemaphoreType.DMA((3 * WEIGHT_PARTS,))],
        cost_estimate=pl.CostEstimate(
            flops=0, bytes_accessed=2 * sum(value.nbytes for value in weights), transcendentals=0
        ),
    )(ids, scores, outgoing[0], *(far(value) for value in weights))
    arrived = across_experts(outgoing, resident)
    packed = call(
        pack,
        "pack",
        rows_of(members * kept),
        in_specs=[pl.BlockSpec(memory_space=pl.ANY)] + [vmem] * len(arrived),
    )(weight, *arrived)
    incoming = lax.all_to_all(packed, NEAR, split_axis=0, concat_axis=0, tiled=True)
    across = lax.ppermute(incoming, "core", SWAP)
    acts = (jax.ShapeDtypeStruct((2 * kept, hidden_count), jnp.float32),) * 2
    begun = call(lambda *refs: begin(chips, *refs), "begin", acts)(incoming, held[0], held[1])
    mine, other = call(
        lambda *refs: finish(chips, *refs), "finish", (rows_of(members * kept),) * 2
    )(across, *begun, *held)
    summed = call(add, "add", rows_of(members * kept))(mine, lax.ppermute(other, "core", SWAP))
    returned = lax.all_to_all(summed, NEAR, split_axis=0, concat_axis=0, tiled=True)
    blocks = call(total, "total", blocks_shape)(returned)
    return call(combine, "combine", rows_of(row_count))(
        match, weight, *across_experts(blocks, resident)
    )


def solution(mesh):
    groups, ep_count, tp_count = (mesh.shape[name] for name in ("groups", "ep", "tp"))
    split = jax.sharding.Mesh(
        mesh.devices.reshape(groups, ep_count // 2, 2, tp_count // 2, 2),
        ("groups", "expert", "half", "chip", "core"),
    )
    ep, tp = ("expert", "half"), ("chip", "core")
    placed = (
        P(("groups", *ep), tp),
        P(("groups", *ep), None),
        P(("groups", *ep), None),
        P(ep, None, tp),
        P(ep, None, tp),
        P(ep, tp, None),
    )
    return jax.shard_map(
        shards, mesh=split, in_specs=placed, out_specs=P(("groups", *ep), tp), check_vma=False
    )
```

time: 30.8 us -> 32.3 us (1.049)
  blocking collectives: 24.3 us -> 16 us
  starting transfers between devices: 0.22 us -> 7.01 us
  waiting for transfers between devices: 2.23 us -> 4.22 us
  Pallas kernels: 3.81 us -> 4.78 us
    all_to_all x2, blocking collectives: 24.3 us -> 16 us  [the longest x1 8.61 us: shards(): lax.all_to_all(packed, NEAR, split_axis=0, concat_axis=0, tiled=True)]
    ppermute x2 -> x4, starting transfers between devices: 0.22 us -> 7.01 us  [the longest x2 6.79 us: across_experts(): return [blocks[0], lax.ppermute(blocks[1], 'expert', SWAP)]]
    ppermute x2 -> x4, waiting for transfers between devices: 2.23 us -> 4.22 us  [the longest x2 1.99 us: across_experts(): return [blocks[0], lax.ppermute(blocks[1], 'expert', SWAP)]]
    pallas_call x5 -> x8, Pallas kernels: 3.81 us -> 4.78 us  [the longest x1 1.94 us: shards(): call(lambda *refs: prepare(resident, *refs), 'prepare', (jax.ShapeDtypeSt...]
  transfers between devices with their start and end apart: 2 -> 4, of which waited for: 2 -> 3; matrix products, arithmetic and copies ran while one was open for 0% -> 0% of each run, Pallas kernels for 1% -> 7%
where the time goes in v5:
time: 32.3 us; the launch traced here: 32.1 us
  blocking collectives  16 us (50%)
  starting transfers between devices  7.01 us (22%)
  Pallas kernels  4.78 us (15%)
  waiting for transfers between devices  4.22 us (13%)
    all_to_all x1, blocking collectives, shards(): lax.all_to_all(packed, NEAR, split_axis=0, concat_axis=0, tiled=True)  8.61 us
    all_to_all x1, blocking collectives, shards(): lax.all_to_all(summed, NEAR, split_axis=0, concat_axis=0, tiled=True)  7.36 us
    ppermute x2, starting transfers between devices, across_experts(): return [blocks[0], lax.ppermute(blocks[1], 'expert', SWAP)]  6.79 us
    ppermute x2, waiting for transfers between devices, across_experts(): return [blocks[0], lax.ppermute(blocks[1], 'expert', SWAP)]  1.99 us
    pallas_call x1, Pallas kernels, shards(): call(lambda *refs: prepare(resident, *refs), 'prepare', (jax.ShapeDtypeSt...  1.94 us
    ppermute x1, waiting for transfers between devices, shards(): lax.ppermute(other, 'core', SWAP)  1.17 us
    pallas_call x1, Pallas kernels, shards(): call(lambda *refs: route(resident, *refs), 'route', blocks_shape, in_spec...  1.12 us
    ppermute x1, waiting for transfers between devices, shards(): across = lax.ppermute(incoming, 'core', SWAP)  1.06 us
  transfers between devices with their start and end apart: 4, of which 3 were waited for; matrix products, arithmetic and copies ran while one was open for 0% of the time, Pallas kernels for 7%

profile of v5, /device:TPU:0, one launch (start us, length us, event | category | flops | bytes accessed | tf_op | source)
XLA Modules:
  0.0 32.1 jit_solution(10406808626120700540)
XLA Ops:
  0.0 0.0 copy-start.1
  0.0 1.1 %route.1 = (bf16[8,896]{1,0:T(8,128)(2,1)S(1)}, bf16[8,896]{1,0:T(8,128)(2,1)S(1)}) custom-call(s32[8,128]{1,0:T(8,128)} %bitcast.11, bf16[128,896]{1,0:T(8,128)(2,1)} %refs_1_.1), custom_call_target="tpu_custom_call" | custom-call | tf_op jit(solution)/shard_map/route/pallas_call | solution.py:180
  1.1 0.0 copy-start
  1.1 4.1 %collective-permute-start = (bf16[8,896]{1,0:T(8,128)(2,1)S(1)}, bf16[8,896]{1,0:T(8,128)(2,1)S(1)}, u32[]{:S(2)}, u32[]{:S(2)}) collective-permute-start(bf16[8,896]{1,0:T(8,128)(2,1)S(1)} %get-tuple-element.21), channel_id=1, source_target_pairs={{0,8},{8,0},{1,9},{9,1},{2,10},{10,2},{3,11},{11,3},{4,12},{12,4},... | collective-permute-start | bytes 43016 | tf_op jit(solution)/shard_map/ppermute | solution.py:161
  5.2 0.0 copy-done.1
  5.3 0.0 copy-done
  5.3 1.9 %prepare.1 = (bf16[128,16]{1,0:T(8,128)(2,1)S(1)}, f32[128,1]{1,0:T(8,128)S(1)}, bf16[1,3584,128]{2,1,0:T(8,128)(2,1)S(1)}, bf16[1,3584,128]{2,1,0:T(8,128)(2,1)S(1)}, bf16[1,128,3584]{2,1,0:T(8,128)(2,1)S(1)}) custom-call(s32[8,128]{1,0:T(8,128)S(1)} %bitcast.12, f32[8,128]{1,0:T(8,128)S(1)} %bitcast.13, ...), custom_call_target="tpu_custom_call" | custom-call | bytes 5505024 | tf_op jit(solution)/shard_map/prepare/pallas_call | solution.py:193
  7.2 0.0 collective-permute-done.refs_1_
  7.2 8.6 %all_to_all.22 = bf16[4,16,896]{2,1,0:T(8,128)(2,1)S(1)} all-to-all(bf16[4,16,896]{2,1,0:T(8,128)(2,1)S(1)} %bitcast.7), channel_id=1, replica_groups=mesh['groups'=2,'expert'=2,'half'=2,'chip'=2,'core'=2] {'chip','half'}, dimensions={0} | all-to-all | bytes 229376 | tf_op jit(solution)/shard_map/all_to_all | solution.py:214
  15.8 0.0 collective-permute-start.1
  15.8 0.3 begin.1
  16.1 1.1 %collective-permute-done.1.refs_0_ = bf16[64,896]{1,0:T(8,128)(2,1)S(1)} collective-permute-done((bf16[64,896]{1,0:T(8,128)(2,1)S(1)}, bf16[64,896]{1,0:T(8,128)(2,1)S(1)}, u32[]{:S(2)}, u32[]{:S(2)}) %collective-permute-start.1) | collective-permute-done | bytes 114720 | tf_op jit(solution)/shard_map/ppermute | solution.py:215
  17.2 0.5 %finish.1 = (bf16[64,896]{1,0:T(8,128)(2,1)S(1)}, bf16[64,896]{1,0:T(8,128)(2,1)S(1)}) custom-call(bf16[64,896]{1,0:T(8,128)(2,1)S(1)} %collective-permute-done.1.refs_0_, f32[32,128]{1,0:T(8,128)S(1)} %get-tuple-element.24.refs_1_, f32[32,128]{1,0:T(8,128)S(1)} %get-tuple-element.25.refs_2_, bf16[1,3584,128]{2,1,0:T(8,128)(2,1)S(1)} %get-tuple-element.22.refs_1_.refs_3_, ...), custom_call_target="tpu_custom_call" | custom-call | tf_op jit(solution)/shard_map/finish/pallas_call | solution.py:218
  17.7 0.2 collective-permute-start.2
  17.9 1.2 %collective-permute-done.2.other_ref = bf16[64,896]{1,0:T(8,128)(2,1)S(1)} collective-permute-done((bf16[64,896]{1,0:T(8,128)(2,1)S(1)}, bf16[64,896]{1,0:T(8,128)(2,1)S(1)}, u32[]{:S(2)}, u32[]{:S(2)}) %collective-permute-start.2) | collective-permute-done | bytes 114720 | tf_op jit(solution)/shard_map/ppermute | solution.py:221
  19.1 7.4 %all_to_all.23 = bf16[4,16,896]{2,1,0:T(8,128)(2,1)S(1)} all-to-all(bf16[4,16,896]{2,1,0:T(8,128)(2,1)S(1)} %bitcast.8), channel_id=1, replica_groups=mesh['groups'=2,'expert'=2,'half'=2,'chip'=2,'core'=2] {'chip','half'}, dimensions={0} | all-to-all | bytes 229376 | tf_op jit(solution)/shard_map/all_to_all | solution.py:222
  26.5 2.7 %collective-permute-start.3 = (bf16[8,896]{1,0:T(8,128)(2,1)S(1)}, bf16[8,896]{1,0:T(8,128)(2,1)S(1)}, u32[]{:S(2)}, u32[]{:S(2)}) collective-permute-start(bf16[8,896]{1,0:T(8,128)(2,1)S(1)} %get-tuple-element.30), channel_id=1, source_target_pairs={{0,8},{8,0},{1,9},{9,1},{2,10},{10,2},{3,11},{11,3},{4,12},{12,4},... | collective-permute-start | bytes 43016 | tf_op jit(solution)/shard_map/ppermute | solution.py:161
  29.2 2.0 %collective-permute-done.3.refs_1_ = bf16[8,896]{1,0:T(8,128)(2,1)S(1)} collective-permute-done((bf16[8,896]{1,0:T(8,128)(2,1)S(1)}, bf16[8,896]{1,0:T(8,128)(2,1)S(1)}, u32[]{:S(2)}, u32[]{:S(2)}) %collective-permute-start.3) | collective-permute-done | bytes 14368 | tf_op jit(solution)/shard_map/ppermute | solution.py:161
  31.2 0.9 %combine.1 = bf16[128,896]{1,0:T(8,128)(2,1)} custom-call(bf16[128,16]{1,0:T(8,128)(2,1)S(1)} %get-tuple-element.19.match_ref, f32[128,1]{1,0:T(8,128)S(1)} %get-tuple-element.20._.weight_ref, bf16[8,896]{1,0:T(8,128)(2,1)S(1)} %get-tuple-element.29.refs_0_, bf16[8,896]{1,0:T(8,128)(2,1)S(1)} %collective-permute-done.3.refs_1_), custom_call_target="tpu_custom_call" | custom-call | tf_op jit(solution)/shard_map/combine/pallas_call | solution.py:224
  (3 shorter events, 0.1 us)
Async XLA Ops:
  0.0 5.3 %copy-start.1 = (f32[128,8]{0,1:T(8,128)S(1)}, f32[128,8]{0,1:T(8,128)}, u32[]{:S(2)}) copy-start(f32[128,8]{0,1:T(8,128)} %param.8) | copy-start | bytes 12292
  1.1 4.1 %copy-start = (s32[128,8]{0,1:T(8,128)S(1)}, s32[128,8]{0,1:T(8,128)}, u32[]{:S(2)}) copy-start(s32[128,8]{0,1:T(8,128)} %param.7) | copy-start | bytes 12292
  1.1 6.1 %collective-permute-start = (bf16[8,896]{1,0:T(8,128)(2,1)S(1)}, bf16[8,896]{1,0:T(8,128)(2,1)S(1)}, u32[]{:S(2)}, u32[]{:S(2)}) collective-permute-start(bf16[8,896]{1,0:T(8,128)(2,1)S(1)} %get-tuple-element.21), channel_id=1, source_target_pairs={{0,8},{8,0},{1,9},{9,1},{2,10},{10,2},{3,11},{11,3},{4,12},{12,4},... | collective-permute-start | bytes 43016 | tf_op jit(solution)/shard_map/ppermute | solution.py:161
  15.8 1.3 %collective-permute-start.1 = (bf16[64,896]{1,0:T(8,128)(2,1)S(1)}, bf16[64,896]{1,0:T(8,128)(2,1)S(1)}, u32[]{:S(2)}, u32[]{:S(2)}) collective-permute-start(bf16[64,896]{1,0:T(8,128)(2,1)S(1)} %bitcast.9), channel_id=1, source_target_pairs={{0,1},{1,0},{2,3},{3,2},{4,5},{5,4},{6,7},{7,6},{8,9},{9,8},{10,11... | collective-permute-start | bytes 344072 | tf_op jit(solution)/shard_map/ppermute | solution.py:215
  17.7 1.4 %collective-permute-start.2 = (bf16[64,896]{1,0:T(8,128)(2,1)S(1)}, bf16[64,896]{1,0:T(8,128)(2,1)S(1)}, u32[]{:S(2)}, u32[]{:S(2)}) collective-permute-start(bf16[64,896]{1,0:T(8,128)(2,1)S(1)} %get-tuple-element.28), channel_id=1, source_target_pairs={{0,1},{1,0},{2,3},{3,2},{4,5},{5,4},{6,7},{7,6},{8,9},{9,8},{10,11... | collective-permute-start | bytes 344072 | tf_op jit(solution)/shard_map/ppermute | solution.py:221
  26.5 4.7 %collective-permute-start.3 = (bf16[8,896]{1,0:T(8,128)(2,1)S(1)}, bf16[8,896]{1,0:T(8,128)(2,1)S(1)}, u32[]{:S(2)}, u32[]{:S(2)}) collective-permute-start(bf16[8,896]{1,0:T(8,128)(2,1)S(1)} %get-tuple-element.30), channel_id=1, source_target_pairs={{0,8},{8,0},{1,9},{9,1},{2,10},{10,2},{3,11},{11,3},{4,12},{12,4},... | collective-permute-start | bytes 43016 | tf_op jit(solution)/shard_map/ppermute | solution.py:161

commit v6 on v5

v6 whole, which is shorter than its diff:
```python
import jax
import jax.numpy as jnp
from jax import lax
from jax.experimental import pallas as pl
from jax.experimental.pallas import tpu as pltpu
from jax.sharding import PartitionSpec as P

CAP = 8
PIECE = 32
FAR = ("chip", "ep")
SWAP = [(0, 1), (1, 0)]
LIMIT = pltpu.CompilerParams(vmem_limit_bytes=16 * 1024 * 1024)


def iota(shape, dim):
    return lax.broadcasted_iota(jnp.int32, shape, dim)


def to_column(row):
    size = row.shape[1]
    square = (size, size)
    return jnp.sum(jnp.where(iota(square, 0) == iota(square, 1), row, 0.0), axis=1, keepdims=True)


def slot_codes(ids, resident):
    row_count = ids.shape[1]
    expert = jnp.min(ids, axis=0, keepdims=True)
    onehot_shape = (-(-resident // 16) * 16, row_count)
    onehot = jnp.where(expert == iota(onehot_shape, 0).astype(jnp.float32), 1.0, 0.0)
    square = (row_count, row_count)
    earlier = jnp.where(iota(square, 0) < iota(square, 1), 1.0, 0.0).astype(jnp.bfloat16)
    counts = jnp.dot(onehot.astype(jnp.bfloat16), earlier, preferred_element_type=jnp.float32)
    return expert * CAP + jnp.sum(counts * onehot, axis=0, keepdims=True), expert


def row_codes(index, ep_count):
    index = lax.rem(index, ep_count * CAP)
    return ((index // (2 * CAP)) * CAP + lax.rem(index, CAP)).astype(jnp.float32)


def route(ep_count, ids_hbm, tokens_hbm, outgoing_ref, ids_ref, tokens_ref, sems):
    row_count = ids_ref.shape[1]
    parts = row_count // PIECE
    copies = [pltpu.make_async_copy(ids_hbm, ids_ref, sems.at[parts])] + [
        pltpu.make_async_copy(
            tokens_hbm.at[pl.ds(part * PIECE, PIECE), :],
            tokens_ref.at[pl.ds(part * PIECE, PIECE), :],
            sems.at[part],
        )
        for part in range(parts)
    ]
    for copy in copies:
        copy.start()
    copies[0].wait()
    code, _ = slot_codes(ids_ref[...].astype(jnp.float32), ep_count // 2)
    wanted = row_codes(iota((outgoing_ref.shape[0], row_count), 0), ep_count)
    dispatch = jnp.where(code == wanted, 1.0, 0.0).astype(jnp.bfloat16)
    for copy in copies[1:]:
        copy.wait()
    outgoing_ref[...] = jnp.dot(
        dispatch, tokens_ref[...], preferred_element_type=jnp.float32
    ).astype(jnp.bfloat16)


def score(ep_count, ids_ref, scores_ref, _, match_ref, weight_ref):
    ids = ids_ref[...].astype(jnp.float32)
    code, expert = slot_codes(ids, ep_count // 2)
    wanted = row_codes(iota(match_ref.shape, 1), ep_count)
    match_ref[...] = jnp.where(to_column(code) == wanted, 1.0, 0.0).astype(jnp.bfloat16)
    squashed = jax.nn.sigmoid(scores_ref[...])
    chosen = jnp.sum(jnp.where(ids == expert, squashed, 0.0), axis=0, keepdims=True)
    weight_ref[...] = to_column(2.5 * chosen / jnp.sum(squashed, axis=0, keepdims=True))


def lift(chips, own, rows_ref, gate_ref, up_ref):
    part_rows, features = rows_ref.shape[0] // chips, rows_ref.shape[1]
    core = lax.axis_index("core")
    core = core if own else 1 - core
    gate_act = jnp.zeros((part_rows, gate_ref.shape[2]), jnp.float32)
    up_act = jnp.zeros((part_rows, up_ref.shape[2]), jnp.float32)
    for chip in range(chips):
        rows = rows_ref[chip * part_rows : (chip + 1) * part_rows, :]
        columns = pl.ds(pl.multiple_of((2 * chip + core) * features, features), features)
        gate_act += jnp.dot(rows, gate_ref[0, columns, :], preferred_element_type=jnp.float32)
        up_act += jnp.dot(rows, up_ref[0, columns, :], preferred_element_type=jnp.float32)
    return gate_act, up_act


def lower(chips, own, hidden, down_ref, out_ref):
    part_rows, features = out_ref.shape[0] // chips, out_ref.shape[1]
    core = lax.axis_index("core")
    core = core if own else 1 - core
    for chip in range(chips):
        columns = pl.ds(pl.multiple_of((2 * chip + core) * features, features), features)
        out_ref[chip * part_rows : (chip + 1) * part_rows, :] = jnp.dot(
            hidden, down_ref[0, :, columns], preferred_element_type=jnp.float32
        ).astype(jnp.bfloat16)


def begin(chips, rows_ref, gate_ref, up_ref, gate_act_ref, up_act_ref):
    gate_act_ref[...], up_act_ref[...] = lift(chips, True, rows_ref, gate_ref, up_ref)


def theirs(chips, *refs):
    rows_ref, gate_act_ref, up_act_ref, gate_ref, up_ref, down_ref, hidden_ref, other_ref = refs
    gate_act, up_act = lift(chips, False, rows_ref, gate_ref, up_ref)
    gate_act += gate_act_ref[...]
    up_act += up_act_ref[...]
    hidden = (gate_act / (1.0 + jnp.exp(-gate_act)) * up_act).astype(jnp.bfloat16)
    hidden_ref[...] = hidden
    lower(chips, False, hidden, down_ref, other_ref)


def ours(chips, hidden_ref, down_ref, mine_ref):
    lower(chips, True, hidden_ref[...], down_ref, mine_ref)


def add(mine_ref, other_ref, out_ref):
    total = mine_ref[...].astype(jnp.float32) + other_ref[...].astype(jnp.float32)
    out_ref[...] = total.astype(jnp.bfloat16)


def combine(match_ref, weight_ref, returned_ref, out_hbm, out_ref, sems):
    copies = []
    for part in range(out_ref.shape[0] // PIECE):
        rows = pl.ds(part * PIECE, PIECE)
        summed = jnp.dot(match_ref[rows, :], returned_ref[...], preferred_element_type=jnp.float32)
        out_ref[rows, :] = (weight_ref[rows, :] * summed).astype(jnp.bfloat16)
        copies.append(pltpu.make_async_copy(out_ref.at[rows, :], out_hbm.at[rows, :], sems.at[part]))
        copies[-1].start()
    for copy in copies:
        copy.wait()


def shards(tokens, expert_ids, route_scores, w_gate, w_up, w_down):
    row_count, features = tokens.shape
    top_count, hidden_count = expert_ids.shape[1], w_gate.shape[2]
    ep_count, chips = lax.axis_size("ep"), lax.axis_size("chip")
    slot_count = ep_count * CAP
    half = jax.ShapeDtypeStruct((chips * slot_count, features), jnp.bfloat16)
    ids, scores = expert_ids.T, route_scores.T
    hbm, vmem = (pl.BlockSpec(memory_space=space) for space in (pltpu.HBM, pltpu.VMEM))
    anywhere = pl.BlockSpec(memory_space=pl.ANY)

    def call(kernel, name, out_shape, **rest):
        return pl.pallas_call(kernel, out_shape=out_shape, name=name, compiler_params=LIMIT, **rest)

    outgoing = call(
        lambda *refs: route(ep_count, *refs),
        "route",
        half,
        in_specs=[hbm] * 2,
        scratch_shapes=[
            pltpu.VMEM((top_count, row_count), jnp.int32),
            pltpu.VMEM((row_count, features), jnp.bfloat16),
            pltpu.SemaphoreType.DMA((row_count // PIECE + 1,)),
        ],
        cost_estimate=pl.CostEstimate(flops=2 * 10**9, bytes_accessed=0, transcendentals=0),
    )(*(pltpu.with_memory_space_constraint(value, pltpu.HBM) for value in (ids, tokens)))
    incoming = lax.all_to_all(outgoing, FAR, split_axis=0, concat_axis=0, tiled=True)
    across = lax.ppermute(incoming, "core", SWAP)
    acts = (jax.ShapeDtypeStruct((slot_count, hidden_count), jnp.float32),) * 2
    begun = call(lambda *refs: begin(chips, *refs), "begin", acts)(incoming, w_gate, w_up)
    hidden_shape = jax.ShapeDtypeStruct((slot_count, hidden_count), jnp.bfloat16)
    hidden, other = call(lambda *refs: theirs(chips, *refs), "theirs", (hidden_shape, half))(
        across, *begun, w_gate, w_up, w_down
    )
    crossed = lax.ppermute(other, "core", SWAP)
    mine = call(lambda *refs: ours(chips, *refs), "ours", half)(hidden, w_down)
    match, weight = call(
        lambda *refs: score(ep_count, *refs),
        "score",
        (
            jax.ShapeDtypeStruct((row_count, chips * slot_count), jnp.bfloat16),
            jax.ShapeDtypeStruct((row_count, 1), jnp.float32),
        ),
        in_specs=[vmem] * 2 + [anywhere],
    )(ids, scores, other)
    summed = call(add, "add", half)(mine, crossed)
    returned = lax.all_to_all(summed, FAR, split_axis=0, concat_axis=0, tiled=True)
    return call(
        combine,
        "combine",
        jax.ShapeDtypeStruct((row_count, features), jnp.bfloat16),
        out_specs=hbm,
        scratch_shapes=[
            pltpu.VMEM((row_count, features), jnp.bfloat16),
            pltpu.SemaphoreType.DMA((row_count // PIECE,)),
        ],
    )(match, weight, returned)


def solution(mesh):
    groups, ep_count, tp_count = (mesh.shape[name] for name in ("groups", "ep", "tp"))
    split = jax.sharding.Mesh(
        mesh.devices.reshape(groups, ep_count, tp_count // 2, 2), ("groups", "ep", "chip", "core")
    )
    tp = ("chip", "core")
    placed = (
        P(("groups", "ep"), tp),
        P(("groups", "ep"), None),
        P(("groups", "ep"), None),
        P("ep", None, tp),
        P("ep", None, tp),
        P("ep", tp, None),
    )
    return jax.shard_map(
        shards, mesh=split, in_specs=placed, out_specs=P(("groups", "ep"), tp), check_vma=False
    )
```

time: 32.3 us -> 31.7 us (0.981)
  waiting for transfers between devices: 4.22 us -> 9.17 us
  starting transfers between devices: 7.01 us -> 3.72 us
  blocking collectives: 16 us -> 14.4 us
  Pallas kernels: 4.78 us -> 3.95 us
    all_to_all x0 -> x1, waiting for transfers between devices: none -> 7.16 us  [shards(): lax.all_to_all(summed, FAR, split_axis=0, concat_axis=0, tiled=True)]
    ppermute x3 -> x1, starting transfers between devices: 7.01 us -> 0.22 us  [shards(): crossed = lax.ppermute(other, 'core', SWAP)]
    all_to_all x0 -> x1, starting transfers between devices: none -> 3.5 us  [shards(): lax.all_to_all(summed, FAR, split_axis=0, concat_axis=0, tiled=True)]
    ppermute x3 -> x1, waiting for transfers between devices: 3.16 us -> 0.98 us  [shards(): crossed = lax.ppermute(other, 'core', SWAP)]
    all_to_all x2 -> x1, blocking collectives: 16 us -> 14.4 us  [shards(): lax.all_to_all(outgoing, FAR, split_axis=0, concat_axis=0, tiled=True)]
    pallas_call x7 -> x6, Pallas kernels: 4.52 us -> 3.68 us  [the longest x1 1.27 us: shards(): call(lambda *refs: route(ep_count, *refs), 'route', half, in_specs=[hbm]...]
  transfers between devices with their start and end apart: 4 -> 3, of which waited for: 3 -> 3; matrix products, arithmetic and copies ran while one was open for 0% -> 0% of each run, Pallas kernels for 7% -> 2%
where the time goes in v6:
time: 31.7 us; the launch traced here: 31.4 us
  blocking collectives  14.4 us (45%)
  waiting for transfers between devices  9.17 us (29%)
  Pallas kernels  3.95 us (12%)
  starting transfers between devices  3.72 us (12%)
    all_to_all x1, blocking collectives, shards(): lax.all_to_all(outgoing, FAR, split_axis=0, concat_axis=0, tiled=True)  14.4 us
    all_to_all x1, waiting for transfers between devices, shards(): lax.all_to_all(summed, FAR, split_axis=0, concat_axis=0, tiled=True)  7.16 us
    all_to_all x1, starting transfers between devices, shards(): lax.all_to_all(summed, FAR, split_axis=0, concat_axis=0, tiled=True)  3.5 us
    pallas_call x1, Pallas kernels, shards(): call(lambda *refs: route(ep_count, *refs), 'route', half, in_specs=[hbm]...  1.27 us
    ppermute x1, waiting for transfers between devices, shards(): across = lax.ppermute(incoming, 'core', SWAP)  1.03 us
    ppermute x1, waiting for transfers between devices, shards(): crossed = lax.ppermute(other, 'core', SWAP)  0.98 us
    pallas_call x1, Pallas kernels, shards(): call(combine, 'combine', jax.ShapeDtypeStruct((row_count, features), jnp....  0.87 us
    pallas_call x1, Pallas kernels, shards(): summed = call(add, 'add', half)(mine, crossed)  0.67 us
  transfers between devices with their start and end apart: 3, of which 3 were waited for; matrix products, arithmetic and copies ran while one was open for 0% of the time, Pallas kernels for 2%

profile of v6, /device:TPU:0, one launch (start us, length us, event | category | flops | bytes accessed | tf_op | source)
XLA Modules:
  0.0 31.4 jit_solution(14917573520064138742)
XLA Ops:
  0.0 0.0 copy-start
  0.0 0.0 copy-start.1
  0.0 1.3 %route.1 = bf16[64,896]{1,0:T(8,128)(2,1)S(1)} custom-call(s32[8,128]{1,0:T(8,128)} %bitcast.10, bf16[128,896]{1,0:T(8,128)(2,1)} %refs_1_.3), custom_call_target="tpu_custom_call" | custom-call | flops 2000000000 | tf_op jit(solution)/shard_map/route/pallas_call | solution.py:148
  1.3 14.4 %all_to_all.22 = bf16[8,8,896]{2,1,0:T(8,128)(2,1)S(1)} all-to-all(bf16[8,8,896]{2,1,0:T(8,128)(2,1)S(1)} %bitcast.9), channel_id=1, replica_groups=mesh['groups'=2,'ep'=4,'chip'=2,'core'=2] {'chip','ep'}, dimensions={0} | all-to-all | bytes 229376 | tf_op jit(solution)/shard_map/all_to_all | solution.py:160
  15.7 0.0 copy-start.2
  15.7 0.0 collective-permute-start
  15.7 0.0 copy-done
  15.7 0.0 copy-done.1
  15.7 0.3 begin.1
  16.0 1.0 %collective-permute-done.refs_0_ = bf16[64,896]{1,0:T(8,128)(2,1)S(1)} collective-permute-done((bf16[64,896]{1,0:T(8,128)(2,1)S(1)}, bf16[64,896]{1,0:T(8,128)(2,1)S(1)}, u32[]{:S(2)}, u32[]{:S(2)}) %collective-permute-start) | collective-permute-done | bytes 114720 | tf_op jit(solution)/shard_map/ppermute | solution.py:161
  17.1 0.0 copy-done.2
  17.1 0.4 %theirs.1 = (bf16[32,128]{1,0:T(8,128)(2,1)S(1)}, bf16[64,896]{1,0:T(8,128)(2,1)S(1)}) custom-call(bf16[64,896]{1,0:T(8,128)(2,1)S(1)} %collective-permute-done.refs_0_, f32[32,128]{1,0:T(8,128)S(1)} %get-tuple-element.11.refs_1_, f32[32,128]{1,0:T(8,128)S(1)} %get-tuple-element.12.refs_2_, bf16[1,3584,128]{2,1,0:T(8,128)(2,1)S(1)} %copy-done, ...), custom_call_target="tpu_custom_call" | custom-call | tf_op jit(solution)/shard_map/theirs/pallas_call | solution.py:165
  17.5 0.2 collective-permute-start.1
  17.7 0.2 ours.1.mine_ref
  17.9 1.0 %collective-permute-done.1.other_ref = bf16[64,896]{1,0:T(8,128)(2,1)S(1)} collective-permute-done((bf16[64,896]{1,0:T(8,128)(2,1)S(1)}, bf16[64,896]{1,0:T(8,128)(2,1)S(1)}, u32[]{:S(2)}, u32[]{:S(2)}) %collective-permute-start.1) | collective-permute-done | bytes 114720 | tf_op jit(solution)/shard_map/ppermute | solution.py:168
  18.9 0.7 %add.1 = bf16[64,896]{1,0:T(8,128)(2,1)} custom-call(bf16[64,896]{1,0:T(8,128)(2,1)S(1)} %ours.1.mine_ref, bf16[64,896]{1,0:T(8,128)(2,1)S(1)} %collective-permute-done.1.other_ref), custom_call_target="tpu_custom_call" | custom-call | tf_op jit(solution)/shard_map/add/pallas_call | solution.py:179
  19.6 0.0 copy-start.3
  19.6 0.0 copy-start.4
  19.6 3.5 %all-to-all-start.1 = ((bf16[8,8,896]{2,1,0:T(8,128)(2,1)}), bf16[8,8,896]{2,1,0:T(8,128)(2,1)S(1)}, u32[]{:S(2)}, u32[]{:S(2)}) async-start(bf16[8,8,896]{2,1,0:T(8,128)(2,1)} %bitcast.4), calls=%async_computation.1 | async-start | bytes 229376 | tf_op jit(solution)/shard_map/all_to_all | solution.py:180
  23.1 0.0 copy-done.3
  23.1 0.0 copy-done.4
  23.1 0.2 score.1
  23.3 7.2 %all-to-all-done.1 = bf16[8,8,896]{2,1,0:T(8,128)(2,1)S(1)} async-done(((bf16[8,8,896]{2,1,0:T(8,128)(2,1)}), bf16[8,8,896]{2,1,0:T(8,128)(2,1)S(1)}, u32[]{:S(2)}, u32[]{:S(2)}) %all-to-all-start.1) | async-done | bytes 114720 | tf_op jit(solution)/shard_map/all_to_all | solution.py:180
  30.5 0.9 %combine.1 = bf16[128,896]{1,0:T(8,128)(2,1)} custom-call(bf16[128,64]{1,0:T(8,128)(2,1)S(1)} %get-tuple-element.14.match_ref, f32[128,1]{1,0:T(8,128)S(1)} %get-tuple-element.15.weight_ref, bf16[64,896]{1,0:T(8,128)(2,1)S(1)} %bitcast.6), custom_call_target="tpu_custom_call" | custom-call | tf_op jit(solution)/shard_map/combine/pallas_call | solution.py:181
Async XLA Ops:
  0.0 15.7 %copy-start = (bf16[1,3584,128]{2,1,0:T(8,128)(2,1)S(1)}, bf16[1,3584,128]{2,1,0:T(8,128)(2,1)}, u32[]{:S(2)}) copy-start(bf16[1,3584,128]{2,1,0:T(8,128)(2,1)} %refs_3_.1) | copy-start | bytes 2752516
  0.0 15.7 %copy-start.1 = (bf16[1,3584,128]{2,1,0:T(8,128)(2,1)S(1)}, bf16[1,3584,128]{2,1,0:T(8,128)(2,1)}, u32[]{:S(2)}) copy-start(bf16[1,3584,128]{2,1,0:T(8,128)(2,1)} %refs_4_.1) | copy-start | bytes 2752516
  15.7 1.3 %copy-start.2 = (bf16[1,128,3584]{2,1,0:T(8,128)(2,1)S(1)}, bf16[1,128,3584]{2,1,0:T(8,128)(2,1)}, u32[]{:S(2)}) copy-start(bf16[1,128,3584]{2,1,0:T(8,128)(2,1)} %refs_1_.5) | copy-start | bytes 2752516
  15.7 1.3 %collective-permute-start = (bf16[64,896]{1,0:T(8,128)(2,1)S(1)}, bf16[64,896]{1,0:T(8,128)(2,1)S(1)}, u32[]{:S(2)}, u32[]{:S(2)}) collective-permute-start(bf16[64,896]{1,0:T(8,128)(2,1)S(1)} %bitcast.7), channel_id=1, source_target_pairs={{0,1},{1,0},{2,3},{3,2},{4,5},{5,4},{6,7},{7,6},{8,9},{9,8},{10,11... | collective-permute-start | bytes 344072 | tf_op jit(solution)/shard_map/ppermute | solution.py:161
  17.5 1.4 %collective-permute-start.1 = (bf16[64,896]{1,0:T(8,128)(2,1)S(1)}, bf16[64,896]{1,0:T(8,128)(2,1)S(1)}, u32[]{:S(2)}, u32[]{:S(2)}) collective-permute-start(bf16[64,896]{1,0:T(8,128)(2,1)S(1)} %get-tuple-element.13.refs_2_), channel_id=1, source_target_pairs={{0,1},{1,0},{2,3},{3,2},{4,5},{5,4},{6,7},{7,6},{8,9},{9,8},{10,11... | collective-permute-start | bytes 344072 | tf_op jit(solution)/shard_map/ppermute | solution.py:168
  19.6 3.5 %copy-start.3 = (s32[128,8]{0,1:T(8,128)S(1)}, s32[128,8]{0,1:T(8,128)}, u32[]{:S(2)}) copy-start(s32[128,8]{0,1:T(8,128)} %param.7) | copy-start | bytes 12292
  19.6 3.5 %copy-start.4 = (f32[128,8]{0,1:T(8,128)S(1)}, f32[128,8]{0,1:T(8,128)}, u32[]{:S(2)}) copy-start(f32[128,8]{0,1:T(8,128)} %param.8) | copy-start | bytes 12292
  19.6 10.9 %all-to-all-start.1 = ((bf16[8,8,896]{2,1,0:T(8,128)(2,1)}), bf16[8,8,896]{2,1,0:T(8,128)(2,1)S(1)}, u32[]{:S(2)}, u32[]{:S(2)}) async-start(bf16[8,8,896]{2,1,0:T(8,128)(2,1)} %bitcast.4), calls=%async_computation.1 | async-start | bytes 229376 | tf_op jit(solution)/shard_map/all_to_all | solution.py:180

commit v7 on v6

--- a/solution.py
+++ b/solution.py
@@ -115,7 +115,7 @@
     lower(chips, True, hidden_ref[...], down_ref, mine_ref)
 
 
-def add(mine_ref, other_ref, out_ref):
+def add(mine_ref, other_ref, _, out_ref):
     total = mine_ref[...].astype(jnp.float32) + other_ref[...].astype(jnp.float32)
     out_ref[...] = total.astype(jnp.bfloat16)
 
@@ -176,7 +176,7 @@
         ),
         in_specs=[vmem] * 2 + [anywhere],
     )(ids, scores, other)
-    summed = call(add, "add", half)(mine, crossed)
+    summed = call(add, "add", half, in_specs=[vmem] * 2 + [anywhere])(mine, crossed, weight)
     returned = lax.all_to_all(summed, FAR, split_axis=0, concat_axis=0, tiled=True)
     return call(
         combine,

time: 31.7 us -> 29.9 us (0.943)
  blocking collectives: 14.4 us -> 24.3 us
  waiting for transfers between devices: 9.17 us -> 1.72 us
  starting transfers between devices: 3.72 us -> 0.22 us
  Pallas kernels: 3.95 us -> 3.32 us
    all_to_all x0 -> x1, blocking collectives: none -> 9.88 us  [shards(): lax.all_to_all(summed, FAR, split_axis=0, concat_axis=0, tiled=True)]
    all_to_all x1 -> x0, waiting for transfers between devices: 7.16 us -> none  [shards(): lax.all_to_all(summed, FAR, split_axis=0, concat_axis=0, tiled=True)]
    all_to_all x1 -> x0, starting transfers between devices: 3.5 us -> none  [shards(): lax.all_to_all(summed, FAR, split_axis=0, concat_axis=0, tiled=True)]
    pallas_call x1, Pallas kernels: 0.67 us -> 0.03 us  [shards(): call(add, 'add', half, in_specs=[vmem] * 2 + [anywhere])]
  transfers between devices with their start and end apart: 3 -> 2, of which waited for: 3 -> 2; matrix products, arithmetic and copies ran while one was open for 0% -> 0% of each run, Pallas kernels for 2% -> 2%
where the time goes in v7:
time: 29.9 us; the launch traced here: 29.7 us
  blocking collectives  24.3 us (81%)
  Pallas kernels  3.32 us (11%)
  waiting for transfers between devices  1.72 us (6%)
    all_to_all x1, blocking collectives, shards(): lax.all_to_all(outgoing, FAR, split_axis=0, concat_axis=0, tiled=True)  14.4 us
    all_to_all x1, blocking collectives, shards(): lax.all_to_all(summed, FAR, split_axis=0, concat_axis=0, tiled=True)  9.88 us
    pallas_call x1, Pallas kernels, shards(): call(lambda *refs: route(ep_count, *refs), 'route', half, in_specs=[hbm]...  1.27 us
    ppermute x1, waiting for transfers between devices, shards(): across = lax.ppermute(incoming, 'core', SWAP)  1.03 us
    pallas_call x1, Pallas kernels, shards(): call(combine, 'combine', jax.ShapeDtypeStruct((row_count, features), jnp....  0.87 us
    ppermute x1, waiting for transfers between devices, shards(): crossed = lax.ppermute(other, 'core', SWAP)  0.7 us
  transfers between devices with their start and end apart: 2, of which 2 were waited for; matrix products, arithmetic and copies ran while one was open for 0% of the time, Pallas kernels for 2%

profile of v7, /device:TPU:0, one launch (start us, length us, event | category | flops | bytes accessed | tf_op | source)
XLA Modules:
  0.0 29.7 jit_solution(12297221915969804059)
XLA Ops:
  0.0 0.0 copy-start
  0.0 0.0 copy-start.1
  0.0 1.3 %route.1 = bf16[64,896]{1,0:T(8,128)(2,1)S(1)} custom-call(s32[8,128]{1,0:T(8,128)} %bitcast.11, bf16[128,896]{1,0:T(8,128)(2,1)} %refs_1_.3), custom_call_target="tpu_custom_call" | custom-call | flops 2000000000 | tf_op jit(solution)/shard_map/route/pallas_call | solution.py:148
  1.3 14.4 %all_to_all.22 = bf16[8,8,896]{2,1,0:T(8,128)(2,1)S(1)} all-to-all(bf16[8,8,896]{2,1,0:T(8,128)(2,1)S(1)} %bitcast.10), channel_id=1, replica_groups=mesh['groups'=2,'ep'=4,'chip'=2,'core'=2] {'chip','ep'}, dimensions={0} | all-to-all | bytes 229376 | tf_op jit(solution)/shard_map/all_to_all | solution.py:160
  15.7 0.0 copy-start.2
  15.7 0.0 collective-permute-start
  15.7 0.0 copy-done
  15.7 0.0 copy-done.1
  15.7 0.3 begin.1
  16.0 1.0 %collective-permute-done.refs_0_ = bf16[64,896]{1,0:T(8,128)(2,1)S(1)} collective-permute-done((bf16[64,896]{1,0:T(8,128)(2,1)S(1)}, bf16[64,896]{1,0:T(8,128)(2,1)S(1)}, u32[]{:S(2)}, u32[]{:S(2)}) %collective-permute-start) | collective-permute-done | bytes 114720 | tf_op jit(solution)/shard_map/ppermute | solution.py:161
  17.1 0.0 copy-done.2
  17.1 0.0 copy-start.3
  17.1 0.0 copy-start.4
  17.1 0.4 %theirs.1 = (bf16[32,128]{1,0:T(8,128)(2,1)S(1)}, bf16[64,896]{1,0:T(8,128)(2,1)S(1)}) custom-call(bf16[64,896]{1,0:T(8,128)(2,1)S(1)} %collective-permute-done.refs_0_, f32[32,128]{1,0:T(8,128)S(1)} %get-tuple-element.11.refs_1_, f32[32,128]{1,0:T(8,128)S(1)} %get-tuple-element.12.refs_2_, bf16[1,3584,128]{2,1,0:T(8,128)(2,1)S(1)} %copy-done, ...), custom_call_target="tpu_custom_call" | custom-call | tf_op jit(solution)/shard_map/theirs/pallas_call | solution.py:165
  17.5 0.2 collective-permute-start.1
  17.7 0.0 copy-done.3
  17.7 0.0 copy-done.4
  17.8 0.2 score.1
  18.0 0.2 ours.1.mine_ref
  18.2 0.7 %collective-permute-done.1.other_ref = bf16[64,896]{1,0:T(8,128)(2,1)S(1)} collective-permute-done((bf16[64,896]{1,0:T(8,128)(2,1)S(1)}, bf16[64,896]{1,0:T(8,128)(2,1)S(1)}, u32[]{:S(2)}, u32[]{:S(2)}) %collective-permute-start.1) | collective-permute-done | bytes 114720 | tf_op jit(solution)/shard_map/ppermute | solution.py:168
  18.9 9.9 %all_to_all.23 = bf16[8,8,896]{2,1,0:T(8,128)(2,1)S(1)} all-to-all(bf16[8,8,896]{2,1,0:T(8,128)(2,1)S(1)} %bitcast.7), channel_id=1, replica_groups=mesh['groups'=2,'ep'=4,'chip'=2,'core'=2] {'chip','ep'}, dimensions={0} | all-to-all | bytes 229376 | tf_op jit(solution)/shard_map/all_to_all | solution.py:180
  28.8 0.9 %combine.1 = bf16[128,896]{1,0:T(8,128)(2,1)} custom-call(bf16[128,64]{1,0:T(8,128)(2,1)S(1)} %get-tuple-element.14.match_ref, f32[128,1]{1,0:T(8,128)S(1)} %get-tuple-element.15._.weight_ref, bf16[64,896]{1,0:T(8,128)(2,1)S(1)} %bitcast.6), custom_call_target="tpu_custom_call" | custom-call | tf_op jit(solution)/shard_map/combine/pallas_call | solution.py:181
  (1 shorter events, 0.0 us)
Async XLA Ops:
  0.0 15.7 %copy-start = (bf16[1,3584,128]{2,1,0:T(8,128)(2,1)S(1)}, bf16[1,3584,128]{2,1,0:T(8,128)(2,1)}, u32[]{:S(2)}) copy-start(bf16[1,3584,128]{2,1,0:T(8,128)(2,1)} %refs_3_.1) | copy-start | bytes 2752516
  0.0 15.7 %copy-start.1 = (bf16[1,3584,128]{2,1,0:T(8,128)(2,1)S(1)}, bf16[1,3584,128]{2,1,0:T(8,128)(2,1)}, u32[]{:S(2)}) copy-start(bf16[1,3584,128]{2,1,0:T(8,128)(2,1)} %refs_4_.1) | copy-start | bytes 2752516
  15.7 1.3 %copy-start.2 = (bf16[1,128,3584]{2,1,0:T(8,128)(2,1)S(1)}, bf16[1,128,3584]{2,1,0:T(8,128)(2,1)}, u32[]{:S(2)}) copy-start(bf16[1,128,3584]{2,1,0:T(8,128)(2,1)} %refs_1_.5) | copy-start | bytes 2752516
  15.7 1.3 %collective-permute-start = (bf16[64,896]{1,0:T(8,128)(2,1)S(1)}, bf16[64,896]{1,0:T(8,128)(2,1)S(1)}, u32[]{:S(2)}, u32[]{:S(2)}) collective-permute-start(bf16[64,896]{1,0:T(8,128)(2,1)S(1)} %bitcast.8), channel_id=1, source_target_pairs={{0,1},{1,0},{2,3},{3,2},{4,5},{5,4},{6,7},{7,6},{8,9},{9,8},{10,11... | collective-permute-start | bytes 344072 | tf_op jit(solution)/shard_map/ppermute | solution.py:161
  17.1 0.7 %copy-start.3 = (s32[128,8]{0,1:T(8,128)S(1)}, s32[128,8]{0,1:T(8,128)}, u32[]{:S(2)}) copy-start(s32[128,8]{0,1:T(8,128)} %param.7) | copy-start | bytes 12292
  17.1 0.7 %copy-start.4 = (f32[128,8]{0,1:T(8,128)S(1)}, f32[128,8]{0,1:T(8,128)}, u32[]{:S(2)}) copy-start(f32[128,8]{0,1:T(8,128)} %param.8) | copy-start | bytes 12292
  17.5 1.4 %collective-permute-start.1 = (bf16[64,896]{1,0:T(8,128)(2,1)S(1)}, bf16[64,896]{1,0:T(8,128)(2,1)S(1)}, u32[]{:S(2)}, u32[]{:S(2)}) collective-permute-start(bf16[64,896]{1,0:T(8,128)(2,1)S(1)} %get-tuple-element.13.refs_2_), channel_id=1, source_target_pairs={{0,1},{1,0},{2,3},{3,2},{4,5},{5,4},{6,7},{7,6},{8,9},{9,8},{10,11... | collective-permute-start | bytes 344072 | tf_op jit(solution)/shard_map/ppermute | solution.py:168

commit v8 on v7

--- a/solution.py
+++ b/solution.py
@@ -7,7 +7,7 @@
 
 CAP = 8
 PIECE = 32
-FAR = ("chip", "ep")
+FAR = ("ep", "chip", "core")
 SWAP = [(0, 1), (1, 0)]
 LIMIT = pltpu.CompilerParams(vmem_limit_bytes=16 * 1024 * 1024)
 
@@ -72,15 +72,25 @@
     weight_ref[...] = to_column(2.5 * chosen / jnp.sum(squashed, axis=0, keepdims=True))
 
 
+def far_groups(ep_count, chips):
+    return [
+        [(z * chips + x) * 2 + (side + x) % 2 for x in range(chips) for z in range(ep_count)]
+        for side in range(2)
+    ]
+
+
+def columns_of(chip, own, features):
+    core = lax.rem(lax.axis_index("core") + lax.axis_index("chip") + chip + (0 if own else 1), 2)
+    return pl.ds(pl.multiple_of((2 * chip + core) * features, features), features)
+
+
 def lift(chips, own, rows_ref, gate_ref, up_ref):
     part_rows, features = rows_ref.shape[0] // chips, rows_ref.shape[1]
-    core = lax.axis_index("core")
-    core = core if own else 1 - core
     gate_act = jnp.zeros((part_rows, gate_ref.shape[2]), jnp.float32)
     up_act = jnp.zeros((part_rows, up_ref.shape[2]), jnp.float32)
     for chip in range(chips):
         rows = rows_ref[chip * part_rows : (chip + 1) * part_rows, :]
-        columns = pl.ds(pl.multiple_of((2 * chip + core) * features, features), features)
+        columns = columns_of(chip, own, features)
         gate_act += jnp.dot(rows, gate_ref[0, columns, :], preferred_element_type=jnp.float32)
         up_act += jnp.dot(rows, up_ref[0, columns, :], preferred_element_type=jnp.float32)
     return gate_act, up_act
@@ -88,10 +98,8 @@
 
 def lower(chips, own, hidden, down_ref, out_ref):
     part_rows, features = out_ref.shape[0] // chips, out_ref.shape[1]
-    core = lax.axis_index("core")
-    core = core if own else 1 - core
     for chip in range(chips):
-        columns = pl.ds(pl.multiple_of((2 * chip + core) * features, features), features)
+        columns = columns_of(chip, own, features)
         out_ref[chip * part_rows : (chip + 1) * part_rows, :] = jnp.dot(
             hidden, down_ref[0, :, columns], preferred_element_type=jnp.float32
         ).astype(jnp.bfloat16)
@@ -141,6 +149,10 @@
     ids, scores = expert_ids.T, route_scores.T
     hbm, vmem = (pl.BlockSpec(memory_space=space) for space in (pltpu.HBM, pltpu.VMEM))
     anywhere = pl.BlockSpec(memory_space=pl.ANY)
+
+    def exchange(rows):
+        groups = far_groups(ep_count, chips)
+        return lax.all_to_all(rows, FAR, 0, 0, axis_index_groups=groups, tiled=True)
 
     def call(kernel, name, out_shape, **rest):
         return pl.pallas_call(kernel, out_shape=out_shape, name=name, compiler_params=LIMIT, **rest)
@@ -157,7 +169,7 @@
         ],
         cost_estimate=pl.CostEstimate(flops=2 * 10**9, bytes_accessed=0, transcendentals=0),
     )(*(pltpu.with_memory_space_constraint(value, pltpu.HBM) for value in (ids, tokens)))
-    incoming = lax.all_to_all(outgoing, FAR, split_axis=0, concat_axis=0, tiled=True)
+    incoming = exchange(outgoing)
     across = lax.ppermute(incoming, "core", SWAP)
     acts = (jax.ShapeDtypeStruct((slot_count, hidden_count), jnp.float32),) * 2
     begun = call(lambda *refs: begin(chips, *refs), "begin", acts)(incoming, w_gate, w_up)
@@ -177,7 +189,7 @@
         in_specs=[vmem] * 2 + [anywhere],
     )(ids, scores, other)
     summed = call(add, "add", half, in_specs=[vmem] * 2 + [anywhere])(mine, crossed, weight)
-    returned = lax.all_to_all(summed, FAR, split_axis=0, concat_axis=0, tiled=True)
+    returned = exchange(summed)
     return call(
         combine,
         "combine",

time: 29.9 us -> 28.9 us (0.967)
  blocking collectives: 24.3 us -> 23.1 us
  starting transfers between devices: 0.22 us -> 1.02 us
  waiting for transfers between devices: 1.72 us -> 1.2 us
    all_to_all x2, blocking collectives: 24.3 us -> 23.1 us  [exchange(): return lax.all_to_all(rows, FAR, 0, 0, axis_index_groups=groups, tiled=True)]
    ppermute x1, starting transfers between devices: 0.01 us -> 0.59 us  [shards(): across = lax.ppermute(incoming, 'core', SWAP)]
    ppermute x1, waiting for transfers between devices: 1.03 us -> 0.69 us  [shards(): across = lax.ppermute(incoming, 'core', SWAP)]
where the time goes in v8:
time: 28.9 us; the launch traced here: 28.7 us
  blocking collectives  23.1 us (80%)
  Pallas kernels  3.33 us (12%)
  waiting for transfers between devices  1.2 us (4%)
  starting transfers between devices  1.02 us (4%)
    all_to_all x2, blocking collectives, exchange(): return lax.all_to_all(rows, FAR, 0, 0, axis_index_groups=groups, tiled=True)  23.1 us
    pallas_call x1, Pallas kernels, shards(): call(lambda *refs: route(ep_count, *refs), 'route', half, in_specs=[hbm]...  1.27 us
    pallas_call x1, Pallas kernels, shards(): call(combine, 'combine', jax.ShapeDtypeStruct((row_count, features), jnp....  0.87 us
    ppermute x1, waiting for transfers between devices, shards(): across = lax.ppermute(incoming, 'core', SWAP)  0.69 us
    ppermute x1, starting transfers between devices, shards(): across = lax.ppermute(incoming, 'core', SWAP)  0.59 us
  transfers between devices with their start and end apart: 2, of which 2 were waited for; matrix products, arithmetic and copies ran while one was open for 0% of the time, Pallas kernels for 2%

profile of v8, /device:TPU:0, one launch (start us, length us, event | category | flops | bytes accessed | tf_op | source)
XLA Modules:
  0.0 28.7 jit_solution(11211513572376315333)
XLA Ops:
  0.0 0.0 copy-start
  0.0 0.0 copy-start.1
  0.0 1.3 %route.1 = bf16[64,896]{1,0:T(8,128)(2,1)S(1)} custom-call(s32[8,128]{1,0:T(8,128)} %bitcast.11, bf16[128,896]{1,0:T(8,128)(2,1)} %refs_1_.3), custom_call_target="tpu_custom_call" | custom-call | flops 2000000000 | tf_op jit(solution)/shard_map/route/pallas_call | solution.py:160
  1.3 13.4 %all_to_all.22 = bf16[8,8,896]{2,1,0:T(8,128)(2,1)S(1)} all-to-all(bf16[8,8,896]{2,1,0:T(8,128)(2,1)S(1)} %bitcast.10), channel_id=1, replica_groups={{0,4,8,12,3,7,11,15},{1,5,9,13,2,6,10,14},{16,20,24,28,19,23,27,31},{17..., dimensions={0} | all-to-all | bytes 229376 | tf_op jit(solution)/shard_map/all_to_all | solution.py:155
  14.7 0.0 copy-start.2
  14.7 0.6 %collective-permute-start = (bf16[64,896]{1,0:T(8,128)(2,1)S(1)}, bf16[64,896]{1,0:T(8,128)(2,1)S(1)}, u32[]{:S(2)}, u32[]{:S(2)}) collective-permute-start(bf16[64,896]{1,0:T(8,128)(2,1)S(1)} %bitcast.8), channel_id=1, source_target_pairs={{0,1},{1,0},{2,3},{3,2},{4,5},{5,4},{6,7},{7,6},{8,9},{9,8},{10,11... | collective-permute-start | bytes 344072 | tf_op jit(solution)/shard_map/ppermute | solution.py:173
  15.3 0.0 copy-done
  15.3 0.0 copy-done.1
  15.3 0.3 begin.1
  15.6 0.7 %collective-permute-done.refs_0_ = bf16[64,896]{1,0:T(8,128)(2,1)S(1)} collective-permute-done((bf16[64,896]{1,0:T(8,128)(2,1)S(1)}, bf16[64,896]{1,0:T(8,128)(2,1)S(1)}, u32[]{:S(2)}, u32[]{:S(2)}) %collective-permute-start) | collective-permute-done | bytes 114720 | tf_op jit(solution)/shard_map/ppermute | solution.py:173
  16.3 0.0 copy-done.2
  16.3 0.0 copy-start.3
  16.3 0.0 copy-start.4
  16.3 0.5 %theirs.1 = (bf16[32,128]{1,0:T(8,128)(2,1)S(1)}, bf16[64,896]{1,0:T(8,128)(2,1)S(1)}) custom-call(bf16[64,896]{1,0:T(8,128)(2,1)S(1)} %collective-permute-done.refs_0_, f32[32,128]{1,0:T(8,128)S(1)} %get-tuple-element.11.refs_1_, f32[32,128]{1,0:T(8,128)S(1)} %get-tuple-element.12.refs_2_, bf16[1,3584,128]{2,1,0:T(8,128)(2,1)S(1)} %copy-done, ...), custom_call_target="tpu_custom_call" | custom-call | tf_op jit(solution)/shard_map/theirs/pallas_call | solution.py:177
  16.8 0.4 %collective-permute-start.1 = (bf16[64,896]{1,0:T(8,128)(2,1)S(1)}, bf16[64,896]{1,0:T(8,128)(2,1)S(1)}, u32[]{:S(2)}, u32[]{:S(2)}) collective-permute-start(bf16[64,896]{1,0:T(8,128)(2,1)S(1)} %get-tuple-element.13.refs_2_), channel_id=1, source_target_pairs={{0,1},{1,0},{2,3},{3,2},{4,5},{5,4},{6,7},{7,6},{8,9},{9,8},{10,11... | collective-permute-start | bytes 344072 | tf_op jit(solution)/shard_map/ppermute | solution.py:180
  17.2 0.0 copy-done.3
  17.2 0.0 copy-done.4
  17.2 0.2 score.1
  17.4 0.2 ours.1.mine_ref
  17.7 0.5 %collective-permute-done.1.other_ref = bf16[64,896]{1,0:T(8,128)(2,1)S(1)} collective-permute-done((bf16[64,896]{1,0:T(8,128)(2,1)S(1)}, bf16[64,896]{1,0:T(8,128)(2,1)S(1)}, u32[]{:S(2)}, u32[]{:S(2)}) %collective-permute-start.1) | collective-permute-done | bytes 114720 | tf_op jit(solution)/shard_map/ppermute | solution.py:180
  18.2 9.7 %all_to_all.23 = bf16[8,8,896]{2,1,0:T(8,128)(2,1)S(1)} all-to-all(bf16[8,8,896]{2,1,0:T(8,128)(2,1)S(1)} %bitcast.7), channel_id=1, replica_groups={{0,4,8,12,3,7,11,15},{1,5,9,13,2,6,10,14},{16,20,24,28,19,23,27,31},{17..., dimensions={0} | all-to-all | bytes 229376 | tf_op jit(solution)/shard_map/all_to_all | solution.py:155
  27.9 0.9 %combine.1 = bf16[128,896]{1,0:T(8,128)(2,1)} custom-call(bf16[128,64]{1,0:T(8,128)(2,1)S(1)} %get-tuple-element.14.match_ref, f32[128,1]{1,0:T(8,128)S(1)} %get-tuple-element.15._.weight_ref, bf16[64,896]{1,0:T(8,128)(2,1)S(1)} %bitcast.6), custom_call_target="tpu_custom_call" | custom-call | tf_op jit(solution)/shard_map/combine/pallas_call | solution.py:193
  (1 shorter events, 0.0 us)
Async XLA Ops:
  0.0 15.3 %copy-start = (bf16[1,3584,128]{2,1,0:T(8,128)(2,1)S(1)}, bf16[1,3584,128]{2,1,0:T(8,128)(2,1)}, u32[]{:S(2)}) copy-start(bf16[1,3584,128]{2,1,0:T(8,128)(2,1)} %refs_3_.1) | copy-start | bytes 2752516
  0.0 15.3 %copy-start.1 = (bf16[1,3584,128]{2,1,0:T(8,128)(2,1)S(1)}, bf16[1,3584,128]{2,1,0:T(8,128)(2,1)}, u32[]{:S(2)}) copy-start(bf16[1,3584,128]{2,1,0:T(8,128)(2,1)} %refs_4_.1) | copy-start | bytes 2752516
  14.7 1.6 %copy-start.2 = (bf16[1,128,3584]{2,1,0:T(8,128)(2,1)S(1)}, bf16[1,128,3584]{2,1,0:T(8,128)(2,1)}, u32[]{:S(2)}) copy-start(bf16[1,128,3584]{2,1,0:T(8,128)(2,1)} %refs_1_.5) | copy-start | bytes 2752516
  14.7 1.6 %collective-permute-start = (bf16[64,896]{1,0:T(8,128)(2,1)S(1)}, bf16[64,896]{1,0:T(8,128)(2,1)S(1)}, u32[]{:S(2)}, u32[]{:S(2)}) collective-permute-start(bf16[64,896]{1,0:T(8,128)(2,1)S(1)} %bitcast.8), channel_id=1, source_target_pairs={{0,1},{1,0},{2,3},{3,2},{4,5},{5,4},{6,7},{7,6},{8,9},{9,8},{10,11... | collective-permute-start | bytes 344072 | tf_op jit(solution)/shard_map/ppermute | solution.py:173
  16.3 0.9 %copy-start.3 = (s32[128,8]{0,1:T(8,128)S(1)}, s32[128,8]{0,1:T(8,128)}, u32[]{:S(2)}) copy-start(s32[128,8]{0,1:T(8,128)} %param.7) | copy-start | bytes 12292
  16.3 0.9 %copy-start.4 = (f32[128,8]{0,1:T(8,128)S(1)}, f32[128,8]{0,1:T(8,128)}, u32[]{:S(2)}) copy-start(f32[128,8]{0,1:T(8,128)} %param.8) | copy-start | bytes 12292
  16.8 1.4 %collective-permute-start.1 = (bf16[64,896]{1,0:T(8,128)(2,1)S(1)}, bf16[64,896]{1,0:T(8,128)(2,1)S(1)}, u32[]{:S(2)}, u32[]{:S(2)}) collective-permute-start(bf16[64,896]{1,0:T(8,128)(2,1)S(1)} %get-tuple-element.13.refs_2_), channel_id=1, source_target_pairs={{0,1},{1,0},{2,3},{3,2},{4,5},{5,4},{6,7},{7,6},{8,9},{9,8},{10,11... | collective-permute-start | bytes 344072 | tf_op jit(solution)/shard_map/ppermute | solution.py:180

commit v9 on v8

--- a/solution.py
+++ b/solution.py
@@ -79,53 +79,45 @@
     ]
 
 
-def columns_of(chip, own, features):
-    core = lax.rem(lax.axis_index("core") + lax.axis_index("chip") + chip + (0 if own else 1), 2)
+def columns_of(chip, features):
+    core = lax.rem(lax.axis_index("core") + lax.axis_index("chip") + chip, 2)
     return pl.ds(pl.multiple_of((2 * chip + core) * features, features), features)
 
 
-def lift(chips, own, rows_ref, gate_ref, up_ref):
+def lift(chips, rows_ref, *refs):
+    weights, acts_ref = refs[:4], refs[4]
     part_rows, features = rows_ref.shape[0] // chips, rows_ref.shape[1]
-    gate_act = jnp.zeros((part_rows, gate_ref.shape[2]), jnp.float32)
-    up_act = jnp.zeros((part_rows, up_ref.shape[2]), jnp.float32)
+    width = 2 * weights[0].shape[2]
+    for pair in range(2):
+        acts = jnp.zeros((part_rows, width), jnp.float32)
+        for chip in range(chips):
+            rows = rows_ref[chip * part_rows : (chip + 1) * part_rows, :]
+            columns = columns_of(chip, features)
+            both = [ref[0, columns, :] for ref in weights[2 * pair : 2 * pair + 2]]
+            acts += jnp.dot(
+                rows, jnp.concatenate(both, axis=1), preferred_element_type=jnp.float32
+            )
+        acts_ref[:, pair * width : (pair + 1) * width] = acts
+
+
+def finish(chips, acts_ref, across_ref, down_ref, across_down_ref, out_ref):
+    part_rows, features = out_ref.shape[0] // chips, out_ref.shape[1]
+    width = acts_ref.shape[1] // 4
+    hidden = []
+    for pair in range(2):
+        gate_act, up_act = (
+            acts_ref[:, (2 * pair + which) * width : (2 * pair + which + 1) * width]
+            + across_ref[:, (2 - 2 * pair + which) * width : (3 - 2 * pair + which) * width]
+            for which in range(2)
+        )
+        hidden.append((gate_act / (1.0 + jnp.exp(-gate_act)) * up_act).astype(jnp.bfloat16))
     for chip in range(chips):
-        rows = rows_ref[chip * part_rows : (chip + 1) * part_rows, :]
-        columns = columns_of(chip, own, features)
-        gate_act += jnp.dot(rows, gate_ref[0, columns, :], preferred_element_type=jnp.float32)
-        up_act += jnp.dot(rows, up_ref[0, columns, :], preferred_element_type=jnp.float32)
-    return gate_act, up_act
-
-
-def lower(chips, own, hidden, down_ref, out_ref):
-    part_rows, features = out_ref.shape[0] // chips, out_ref.shape[1]
-    for chip in range(chips):
-        columns = columns_of(chip, own, features)
-        out_ref[chip * part_rows : (chip + 1) * part_rows, :] = jnp.dot(
-            hidden, down_ref[0, :, columns], preferred_element_type=jnp.float32
-        ).astype(jnp.bfloat16)
-
-
-def begin(chips, rows_ref, gate_ref, up_ref, gate_act_ref, up_act_ref):
-    gate_act_ref[...], up_act_ref[...] = lift(chips, True, rows_ref, gate_ref, up_ref)
-
-
-def theirs(chips, *refs):
-    rows_ref, gate_act_ref, up_act_ref, gate_ref, up_ref, down_ref, hidden_ref, other_ref = refs
-    gate_act, up_act = lift(chips, False, rows_ref, gate_ref, up_ref)
-    gate_act += gate_act_ref[...]
-    up_act += up_act_ref[...]
-    hidden = (gate_act / (1.0 + jnp.exp(-gate_act)) * up_act).astype(jnp.bfloat16)
-    hidden_ref[...] = hidden
-    lower(chips, False, hidden, down_ref, other_ref)
-
-
-def ours(chips, hidden_ref, down_ref, mine_ref):
-    lower(chips, True, hidden_ref[...], down_ref, mine_ref)
-
-
-def add(mine_ref, other_ref, _, out_ref):
-    total = mine_ref[...].astype(jnp.float32) + other_ref[...].astype(jnp.float32)
-    out_ref[...] = total.astype(jnp.bfloat16)
+        columns = columns_of(chip, features)
+        summed = jnp.dot(hidden[0], down_ref[0, :, columns], preferred_element_type=jnp.float32)
+        summed += jnp.dot(
+            hidden[1], across_down_ref[0, :, columns], preferred_element_type=jnp.float32
+        )
+        out_ref[chip * part_rows : (chip + 1) * part_rows, :] = summed.astype(jnp.bfloat16)
 
 
 def combine(match_ref, weight_ref, returned_ref, out_hbm, out_ref, sems):
@@ -157,6 +149,7 @@
     def call(kernel, name, out_shape, **rest):
         return pl.pallas_call(kernel, out_shape=out_shape, name=name, compiler_params=LIMIT, **rest)
 
+    across = [lax.ppermute(value, "core", SWAP) for value in (w_gate, w_up, w_down)]
     outgoing = call(
         lambda *refs: route(ep_count, *refs),
         "route",
@@ -170,15 +163,12 @@
         cost_estimate=pl.CostEstimate(flops=2 * 10**9, bytes_accessed=0, transcendentals=0),
     )(*(pltpu.with_memory_space_constraint(value, pltpu.HBM) for value in (ids, tokens)))
     incoming = exchange(outgoing)
-    across = lax.ppermute(incoming, "core", SWAP)
-    acts = (jax.ShapeDtypeStruct((slot_count, hidden_count), jnp.float32),) * 2
-    begun = call(lambda *refs: begin(chips, *refs), "begin", acts)(incoming, w_gate, w_up)
-    hidden_shape = jax.ShapeDtypeStruct((slot_count, hidden_count), jnp.bfloat16)
-    hidden, other = call(lambda *refs: theirs(chips, *refs), "theirs", (hidden_shape, half))(
-        across, *begun, w_gate, w_up, w_down
-    )
-    crossed = lax.ppermute(other, "core", SWAP)
-    mine = call(lambda *refs: ours(chips, *refs), "ours", half)(hidden, w_down)
+    acts = call(
+        lambda *refs: lift(chips, *refs),
+        "lift",
+        jax.ShapeDtypeStruct((slot_count, 4 * hidden_count), jnp.float32),
+    )(incoming, w_gate, w_up, across[0], across[1])
+    crossed = lax.ppermute(acts, "core", SWAP)
     match, weight = call(
         lambda *refs: score(ep_count, *refs),
         "score",
@@ -187,9 +177,11 @@
             jax.ShapeDtypeStruct((row_count, 1), jnp.float32),
         ),
         in_specs=[vmem] * 2 + [anywhere],
-    )(ids, scores, other)
-    summed = call(add, "add", half, in_specs=[vmem] * 2 + [anywhere])(mine, crossed, weight)
-    returned = exchange(summed)
+    )(ids, scores, acts)
+    partial_value = call(
+        lambda _, *refs: finish(chips, *refs), "finish", half, in_specs=[anywhere] + [vmem] * 4
+    )(weight, acts, crossed, w_down, across[2])
+    returned = exchange(partial_value)
     return call(
         combine,
         "combine",

time: 28.9 us -> 29.4 us (1.017)
  blocking collectives: 23.1 us -> 24 us
  waiting for transfers between devices: 1.2 us -> 0.79 us
    all_to_all x2, blocking collectives: 23.1 us -> 24 us  [exchange(): return lax.all_to_all(rows, FAR, 0, 0, axis_index_groups=groups, tiled=True)]
    ppermute x2 -> x4, waiting for transfers between devices: 1.2 us -> 0.79 us  [the longest x1 0.78 us: shards(): crossed = lax.ppermute(acts, 'core', SWAP)]
    pallas_call x4 -> x2, Pallas kernels: 0.95 us -> 0.7 us  [the longest x1 0.43 us: shards(): call(lambda *refs: lift(chips, *refs), 'lift', jax.ShapeDtypeStruct((slot...]
    ppermute x2 -> x4, starting transfers between devices: 1.02 us -> 1.1 us  [the longest x3 0.96 us: shards(): lax.ppermute(value, 'core', SWAP)]
  transfers between devices with their start and end apart: 2 -> 4, of which waited for: 2 -> 1; matrix products, arithmetic and copies ran while one was open for 0% -> 0% of each run, Pallas kernels for 2% -> 7%
where the time goes in v9:
time: 29.4 us; the launch traced here: 29.2 us
  blocking collectives  24 us (82%)
  Pallas kernels  3.07 us (10%)
  starting transfers between devices  1.1 us (4%)
  waiting for transfers between devices  0.79 us (3%)
    all_to_all x2, blocking collectives, exchange(): return lax.all_to_all(rows, FAR, 0, 0, axis_index_groups=groups, tiled=True)  24 us
    pallas_call x1, Pallas kernels, shards(): call(lambda *refs: route(ep_count, *refs), 'route', half, in_specs=[hbm]...  1.27 us
    ppermute x3, starting transfers between devices, shards(): lax.ppermute(value, 'core', SWAP)  0.96 us
    pallas_call x1, Pallas kernels, shards(): call(combine, 'combine', jax.ShapeDtypeStruct((row_count, features), jnp....  0.87 us
    ppermute x1, waiting for transfers between devices, shards(): crossed = lax.ppermute(acts, 'core', SWAP)  0.78 us
  transfers between devices with their start and end apart: 4, of which 1 were waited for; matrix products, arithmetic and copies ran while one was open for 0% of the time, Pallas kernels for 7%

profile of v9, /device:TPU:0, one launch (start us, length us, event | category | flops | bytes accessed | tf_op | source)
XLA Modules:
  0.0 29.2 jit_solution(14440349410191580163)
XLA Ops:
  0.0 0.5 %collective-permute-start = (bf16[1,3584,128]{2,1,0:T(8,128)(2,1)}, bf16[1,3584,128]{2,1,0:T(8,128)(2,1)S(1)}, u32[]{:S(2)}, u32[]{:S(2)}) collective-permute-start(bf16[1,3584,128]{2,1,0:T(8,128)(2,1)} %refs_1_.3), channel_id=1, source_target_pairs={{0,1},{1,0},{2,3},{3,2},{4,5},{5,4},{6,7},{7,6},{8,9},{9,8},{10,11... | collective-permute-start | bytes 2752520 | tf_op jit(solution)/shard_map/ppermute | solution.py:152
  0.5 0.1 collective-permute-start.1
  0.5 0.5 %collective-permute-start.3 = (bf16[1,128,3584]{2,1,0:T(8,128)(2,1)}, bf16[1,128,3584]{2,1,0:T(8,128)(2,1)S(1)}, u32[]{:S(2)}, u32[]{:S(2)}) collective-permute-start(bf16[1,128,3584]{2,1,0:T(8,128)(2,1)} %refs_2_.3), channel_id=1, source_target_pairs={{0,1},{1,0},{2,3},{3,2},{4,5},{5,4},{6,7},{7,6},{8,9},{9,8},{10,11... | collective-permute-start | bytes 2752520 | tf_op jit(solution)/shard_map/ppermute | solution.py:152
  1.0 0.0 copy-start.1
  1.0 0.0 copy-start.2
  1.0 1.3 %route.1 = bf16[64,896]{1,0:T(8,128)(2,1)S(1)} custom-call(s32[8,128]{1,0:T(8,128)} %bitcast.10, bf16[128,896]{1,0:T(8,128)(2,1)} %refs_1_.2), custom_call_target="tpu_custom_call" | custom-call | flops 2000000000 | tf_op jit(solution)/shard_map/route/pallas_call | solution.py:153
  2.3 14.3 %all_to_all.22 = bf16[8,8,896]{2,1,0:T(8,128)(2,1)S(1)} all-to-all(bf16[8,8,896]{2,1,0:T(8,128)(2,1)S(1)} %bitcast.9), channel_id=1, replica_groups={{0,4,8,12,3,7,11,15},{1,5,9,13,2,6,10,14},{16,20,24,28,19,23,27,31},{17..., dimensions={0} | all-to-all | bytes 229376 | tf_op jit(solution)/shard_map/all_to_all | solution.py:147
  16.5 0.0 collective-permute-done.refs_3_
  16.5 0.0 collective-permute-done.1.refs_4_
  16.5 0.0 copy-done.1
  16.5 0.0 copy-done.2
  16.5 0.0 copy-start.3
  16.5 0.0 copy-start.4
  16.6 0.0 copy-start
  16.6 0.4 %lift.1.refs_2_.refs_0_ = f32[32,512]{1,0:T(8,128)S(1)} custom-call(bf16[64,896]{1,0:T(8,128)(2,1)S(1)} %bitcast.8, bf16[1,3584,128]{2,1,0:T(8,128)(2,1)S(1)} %copy-done.1, bf16[1,3584,128]{2,1,0:T(8,128)(2,1)S(1)} %copy-done.2, bf16[1,3584,128]{2,1,0:T(8,128)(2,1)S(1)} %collective-permute-done.refs_3_, bf16[1,3584,128]{2,1,0:T(8,128)(2,1)S(1)} %collective-permute-done.1.refs_4_), custom_call_target="tpu_custom_call" | custom-call | tf_op jit(solution)/shard_map/lift/pallas_call | solution.py:166
  17.0 0.1 collective-permute-start.2
  17.1 0.1 copy-done.3
  17.2 0.0 copy-done.4
  17.2 0.2 score.1
  17.5 0.0 collective-permute-done.3.refs_3_
  17.5 0.8 %collective-permute-done.2.refs_1_ = f32[32,512]{1,0:T(8,128)S(1)} collective-permute-done((f32[32,512]{1,0:T(8,128)S(1)}, f32[32,512]{1,0:T(8,128)S(1)}, u32[]{:S(2)}, u32[]{:S(2)}) %collective-permute-start.2) | collective-permute-done | bytes 65568 | tf_op jit(solution)/shard_map/ppermute | solution.py:171
  18.3 0.0 copy-done
  18.3 0.3 finish.1
  18.6 9.8 %all_to_all.23 = bf16[8,8,896]{2,1,0:T(8,128)(2,1)S(1)} all-to-all(bf16[8,8,896]{2,1,0:T(8,128)(2,1)S(1)} %bitcast.7), channel_id=1, replica_groups={{0,4,8,12,3,7,11,15},{1,5,9,13,2,6,10,14},{16,20,24,28,19,23,27,31},{17..., dimensions={0} | all-to-all | bytes 229376 | tf_op jit(solution)/shard_map/all_to_all | solution.py:147
  28.3 0.9 %combine.1 = bf16[128,896]{1,0:T(8,128)(2,1)} custom-call(bf16[128,64]{1,0:T(8,128)(2,1)S(1)} %get-tuple-element.7.match_ref, f32[128,1]{1,0:T(8,128)S(1)} %get-tuple-element.8._.weight_ref, bf16[64,896]{1,0:T(8,128)(2,1)S(1)} %bitcast.6), custom_call_target="tpu_custom_call" | custom-call | tf_op jit(solution)/shard_map/combine/pallas_call | solution.py:185
Async XLA Ops:
  0.0 16.5 %collective-permute-start = (bf16[1,3584,128]{2,1,0:T(8,128)(2,1)}, bf16[1,3584,128]{2,1,0:T(8,128)(2,1)S(1)}, u32[]{:S(2)}, u32[]{:S(2)}) collective-permute-start(bf16[1,3584,128]{2,1,0:T(8,128)(2,1)} %refs_1_.3), channel_id=1, source_target_pairs={{0,1},{1,0},{2,3},{3,2},{4,5},{5,4},{6,7},{7,6},{8,9},{9,8},{10,11... | collective-permute-start | bytes 2752520 | tf_op jit(solution)/shard_map/ppermute | solution.py:152
  0.5 16.1 %collective-permute-start.1 = (bf16[1,3584,128]{2,1,0:T(8,128)(2,1)}, bf16[1,3584,128]{2,1,0:T(8,128)(2,1)S(1)}, u32[]{:S(2)}, u32[]{:S(2)}) collective-permute-start(bf16[1,3584,128]{2,1,0:T(8,128)(2,1)} %refs_2_.2), channel_id=1, source_target_pairs={{0,1},{1,0},{2,3},{3,2},{4,5},{5,4},{6,7},{7,6},{8,9},{9,8},{10,11... | collective-permute-start | bytes 2752520 | tf_op jit(solution)/shard_map/ppermute | solution.py:152
  0.5 17.0 %collective-permute-start.3 = (bf16[1,128,3584]{2,1,0:T(8,128)(2,1)}, bf16[1,128,3584]{2,1,0:T(8,128)(2,1)S(1)}, u32[]{:S(2)}, u32[]{:S(2)}) collective-permute-start(bf16[1,128,3584]{2,1,0:T(8,128)(2,1)} %refs_2_.3), channel_id=1, source_target_pairs={{0,1},{1,0},{2,3},{3,2},{4,5},{5,4},{6,7},{7,6},{8,9},{9,8},{10,11... | collective-permute-start | bytes 2752520 | tf_op jit(solution)/shard_map/ppermute | solution.py:152
  1.0 15.6 %copy-start.1 = (bf16[1,3584,128]{2,1,0:T(8,128)(2,1)S(1)}, bf16[1,3584,128]{2,1,0:T(8,128)(2,1)}, u32[]{:S(2)}) copy-start(bf16[1,3584,128]{2,1,0:T(8,128)(2,1)} %refs_1_.3) | copy-start | bytes 2752516
  1.0 15.6 %copy-start.2 = (bf16[1,3584,128]{2,1,0:T(8,128)(2,1)S(1)}, bf16[1,3584,128]{2,1,0:T(8,128)(2,1)}, u32[]{:S(2)}) copy-start(bf16[1,3584,128]{2,1,0:T(8,128)(2,1)} %refs_2_.2) | copy-start | bytes 2752516
  16.5 0.7 %copy-start.3 = (s32[128,8]{0,1:T(8,128)S(1)}, s32[128,8]{0,1:T(8,128)}, u32[]{:S(2)}) copy-start(s32[128,8]{0,1:T(8,128)} %param.7) | copy-start | bytes 12292
  16.5 0.7 %copy-start.4 = (f32[128,8]{0,1:T(8,128)S(1)}, f32[128,8]{0,1:T(8,128)}, u32[]{:S(2)}) copy-start(f32[128,8]{0,1:T(8,128)} %param.8) | copy-start | bytes 12292
  16.6 1.7 %copy-start = (bf16[1,128,3584]{2,1,0:T(8,128)(2,1)S(1)}, bf16[1,128,3584]{2,1,0:T(8,128)(2,1)}, u32[]{:S(2)}) copy-start(bf16[1,128,3584]{2,1,0:T(8,128)(2,1)} %refs_2_.3) | copy-start | bytes 2752516
  17.0 1.3 %collective-permute-start.2 = (f32[32,512]{1,0:T(8,128)S(1)}, f32[32,512]{1,0:T(8,128)S(1)}, u32[]{:S(2)}, u32[]{:S(2)}) collective-permute-start(f32[32,512]{1,0:T(8,128)S(1)} %lift.1.refs_2_.refs_0_), channel_id=1, source_target_pairs={{0,1},{1,0},{2,3},{3,2},{4,5},{5,4},{6,7},{7,6},{8,9},{9,8},{10,11... | collective-permute-start | bytes 196616 | tf_op jit(solution)/shard_map/ppermute | solution.py:171

commit v10 on v9

--- a/solution.py
+++ b/solution.py
@@ -38,7 +38,29 @@
     return ((index // (2 * CAP)) * CAP + lax.rem(index, CAP)).astype(jnp.float32)
 
 
-def route(ep_count, ids_hbm, tokens_hbm, outgoing_ref, ids_ref, tokens_ref, sems):
+def pack_pieces(chips, gate_hbm, up_hbm, down_hbm, pack_ref):
+    features, width = down_hbm.shape[2] // (2 * chips), gate_hbm.shape[2]
+    half = features // 2
+    pieces = []
+    for which, source in enumerate((gate_hbm, up_hbm)):
+        for chip in range(chips):
+            start = columns_of(chip, features, True)
+            for at in (0, half):
+                row = (which * chips + chip) * features + at
+                rows = pl.ds(pl.multiple_of(start + at, half), half)
+                pieces.append((source.at[0, rows, :], pack_ref.at[pl.ds(row, half), :]))
+    for chip in range(chips):
+        start = columns_of(chip, features, True)
+        for at in range(0, features, width):
+            row = (2 * chips + chip) * features + at
+            columns = pl.ds(pl.multiple_of(start + at, width), width)
+            pieces.append((down_hbm.at[0, :, columns], pack_ref.at[pl.ds(row, width), :]))
+    return pieces
+
+
+def route(ep_count, chips, ids_hbm, tokens_hbm, *refs):
+    weights, (outgoing_ref, pack_ref) = refs[:3], refs[3:5]
+    ids_ref, tokens_ref, sems, pack_sems = refs[5:]
     row_count = ids_ref.shape[1]
     parts = row_count // PIECE
     copies = [pltpu.make_async_copy(ids_hbm, ids_ref, sems.at[parts])] + [
@@ -49,7 +71,11 @@
         )
         for part in range(parts)
     ]
-    for copy in copies:
+    pieces = [
+        pltpu.make_async_copy(source, target, pack_sems.at[at])
+        for at, (source, target) in enumerate(pack_pieces(chips, *weights, pack_ref))
+    ]
+    for copy in copies + pieces:
         copy.start()
     copies[0].wait()
     code, _ = slot_codes(ids_ref[...].astype(jnp.float32), ep_count // 2)
@@ -60,6 +86,8 @@
     outgoing_ref[...] = jnp.dot(
         dispatch, tokens_ref[...], preferred_element_type=jnp.float32
     ).astype(jnp.bfloat16)
+    for piece in pieces:
+        piece.wait()
 
 
 def score(ep_count, ids_ref, scores_ref, _, match_ref, weight_ref):
@@ -79,28 +107,31 @@
     ]
 
 
-def columns_of(chip, features):
-    core = lax.rem(lax.axis_index("core") + lax.axis_index("chip") + chip, 2)
-    return pl.ds(pl.multiple_of((2 * chip + core) * features, features), features)
-
-
-def lift(chips, rows_ref, *refs):
-    weights, acts_ref = refs[:4], refs[4]
+def columns_of(chip, features, other=False):
+    core = lax.rem(lax.axis_index("core") + lax.axis_index("chip") + chip + (1 if other else 0), 2)
+    return pl.multiple_of((2 * chip + core) * features, features)
+
+
+def lift(chips, rows_ref, gate_ref, up_ref, pack_ref, acts_ref):
     part_rows, features = rows_ref.shape[0] // chips, rows_ref.shape[1]
-    width = 2 * weights[0].shape[2]
-    for pair in range(2):
+    width = 2 * gate_ref.shape[2]
+    for across in range(2):
         acts = jnp.zeros((part_rows, width), jnp.float32)
         for chip in range(chips):
             rows = rows_ref[chip * part_rows : (chip + 1) * part_rows, :]
-            columns = columns_of(chip, features)
-            both = [ref[0, columns, :] for ref in weights[2 * pair : 2 * pair + 2]]
+            if across:
+                at = [(which * chips + chip) * features for which in range(2)]
+                both = [pack_ref[start : start + features, :] for start in at]
+            else:
+                columns = pl.ds(columns_of(chip, features), features)
+                both = [gate_ref[0, columns, :], up_ref[0, columns, :]]
             acts += jnp.dot(
                 rows, jnp.concatenate(both, axis=1), preferred_element_type=jnp.float32
             )
-        acts_ref[:, pair * width : (pair + 1) * width] = acts
-
-
-def finish(chips, acts_ref, across_ref, down_ref, across_down_ref, out_ref):
+        acts_ref[:, across * width : (across + 1) * width] = acts
+
+
+def finish(chips, acts_ref, across_ref, down_ref, pack_ref, out_ref):
     part_rows, features = out_ref.shape[0] // chips, out_ref.shape[1]
     width = acts_ref.shape[1] // 4
     hidden = []
@@ -112,10 +143,12 @@
         )
         hidden.append((gate_act / (1.0 + jnp.exp(-gate_act)) * up_act).astype(jnp.bfloat16))
     for chip in range(chips):
-        columns = columns_of(chip, features)
+        columns = pl.ds(columns_of(chip, features), features)
         summed = jnp.dot(hidden[0], down_ref[0, :, columns], preferred_element_type=jnp.float32)
+        first = (2 * chips + chip) * features
+        tiles = [pack_ref[first + at : first + at + width, :] for at in range(0, features, width)]
         summed += jnp.dot(
-            hidden[1], across_down_ref[0, :, columns], preferred_element_type=jnp.float32
+            hidden[1], jnp.concatenate(tiles, axis=1), preferred_element_type=jnp.float32
         )
         out_ref[chip * part_rows : (chip + 1) * part_rows, :] = summed.astype(jnp.bfloat16)
 
@@ -149,25 +182,28 @@
     def call(kernel, name, out_shape, **rest):
         return pl.pallas_call(kernel, out_shape=out_shape, name=name, compiler_params=LIMIT, **rest)
 
-    across = [lax.ppermute(value, "core", SWAP) for value in (w_gate, w_up, w_down)]
-    outgoing = call(
-        lambda *refs: route(ep_count, *refs),
+    pack_shape = jax.ShapeDtypeStruct((3 * chips * features, hidden_count), jnp.bfloat16)
+    inputs = (ids, tokens, w_gate, w_up, w_down)
+    outgoing, pack = call(
+        lambda *refs: route(ep_count, chips, *refs),
         "route",
-        half,
-        in_specs=[hbm] * 2,
+        (half, pack_shape),
+        in_specs=[hbm] * 5,
         scratch_shapes=[
             pltpu.VMEM((top_count, row_count), jnp.int32),
             pltpu.VMEM((row_count, features), jnp.bfloat16),
             pltpu.SemaphoreType.DMA((row_count // PIECE + 1,)),
+            pltpu.SemaphoreType.DMA((chips * (4 + features // hidden_count),)),
         ],
         cost_estimate=pl.CostEstimate(flops=2 * 10**9, bytes_accessed=0, transcendentals=0),
-    )(*(pltpu.with_memory_space_constraint(value, pltpu.HBM) for value in (ids, tokens)))
+    )(*(pltpu.with_memory_space_constraint(value, pltpu.HBM) for value in inputs))
+    across = lax.ppermute(pack, "core", SWAP)
     incoming = exchange(outgoing)
     acts = call(
         lambda *refs: lift(chips, *refs),
         "lift",
         jax.ShapeDtypeStruct((slot_count, 4 * hidden_count), jnp.float32),
-    )(incoming, w_gate, w_up, across[0], across[1])
+    )(incoming, w_gate, w_up, across)
     crossed = lax.ppermute(acts, "core", SWAP)
     match, weight = call(
         lambda *refs: score(ep_count, *refs),
@@ -180,7 +216,7 @@
     )(ids, scores, acts)
     partial_value = call(
         lambda _, *refs: finish(chips, *refs), "finish", half, in_specs=[anywhere] + [vmem] * 4
-    )(weight, acts, crossed, w_down, across[2])
+    )(weight, acts, crossed, w_down, across)
     returned = exchange(partial_value)
     return call(
         combine,

time: 29.4 us -> 29.6 us (level)
  Pallas kernels: 3.07 us -> 3.7 us
  starting transfers between devices: 1.1 us -> 0.7 us
    pallas_call x1, Pallas kernels: 1.27 us -> 1.98 us  [shards(): call(lambda *refs: route(ep_count, chips, *refs), 'route', (half, pack_sh...]
    ppermute x3 -> x1, starting transfers between devices: 0.96 us -> 0.52 us  [shards(): across = lax.ppermute(pack, 'core', SWAP)]
  transfers between devices with their start and end apart: 4 -> 2, of which waited for: 1 -> 1; matrix products, arithmetic and copies ran while one was open for 0% -> 0% of each run, Pallas kernels for 7% -> 1%
where the time goes in v10:
time: 29.6 us; the launch traced here: 29.4 us
  blocking collectives  24 us (81%)
  Pallas kernels  3.7 us (12%)
  waiting for transfers between devices  0.78 us (3%)
  starting transfers between devices  0.7 us (2%)
    all_to_all x2, blocking collectives, exchange(): return lax.all_to_all(rows, FAR, 0, 0, axis_index_groups=groups, tiled=True)  24 us
    pallas_call x1, Pallas kernels, shards(): call(lambda *refs: route(ep_count, chips, *refs), 'route', (half, pack_sh...  1.98 us
    pallas_call x1, Pallas kernels, shards(): call(combine, 'combine', jax.ShapeDtypeStruct((row_count, features), jnp....  0.87 us
    ppermute x1, waiting for transfers between devices, shards(): crossed = lax.ppermute(acts, 'core', SWAP)  0.77 us
  transfers between devices with their start and end apart: 2, of which 1 were waited for; matrix products, arithmetic and copies ran while one was open for 0% of the time, Pallas kernels for 1%

profile of v10, /device:TPU:0, one launch (start us, length us, event | category | flops | bytes accessed | tf_op | source)
XLA Modules:
  0.0 29.4 jit_solution(15762169807520774756)
XLA Ops:
  0.0 0.0 copy-start
  0.0 0.0 copy-start.1
  0.0 2.0 %route.1 = (bf16[64,896]{1,0:T(8,128)(2,1)S(1)}, bf16[5376,128]{1,0:T(8,128)(2,1)S(1)}) custom-call(s32[8,128]{1,0:T(8,128)} %bitcast.10, bf16[128,896]{1,0:T(8,128)(2,1)} %refs_1_.2, bf16[1,3584,128]{2,1,0:T(8,128)(2,1)} %refs_1_.3, bf16[1,3584,128]{2,1,0:T(8,128)(2,1)} %refs_2_.4, bf16[1,128,3584]{2,1,0:T(8,128)(2,1)} %refs_2_.5), custom_call_target="tpu_custom_call" | custom-call | flops 2000000000 | tf_op jit(solution)/shard_map/route/pallas_call | solution.py:187
  2.0 0.5 %collective-permute-start = (bf16[5376,128]{1,0:T(8,128)(2,1)S(1)}, bf16[5376,128]{1,0:T(8,128)(2,1)S(1)}, u32[]{:S(2)}, u32[]{:S(2)}) collective-permute-start(bf16[5376,128]{1,0:T(8,128)(2,1)S(1)} %get-tuple-element.10), channel_id=1, source_target_pairs={{0,1},{1,0},{2,3},{3,2},{4,5},{5,4},{6,7},{7,6},{8,9},{9,8},{10,11... | collective-permute-start | bytes 4128776 | tf_op jit(solution)/shard_map/ppermute | solution.py:200
  2.5 14.2 %all_to_all.22 = bf16[8,8,896]{2,1,0:T(8,128)(2,1)S(1)} all-to-all(bf16[8,8,896]{2,1,0:T(8,128)(2,1)S(1)} %bitcast.9), channel_id=1, replica_groups={{0,4,8,12,3,7,11,15},{1,5,9,13,2,6,10,14},{16,20,24,28,19,23,27,31},{17..., dimensions={0} | all-to-all | bytes 229376 | tf_op jit(solution)/shard_map/all_to_all | solution.py:180
  16.7 0.0 collective-permute-done.refs_3_
  16.7 0.0 copy-done
  16.7 0.0 copy-done.1
  16.7 0.0 copy-start.3
  16.8 0.0 copy-start.4
  16.8 0.0 copy-start.2
  16.8 0.4 %lift.1.refs_2_.refs_0_ = f32[32,512]{1,0:T(8,128)S(1)} custom-call(bf16[64,896]{1,0:T(8,128)(2,1)S(1)} %bitcast.7, bf16[1,3584,128]{2,1,0:T(8,128)(2,1)S(1)} %copy-done, bf16[1,3584,128]{2,1,0:T(8,128)(2,1)S(1)} %copy-done.1, bf16[5376,128]{1,0:T(8,128)(2,1)S(1)} %collective-permute-done.refs_3_), custom_call_target="tpu_custom_call" | custom-call | tf_op jit(solution)/shard_map/lift/pallas_call | solution.py:202
  17.1 0.2 collective-permute-start.1
  17.3 0.1 copy-done.3
  17.4 0.0 copy-done.4
  17.4 0.2 score.1
  17.7 0.8 %collective-permute-done.1.refs_1_ = f32[32,512]{1,0:T(8,128)S(1)} collective-permute-done((f32[32,512]{1,0:T(8,128)S(1)}, f32[32,512]{1,0:T(8,128)S(1)}, u32[]{:S(2)}, u32[]{:S(2)}) %collective-permute-start.1) | collective-permute-done | bytes 65568 | tf_op jit(solution)/shard_map/ppermute | solution.py:207
  18.5 0.0 copy-done.2
  18.5 0.3 finish.1
  18.7 9.8 %all_to_all.23 = bf16[8,8,896]{2,1,0:T(8,128)(2,1)S(1)} all-to-all(bf16[8,8,896]{2,1,0:T(8,128)(2,1)S(1)} %bitcast.8), channel_id=1, replica_groups={{0,4,8,12,3,7,11,15},{1,5,9,13,2,6,10,14},{16,20,24,28,19,23,27,31},{17..., dimensions={0} | all-to-all | bytes 229376 | tf_op jit(solution)/shard_map/all_to_all | solution.py:180
  28.5 0.9 %combine.1 = bf16[128,896]{1,0:T(8,128)(2,1)} custom-call(bf16[128,64]{1,0:T(8,128)(2,1)S(1)} %get-tuple-element.11.match_ref, f32[128,1]{1,0:T(8,128)S(1)} %get-tuple-element.12._.weight_ref, bf16[64,896]{1,0:T(8,128)(2,1)S(1)} %bitcast.6), custom_call_target="tpu_custom_call" | custom-call | tf_op jit(solution)/shard_map/combine/pallas_call | solution.py:221
Async XLA Ops:
  0.0 16.7 %copy-start = (bf16[1,3584,128]{2,1,0:T(8,128)(2,1)S(1)}, bf16[1,3584,128]{2,1,0:T(8,128)(2,1)}, u32[]{:S(2)}) copy-start(bf16[1,3584,128]{2,1,0:T(8,128)(2,1)} %refs_1_.3) | copy-start | bytes 2752516
  0.0 16.7 %copy-start.1 = (bf16[1,3584,128]{2,1,0:T(8,128)(2,1)S(1)}, bf16[1,3584,128]{2,1,0:T(8,128)(2,1)}, u32[]{:S(2)}) copy-start(bf16[1,3584,128]{2,1,0:T(8,128)(2,1)} %refs_2_.4) | copy-start | bytes 2752516
  2.0 14.7 %collective-permute-start = (bf16[5376,128]{1,0:T(8,128)(2,1)S(1)}, bf16[5376,128]{1,0:T(8,128)(2,1)S(1)}, u32[]{:S(2)}, u32[]{:S(2)}) collective-permute-start(bf16[5376,128]{1,0:T(8,128)(2,1)S(1)} %get-tuple-element.10), channel_id=1, source_target_pairs={{0,1},{1,0},{2,3},{3,2},{4,5},{5,4},{6,7},{7,6},{8,9},{9,8},{10,11... | collective-permute-start | bytes 4128776 | tf_op jit(solution)/shard_map/ppermute | solution.py:200
  16.7 0.7 %copy-start.3 = (s32[128,8]{0,1:T(8,128)S(1)}, s32[128,8]{0,1:T(8,128)}, u32[]{:S(2)}) copy-start(s32[128,8]{0,1:T(8,128)} %param.7) | copy-start | bytes 12292
  16.8 0.7 %copy-start.4 = (f32[128,8]{0,1:T(8,128)S(1)}, f32[128,8]{0,1:T(8,128)}, u32[]{:S(2)}) copy-start(f32[128,8]{0,1:T(8,128)} %param.8) | copy-start | bytes 12292
  16.8 1.7 %copy-start.2 = (bf16[1,128,3584]{2,1,0:T(8,128)(2,1)S(1)}, bf16[1,128,3584]{2,1,0:T(8,128)(2,1)}, u32[]{:S(2)}) copy-start(bf16[1,128,3584]{2,1,0:T(8,128)(2,1)} %refs_2_.5) | copy-start | bytes 2752516
  17.1 1.3 %collective-permute-start.1 = (f32[32,512]{1,0:T(8,128)S(1)}, f32[32,512]{1,0:T(8,128)S(1)}, u32[]{:S(2)}, u32[]{:S(2)}) collective-permute-start(f32[32,512]{1,0:T(8,128)S(1)} %lift.1.refs_2_.refs_0_), channel_id=1, source_target_pairs={{0,1},{1,0},{2,3},{3,2},{4,5},{5,4},{6,7},{7,6},{8,9},{9,8},{10,11... | collective-permute-start | bytes 196616 | tf_op jit(solution)/shard_map/ppermute | solution.py:207

commit v11 on v8

--- a/solution.py
+++ b/solution.py
@@ -34,8 +34,8 @@
 
 
 def row_codes(index, ep_count):
-    index = lax.rem(index, ep_count * CAP)
-    return ((index // (2 * CAP)) * CAP + lax.rem(index, CAP)).astype(jnp.float32)
+    expert = (ep_count - 1 - lax.rem(index // CAP, ep_count)) // 2
+    return (expert * CAP + lax.rem(index, CAP)).astype(jnp.float32)
 
 
 def route(ep_count, ids_hbm, tokens_hbm, outgoing_ref, ids_ref, tokens_ref, sems):
@@ -74,7 +74,7 @@
 
 def far_groups(ep_count, chips):
     return [
-        [(z * chips + x) * 2 + (side + x) % 2 for x in range(chips) for z in range(ep_count)]
+        [(z * chips + x) * 2 + (side + x) % 2 for x in range(chips) for z in reversed(range(ep_count))]
         for side in range(2)
     ]
 

time: 28.9 us -> 26.9 us (0.931)
  blocking collectives: 23.1 us -> 21.2 us
  starting transfers between devices: 1.02 us -> 0.33 us
  waiting for transfers between devices: 1.2 us -> 1.63 us
    all_to_all x2, blocking collectives: 23.1 us -> 21.2 us  [exchange(): return lax.all_to_all(rows, FAR, 0, 0, axis_index_groups=groups, tiled=True)]
    ppermute x1, starting transfers between devices: 0.59 us -> 0.12 us  [shards(): across = lax.ppermute(incoming, 'core', SWAP)]
  transfers between devices with their start and end apart: 2 -> 2, of which waited for: 2 -> 2; matrix products, arithmetic and copies ran while one was open for 0% -> 0% of each run, Pallas kernels for 2% -> 3%
where the time goes in v11:
time: 26.9 us; the launch traced here: 26.6 us
  blocking collectives  21.2 us (79%)
  Pallas kernels  3.32 us (12%)
  waiting for transfers between devices  1.63 us (6%)
  starting transfers between devices  0.33 us (1%)
    all_to_all x2, blocking collectives, exchange(): return lax.all_to_all(rows, FAR, 0, 0, axis_index_groups=groups, tiled=True)  21.2 us
    pallas_call x1, Pallas kernels, shards(): call(lambda *refs: route(ep_count, *refs), 'route', half, in_specs=[hbm]...  1.27 us
    ppermute x1, waiting for transfers between devices, shards(): across = lax.ppermute(incoming, 'core', SWAP)  0.93 us
    pallas_call x1, Pallas kernels, shards(): call(combine, 'combine', jax.ShapeDtypeStruct((row_count, features), jnp....  0.87 us
    ppermute x1, waiting for transfers between devices, shards(): crossed = lax.ppermute(other, 'core', SWAP)  0.7 us
  transfers between devices with their start and end apart: 2, of which 2 were waited for; matrix products, arithmetic and copies ran while one was open for 0% of the time, Pallas kernels for 3%

profile of v11, /device:TPU:0, one launch (start us, length us, event | category | flops | bytes accessed | tf_op | source)
XLA Modules:
  0.0 26.6 jit_solution(2091220435455071947)
XLA Ops:
  0.0 0.0 copy-start
  0.0 0.0 copy-start.1
  0.0 1.3 %route.1 = bf16[64,896]{1,0:T(8,128)(2,1)S(1)} custom-call(s32[8,128]{1,0:T(8,128)} %bitcast.11, bf16[128,896]{1,0:T(8,128)(2,1)} %refs_1_.3), custom_call_target="tpu_custom_call" | custom-call | flops 2000000000 | tf_op jit(solution)/shard_map/route/pallas_call | solution.py:160
  1.3 11.4 %all_to_all.22 = bf16[8,8,896]{2,1,0:T(8,128)(2,1)S(1)} all-to-all(bf16[8,8,896]{2,1,0:T(8,128)(2,1)S(1)} %bitcast.10), channel_id=1, replica_groups={{12,8,4,0,15,11,7,3},{13,9,5,1,14,10,6,2},{28,24,20,16,31,27,23,19},{29..., dimensions={0} | all-to-all | bytes 229376 | tf_op jit(solution)/shard_map/all_to_all | solution.py:155
  12.7 0.0 copy-start.2
  12.7 0.1 collective-permute-start
  12.8 0.0 copy-done
  12.8 0.0 copy-done.1
  12.8 0.3 begin.1
  13.1 0.9 %collective-permute-done.refs_0_ = bf16[64,896]{1,0:T(8,128)(2,1)S(1)} collective-permute-done((bf16[64,896]{1,0:T(8,128)(2,1)S(1)}, bf16[64,896]{1,0:T(8,128)(2,1)S(1)}, u32[]{:S(2)}, u32[]{:S(2)}) %collective-permute-start) | collective-permute-done | bytes 114720 | tf_op jit(solution)/shard_map/ppermute | solution.py:173
  14.0 0.0 copy-done.2
  14.0 0.0 copy-start.3
  14.0 0.0 copy-start.4
  14.0 0.5 %theirs.1 = (bf16[32,128]{1,0:T(8,128)(2,1)S(1)}, bf16[64,896]{1,0:T(8,128)(2,1)S(1)}) custom-call(bf16[64,896]{1,0:T(8,128)(2,1)S(1)} %collective-permute-done.refs_0_, f32[32,128]{1,0:T(8,128)S(1)} %get-tuple-element.11.refs_1_, f32[32,128]{1,0:T(8,128)S(1)} %get-tuple-element.12.refs_2_, bf16[1,3584,128]{2,1,0:T(8,128)(2,1)S(1)} %copy-done, ...), custom_call_target="tpu_custom_call" | custom-call | tf_op jit(solution)/shard_map/theirs/pallas_call | solution.py:177
  14.5 0.2 collective-permute-start.1
  14.7 0.0 copy-done.3
  14.7 0.0 copy-done.4
  14.7 0.2 score.1
  15.0 0.2 ours.1.mine_ref
  15.2 0.7 %collective-permute-done.1.other_ref = bf16[64,896]{1,0:T(8,128)(2,1)S(1)} collective-permute-done((bf16[64,896]{1,0:T(8,128)(2,1)S(1)}, bf16[64,896]{1,0:T(8,128)(2,1)S(1)}, u32[]{:S(2)}, u32[]{:S(2)}) %collective-permute-start.1) | collective-permute-done | bytes 114720 | tf_op jit(solution)/shard_map/ppermute | solution.py:180
  15.9 9.8 %all_to_all.23 = bf16[8,8,896]{2,1,0:T(8,128)(2,1)S(1)} all-to-all(bf16[8,8,896]{2,1,0:T(8,128)(2,1)S(1)} %bitcast.7), channel_id=1, replica_groups={{12,8,4,0,15,11,7,3},{13,9,5,1,14,10,6,2},{28,24,20,16,31,27,23,19},{29..., dimensions={0} | all-to-all | bytes 229376 | tf_op jit(solution)/shard_map/all_to_all | solution.py:155
  25.7 0.9 %combine.1 = bf16[128,896]{1,0:T(8,128)(2,1)} custom-call(bf16[128,64]{1,0:T(8,128)(2,1)S(1)} %get-tuple-element.14.match_ref, f32[128,1]{1,0:T(8,128)S(1)} %get-tuple-element.15._.weight_ref, bf16[64,896]{1,0:T(8,128)(2,1)S(1)} %bitcast.6), custom_call_target="tpu_custom_call" | custom-call | tf_op jit(solution)/shard_map/combine/pallas_call | solution.py:193
  (1 shorter events, 0.0 us)
Async XLA Ops:
  0.0 12.8 %copy-start = (bf16[1,3584,128]{2,1,0:T(8,128)(2,1)S(1)}, bf16[1,3584,128]{2,1,0:T(8,128)(2,1)}, u32[]{:S(2)}) copy-start(bf16[1,3584,128]{2,1,0:T(8,128)(2,1)} %refs_3_.1) | copy-start | bytes 2752516
  0.0 12.8 %copy-start.1 = (bf16[1,3584,128]{2,1,0:T(8,128)(2,1)S(1)}, bf16[1,3584,128]{2,1,0:T(8,128)(2,1)}, u32[]{:S(2)}) copy-start(bf16[1,3584,128]{2,1,0:T(8,128)(2,1)} %refs_4_.1) | copy-start | bytes 2752516
  12.7 1.3 %copy-start.2 = (bf16[1,128,3584]{2,1,0:T(8,128)(2,1)S(1)}, bf16[1,128,3584]{2,1,0:T(8,128)(2,1)}, u32[]{:S(2)}) copy-start(bf16[1,128,3584]{2,1,0:T(8,128)(2,1)} %refs_1_.5) | copy-start | bytes 2752516
  12.7 1.3 %collective-permute-start = (bf16[64,896]{1,0:T(8,128)(2,1)S(1)}, bf16[64,896]{1,0:T(8,128)(2,1)S(1)}, u32[]{:S(2)}, u32[]{:S(2)}) collective-permute-start(bf16[64,896]{1,0:T(8,128)(2,1)S(1)} %bitcast.8), channel_id=1, source_target_pairs={{0,1},{1,0},{2,3},{3,2},{4,5},{5,4},{6,7},{7,6},{8,9},{9,8},{10,11... | collective-permute-start | bytes 344072 | tf_op jit(solution)/shard_map/ppermute | solution.py:173
  14.0 0.7 %copy-start.3 = (s32[128,8]{0,1:T(8,128)S(1)}, s32[128,8]{0,1:T(8,128)}, u32[]{:S(2)}) copy-start(s32[128,8]{0,1:T(8,128)} %param.7) | copy-start | bytes 12292
  14.0 0.7 %copy-start.4 = (f32[128,8]{0,1:T(8,128)S(1)}, f32[128,8]{0,1:T(8,128)}, u32[]{:S(2)}) copy-start(f32[128,8]{0,1:T(8,128)} %param.8) | copy-start | bytes 12292
  14.5 1.4 %collective-permute-start.1 = (bf16[64,896]{1,0:T(8,128)(2,1)S(1)}, bf16[64,896]{1,0:T(8,128)(2,1)S(1)}, u32[]{:S(2)}, u32[]{:S(2)}) collective-permute-start(bf16[64,896]{1,0:T(8,128)(2,1)S(1)} %get-tuple-element.13.refs_2_), channel_id=1, source_target_pairs={{0,1},{1,0},{2,3},{3,2},{4,5},{5,4},{6,7},{7,6},{8,9},{9,8},{10,11... | collective-permute-start | bytes 344072 | tf_op jit(solution)/shard_map/ppermute | solution.py:180

commit v12 on v11

--- a/solution.py
+++ b/solution.py
@@ -33,12 +33,12 @@
     return expert * CAP + jnp.sum(counts * onehot, axis=0, keepdims=True), expert
 
 
-def row_codes(index, ep_count):
-    expert = (ep_count - 1 - lax.rem(index // CAP, ep_count)) // 2
+def row_codes(index, ep_count, chips):
+    expert = (ep_count - 1 - index // (CAP * chips)) // 2
     return (expert * CAP + lax.rem(index, CAP)).astype(jnp.float32)
 
 
-def route(ep_count, ids_hbm, tokens_hbm, outgoing_ref, ids_ref, tokens_ref, sems):
+def route(ep_count, chips, ids_hbm, tokens_hbm, outgoing_ref, ids_ref, tokens_ref, sems):
     row_count = ids_ref.shape[1]
     parts = row_count // PIECE
     copies = [pltpu.make_async_copy(ids_hbm, ids_ref, sems.at[parts])] + [
@@ -53,7 +53,7 @@
         copy.start()
     copies[0].wait()
     code, _ = slot_codes(ids_ref[...].astype(jnp.float32), ep_count // 2)
-    wanted = row_codes(iota((outgoing_ref.shape[0], row_count), 0), ep_count)
+    wanted = row_codes(iota((outgoing_ref.shape[0], row_count), 0), ep_count, chips)
     dispatch = jnp.where(code == wanted, 1.0, 0.0).astype(jnp.bfloat16)
     for copy in copies[1:]:
         copy.wait()
@@ -62,10 +62,10 @@
     ).astype(jnp.bfloat16)
 
 
-def score(ep_count, ids_ref, scores_ref, _, match_ref, weight_ref):
+def score(ep_count, chips, ids_ref, scores_ref, _, match_ref, weight_ref):
     ids = ids_ref[...].astype(jnp.float32)
     code, expert = slot_codes(ids, ep_count // 2)
-    wanted = row_codes(iota(match_ref.shape, 1), ep_count)
+    wanted = row_codes(iota(match_ref.shape, 1), ep_count, chips)
     match_ref[...] = jnp.where(to_column(code) == wanted, 1.0, 0.0).astype(jnp.bfloat16)
     squashed = jax.nn.sigmoid(scores_ref[...])
     chosen = jnp.sum(jnp.where(ids == expert, squashed, 0.0), axis=0, keepdims=True)
@@ -74,7 +74,11 @@
 
 def far_groups(ep_count, chips):
     return [
-        [(z * chips + x) * 2 + (side + x) % 2 for x in range(chips) for z in reversed(range(ep_count))]
+        [
+            (z * chips + x) * 2 + (side + x) % 2
+            for z in reversed(range(ep_count))
+            for x in reversed(range(chips))
+        ]
         for side in range(2)
     ]
 
@@ -85,24 +89,28 @@
 
 
 def lift(chips, own, rows_ref, gate_ref, up_ref):
-    part_rows, features = rows_ref.shape[0] // chips, rows_ref.shape[1]
-    gate_act = jnp.zeros((part_rows, gate_ref.shape[2]), jnp.float32)
-    up_act = jnp.zeros((part_rows, up_ref.shape[2]), jnp.float32)
+    rows, features = rows_ref[...], rows_ref.shape[1]
+    totals = []
+    for ref in (gate_ref, up_ref):
+        total = 0.0
+        for chip in range(chips):
+            weight = ref[0, columns_of(chip, own, features), :]
+            acts = jnp.dot(rows, weight, preferred_element_type=jnp.float32)
+            acts = acts.reshape(-1, chips, CAP, acts.shape[1])
+            total += acts[:, chips - 1 - chip].reshape(-1, acts.shape[3])
+        totals.append(total)
+    return totals
+
+
+def lower(chips, own, hidden, down_ref, out_ref):
+    features = out_ref.shape[3]
     for chip in range(chips):
-        rows = rows_ref[chip * part_rows : (chip + 1) * part_rows, :]
-        columns = columns_of(chip, own, features)
-        gate_act += jnp.dot(rows, gate_ref[0, columns, :], preferred_element_type=jnp.float32)
-        up_act += jnp.dot(rows, up_ref[0, columns, :], preferred_element_type=jnp.float32)
-    return gate_act, up_act
-
-
-def lower(chips, own, hidden, down_ref, out_ref):
-    part_rows, features = out_ref.shape[0] // chips, out_ref.shape[1]
-    for chip in range(chips):
-        columns = columns_of(chip, own, features)
-        out_ref[chip * part_rows : (chip + 1) * part_rows, :] = jnp.dot(
-            hidden, down_ref[0, :, columns], preferred_element_type=jnp.float32
-        ).astype(jnp.bfloat16)
+        values = jnp.dot(
+            hidden,
+            down_ref[0, :, columns_of(chip, own, features)],
+            preferred_element_type=jnp.float32,
+        )
+        out_ref[:, chips - 1 - chip] = values.reshape(-1, CAP, features).astype(jnp.bfloat16)
 
 
 def begin(chips, rows_ref, gate_ref, up_ref, gate_act_ref, up_act_ref):
@@ -146,6 +154,7 @@
     ep_count, chips = lax.axis_size("ep"), lax.axis_size("chip")
     slot_count = ep_count * CAP
     half = jax.ShapeDtypeStruct((chips * slot_count, features), jnp.bfloat16)
+    split = jax.ShapeDtypeStruct((ep_count, chips, CAP, features), jnp.bfloat16)
     ids, scores = expert_ids.T, route_scores.T
     hbm, vmem = (pl.BlockSpec(memory_space=space) for space in (pltpu.HBM, pltpu.VMEM))
     anywhere = pl.BlockSpec(memory_space=pl.ANY)
@@ -158,7 +167,7 @@
         return pl.pallas_call(kernel, out_shape=out_shape, name=name, compiler_params=LIMIT, **rest)
 
     outgoing = call(
-        lambda *refs: route(ep_count, *refs),
+        lambda *refs: route(ep_count, chips, *refs),
         "route",
         half,
         in_specs=[hbm] * 2,
@@ -174,13 +183,13 @@
     acts = (jax.ShapeDtypeStruct((slot_count, hidden_count), jnp.float32),) * 2
     begun = call(lambda *refs: begin(chips, *refs), "begin", acts)(incoming, w_gate, w_up)
     hidden_shape = jax.ShapeDtypeStruct((slot_count, hidden_count), jnp.bfloat16)
-    hidden, other = call(lambda *refs: theirs(chips, *refs), "theirs", (hidden_shape, half))(
+    hidden, other = call(lambda *refs: theirs(chips, *refs), "theirs", (hidden_shape, split))(
         across, *begun, w_gate, w_up, w_down
     )
     crossed = lax.ppermute(other, "core", SWAP)
-    mine = call(lambda *refs: ours(chips, *refs), "ours", half)(hidden, w_down)
+    mine = call(lambda *refs: ours(chips, *refs), "ours", split)(hidden, w_down)
     match, weight = call(
-        lambda *refs: score(ep_count, *refs),
+        lambda *refs: score(ep_count, chips, *refs),
         "score",
         (
             jax.ShapeDtypeStruct((row_count, chips * slot_count), jnp.bfloat16),
@@ -188,8 +197,8 @@
         ),
         in_specs=[vmem] * 2 + [anywhere],
     )(ids, scores, other)
-    summed = call(add, "add", half, in_specs=[vmem] * 2 + [anywhere])(mine, crossed, weight)
-    returned = exchange(summed)
+    summed = call(add, "add", split, in_specs=[vmem] * 2 + [anywhere])(mine, crossed, weight)
+    returned = exchange(summed.reshape(half.shape))
     return call(
         combine,
         "combine",

time: 26.9 us -> 28 us (1.041)
  blocking collectives: 21.2 us -> 22.3 us
    all_to_all x2, blocking collectives: 21.2 us -> 22.3 us  [exchange(): return lax.all_to_all(rows, FAR, 0, 0, axis_index_groups=groups, tiled=True)]
where the time goes in v12:
time: 28 us; the launch traced here: 27.7 us
  blocking collectives  22.3 us (80%)
  Pallas kernels  3.4 us (12%)
  waiting for transfers between devices  1.61 us (6%)
  starting transfers between devices  0.33 us (1%)
    all_to_all x2, blocking collectives, exchange(): return lax.all_to_all(rows, FAR, 0, 0, axis_index_groups=groups, tiled=True)  22.3 us
    pallas_call x1, Pallas kernels, shards(): call(lambda *refs: route(ep_count, chips, *refs), 'route', half, in_specs...  1.27 us
    ppermute x1, waiting for transfers between devices, shards(): across = lax.ppermute(incoming, 'core', SWAP)  0.89 us
    pallas_call x1, Pallas kernels, shards(): call(combine, 'combine', jax.ShapeDtypeStruct((row_count, features), jnp....  0.87 us
    ppermute x1, waiting for transfers between devices, shards(): crossed = lax.ppermute(other, 'core', SWAP)  0.72 us
  transfers between devices with their start and end apart: 2, of which 2 were waited for; matrix products, arithmetic and copies ran while one was open for 0% of the time, Pallas kernels for 3%

profile of v12, /device:TPU:0, one launch (start us, length us, event | category | flops | bytes accessed | tf_op | source)
XLA Modules:
  0.0 27.7 jit_solution(6910849444707653515)
XLA Ops:
  0.0 0.0 copy-start
  0.0 0.0 copy-start.1
  0.0 1.3 %route.1 = bf16[64,896]{1,0:T(8,128)(2,1)S(1)} custom-call(s32[8,128]{1,0:T(8,128)} %bitcast.11, bf16[128,896]{1,0:T(8,128)(2,1)} %refs_1_.3), custom_call_target="tpu_custom_call" | custom-call | flops 2000000000 | tf_op jit(solution)/shard_map/route/pallas_call | solution.py:169
  1.3 12.5 %all_to_all.22 = bf16[8,8,896]{2,1,0:T(8,128)(2,1)S(1)} all-to-all(bf16[8,8,896]{2,1,0:T(8,128)(2,1)S(1)} %bitcast.10), channel_id=1, replica_groups={{15,12,11,8,7,4,3,0},{14,13,10,9,6,5,2,1},{31,28,27,24,23,20,19,16},{30..., dimensions={0} | all-to-all | bytes 229376 | tf_op jit(solution)/shard_map/all_to_all | solution.py:164
  13.8 0.0 copy-start.2
  13.8 0.1 collective-permute-start
  13.9 0.0 copy-done
  13.9 0.0 copy-done.1
  13.9 0.3 %begin.1 = (f32[32,128]{1,0:T(8,128)S(1)}, f32[32,128]{1,0:T(8,128)S(1)}) custom-call(bf16[64,896]{1,0:T(8,128)(2,1)S(1)} %bitcast.9, bf16[1,3584,128]{2,1,0:T(8,128)(2,1)S(1)} %copy-done, bf16[1,3584,128]{2,1,0:T(8,128)(2,1)S(1)} %copy-done.1), custom_call_target="tpu_custom_call" | custom-call | tf_op jit(solution)/shard_map/begin/pallas_call | solution.py:184
  14.3 0.9 %collective-permute-done.refs_0_ = bf16[64,896]{1,0:T(8,128)(2,1)S(1)} collective-permute-done((bf16[64,896]{1,0:T(8,128)(2,1)S(1)}, bf16[64,896]{1,0:T(8,128)(2,1)S(1)}, u32[]{:S(2)}, u32[]{:S(2)}) %collective-permute-start) | collective-permute-done | bytes 114720 | tf_op jit(solution)/shard_map/ppermute | solution.py:182
  15.1 0.0 copy-done.2
  15.1 0.0 copy-start.3
  15.2 0.0 copy-start.4
  15.2 0.5 %theirs.1 = (bf16[32,128]{1,0:T(8,128)(2,1)S(1)}, bf16[4,2,8,896]{3,2,1,0:T(8,128)(2,1)S(1)}) custom-call(bf16[64,896]{1,0:T(8,128)(2,1)S(1)} %collective-permute-done.refs_0_, f32[32,128]{1,0:T(8,128)S(1)} %get-tuple-element.11.refs_1_, f32[32,128]{1,0:T(8,128)S(1)} %get-tuple-element.12.refs_2_, bf16[1,3584,128]{2,1,0:T(8,128)(2,1)S(1)} %copy-done, ...), custom_call_target="tpu_custom_call" | custom-call | tf_op jit(solution)/shard_map/theirs/pallas_call | solution.py:186
  15.6 0.2 collective-permute-start.1
  15.9 0.0 copy-done.3
  15.9 0.0 copy-done.4
  15.9 0.2 score.1
  16.1 0.2 ours.1.mine_ref
  16.3 0.7 %collective-permute-done.1.other_ref = bf16[4,2,8,896]{3,2,1,0:T(8,128)(2,1)S(1)} collective-permute-done((bf16[4,2,8,896]{3,2,1,0:T(8,128)(2,1)S(1)}, bf16[4,2,8,896]{3,2,1,0:T(8,128)(2,1)S(1)}, u32[]{:S(2)}, u32[]{:S(2)}) %collective-permute-start.1) | collective-permute-done | bytes 114720 | tf_op jit(solution)/shard_map/ppermute | solution.py:189
  17.1 9.8 %all_to_all.23 = bf16[8,8,896]{2,1,0:T(8,128)(2,1)S(1)} all-to-all(bf16[8,8,896]{2,1,0:T(8,128)(2,1)S(1)} %bitcast.7), channel_id=1, replica_groups={{15,12,11,8,7,4,3,0},{14,13,10,9,6,5,2,1},{31,28,27,24,23,20,19,16},{30..., dimensions={0} | all-to-all | bytes 229376 | tf_op jit(solution)/shard_map/all_to_all | solution.py:164
  26.9 0.9 %combine.1 = bf16[128,896]{1,0:T(8,128)(2,1)} custom-call(bf16[128,64]{1,0:T(8,128)(2,1)S(1)} %get-tuple-element.14.match_ref, f32[128,1]{1,0:T(8,128)S(1)} %get-tuple-element.15._.weight_ref, bf16[64,896]{1,0:T(8,128)(2,1)S(1)} %bitcast.6), custom_call_target="tpu_custom_call" | custom-call | tf_op jit(solution)/shard_map/combine/pallas_call | solution.py:202
  (1 shorter events, 0.0 us)
Async XLA Ops:
  0.0 13.9 %copy-start = (bf16[1,3584,128]{2,1,0:T(8,128)(2,1)S(1)}, bf16[1,3584,128]{2,1,0:T(8,128)(2,1)}, u32[]{:S(2)}) copy-start(bf16[1,3584,128]{2,1,0:T(8,128)(2,1)} %refs_3_.1) | copy-start | bytes 2752516
  0.0 13.9 %copy-start.1 = (bf16[1,3584,128]{2,1,0:T(8,128)(2,1)S(1)}, bf16[1,3584,128]{2,1,0:T(8,128)(2,1)}, u32[]{:S(2)}) copy-start(bf16[1,3584,128]{2,1,0:T(8,128)(2,1)} %refs_4_.1) | copy-start | bytes 2752516
  13.8 1.3 %copy-start.2 = (bf16[1,128,3584]{2,1,0:T(8,128)(2,1)S(1)}, bf16[1,128,3584]{2,1,0:T(8,128)(2,1)}, u32[]{:S(2)}) copy-start(bf16[1,128,3584]{2,1,0:T(8,128)(2,1)} %refs_1_.5) | copy-start | bytes 2752516
  13.8 1.3 %collective-permute-start = (bf16[64,896]{1,0:T(8,128)(2,1)S(1)}, bf16[64,896]{1,0:T(8,128)(2,1)S(1)}, u32[]{:S(2)}, u32[]{:S(2)}) collective-permute-start(bf16[64,896]{1,0:T(8,128)(2,1)S(1)} %bitcast.8), channel_id=1, source_target_pairs={{0,1},{1,0},{2,3},{3,2},{4,5},{5,4},{6,7},{7,6},{8,9},{9,8},{10,11... | collective-permute-start | bytes 344072 | tf_op jit(solution)/shard_map/ppermute | solution.py:182
  15.1 0.7 %copy-start.3 = (s32[128,8]{0,1:T(8,128)S(1)}, s32[128,8]{0,1:T(8,128)}, u32[]{:S(2)}) copy-start(s32[128,8]{0,1:T(8,128)} %param.7) | copy-start | bytes 12292
  15.2 0.7 %copy-start.4 = (f32[128,8]{0,1:T(8,128)S(1)}, f32[128,8]{0,1:T(8,128)}, u32[]{:S(2)}) copy-start(f32[128,8]{0,1:T(8,128)} %param.8) | copy-start | bytes 12292
  15.6 1.4 %collective-permute-start.1 = (bf16[4,2,8,896]{3,2,1,0:T(8,128)(2,1)S(1)}, bf16[4,2,8,896]{3,2,1,0:T(8,128)(2,1)S(1)}, u32[]{:S(2)}, u32[]{:S(2)}) collective-permute-start(bf16[4,2,8,896]{3,2,1,0:T(8,128)(2,1)S(1)} %get-tuple-element.13.refs_2_), channel_id=1, source_target_pairs={{0,1},{1,0},{2,3},{3,2},{4,5},{5,4},{6,7},{7,6},{8,9},{9,8},{10,11... | collective-permute-start | bytes 344072 | tf_op jit(solution)/shard_map/ppermute | solution.py:189

commit v13 on v11

--- a/solution.py
+++ b/solution.py
@@ -33,8 +33,17 @@
     return expert * CAP + jnp.sum(counts * onehot, axis=0, keepdims=True), expert
 
 
-def row_codes(index, ep_count):
-    expert = (ep_count - 1 - lax.rem(index // CAP, ep_count)) // 2
+def first_order(ep_count):
+    return [z ^ 2 for z in range(ep_count)]
+
+
+def second_order(ep_count):
+    return list(reversed(range(ep_count)))
+
+
+def row_codes(index, order):
+    listed = lax.rem(index // CAP, len(order))
+    expert = sum(jnp.where(listed == at, z // 2, 0) for at, z in enumerate(order))
     return (expert * CAP + lax.rem(index, CAP)).astype(jnp.float32)
 
 
@@ -51,9 +60,9 @@
     ]
     for copy in copies:
         copy.start()
+    wanted = row_codes(iota((outgoing_ref.shape[0], row_count), 0), first_order(ep_count))
     copies[0].wait()
     code, _ = slot_codes(ids_ref[...].astype(jnp.float32), ep_count // 2)
-    wanted = row_codes(iota((outgoing_ref.shape[0], row_count), 0), ep_count)
     dispatch = jnp.where(code == wanted, 1.0, 0.0).astype(jnp.bfloat16)
     for copy in copies[1:]:
         copy.wait()
@@ -65,16 +74,16 @@
 def score(ep_count, ids_ref, scores_ref, _, match_ref, weight_ref):
     ids = ids_ref[...].astype(jnp.float32)
     code, expert = slot_codes(ids, ep_count // 2)
-    wanted = row_codes(iota(match_ref.shape, 1), ep_count)
+    wanted = row_codes(iota(match_ref.shape, 1), second_order(ep_count))
     match_ref[...] = jnp.where(to_column(code) == wanted, 1.0, 0.0).astype(jnp.bfloat16)
     squashed = jax.nn.sigmoid(scores_ref[...])
     chosen = jnp.sum(jnp.where(ids == expert, squashed, 0.0), axis=0, keepdims=True)
     weight_ref[...] = to_column(2.5 * chosen / jnp.sum(squashed, axis=0, keepdims=True))
 
 
-def far_groups(ep_count, chips):
+def far_groups(order, chips):
     return [
-        [(z * chips + x) * 2 + (side + x) % 2 for x in range(chips) for z in reversed(range(ep_count))]
+        [(z * chips + x) * 2 + (side + x) % 2 for x in range(chips) for z in order]
         for side in range(2)
     ]
 
@@ -98,10 +107,14 @@
 
 def lower(chips, own, hidden, down_ref, out_ref):
     part_rows, features = out_ref.shape[0] // chips, out_ref.shape[1]
+    first = first_order(part_rows // CAP)
+    moves = [first.index(z) for z in second_order(part_rows // CAP)]
     for chip in range(chips):
         columns = columns_of(chip, own, features)
-        out_ref[chip * part_rows : (chip + 1) * part_rows, :] = jnp.dot(
-            hidden, down_ref[0, :, columns], preferred_element_type=jnp.float32
+        values = jnp.dot(hidden, down_ref[0, :, columns], preferred_element_type=jnp.float32)
+        blocks = [values[at * CAP : (at + 1) * CAP, :] for at in moves]
+        out_ref[chip * part_rows : (chip + 1) * part_rows, :] = jnp.concatenate(
+            blocks, axis=0
         ).astype(jnp.bfloat16)
 
 
@@ -150,8 +163,8 @@
     hbm, vmem = (pl.BlockSpec(memory_space=space) for space in (pltpu.HBM, pltpu.VMEM))
     anywhere = pl.BlockSpec(memory_space=pl.ANY)
 
-    def exchange(rows):
-        groups = far_groups(ep_count, chips)
+    def exchange(rows, order):
+        groups = far_groups(order(ep_count), chips)
         return lax.all_to_all(rows, FAR, 0, 0, axis_index_groups=groups, tiled=True)
 
     def call(kernel, name, out_shape, **rest):
@@ -169,7 +182,7 @@
         ],
         cost_estimate=pl.CostEstimate(flops=2 * 10**9, bytes_accessed=0, transcendentals=0),
     )(*(pltpu.with_memory_space_constraint(value, pltpu.HBM) for value in (ids, tokens)))
-    incoming = exchange(outgoing)
+    incoming = exchange(outgoing, first_order)
     across = lax.ppermute(incoming, "core", SWAP)
     acts = (jax.ShapeDtypeStruct((slot_count, hidden_count), jnp.float32),) * 2
     begun = call(lambda *refs: begin(chips, *refs), "begin", acts)(incoming, w_gate, w_up)
@@ -189,7 +202,7 @@
         in_specs=[vmem] * 2 + [anywhere],
     )(ids, scores, other)
     summed = call(add, "add", half, in_specs=[vmem] * 2 + [anywhere])(mine, crossed, weight)
-    returned = exchange(summed)
+    returned = exchange(summed, second_order)
     return call(
         combine,
         "combine",

time: 26.9 us -> 26.6 us (0.989)
  starting transfers between devices: 0.33 us -> 0.64 us
  waiting for transfers between devices: 1.63 us -> 1.34 us
where the time goes in v13:
time: 26.6 us; the launch traced here: 26.4 us
  blocking collectives  21 us (79%)
  Pallas kernels  3.32 us (12%)
  waiting for transfers between devices  1.34 us (5%)
  starting transfers between devices  0.64 us (2%)
    all_to_all x2, blocking collectives, exchange(): return lax.all_to_all(rows, FAR, 0, 0, axis_index_groups=groups, tiled=True)  21 us
    pallas_call x1, Pallas kernels, shards(): call(lambda *refs: route(ep_count, *refs), 'route', half, in_specs=[hbm]...  1.27 us
    pallas_call x1, Pallas kernels, shards(): call(combine, 'combine', jax.ShapeDtypeStruct((row_count, features), jnp....  0.87 us
    ppermute x1, waiting for transfers between devices, shards(): across = lax.ppermute(incoming, 'core', SWAP)  0.76 us
    ppermute x1, waiting for transfers between devices, shards(): crossed = lax.ppermute(other, 'core', SWAP)  0.58 us
  transfers between devices with their start and end apart: 2, of which 2 were waited for; matrix products, arithmetic and copies ran while one was open for 0% of the time, Pallas kernels for 3%

profile of v13, /device:TPU:0, one launch (start us, length us, event | category | flops | bytes accessed | tf_op | source)
XLA Modules:
  0.0 26.4 jit_solution(4284812078432306832)
XLA Ops:
  0.0 0.0 copy-start
  0.0 0.0 copy-start.1
  0.0 1.3 %route.1 = bf16[64,896]{1,0:T(8,128)(2,1)S(1)} custom-call(s32[8,128]{1,0:T(8,128)} %bitcast.11, bf16[128,896]{1,0:T(8,128)(2,1)} %refs_1_.3), custom_call_target="tpu_custom_call" | custom-call | flops 2000000000 | tf_op jit(solution)/shard_map/route/pallas_call | solution.py:173
  1.3 11.8 %all_to_all.22 = bf16[8,8,896]{2,1,0:T(8,128)(2,1)S(1)} all-to-all(bf16[8,8,896]{2,1,0:T(8,128)(2,1)S(1)} %bitcast.10), channel_id=1, replica_groups={{8,12,0,4,11,15,3,7},{9,13,1,5,10,14,2,6},{24,28,16,20,27,31,19,23},{25..., dimensions={0} | all-to-all | bytes 229376 | tf_op jit(solution)/shard_map/all_to_all | solution.py:168
  13.1 0.0 copy-start.2
  13.1 0.3 %collective-permute-start = (bf16[64,896]{1,0:T(8,128)(2,1)S(1)}, bf16[64,896]{1,0:T(8,128)(2,1)S(1)}, u32[]{:S(2)}, u32[]{:S(2)}) collective-permute-start(bf16[64,896]{1,0:T(8,128)(2,1)S(1)} %bitcast.8), channel_id=1, source_target_pairs={{0,1},{1,0},{2,3},{3,2},{4,5},{5,4},{6,7},{7,6},{8,9},{9,8},{10,11... | collective-permute-start | bytes 344072 | tf_op jit(solution)/shard_map/ppermute | solution.py:186
  13.4 0.0 copy-done
  13.4 0.0 copy-done.1
  13.4 0.3 begin.1
  13.7 0.8 %collective-permute-done.refs_0_ = bf16[64,896]{1,0:T(8,128)(2,1)S(1)} collective-permute-done((bf16[64,896]{1,0:T(8,128)(2,1)S(1)}, bf16[64,896]{1,0:T(8,128)(2,1)S(1)}, u32[]{:S(2)}, u32[]{:S(2)}) %collective-permute-start) | collective-permute-done | bytes 114720 | tf_op jit(solution)/shard_map/ppermute | solution.py:186
  14.4 0.0 copy-done.2
  14.4 0.0 copy-start.3
  14.4 0.0 copy-start.4
  14.4 0.5 %theirs.1 = (bf16[32,128]{1,0:T(8,128)(2,1)S(1)}, bf16[64,896]{1,0:T(8,128)(2,1)S(1)}) custom-call(bf16[64,896]{1,0:T(8,128)(2,1)S(1)} %collective-permute-done.refs_0_, f32[32,128]{1,0:T(8,128)S(1)} %get-tuple-element.11.refs_1_, f32[32,128]{1,0:T(8,128)S(1)} %get-tuple-element.12.refs_2_, bf16[1,3584,128]{2,1,0:T(8,128)(2,1)S(1)} %copy-done, ...), custom_call_target="tpu_custom_call" | custom-call | tf_op jit(solution)/shard_map/theirs/pallas_call | solution.py:190
  14.9 0.4 %collective-permute-start.1 = (bf16[64,896]{1,0:T(8,128)(2,1)S(1)}, bf16[64,896]{1,0:T(8,128)(2,1)S(1)}, u32[]{:S(2)}, u32[]{:S(2)}) collective-permute-start(bf16[64,896]{1,0:T(8,128)(2,1)S(1)} %get-tuple-element.13.refs_2_), channel_id=1, source_target_pairs={{0,1},{1,0},{2,3},{3,2},{4,5},{5,4},{6,7},{7,6},{8,9},{9,8},{10,11... | collective-permute-start | bytes 344072 | tf_op jit(solution)/shard_map/ppermute | solution.py:193
  15.2 0.0 copy-done.3
  15.2 0.0 copy-done.4
  15.2 0.2 score.1
  15.5 0.2 ours.1.mine_ref
  15.7 0.6 %collective-permute-done.1.other_ref = bf16[64,896]{1,0:T(8,128)(2,1)S(1)} collective-permute-done((bf16[64,896]{1,0:T(8,128)(2,1)S(1)}, bf16[64,896]{1,0:T(8,128)(2,1)S(1)}, u32[]{:S(2)}, u32[]{:S(2)}) %collective-permute-start.1) | collective-permute-done | bytes 114720 | tf_op jit(solution)/shard_map/ppermute | solution.py:193
  16.3 9.2 %all_to_all.23 = bf16[8,8,896]{2,1,0:T(8,128)(2,1)S(1)} all-to-all(bf16[8,8,896]{2,1,0:T(8,128)(2,1)S(1)} %bitcast.7), channel_id=1, replica_groups={{12,8,4,0,15,11,7,3},{13,9,5,1,14,10,6,2},{28,24,20,16,31,27,23,19},{29..., dimensions={0} | all-to-all | bytes 229376 | tf_op jit(solution)/shard_map/all_to_all | solution.py:168
  25.5 0.9 %combine.1 = bf16[128,896]{1,0:T(8,128)(2,1)} custom-call(bf16[128,64]{1,0:T(8,128)(2,1)S(1)} %get-tuple-element.14.match_ref, f32[128,1]{1,0:T(8,128)S(1)} %get-tuple-element.15._.weight_ref, bf16[64,896]{1,0:T(8,128)(2,1)S(1)} %bitcast.6), custom_call_target="tpu_custom_call" | custom-call | tf_op jit(solution)/shard_map/combine/pallas_call | solution.py:206
  (1 shorter events, 0.0 us)
Async XLA Ops:
  0.0 13.4 %copy-start = (bf16[1,3584,128]{2,1,0:T(8,128)(2,1)S(1)}, bf16[1,3584,128]{2,1,0:T(8,128)(2,1)}, u32[]{:S(2)}) copy-start(bf16[1,3584,128]{2,1,0:T(8,128)(2,1)} %refs_3_.1) | copy-start | bytes 2752516
  0.0 13.4 %copy-start.1 = (bf16[1,3584,128]{2,1,0:T(8,128)(2,1)S(1)}, bf16[1,3584,128]{2,1,0:T(8,128)(2,1)}, u32[]{:S(2)}) copy-start(bf16[1,3584,128]{2,1,0:T(8,128)(2,1)} %refs_4_.1) | copy-start | bytes 2752516
  13.1 1.3 %copy-start.2 = (bf16[1,128,3584]{2,1,0:T(8,128)(2,1)S(1)}, bf16[1,128,3584]{2,1,0:T(8,128)(2,1)}, u32[]{:S(2)}) copy-start(bf16[1,128,3584]{2,1,0:T(8,128)(2,1)} %refs_1_.5) | copy-start | bytes 2752516
  13.1 1.3 %collective-permute-start = (bf16[64,896]{1,0:T(8,128)(2,1)S(1)}, bf16[64,896]{1,0:T(8,128)(2,1)S(1)}, u32[]{:S(2)}, u32[]{:S(2)}) collective-permute-start(bf16[64,896]{1,0:T(8,128)(2,1)S(1)} %bitcast.8), channel_id=1, source_target_pairs={{0,1},{1,0},{2,3},{3,2},{4,5},{5,4},{6,7},{7,6},{8,9},{9,8},{10,11... | collective-permute-start | bytes 344072 | tf_op jit(solution)/shard_map/ppermute | solution.py:186
  14.4 0.8 %copy-start.3 = (s32[128,8]{0,1:T(8,128)S(1)}, s32[128,8]{0,1:T(8,128)}, u32[]{:S(2)}) copy-start(s32[128,8]{0,1:T(8,128)} %param.7) | copy-start | bytes 12292
  14.4 0.8 %copy-start.4 = (f32[128,8]{0,1:T(8,128)S(1)}, f32[128,8]{0,1:T(8,128)}, u32[]{:S(2)}) copy-start(f32[128,8]{0,1:T(8,128)} %param.8) | copy-start | bytes 12292
  14.9 1.4 %collective-permute-start.1 = (bf16[64,896]{1,0:T(8,128)(2,1)S(1)}, bf16[64,896]{1,0:T(8,128)(2,1)S(1)}, u32[]{:S(2)}, u32[]{:S(2)}) collective-permute-start(bf16[64,896]{1,0:T(8,128)(2,1)S(1)} %get-tuple-element.13.refs_2_), channel_id=1, source_target_pairs={{0,1},{1,0},{2,3},{3,2},{4,5},{5,4},{6,7},{7,6},{8,9},{9,8},{10,11... | collective-permute-start | bytes 344072 | tf_op jit(solution)/shard_map/ppermute | solution.py:193

commit v14 on v13

--- a/solution.py
+++ b/solution.py
@@ -38,7 +38,7 @@
 
 
 def second_order(ep_count):
-    return list(reversed(range(ep_count)))
+    return [z // 4 * 4 + (3, 1, 2, 0)[z % 4] for z in range(ep_count)]
 
 
 def row_codes(index, order):

time: 26.6 us -> 27.2 us (1.023)
  blocking collectives: 21 us -> 21.7 us
    all_to_all x2, blocking collectives: 21 us -> 21.7 us  [exchange(): return lax.all_to_all(rows, FAR, 0, 0, axis_index_groups=groups, tiled=True)]
where the time goes in v14:
time: 27.2 us; the launch traced here: 27 us
  blocking collectives  21.7 us (80%)
  Pallas kernels  3.33 us (12%)
  waiting for transfers between devices  1.34 us (5%)
  starting transfers between devices  0.64 us (2%)
    all_to_all x2, blocking collectives, exchange(): return lax.all_to_all(rows, FAR, 0, 0, axis_index_groups=groups, tiled=True)  21.7 us
    pallas_call x1, Pallas kernels, shards(): call(lambda *refs: route(ep_count, *refs), 'route', half, in_specs=[hbm]...  1.27 us
    pallas_call x1, Pallas kernels, shards(): call(combine, 'combine', jax.ShapeDtypeStruct((row_count, features), jnp....  0.87 us
    ppermute x1, waiting for transfers between devices, shards(): across = lax.ppermute(incoming, 'core', SWAP)  0.76 us
    ppermute x1, waiting for transfers between devices, shards(): crossed = lax.ppermute(other, 'core', SWAP)  0.58 us
  transfers between devices with their start and end apart: 2, of which 2 were waited for; matrix products, arithmetic and copies ran while one was open for 0% of the time, Pallas kernels for 3%

profile of v14, /device:TPU:0, one launch (start us, length us, event | category | flops | bytes accessed | tf_op | source)
XLA Modules:
  0.0 27.0 jit_solution(16848033792939106578)
XLA Ops:
  0.0 0.0 copy-start
  0.0 0.0 copy-start.1
  0.0 1.3 %route.1 = bf16[64,896]{1,0:T(8,128)(2,1)S(1)} custom-call(s32[8,128]{1,0:T(8,128)} %bitcast.11, bf16[128,896]{1,0:T(8,128)(2,1)} %refs_1_.3), custom_call_target="tpu_custom_call" | custom-call | flops 2000000000 | tf_op jit(solution)/shard_map/route/pallas_call | solution.py:173
  1.3 11.8 %all_to_all.22 = bf16[8,8,896]{2,1,0:T(8,128)(2,1)S(1)} all-to-all(bf16[8,8,896]{2,1,0:T(8,128)(2,1)S(1)} %bitcast.10), channel_id=1, replica_groups={{8,12,0,4,11,15,3,7},{9,13,1,5,10,14,2,6},{24,28,16,20,27,31,19,23},{25..., dimensions={0} | all-to-all | bytes 229376 | tf_op jit(solution)/shard_map/all_to_all | solution.py:168
  13.1 0.0 copy-start.2
  13.1 0.3 %collective-permute-start = (bf16[64,896]{1,0:T(8,128)(2,1)S(1)}, bf16[64,896]{1,0:T(8,128)(2,1)S(1)}, u32[]{:S(2)}, u32[]{:S(2)}) collective-permute-start(bf16[64,896]{1,0:T(8,128)(2,1)S(1)} %bitcast.8), channel_id=1, source_target_pairs={{0,1},{1,0},{2,3},{3,2},{4,5},{5,4},{6,7},{7,6},{8,9},{9,8},{10,11... | collective-permute-start | bytes 344072 | tf_op jit(solution)/shard_map/ppermute | solution.py:186
  13.4 0.0 copy-done
  13.4 0.0 copy-done.1
  13.4 0.3 begin.1
  13.7 0.8 %collective-permute-done.refs_0_ = bf16[64,896]{1,0:T(8,128)(2,1)S(1)} collective-permute-done((bf16[64,896]{1,0:T(8,128)(2,1)S(1)}, bf16[64,896]{1,0:T(8,128)(2,1)S(1)}, u32[]{:S(2)}, u32[]{:S(2)}) %collective-permute-start) | collective-permute-done | bytes 114720 | tf_op jit(solution)/shard_map/ppermute | solution.py:186
  14.4 0.0 copy-done.2
  14.4 0.0 copy-start.3
  14.4 0.0 copy-start.4
  14.4 0.5 %theirs.1 = (bf16[32,128]{1,0:T(8,128)(2,1)S(1)}, bf16[64,896]{1,0:T(8,128)(2,1)S(1)}) custom-call(bf16[64,896]{1,0:T(8,128)(2,1)S(1)} %collective-permute-done.refs_0_, f32[32,128]{1,0:T(8,128)S(1)} %get-tuple-element.11.refs_1_, f32[32,128]{1,0:T(8,128)S(1)} %get-tuple-element.12.refs_2_, bf16[1,3584,128]{2,1,0:T(8,128)(2,1)S(1)} %copy-done, ...), custom_call_target="tpu_custom_call" | custom-call | tf_op jit(solution)/shard_map/theirs/pallas_call | solution.py:190
  14.9 0.4 %collective-permute-start.1 = (bf16[64,896]{1,0:T(8,128)(2,1)S(1)}, bf16[64,896]{1,0:T(8,128)(2,1)S(1)}, u32[]{:S(2)}, u32[]{:S(2)}) collective-permute-start(bf16[64,896]{1,0:T(8,128)(2,1)S(1)} %get-tuple-element.13.refs_2_), channel_id=1, source_target_pairs={{0,1},{1,0},{2,3},{3,2},{4,5},{5,4},{6,7},{7,6},{8,9},{9,8},{10,11... | collective-permute-start | bytes 344072 | tf_op jit(solution)/shard_map/ppermute | solution.py:193
  15.2 0.0 copy-done.3
  15.2 0.0 copy-done.4
  15.2 0.2 score.1
  15.5 0.2 ours.1.mine_ref
  15.7 0.6 %collective-permute-done.1.other_ref = bf16[64,896]{1,0:T(8,128)(2,1)S(1)} collective-permute-done((bf16[64,896]{1,0:T(8,128)(2,1)S(1)}, bf16[64,896]{1,0:T(8,128)(2,1)S(1)}, u32[]{:S(2)}, u32[]{:S(2)}) %collective-permute-start.1) | collective-permute-done | bytes 114720 | tf_op jit(solution)/shard_map/ppermute | solution.py:193
  16.3 9.8 %all_to_all.23 = bf16[8,8,896]{2,1,0:T(8,128)(2,1)S(1)} all-to-all(bf16[8,8,896]{2,1,0:T(8,128)(2,1)S(1)} %bitcast.7), channel_id=1, replica_groups={{12,4,8,0,15,7,11,3},{13,5,9,1,14,6,10,2},{28,20,24,16,31,23,27,19},{29..., dimensions={0} | all-to-all | bytes 229376 | tf_op jit(solution)/shard_map/all_to_all | solution.py:168
  26.2 0.9 %combine.1 = bf16[128,896]{1,0:T(8,128)(2,1)} custom-call(bf16[128,64]{1,0:T(8,128)(2,1)S(1)} %get-tuple-element.14.match_ref, f32[128,1]{1,0:T(8,128)S(1)} %get-tuple-element.15._.weight_ref, bf16[64,896]{1,0:T(8,128)(2,1)S(1)} %bitcast.6), custom_call_target="tpu_custom_call" | custom-call | tf_op jit(solution)/shard_map/combine/pallas_call | solution.py:206
  (1 shorter events, 0.0 us)
Async XLA Ops:
  0.0 13.4 %copy-start = (bf16[1,3584,128]{2,1,0:T(8,128)(2,1)S(1)}, bf16[1,3584,128]{2,1,0:T(8,128)(2,1)}, u32[]{:S(2)}) copy-start(bf16[1,3584,128]{2,1,0:T(8,128)(2,1)} %refs_3_.1) | copy-start | bytes 2752516
  0.0 13.4 %copy-start.1 = (bf16[1,3584,128]{2,1,0:T(8,128)(2,1)S(1)}, bf16[1,3584,128]{2,1,0:T(8,128)(2,1)}, u32[]{:S(2)}) copy-start(bf16[1,3584,128]{2,1,0:T(8,128)(2,1)} %refs_4_.1) | copy-start | bytes 2752516
  13.1 1.3 %copy-start.2 = (bf16[1,128,3584]{2,1,0:T(8,128)(2,1)S(1)}, bf16[1,128,3584]{2,1,0:T(8,128)(2,1)}, u32[]{:S(2)}) copy-start(bf16[1,128,3584]{2,1,0:T(8,128)(2,1)} %refs_1_.5) | copy-start | bytes 2752516
  13.1 1.3 %collective-permute-start = (bf16[64,896]{1,0:T(8,128)(2,1)S(1)}, bf16[64,896]{1,0:T(8,128)(2,1)S(1)}, u32[]{:S(2)}, u32[]{:S(2)}) collective-permute-start(bf16[64,896]{1,0:T(8,128)(2,1)S(1)} %bitcast.8), channel_id=1, source_target_pairs={{0,1},{1,0},{2,3},{3,2},{4,5},{5,4},{6,7},{7,6},{8,9},{9,8},{10,11... | collective-permute-start | bytes 344072 | tf_op jit(solution)/shard_map/ppermute | solution.py:186
  14.4 0.8 %copy-start.3 = (s32[128,8]{0,1:T(8,128)S(1)}, s32[128,8]{0,1:T(8,128)}, u32[]{:S(2)}) copy-start(s32[128,8]{0,1:T(8,128)} %param.7) | copy-start | bytes 12292
  14.4 0.8 %copy-start.4 = (f32[128,8]{0,1:T(8,128)S(1)}, f32[128,8]{0,1:T(8,128)}, u32[]{:S(2)}) copy-start(f32[128,8]{0,1:T(8,128)} %param.8) | copy-start | bytes 12292
  14.9 1.4 %collective-permute-start.1 = (bf16[64,896]{1,0:T(8,128)(2,1)S(1)}, bf16[64,896]{1,0:T(8,128)(2,1)S(1)}, u32[]{:S(2)}, u32[]{:S(2)}) collective-permute-start(bf16[64,896]{1,0:T(8,128)(2,1)S(1)} %get-tuple-element.13.refs_2_), channel_id=1, source_target_pairs={{0,1},{1,0},{2,3},{3,2},{4,5},{5,4},{6,7},{7,6},{8,9},{9,8},{10,11... | collective-permute-start | bytes 344072 | tf_op jit(solution)/shard_map/ppermute | solution.py:193

commit v15 on v13

--- a/solution.py
+++ b/solution.py
@@ -39,6 +39,10 @@
 
 def second_order(ep_count):
     return list(reversed(range(ep_count)))
+
+
+def flip(chip, z):
+    return (z >> 1) & 1
 
 
 def row_codes(index, order):
@@ -83,57 +87,57 @@
 
 def far_groups(order, chips):
     return [
-        [(z * chips + x) * 2 + (side + x) % 2 for x in range(chips) for z in order]
+        [(z * chips + x) * 2 + (side + flip(x, z)) % 2 for x in range(chips) for z in order]
         for side in range(2)
     ]
 
 
-def columns_of(chip, own, features):
-    core = lax.rem(lax.axis_index("core") + lax.axis_index("chip") + chip + (0 if own else 1), 2)
-    return pl.ds(pl.multiple_of((2 * chip + core) * features, features), features)
-
-
-def lift(chips, own, rows_ref, gate_ref, up_ref):
-    part_rows, features = rows_ref.shape[0] // chips, rows_ref.shape[1]
-    gate_act = jnp.zeros((part_rows, gate_ref.shape[2]), jnp.float32)
-    up_act = jnp.zeros((part_rows, up_ref.shape[2]), jnp.float32)
+def turned(chip, z):
+    side = lax.axis_index("core") ^ flip(lax.axis_index("chip"), lax.axis_index("ep"))
+    return (side ^ flip(chip, z)) == 1
+
+
+def theirs(chips, own_ref, across_ref, gate_ref, up_ref, down_ref, mine_ref, other_ref):
+    part_rows, features = own_ref.shape[0] // chips, own_ref.shape[1]
+    first, second = first_order(part_rows // CAP), second_order(part_rows // CAP)
+    width = gate_ref.shape[2]
+    acts = jnp.zeros((part_rows, 2 * width), jnp.float32)
     for chip in range(chips):
-        rows = rows_ref[chip * part_rows : (chip + 1) * part_rows, :]
-        columns = columns_of(chip, own, features)
-        gate_act += jnp.dot(rows, gate_ref[0, columns, :], preferred_element_type=jnp.float32)
-        up_act += jnp.dot(rows, up_ref[0, columns, :], preferred_element_type=jnp.float32)
-    return gate_act, up_act
-
-
-def lower(chips, own, hidden, down_ref, out_ref):
-    part_rows, features = out_ref.shape[0] // chips, out_ref.shape[1]
-    first = first_order(part_rows // CAP)
-    moves = [first.index(z) for z in second_order(part_rows // CAP)]
+        sides = [[], []]
+        at = 0
+        while at < len(first):
+            end = at + 1
+            while end < len(first) and flip(chip, first[end]) == flip(chip, first[at]):
+                end += 1
+            rows = slice(chip * part_rows + at * CAP, chip * part_rows + end * CAP)
+            own, across = own_ref[rows, :], across_ref[rows, :]
+            second_core = turned(chip, first[at])
+            sides[0].append(jnp.where(second_core, across, own))
+            sides[1].append(jnp.where(second_core, own, across))
+            at = end
+        for core in range(2):
+            columns = slice((2 * chip + core) * features, (2 * chip + core + 1) * features)
+            both = jnp.concatenate([gate_ref[0, columns, :], up_ref[0, columns, :]], axis=1)
+            rows = jnp.concatenate(sides[core], axis=0)
+            acts += jnp.dot(rows, both, preferred_element_type=jnp.float32)
+    gate_act, up_act = acts[:, :width], acts[:, width:]
+    hidden = (gate_act / (1.0 + jnp.exp(-gate_act)) * up_act).astype(jnp.bfloat16)
     for chip in range(chips):
-        columns = columns_of(chip, own, features)
-        values = jnp.dot(hidden, down_ref[0, :, columns], preferred_element_type=jnp.float32)
-        blocks = [values[at * CAP : (at + 1) * CAP, :] for at in moves]
-        out_ref[chip * part_rows : (chip + 1) * part_rows, :] = jnp.concatenate(
-            blocks, axis=0
-        ).astype(jnp.bfloat16)
-
-
-def begin(chips, rows_ref, gate_ref, up_ref, gate_act_ref, up_act_ref):
-    gate_act_ref[...], up_act_ref[...] = lift(chips, True, rows_ref, gate_ref, up_ref)
-
-
-def theirs(chips, *refs):
-    rows_ref, gate_act_ref, up_act_ref, gate_ref, up_ref, down_ref, hidden_ref, other_ref = refs
-    gate_act, up_act = lift(chips, False, rows_ref, gate_ref, up_ref)
-    gate_act += gate_act_ref[...]
-    up_act += up_act_ref[...]
-    hidden = (gate_act / (1.0 + jnp.exp(-gate_act)) * up_act).astype(jnp.bfloat16)
-    hidden_ref[...] = hidden
-    lower(chips, False, hidden, down_ref, other_ref)
-
-
-def ours(chips, hidden_ref, down_ref, mine_ref):
-    lower(chips, True, hidden_ref[...], down_ref, mine_ref)
+        values = []
+        for core in range(2):
+            columns = slice((2 * chip + core) * features, (2 * chip + core + 1) * features)
+            values.append(
+                jnp.dot(hidden, down_ref[0, :, columns], preferred_element_type=jnp.float32)
+            )
+        mine, other = [], []
+        for z in second:
+            rows = slice(first.index(z) * CAP, (first.index(z) + 1) * CAP)
+            second_core = turned(chip, z)
+            mine.append(jnp.where(second_core, values[1][rows, :], values[0][rows, :]))
+            other.append(jnp.where(second_core, values[0][rows, :], values[1][rows, :]))
+        rows = slice(chip * part_rows, (chip + 1) * part_rows)
+        mine_ref[rows, :] = jnp.concatenate(mine, axis=0).astype(jnp.bfloat16)
+        other_ref[rows, :] = jnp.concatenate(other, axis=0).astype(jnp.bfloat16)
 
 
 def add(mine_ref, other_ref, _, out_ref):
@@ -155,7 +159,7 @@
 
 def shards(tokens, expert_ids, route_scores, w_gate, w_up, w_down):
     row_count, features = tokens.shape
-    top_count, hidden_count = expert_ids.shape[1], w_gate.shape[2]
+    top_count = expert_ids.shape[1]
     ep_count, chips = lax.axis_size("ep"), lax.axis_size("chip")
     slot_count = ep_count * CAP
     half = jax.ShapeDtypeStruct((chips * slot_count, features), jnp.bfloat16)
@@ -184,14 +188,10 @@
     )(*(pltpu.with_memory_space_constraint(value, pltpu.HBM) for value in (ids, tokens)))
     incoming = exchange(outgoing, first_order)
     across = lax.ppermute(incoming, "core", SWAP)
-    acts = (jax.ShapeDtypeStruct((slot_count, hidden_count), jnp.float32),) * 2
-    begun = call(lambda *refs: begin(chips, *refs), "begin", acts)(incoming, w_gate, w_up)
-    hidden_shape = jax.ShapeDtypeStruct((slot_count, hidden_count), jnp.bfloat16)
-    hidden, other = call(lambda *refs: theirs(chips, *refs), "theirs", (hidden_shape, half))(
-        across, *begun, w_gate, w_up, w_down
+    mine, other = call(lambda *refs: theirs(chips, *refs), "theirs", (half, half))(
+        incoming, across, w_gate, w_up, w_down
     )
     crossed = lax.ppermute(other, "core", SWAP)
-    mine = call(lambda *refs: ours(chips, *refs), "ours", half)(hidden, w_down)
     match, weight = call(
         lambda *refs: score(ep_count, *refs),
         "score",
@@ -200,7 +200,7 @@
             jax.ShapeDtypeStruct((row_count, 1), jnp.float32),
         ),
         in_specs=[vmem] * 2 + [anywhere],
-    )(ids, scores, other)
+    )(ids, scores, incoming)
     summed = call(add, "add", half, in_specs=[vmem] * 2 + [anywhere])(mine, crossed, weight)
     returned = exchange(summed, second_order)
     return call(

time: 26.6 us -> 26.8 us (level)
  blocking collectives: 21 us -> 19.9 us
  starting transfers between devices: 0.64 us -> 1.65 us
  waiting for transfers between devices: 1.34 us -> 1.68 us
    all_to_all x2, blocking collectives: 21 us -> 19.9 us  [exchange(): return lax.all_to_all(rows, FAR, 0, 0, axis_index_groups=groups, tiled=True)]
    ppermute x1, starting transfers between devices: 0.29 us -> 1.21 us  [shards(): across = lax.ppermute(incoming, 'core', SWAP)]
    pallas_call x3 -> x1, Pallas kernels: 0.92 us -> 0.87 us  [shards(): call(lambda *refs: theirs(chips, *refs), 'theirs', (half, half))]
  transfers between devices with their start and end apart: 2 -> 2, of which waited for: 2 -> 2; matrix products, arithmetic and copies ran while one was open for 0% -> 0% of each run, Pallas kernels for 3% -> 1%
where the time goes in v15:
time: 26.8 us; the launch traced here: 26.6 us
  blocking collectives  19.9 us (74%)
  Pallas kernels  3.29 us (12%)
  waiting for transfers between devices  1.68 us (6%)
  starting transfers between devices  1.65 us (6%)
    all_to_all x2, blocking collectives, exchange(): return lax.all_to_all(rows, FAR, 0, 0, axis_index_groups=groups, tiled=True)  19.9 us
    pallas_call x1, Pallas kernels, shards(): call(lambda *refs: route(ep_count, *refs), 'route', half, in_specs=[hbm]...  1.29 us
    ppermute x1, starting transfers between devices, shards(): across = lax.ppermute(incoming, 'core', SWAP)  1.21 us
    ppermute x1, waiting for transfers between devices, shards(): across = lax.ppermute(incoming, 'core', SWAP)  0.97 us
    pallas_call x1, Pallas kernels, shards(): call(combine, 'combine', jax.ShapeDtypeStruct((row_count, features), jnp....  0.87 us
    pallas_call x1, Pallas kernels, shards(): call(lambda *refs: theirs(chips, *refs), 'theirs', (half, half))  0.87 us
    ppermute x1, waiting for transfers between devices, shards(): crossed = lax.ppermute(other, 'core', SWAP)  0.72 us
  transfers between devices with their start and end apart: 2, of which 2 were waited for; matrix products, arithmetic and copies ran while one was open for 0% of the time, Pallas kernels for 1%

profile of v15, /device:TPU:0, one launch (start us, length us, event | category | flops | bytes accessed | tf_op | source)
XLA Modules:
  0.0 26.6 jit_solution(12221245265745912839)
XLA Ops:
  0.0 0.0 copy-start
  0.0 0.0 copy-start.1
  0.0 0.0 copy-start.2
  0.0 1.3 %route.1 = bf16[64,896]{1,0:T(8,128)(2,1)S(1)} custom-call(s32[8,128]{1,0:T(8,128)} %bitcast.12, bf16[128,896]{1,0:T(8,128)(2,1)} %refs_1_.1), custom_call_target="tpu_custom_call" | custom-call | flops 2000000000 | tf_op jit(solution)/shard_map/route/pallas_call | solution.py:177
  1.3 11.1 %all_to_all.22 = bf16[8,8,896]{2,1,0:T(8,128)(2,1)S(1)} all-to-all(bf16[8,8,896]{2,1,0:T(8,128)(2,1)S(1)} %bitcast.11), channel_id=1, replica_groups={{9,13,0,4,11,15,2,6},{8,12,1,5,10,14,3,7},{25,29,16,20,27,31,18,22},{24..., dimensions={0} | all-to-all | bytes 229376 | tf_op jit(solution)/shard_map/all_to_all | solution.py:172
  12.4 1.2 %collective-permute-start = (bf16[64,896]{1,0:T(8,128)(2,1)S(1)}, bf16[64,896]{1,0:T(8,128)(2,1)S(1)}, u32[]{:S(2)}, u32[]{:S(2)}) collective-permute-start(bf16[64,896]{1,0:T(8,128)(2,1)S(1)} %bitcast.6), channel_id=1, source_target_pairs={{0,1},{1,0},{2,3},{3,2},{4,5},{5,4},{6,7},{7,6},{8,9},{9,8},{10,11... | collective-permute-start | bytes 344072 | tf_op jit(solution)/shard_map/ppermute | solution.py:190
  13.6 1.0 %collective-permute-done.refs_1_ = bf16[64,896]{1,0:T(8,128)(2,1)S(1)} collective-permute-done((bf16[64,896]{1,0:T(8,128)(2,1)S(1)}, bf16[64,896]{1,0:T(8,128)(2,1)S(1)}, u32[]{:S(2)}, u32[]{:S(2)}) %collective-permute-start) | collective-permute-done | bytes 114720 | tf_op jit(solution)/shard_map/ppermute | solution.py:190
  14.6 0.0 copy-done
  14.6 0.0 copy-done.1
  14.6 0.0 copy-done.2
  14.6 0.0 copy-start.3
  14.6 0.0 copy-start.4
  14.6 0.9 %theirs.1 = (bf16[64,896]{1,0:T(8,128)(2,1)S(1)}, bf16[64,896]{1,0:T(8,128)(2,1)S(1)}) custom-call(bf16[64,896]{1,0:T(8,128)(2,1)S(1)} %bitcast.7, bf16[64,896]{1,0:T(8,128)(2,1)S(1)} %collective-permute-done.refs_1_, bf16[1,3584,128]{2,1,0:T(8,128)(2,1)S(1)} %copy-done, bf16[1,3584,128]{2,1,0:T(8,128)(2,1)S(1)} %copy-done.1, bf16[1,128,3584]{2,1,0:T(8,128)(2,1)S(1)} %copy-done.2), custom_call_target="tpu_custom_call" | custom-call | tf_op jit(solution)/shard_map/theirs/pallas_call | solution.py:191
  15.5 0.4 %collective-permute-start.1 = (bf16[64,896]{1,0:T(8,128)(2,1)S(1)}, bf16[64,896]{1,0:T(8,128)(2,1)S(1)}, u32[]{:S(2)}, u32[]{:S(2)}) collective-permute-start(bf16[64,896]{1,0:T(8,128)(2,1)S(1)} %get-tuple-element.12), channel_id=1, source_target_pairs={{0,1},{1,0},{2,3},{3,2},{4,5},{5,4},{6,7},{7,6},{8,9},{9,8},{10,11... | collective-permute-start | bytes 344072 | tf_op jit(solution)/shard_map/ppermute | solution.py:194
  15.9 0.0 copy-done.3
  15.9 0.0 copy-done.4
  15.9 0.2 score.1
  16.2 0.7 %collective-permute-done.1.other_ref = bf16[64,896]{1,0:T(8,128)(2,1)S(1)} collective-permute-done((bf16[64,896]{1,0:T(8,128)(2,1)S(1)}, bf16[64,896]{1,0:T(8,128)(2,1)S(1)}, u32[]{:S(2)}, u32[]{:S(2)}) %collective-permute-start.1) | collective-permute-done | bytes 114720 | tf_op jit(solution)/shard_map/ppermute | solution.py:194
  16.9 8.8 %all_to_all.23 = bf16[8,8,896]{2,1,0:T(8,128)(2,1)S(1)} all-to-all(bf16[8,8,896]{2,1,0:T(8,128)(2,1)S(1)} %bitcast.10), channel_id=1, replica_groups={{13,9,4,0,15,11,6,2},{12,8,5,1,14,10,7,3},{29,25,20,16,31,27,22,18},{28..., dimensions={0} | all-to-all | bytes 229376 | tf_op jit(solution)/shard_map/all_to_all | solution.py:172
  25.7 0.9 %combine.1 = bf16[128,896]{1,0:T(8,128)(2,1)} custom-call(bf16[128,64]{1,0:T(8,128)(2,1)S(1)} %get-tuple-element.9.match_ref, f32[128,1]{1,0:T(8,128)S(1)} %get-tuple-element.10._.weight_ref, bf16[64,896]{1,0:T(8,128)(2,1)S(1)} %bitcast.9), custom_call_target="tpu_custom_call" | custom-call | tf_op jit(solution)/shard_map/combine/pallas_call | solution.py:206
  (1 shorter events, 0.0 us)
Async XLA Ops:
  0.0 14.6 %copy-start = (bf16[1,3584,128]{2,1,0:T(8,128)(2,1)S(1)}, bf16[1,3584,128]{2,1,0:T(8,128)(2,1)}, u32[]{:S(2)}) copy-start(bf16[1,3584,128]{2,1,0:T(8,128)(2,1)} %refs_2_.1) | copy-start | bytes 2752516
  0.0 14.6 %copy-start.1 = (bf16[1,3584,128]{2,1,0:T(8,128)(2,1)S(1)}, bf16[1,3584,128]{2,1,0:T(8,128)(2,1)}, u32[]{:S(2)}) copy-start(bf16[1,3584,128]{2,1,0:T(8,128)(2,1)} %refs_3_.1) | copy-start | bytes 2752516
  0.0 14.6 %copy-start.2 = (bf16[1,128,3584]{2,1,0:T(8,128)(2,1)S(1)}, bf16[1,128,3584]{2,1,0:T(8,128)(2,1)}, u32[]{:S(2)}) copy-start(bf16[1,128,3584]{2,1,0:T(8,128)(2,1)} %refs_4_.1) | copy-start | bytes 2752516
  12.4 2.2 %collective-permute-start = (bf16[64,896]{1,0:T(8,128)(2,1)S(1)}, bf16[64,896]{1,0:T(8,128)(2,1)S(1)}, u32[]{:S(2)}, u32[]{:S(2)}) collective-permute-start(bf16[64,896]{1,0:T(8,128)(2,1)S(1)} %bitcast.6), channel_id=1, source_target_pairs={{0,1},{1,0},{2,3},{3,2},{4,5},{5,4},{6,7},{7,6},{8,9},{9,8},{10,11... | collective-permute-start | bytes 344072 | tf_op jit(solution)/shard_map/ppermute | solution.py:190
  14.6 1.3 %copy-start.3 = (s32[128,8]{0,1:T(8,128)S(1)}, s32[128,8]{0,1:T(8,128)}, u32[]{:S(2)}) copy-start(s32[128,8]{0,1:T(8,128)} %param.7) | copy-start | bytes 12292
  14.6 1.3 %copy-start.4 = (f32[128,8]{0,1:T(8,128)S(1)}, f32[128,8]{0,1:T(8,128)}, u32[]{:S(2)}) copy-start(f32[128,8]{0,1:T(8,128)} %param.8) | copy-start | bytes 12292
  15.5 1.4 %collective-permute-start.1 = (bf16[64,896]{1,0:T(8,128)(2,1)S(1)}, bf16[64,896]{1,0:T(8,128)(2,1)S(1)}, u32[]{:S(2)}, u32[]{:S(2)}) collective-permute-start(bf16[64,896]{1,0:T(8,128)(2,1)S(1)} %get-tuple-element.12), channel_id=1, source_target_pairs={{0,1},{1,0},{2,3},{3,2},{4,5},{5,4},{6,7},{7,6},{8,9},{9,8},{10,11... | collective-permute-start | bytes 344072 | tf_op jit(solution)/shard_map/ppermute | solution.py:194

commit v16 on v15

--- a/solution.py
+++ b/solution.py
@@ -41,7 +41,11 @@
     return list(reversed(range(ep_count)))
 
 
-def flip(chip, z):
+def first_flip(chip, z):
+    return chip & 1
+
+
+def second_flip(chip, z):
     return (z >> 1) & 1
 
 
@@ -85,41 +89,40 @@
     weight_ref[...] = to_column(2.5 * chosen / jnp.sum(squashed, axis=0, keepdims=True))
 
 
-def far_groups(order, chips):
+def far_groups(order, flip, chips):
     return [
         [(z * chips + x) * 2 + (side + flip(x, z)) % 2 for x in range(chips) for z in order]
         for side in range(2)
     ]
 
 
-def turned(chip, z):
-    side = lax.axis_index("core") ^ flip(lax.axis_index("chip"), lax.axis_index("ep"))
-    return (side ^ flip(chip, z)) == 1
-
-
-def theirs(chips, own_ref, across_ref, gate_ref, up_ref, down_ref, mine_ref, other_ref):
-    part_rows, features = own_ref.shape[0] // chips, own_ref.shape[1]
+def core_there(flip, chip, z):
+    here = flip(lax.axis_index("chip"), lax.axis_index("ep"))
+    return lax.axis_index("core") ^ here ^ flip(chip, z)
+
+
+def lift(chips, own, rows_ref, gate_ref, up_ref):
+    part_rows, features = rows_ref.shape[0] // chips, rows_ref.shape[1]
+    acts = jnp.zeros((part_rows, 2 * gate_ref.shape[2]), jnp.float32)
+    for chip in range(chips):
+        rows = rows_ref[chip * part_rows : (chip + 1) * part_rows, :]
+        core = core_there(first_flip, chip, 0)
+        core = core if own else 1 - core
+        columns = pl.ds(pl.multiple_of((2 * chip + core) * features, features), features)
+        both = jnp.concatenate([gate_ref[0, columns, :], up_ref[0, columns, :]], axis=1)
+        acts += jnp.dot(rows, both, preferred_element_type=jnp.float32)
+    return acts
+
+
+def begin(chips, rows_ref, gate_ref, up_ref, acts_ref):
+    acts_ref[...] = lift(chips, True, rows_ref, gate_ref, up_ref)
+
+
+def theirs(chips, rows_ref, acts_ref, gate_ref, up_ref, down_ref, mine_ref, other_ref):
+    part_rows, features = mine_ref.shape[0] // chips, mine_ref.shape[1]
     first, second = first_order(part_rows // CAP), second_order(part_rows // CAP)
     width = gate_ref.shape[2]
-    acts = jnp.zeros((part_rows, 2 * width), jnp.float32)
-    for chip in range(chips):
-        sides = [[], []]
-        at = 0
-        while at < len(first):
-            end = at + 1
-            while end < len(first) and flip(chip, first[end]) == flip(chip, first[at]):
-                end += 1
-            rows = slice(chip * part_rows + at * CAP, chip * part_rows + end * CAP)
-            own, across = own_ref[rows, :], across_ref[rows, :]
-            second_core = turned(chip, first[at])
-            sides[0].append(jnp.where(second_core, across, own))
-            sides[1].append(jnp.where(second_core, own, across))
-            at = end
-        for core in range(2):
-            columns = slice((2 * chip + core) * features, (2 * chip + core + 1) * features)
-            both = jnp.concatenate([gate_ref[0, columns, :], up_ref[0, columns, :]], axis=1)
-            rows = jnp.concatenate(sides[core], axis=0)
-            acts += jnp.dot(rows, both, preferred_element_type=jnp.float32)
+    acts = acts_ref[...] + lift(chips, False, rows_ref, gate_ref, up_ref)
     gate_act, up_act = acts[:, :width], acts[:, width:]
     hidden = (gate_act / (1.0 + jnp.exp(-gate_act)) * up_act).astype(jnp.bfloat16)
     for chip in range(chips):
@@ -132,7 +135,7 @@
         mine, other = [], []
         for z in second:
             rows = slice(first.index(z) * CAP, (first.index(z) + 1) * CAP)
-            second_core = turned(chip, z)
+            second_core = core_there(second_flip, chip, z) == 1
             mine.append(jnp.where(second_core, values[1][rows, :], values[0][rows, :]))
             other.append(jnp.where(second_core, values[0][rows, :], values[1][rows, :]))
         rows = slice(chip * part_rows, (chip + 1) * part_rows)
@@ -159,7 +162,7 @@
 
 def shards(tokens, expert_ids, route_scores, w_gate, w_up, w_down):
     row_count, features = tokens.shape
-    top_count = expert_ids.shape[1]
+    top_count, hidden_count = expert_ids.shape[1], w_gate.shape[2]
     ep_count, chips = lax.axis_size("ep"), lax.axis_size("chip")
     slot_count = ep_count * CAP
     half = jax.ShapeDtypeStruct((chips * slot_count, features), jnp.bfloat16)
@@ -167,8 +170,8 @@
     hbm, vmem = (pl.BlockSpec(memory_space=space) for space in (pltpu.HBM, pltpu.VMEM))
     anywhere = pl.BlockSpec(memory_space=pl.ANY)
 
-    def exchange(rows, order):
-        groups = far_groups(order(ep_count), chips)
+    def exchange(rows, order, flip):
+        groups = far_groups(order(ep_count), flip, chips)
         return lax.all_to_all(rows, FAR, 0, 0, axis_index_groups=groups, tiled=True)
 
     def call(kernel, name, out_shape, **rest):
@@ -186,10 +189,12 @@
         ],
         cost_estimate=pl.CostEstimate(flops=2 * 10**9, bytes_accessed=0, transcendentals=0),
     )(*(pltpu.with_memory_space_constraint(value, pltpu.HBM) for value in (ids, tokens)))
-    incoming = exchange(outgoing, first_order)
+    incoming = exchange(outgoing, first_order, first_flip)
     across = lax.ppermute(incoming, "core", SWAP)
+    acts = jax.ShapeDtypeStruct((slot_count, 2 * hidden_count), jnp.float32)
+    begun = call(lambda *refs: begin(chips, *refs), "begin", acts)(incoming, w_gate, w_up)
     mine, other = call(lambda *refs: theirs(chips, *refs), "theirs", (half, half))(
-        incoming, across, w_gate, w_up, w_down
+        across, begun, w_gate, w_up, w_down
     )
     crossed = lax.ppermute(other, "core", SWAP)
     match, weight = call(
@@ -200,9 +205,9 @@
             jax.ShapeDtypeStruct((row_count, 1), jnp.float32),
         ),
         in_specs=[vmem] * 2 + [anywhere],
-    )(ids, scores, incoming)
+    )(ids, scores, other)
     summed = call(add, "add", half, in_specs=[vmem] * 2 + [anywhere])(mine, crossed, weight)
-    returned = exchange(summed, second_order)
+    returned = exchange(summed, second_order, second_flip)
     return call(
         combine,
         "combine",

time: 26.8 us -> 26.9 us (level)
  blocking collectives: 19.9 us -> 21.1 us
  starting transfers between devices: 1.65 us -> 0.64 us
    all_to_all x2, blocking collectives: 19.9 us -> 21.1 us  [exchange(): return lax.all_to_all(rows, FAR, 0, 0, axis_index_groups=groups, tiled=True)]
    ppermute x1, starting transfers between devices: 1.21 us -> 0.29 us  [shards(): across = lax.ppermute(incoming, 'core', SWAP)]
  transfers between devices with their start and end apart: 2 -> 2, of which waited for: 2 -> 2; matrix products, arithmetic and copies ran while one was open for 0% -> 0% of each run, Pallas kernels for 1% -> 2%
where the time goes in v16:
time: 26.9 us; the launch traced here: 26.7 us
  blocking collectives  21.1 us (78%)
  Pallas kernels  3.39 us (13%)
  waiting for transfers between devices  1.55 us (6%)
  starting transfers between devices  0.64 us (2%)
    all_to_all x2, blocking collectives, exchange(): return lax.all_to_all(rows, FAR, 0, 0, axis_index_groups=groups, tiled=True)  21.1 us
    pallas_call x1, Pallas kernels, shards(): call(lambda *refs: route(ep_count, *refs), 'route', half, in_specs=[hbm]...  1.27 us
    pallas_call x1, Pallas kernels, shards(): call(combine, 'combine', jax.ShapeDtypeStruct((row_count, features), jnp....  0.87 us
    ppermute x1, waiting for transfers between devices, shards(): crossed = lax.ppermute(other, 'core', SWAP)  0.79 us
    ppermute x1, waiting for transfers between devices, shards(): across = lax.ppermute(incoming, 'core', SWAP)  0.76 us
    pallas_call x1, Pallas kernels, shards(): call(lambda *refs: theirs(chips, *refs), 'theirs', (half, half))  0.73 us
  transfers between devices with their start and end apart: 2, of which 2 were waited for; matrix products, arithmetic and copies ran while one was open for 0% of the time, Pallas kernels for 2%

profile of v16, /device:TPU:0, one launch (start us, length us, event | category | flops | bytes accessed | tf_op | source)
XLA Modules:
  0.0 26.7 jit_solution(12221045091051913030)
XLA Ops:
  0.0 0.0 copy-start
  0.0 0.0 copy-start.1
  0.0 1.3 %route.1 = bf16[64,896]{1,0:T(8,128)(2,1)S(1)} custom-call(s32[8,128]{1,0:T(8,128)} %bitcast.11, bf16[128,896]{1,0:T(8,128)(2,1)} %refs_1_.2), custom_call_target="tpu_custom_call" | custom-call | flops 2000000000 | tf_op jit(solution)/shard_map/route/pallas_call | solution.py:180
  1.3 11.8 %all_to_all.22 = bf16[8,8,896]{2,1,0:T(8,128)(2,1)S(1)} all-to-all(bf16[8,8,896]{2,1,0:T(8,128)(2,1)S(1)} %bitcast.10), channel_id=1, replica_groups={{8,12,0,4,11,15,3,7},{9,13,1,5,10,14,2,6},{24,28,16,20,27,31,19,23},{25..., dimensions={0} | all-to-all | bytes 229376 | tf_op jit(solution)/shard_map/all_to_all | solution.py:175
  13.1 0.0 copy-start.2
  13.1 0.3 %collective-permute-start = (bf16[64,896]{1,0:T(8,128)(2,1)S(1)}, bf16[64,896]{1,0:T(8,128)(2,1)S(1)}, u32[]{:S(2)}, u32[]{:S(2)}) collective-permute-start(bf16[64,896]{1,0:T(8,128)(2,1)S(1)} %bitcast.8), channel_id=1, source_target_pairs={{0,1},{1,0},{2,3},{3,2},{4,5},{5,4},{6,7},{7,6},{8,9},{9,8},{10,11... | collective-permute-start | bytes 344072 | tf_op jit(solution)/shard_map/ppermute | solution.py:193
  13.4 0.0 copy-done
  13.4 0.0 copy-done.1
  13.4 0.2 begin.1.refs_1_
  13.7 0.8 %collective-permute-done.refs_0_ = bf16[64,896]{1,0:T(8,128)(2,1)S(1)} collective-permute-done((bf16[64,896]{1,0:T(8,128)(2,1)S(1)}, bf16[64,896]{1,0:T(8,128)(2,1)S(1)}, u32[]{:S(2)}, u32[]{:S(2)}) %collective-permute-start) | collective-permute-done | bytes 114720 | tf_op jit(solution)/shard_map/ppermute | solution.py:193
  14.4 0.0 copy-done.2
  14.4 0.0 copy-start.3
  14.4 0.0 copy-start.4
  14.4 0.7 %theirs.1 = (bf16[64,896]{1,0:T(8,128)(2,1)S(1)}, bf16[64,896]{1,0:T(8,128)(2,1)S(1)}) custom-call(bf16[64,896]{1,0:T(8,128)(2,1)S(1)} %collective-permute-done.refs_0_, f32[32,256]{1,0:T(8,128)S(1)} %begin.1.refs_1_, bf16[1,3584,128]{2,1,0:T(8,128)(2,1)S(1)} %copy-done, bf16[1,3584,128]{2,1,0:T(8,128)(2,1)S(1)} %copy-done.1, bf16[1,128,3584]{2,1,0:T(8,128)(2,1)S(1)} %copy-done.2), custom_call_target="tpu_custom_call" | custom-call | tf_op jit(solution)/shard_map/theirs/pallas_call | solution.py:196
  15.2 0.4 %collective-permute-start.1 = (bf16[64,896]{1,0:T(8,128)(2,1)S(1)}, bf16[64,896]{1,0:T(8,128)(2,1)S(1)}, u32[]{:S(2)}, u32[]{:S(2)}) collective-permute-start(bf16[64,896]{1,0:T(8,128)(2,1)S(1)} %get-tuple-element.9.refs_2_), channel_id=1, source_target_pairs={{0,1},{1,0},{2,3},{3,2},{4,5},{5,4},{6,7},{7,6},{8,9},{9,8},{10,11... | collective-permute-start | bytes 344072 | tf_op jit(solution)/shard_map/ppermute | solution.py:199
  15.5 0.0 copy-done.3
  15.5 0.0 copy-done.4
  15.5 0.2 score.1
  15.8 0.8 %collective-permute-done.1.other_ref = bf16[64,896]{1,0:T(8,128)(2,1)S(1)} collective-permute-done((bf16[64,896]{1,0:T(8,128)(2,1)S(1)}, bf16[64,896]{1,0:T(8,128)(2,1)S(1)}, u32[]{:S(2)}, u32[]{:S(2)}) %collective-permute-start.1) | collective-permute-done | bytes 114720 | tf_op jit(solution)/shard_map/ppermute | solution.py:199
  16.6 9.2 %all_to_all.23 = bf16[8,8,896]{2,1,0:T(8,128)(2,1)S(1)} all-to-all(bf16[8,8,896]{2,1,0:T(8,128)(2,1)S(1)} %bitcast.7), channel_id=1, replica_groups={{13,9,4,0,15,11,6,2},{12,8,5,1,14,10,7,3},{29,25,20,16,31,27,22,18},{28..., dimensions={0} | all-to-all | bytes 229376 | tf_op jit(solution)/shard_map/all_to_all | solution.py:175
  25.8 0.9 %combine.1 = bf16[128,896]{1,0:T(8,128)(2,1)} custom-call(bf16[128,64]{1,0:T(8,128)(2,1)S(1)} %get-tuple-element.10.match_ref, f32[128,1]{1,0:T(8,128)S(1)} %get-tuple-element.11._.weight_ref, bf16[64,896]{1,0:T(8,128)(2,1)S(1)} %bitcast.6), custom_call_target="tpu_custom_call" | custom-call | tf_op jit(solution)/shard_map/combine/pallas_call | solution.py:211
  (1 shorter events, 0.0 us)
Async XLA Ops:
  0.0 13.4 %copy-start = (bf16[1,3584,128]{2,1,0:T(8,128)(2,1)S(1)}, bf16[1,3584,128]{2,1,0:T(8,128)(2,1)}, u32[]{:S(2)}) copy-start(bf16[1,3584,128]{2,1,0:T(8,128)(2,1)} %refs_2_.3) | copy-start | bytes 2752516
  0.0 13.4 %copy-start.1 = (bf16[1,3584,128]{2,1,0:T(8,128)(2,1)S(1)}, bf16[1,3584,128]{2,1,0:T(8,128)(2,1)}, u32[]{:S(2)}) copy-start(bf16[1,3584,128]{2,1,0:T(8,128)(2,1)} %refs_3_.1) | copy-start | bytes 2752516
  13.1 1.3 %copy-start.2 = (bf16[1,128,3584]{2,1,0:T(8,128)(2,1)S(1)}, bf16[1,128,3584]{2,1,0:T(8,128)(2,1)}, u32[]{:S(2)}) copy-start(bf16[1,128,3584]{2,1,0:T(8,128)(2,1)} %refs_4_.1) | copy-start | bytes 2752516
  13.1 1.3 %collective-permute-start = (bf16[64,896]{1,0:T(8,128)(2,1)S(1)}, bf16[64,896]{1,0:T(8,128)(2,1)S(1)}, u32[]{:S(2)}, u32[]{:S(2)}) collective-permute-start(bf16[64,896]{1,0:T(8,128)(2,1)S(1)} %bitcast.8), channel_id=1, source_target_pairs={{0,1},{1,0},{2,3},{3,2},{4,5},{5,4},{6,7},{7,6},{8,9},{9,8},{10,11... | collective-permute-start | bytes 344072 | tf_op jit(solution)/shard_map/ppermute | solution.py:193
  14.4 1.1 %copy-start.3 = (s32[128,8]{0,1:T(8,128)S(1)}, s32[128,8]{0,1:T(8,128)}, u32[]{:S(2)}) copy-start(s32[128,8]{0,1:T(8,128)} %param.7) | copy-start | bytes 12292
  14.4 1.1 %copy-start.4 = (f32[128,8]{0,1:T(8,128)S(1)}, f32[128,8]{0,1:T(8,128)}, u32[]{:S(2)}) copy-start(f32[128,8]{0,1:T(8,128)} %param.8) | copy-start | bytes 12292
  15.2 1.4 %collective-permute-start.1 = (bf16[64,896]{1,0:T(8,128)(2,1)S(1)}, bf16[64,896]{1,0:T(8,128)(2,1)S(1)}, u32[]{:S(2)}, u32[]{:S(2)}) collective-permute-start(bf16[64,896]{1,0:T(8,128)(2,1)S(1)} %get-tuple-element.9.refs_2_), channel_id=1, source_target_pairs={{0,1},{1,0},{2,3},{3,2},{4,5},{5,4},{6,7},{7,6},{8,9},{9,8},{10,11... | collective-permute-start | bytes 344072 | tf_op jit(solution)/shard_map/ppermute | solution.py:199

commit v17 on v13

--- a/solution.py
+++ b/solution.py
@@ -33,21 +33,21 @@
     return expert * CAP + jnp.sum(counts * onehot, axis=0, keepdims=True), expert
 
 
-def first_order(ep_count):
-    return [z ^ 2 for z in range(ep_count)]
-
-
-def second_order(ep_count):
+def first_order(ep_count, chip):
+    return [z ^ 2 for z in range(ep_count)] if chip % 2 == 0 else list(reversed(range(ep_count)))
+
+
+def second_order(ep_count, chip):
     return list(reversed(range(ep_count)))
 
 
-def row_codes(index, order):
-    listed = lax.rem(index // CAP, len(order))
-    expert = sum(jnp.where(listed == at, z // 2, 0) for at, z in enumerate(order))
+def row_codes(index, order, ep_count, chips):
+    listed = [z for chip in range(chips) for z in order(ep_count, chip)]
+    expert = sum(jnp.where(index // CAP == at, z // 2, 0) for at, z in enumerate(listed))
     return (expert * CAP + lax.rem(index, CAP)).astype(jnp.float32)
 
 
-def route(ep_count, ids_hbm, tokens_hbm, outgoing_ref, ids_ref, tokens_ref, sems):
+def route(ep_count, chips, ids_hbm, tokens_hbm, outgoing_ref, ids_ref, tokens_ref, sems):
     row_count = ids_ref.shape[1]
     parts = row_count // PIECE
     copies = [pltpu.make_async_copy(ids_hbm, ids_ref, sems.at[parts])] + [
@@ -60,7 +60,7 @@
     ]
     for copy in copies:
         copy.start()
-    wanted = row_codes(iota((outgoing_ref.shape[0], row_count), 0), first_order(ep_count))
+    wanted = row_codes(iota((outgoing_ref.shape[0], row_count), 0), first_order, ep_count, chips)
     copies[0].wait()
     code, _ = slot_codes(ids_ref[...].astype(jnp.float32), ep_count // 2)
     dispatch = jnp.where(code == wanted, 1.0, 0.0).astype(jnp.bfloat16)
@@ -71,19 +71,19 @@
     ).astype(jnp.bfloat16)
 
 
-def score(ep_count, ids_ref, scores_ref, _, match_ref, weight_ref):
+def score(ep_count, chips, ids_ref, scores_ref, _, match_ref, weight_ref):
     ids = ids_ref[...].astype(jnp.float32)
     code, expert = slot_codes(ids, ep_count // 2)
-    wanted = row_codes(iota(match_ref.shape, 1), second_order(ep_count))
+    wanted = row_codes(iota(match_ref.shape, 1), second_order, ep_count, chips)
     match_ref[...] = jnp.where(to_column(code) == wanted, 1.0, 0.0).astype(jnp.bfloat16)
     squashed = jax.nn.sigmoid(scores_ref[...])
     chosen = jnp.sum(jnp.where(ids == expert, squashed, 0.0), axis=0, keepdims=True)
     weight_ref[...] = to_column(2.5 * chosen / jnp.sum(squashed, axis=0, keepdims=True))
 
 
-def far_groups(order, chips):
+def far_groups(order, ep_count, chips):
     return [
-        [(z * chips + x) * 2 + (side + x) % 2 for x in range(chips) for z in order]
+        [(z * chips + x) * 2 + (side + x) % 2 for x in range(chips) for z in order(ep_count, x)]
         for side in range(2)
     ]
 
@@ -93,40 +93,44 @@
     return pl.ds(pl.multiple_of((2 * chip + core) * features, features), features)
 
 
+def in_order(values, held, wanted):
+    if held == wanted:
+        return values
+    blocks = [values[held.index(z) * CAP : (held.index(z) + 1) * CAP, :] for z in wanted]
+    return jnp.concatenate(blocks, axis=0)
+
+
 def lift(chips, own, rows_ref, gate_ref, up_ref):
     part_rows, features = rows_ref.shape[0] // chips, rows_ref.shape[1]
-    gate_act = jnp.zeros((part_rows, gate_ref.shape[2]), jnp.float32)
-    up_act = jnp.zeros((part_rows, up_ref.shape[2]), jnp.float32)
+    ep_count = part_rows // CAP
+    total = jnp.zeros((part_rows, 2 * gate_ref.shape[2]), jnp.float32)
     for chip in range(chips):
         rows = rows_ref[chip * part_rows : (chip + 1) * part_rows, :]
         columns = columns_of(chip, own, features)
-        gate_act += jnp.dot(rows, gate_ref[0, columns, :], preferred_element_type=jnp.float32)
-        up_act += jnp.dot(rows, up_ref[0, columns, :], preferred_element_type=jnp.float32)
-    return gate_act, up_act
+        both = jnp.concatenate([gate_ref[0, columns, :], up_ref[0, columns, :]], axis=1)
+        acts = jnp.dot(rows, both, preferred_element_type=jnp.float32)
+        total += in_order(acts, first_order(ep_count, chip), first_order(ep_count, 0))
+    return total
 
 
 def lower(chips, own, hidden, down_ref, out_ref):
     part_rows, features = out_ref.shape[0] // chips, out_ref.shape[1]
-    first = first_order(part_rows // CAP)
-    moves = [first.index(z) for z in second_order(part_rows // CAP)]
+    ep_count = part_rows // CAP
     for chip in range(chips):
         columns = columns_of(chip, own, features)
         values = jnp.dot(hidden, down_ref[0, :, columns], preferred_element_type=jnp.float32)
-        blocks = [values[at * CAP : (at + 1) * CAP, :] for at in moves]
-        out_ref[chip * part_rows : (chip + 1) * part_rows, :] = jnp.concatenate(
-            blocks, axis=0
-        ).astype(jnp.bfloat16)
-
-
-def begin(chips, rows_ref, gate_ref, up_ref, gate_act_ref, up_act_ref):
-    gate_act_ref[...], up_act_ref[...] = lift(chips, True, rows_ref, gate_ref, up_ref)
-
-
-def theirs(chips, *refs):
-    rows_ref, gate_act_ref, up_act_ref, gate_ref, up_ref, down_ref, hidden_ref, other_ref = refs
-    gate_act, up_act = lift(chips, False, rows_ref, gate_ref, up_ref)
-    gate_act += gate_act_ref[...]
-    up_act += up_act_ref[...]
+        values = in_order(values, first_order(ep_count, 0), second_order(ep_count, chip))
+        out_ref[chip * part_rows : (chip + 1) * part_rows, :] = values.astype(jnp.bfloat16)
+
+
+def begin(chips, rows_ref, gate_ref, up_ref, acts_ref):
+    acts_ref[...] = lift(chips, True, rows_ref, gate_ref, up_ref)
+
+
+def theirs(chips, rows_ref, acts_ref, gate_ref, up_ref, down_ref, hidden_ref, other_ref):
+    width = gate_ref.shape[2]
+    acts = acts_ref[...] + lift(chips, False, rows_ref, gate_ref, up_ref)
+    gate_act, up_act = acts[:, :width], acts[:, width:]
     hidden = (gate_act / (1.0 + jnp.exp(-gate_act)) * up_act).astype(jnp.bfloat16)
     hidden_ref[...] = hidden
     lower(chips, False, hidden, down_ref, other_ref)
@@ -164,14 +168,14 @@
     anywhere = pl.BlockSpec(memory_space=pl.ANY)
 
     def exchange(rows, order):
-        groups = far_groups(order(ep_count), chips)
+        groups = far_groups(order, ep_count, chips)
         return lax.all_to_all(rows, FAR, 0, 0, axis_index_groups=groups, tiled=True)
 
     def call(kernel, name, out_shape, **rest):
         return pl.pallas_call(kernel, out_shape=out_shape, name=name, compiler_params=LIMIT, **rest)
 
     outgoing = call(
-        lambda *refs: route(ep_count, *refs),
+        lambda *refs: route(ep_count, chips, *refs),
         "route",
         half,
         in_specs=[hbm] * 2,
@@ -184,16 +188,16 @@
     )(*(pltpu.with_memory_space_constraint(value, pltpu.HBM) for value in (ids, tokens)))
     incoming = exchange(outgoing, first_order)
     across = lax.ppermute(incoming, "core", SWAP)
-    acts = (jax.ShapeDtypeStruct((slot_count, hidden_count), jnp.float32),) * 2
+    acts = jax.ShapeDtypeStruct((slot_count, 2 * hidden_count), jnp.float32)
     begun = call(lambda *refs: begin(chips, *refs), "begin", acts)(incoming, w_gate, w_up)
     hidden_shape = jax.ShapeDtypeStruct((slot_count, hidden_count), jnp.bfloat16)
     hidden, other = call(lambda *refs: theirs(chips, *refs), "theirs", (hidden_shape, half))(
-        across, *begun, w_gate, w_up, w_down
+        across, begun, w_gate, w_up, w_down
     )
     crossed = lax.ppermute(other, "core", SWAP)
     mine = call(lambda *refs: ours(chips, *refs), "ours", half)(hidden, w_down)
     match, weight = call(
-        lambda *refs: score(ep_count, *refs),
+        lambda *refs: score(ep_count, chips, *refs),
         "score",
         (
             jax.ShapeDtypeStruct((row_count, chips * slot_count), jnp.bfloat16),

time: 26.6 us -> 26.3 us (0.989)
  blocking collectives: 21 us -> 20.6 us
    all_to_all x2, blocking collectives: 21 us -> 20.6 us  [exchange(): return lax.all_to_all(rows, FAR, 0, 0, axis_index_groups=groups, tiled=True)]
where the time goes in v17:
time: 26.3 us; the launch traced here: 26.1 us
  blocking collectives  20.6 us (78%)
  Pallas kernels  3.34 us (13%)
  waiting for transfers between devices  1.19 us (5%)
  starting transfers between devices  0.83 us (3%)
    all_to_all x2, blocking collectives, exchange(): return lax.all_to_all(rows, FAR, 0, 0, axis_index_groups=groups, tiled=True)  20.6 us
    pallas_call x1, Pallas kernels, shards(): call(lambda *refs: route(ep_count, chips, *refs), 'route', half, in_specs...  1.27 us
    pallas_call x1, Pallas kernels, shards(): call(combine, 'combine', jax.ShapeDtypeStruct((row_count, features), jnp....  0.87 us
    ppermute x1, waiting for transfers between devices, shards(): across = lax.ppermute(incoming, 'core', SWAP)  0.68 us
  transfers between devices with their start and end apart: 2, of which 2 were waited for; matrix products, arithmetic and copies ran while one was open for 0% of the time, Pallas kernels for 3%

profile of v17, /device:TPU:0, one launch (start us, length us, event | category | flops | bytes accessed | tf_op | source)
XLA Modules:
  0.0 26.1 jit_solution(14845268748524810996)
XLA Ops:
  0.0 0.0 copy-start
  0.0 0.0 copy-start.1
  0.0 1.3 %route.1 = bf16[64,896]{1,0:T(8,128)(2,1)S(1)} custom-call(s32[8,128]{1,0:T(8,128)} %bitcast.11, bf16[128,896]{1,0:T(8,128)(2,1)} %refs_1_.3), custom_call_target="tpu_custom_call" | custom-call | flops 2000000000 | tf_op jit(solution)/shard_map/route/pallas_call | solution.py:177
  1.3 11.7 %all_to_all.22 = bf16[8,8,896]{2,1,0:T(8,128)(2,1)S(1)} all-to-all(bf16[8,8,896]{2,1,0:T(8,128)(2,1)S(1)} %bitcast.10), channel_id=1, replica_groups={{8,12,0,4,15,11,7,3},{9,13,1,5,14,10,6,2},{24,28,16,20,31,27,23,19},{25..., dimensions={0} | all-to-all | bytes 229376 | tf_op jit(solution)/shard_map/all_to_all | solution.py:172
  12.9 0.0 copy-start.2
  12.9 0.4 %collective-permute-start = (bf16[64,896]{1,0:T(8,128)(2,1)S(1)}, bf16[64,896]{1,0:T(8,128)(2,1)S(1)}, u32[]{:S(2)}, u32[]{:S(2)}) collective-permute-start(bf16[64,896]{1,0:T(8,128)(2,1)S(1)} %bitcast.8), channel_id=1, source_target_pairs={{0,1},{1,0},{2,3},{3,2},{4,5},{5,4},{6,7},{7,6},{8,9},{9,8},{10,11... | collective-permute-start | bytes 344072 | tf_op jit(solution)/shard_map/ppermute | solution.py:190
  13.3 0.0 copy-done
  13.3 0.0 copy-done.1
  13.3 0.3 %begin.1.refs_1_ = f32[32,256]{1,0:T(8,128)S(1)} custom-call(bf16[64,896]{1,0:T(8,128)(2,1)S(1)} %bitcast.9, bf16[1,3584,128]{2,1,0:T(8,128)(2,1)S(1)} %copy-done, bf16[1,3584,128]{2,1,0:T(8,128)(2,1)S(1)} %copy-done.1), custom_call_target="tpu_custom_call" | custom-call | tf_op jit(solution)/shard_map/begin/pallas_call | solution.py:192
  13.6 0.7 %collective-permute-done.refs_0_ = bf16[64,896]{1,0:T(8,128)(2,1)S(1)} collective-permute-done((bf16[64,896]{1,0:T(8,128)(2,1)S(1)}, bf16[64,896]{1,0:T(8,128)(2,1)S(1)}, u32[]{:S(2)}, u32[]{:S(2)}) %collective-permute-start) | collective-permute-done | bytes 114720 | tf_op jit(solution)/shard_map/ppermute | solution.py:190
  14.3 0.0 copy-done.2
  14.3 0.0 copy-start.3
  14.3 0.0 copy-start.4
  14.3 0.5 %theirs.1 = (bf16[32,128]{1,0:T(8,128)(2,1)S(1)}, bf16[64,896]{1,0:T(8,128)(2,1)S(1)}) custom-call(bf16[64,896]{1,0:T(8,128)(2,1)S(1)} %collective-permute-done.refs_0_, f32[32,256]{1,0:T(8,128)S(1)} %begin.1.refs_1_, bf16[1,3584,128]{2,1,0:T(8,128)(2,1)S(1)} %copy-done, bf16[1,3584,128]{2,1,0:T(8,128)(2,1)S(1)} %copy-done.1, bf16[1,128,3584]{2,1,0:T(8,128)(2,1)S(1)} %copy-done.2), custom_call_target="tpu_custom_call" | custom-call | tf_op jit(solution)/shard_map/theirs/pallas_call | solution.py:194
  14.8 0.4 %collective-permute-start.1 = (bf16[64,896]{1,0:T(8,128)(2,1)S(1)}, bf16[64,896]{1,0:T(8,128)(2,1)S(1)}, u32[]{:S(2)}, u32[]{:S(2)}) collective-permute-start(bf16[64,896]{1,0:T(8,128)(2,1)S(1)} %get-tuple-element.9.refs_2_), channel_id=1, source_target_pairs={{0,1},{1,0},{2,3},{3,2},{4,5},{5,4},{6,7},{7,6},{8,9},{9,8},{10,11... | collective-permute-start | bytes 344072 | tf_op jit(solution)/shard_map/ppermute | solution.py:197
  15.2 0.0 copy-done.3
  15.2 0.0 copy-done.4
  15.2 0.2 score.1
  15.5 0.2 ours.1.mine_ref
  15.7 0.5 %collective-permute-done.1.other_ref = bf16[64,896]{1,0:T(8,128)(2,1)S(1)} collective-permute-done((bf16[64,896]{1,0:T(8,128)(2,1)S(1)}, bf16[64,896]{1,0:T(8,128)(2,1)S(1)}, u32[]{:S(2)}, u32[]{:S(2)}) %collective-permute-start.1) | collective-permute-done | bytes 114720 | tf_op jit(solution)/shard_map/ppermute | solution.py:197
  16.2 9.0 %all_to_all.23 = bf16[8,8,896]{2,1,0:T(8,128)(2,1)S(1)} all-to-all(bf16[8,8,896]{2,1,0:T(8,128)(2,1)S(1)} %bitcast.7), channel_id=1, replica_groups={{12,8,4,0,15,11,7,3},{13,9,5,1,14,10,6,2},{28,24,20,16,31,27,23,19},{29..., dimensions={0} | all-to-all | bytes 229376 | tf_op jit(solution)/shard_map/all_to_all | solution.py:172
  25.2 0.9 %combine.1 = bf16[128,896]{1,0:T(8,128)(2,1)} custom-call(bf16[128,64]{1,0:T(8,128)(2,1)S(1)} %get-tuple-element.10.match_ref, f32[128,1]{1,0:T(8,128)S(1)} %get-tuple-element.11._.weight_ref, bf16[64,896]{1,0:T(8,128)(2,1)S(1)} %bitcast.6), custom_call_target="tpu_custom_call" | custom-call | tf_op jit(solution)/shard_map/combine/pallas_call | solution.py:210
  (1 shorter events, 0.0 us)
Async XLA Ops:
  0.0 13.3 %copy-start = (bf16[1,3584,128]{2,1,0:T(8,128)(2,1)S(1)}, bf16[1,3584,128]{2,1,0:T(8,128)(2,1)}, u32[]{:S(2)}) copy-start(bf16[1,3584,128]{2,1,0:T(8,128)(2,1)} %refs_2_.3) | copy-start | bytes 2752516
  0.0 13.3 %copy-start.1 = (bf16[1,3584,128]{2,1,0:T(8,128)(2,1)S(1)}, bf16[1,3584,128]{2,1,0:T(8,128)(2,1)}, u32[]{:S(2)}) copy-start(bf16[1,3584,128]{2,1,0:T(8,128)(2,1)} %refs_3_.1) | copy-start | bytes 2752516
  12.9 1.4 %copy-start.2 = (bf16[1,128,3584]{2,1,0:T(8,128)(2,1)S(1)}, bf16[1,128,3584]{2,1,0:T(8,128)(2,1)}, u32[]{:S(2)}) copy-start(bf16[1,128,3584]{2,1,0:T(8,128)(2,1)} %refs_1_.5) | copy-start | bytes 2752516
  12.9 1.4 %collective-permute-start = (bf16[64,896]{1,0:T(8,128)(2,1)S(1)}, bf16[64,896]{1,0:T(8,128)(2,1)S(1)}, u32[]{:S(2)}, u32[]{:S(2)}) collective-permute-start(bf16[64,896]{1,0:T(8,128)(2,1)S(1)} %bitcast.8), channel_id=1, source_target_pairs={{0,1},{1,0},{2,3},{3,2},{4,5},{5,4},{6,7},{7,6},{8,9},{9,8},{10,11... | collective-permute-start | bytes 344072 | tf_op jit(solution)/shard_map/ppermute | solution.py:190
  14.3 0.9 %copy-start.3 = (s32[128,8]{0,1:T(8,128)S(1)}, s32[128,8]{0,1:T(8,128)}, u32[]{:S(2)}) copy-start(s32[128,8]{0,1:T(8,128)} %param.7) | copy-start | bytes 12292
  14.3 0.9 %copy-start.4 = (f32[128,8]{0,1:T(8,128)S(1)}, f32[128,8]{0,1:T(8,128)}, u32[]{:S(2)}) copy-start(f32[128,8]{0,1:T(8,128)} %param.8) | copy-start | bytes 12292
  14.8 1.4 %collective-permute-start.1 = (bf16[64,896]{1,0:T(8,128)(2,1)S(1)}, bf16[64,896]{1,0:T(8,128)(2,1)S(1)}, u32[]{:S(2)}, u32[]{:S(2)}) collective-permute-start(bf16[64,896]{1,0:T(8,128)(2,1)S(1)} %get-tuple-element.9.refs_2_), channel_id=1, source_target_pairs={{0,1},{1,0},{2,3},{3,2},{4,5},{5,4},{6,7},{7,6},{8,9},{9,8},{10,11... | collective-permute-start | bytes 344072 | tf_op jit(solution)/shard_map/ppermute | solution.py:197

commit v18 on v17

--- a/solution.py
+++ b/solution.py
@@ -34,11 +34,13 @@
 
 
 def first_order(ep_count, chip):
-    return [z ^ 2 for z in range(ep_count)] if chip % 2 == 0 else list(reversed(range(ep_count)))
+    listed = ((1, 0, 2, 3), (3, 1, 2, 0))[chip % 2]
+    return [z // 4 * 4 + listed[z % 4] for z in range(ep_count)]
 
 
 def second_order(ep_count, chip):
-    return list(reversed(range(ep_count)))
+    listed = ((2, 1, 0, 3), (3, 0, 2, 1))[chip % 2]
+    return [z // 4 * 4 + listed[z % 4] for z in range(ep_count)]
 
 
 def row_codes(index, order, ep_count, chips):

time: 26.3 us -> 26.8 us (1.019)
  starting transfers between devices: 0.83 us -> 1.17 us
    ppermute x1, starting transfers between devices: 0.4 us -> 0.74 us  [shards(): across = lax.ppermute(incoming, 'core', SWAP)]
where the time goes in v18:
time: 26.8 us; the launch traced here: 26.4 us
  blocking collectives  20.6 us (77%)
  Pallas kernels  3.35 us (12%)
  waiting for transfers between devices  1.18 us (4%)
  starting transfers between devices  1.17 us (4%)
    all_to_all x2, blocking collectives, exchange(): return lax.all_to_all(rows, FAR, 0, 0, axis_index_groups=groups, tiled=True)  20.6 us
    pallas_call x1, Pallas kernels, shards(): call(lambda *refs: route(ep_count, chips, *refs), 'route', half, in_specs...  1.27 us
    pallas_call x1, Pallas kernels, shards(): call(combine, 'combine', jax.ShapeDtypeStruct((row_count, features), jnp....  0.87 us
    ppermute x1, starting transfers between devices, shards(): across = lax.ppermute(incoming, 'core', SWAP)  0.74 us
    ppermute x1, waiting for transfers between devices, shards(): across = lax.ppermute(incoming, 'core', SWAP)  0.68 us
  transfers between devices with their start and end apart: 2, of which 2 were waited for; matrix products, arithmetic and copies ran while one was open for 0% of the time, Pallas kernels for 3%

profile of v18, /device:TPU:0, one launch (start us, length us, event | category | flops | bytes accessed | tf_op | source)
XLA Modules:
  0.0 26.4 jit_solution(2378229421995295311)
XLA Ops:
  0.0 0.0 copy-start
  0.0 0.0 copy-start.1
  0.0 1.3 %route.1 = bf16[64,896]{1,0:T(8,128)(2,1)S(1)} custom-call(s32[8,128]{1,0:T(8,128)} %bitcast.11, bf16[128,896]{1,0:T(8,128)(2,1)} %refs_1_.3), custom_call_target="tpu_custom_call" | custom-call | flops 2000000000 | tf_op jit(solution)/shard_map/route/pallas_call | solution.py:179
  1.3 12.1 %all_to_all.22 = bf16[8,8,896]{2,1,0:T(8,128)(2,1)S(1)} all-to-all(bf16[8,8,896]{2,1,0:T(8,128)(2,1)S(1)} %bitcast.10), channel_id=1, replica_groups={{4,0,8,12,15,7,11,3},{5,1,9,13,14,6,10,2},{20,16,24,28,31,23,27,19},{21..., dimensions={0} | all-to-all | bytes 229376 | tf_op jit(solution)/shard_map/all_to_all | solution.py:174
  13.4 0.0 copy-start.2
  13.4 0.7 %collective-permute-start = (bf16[64,896]{1,0:T(8,128)(2,1)S(1)}, bf16[64,896]{1,0:T(8,128)(2,1)S(1)}, u32[]{:S(2)}, u32[]{:S(2)}) collective-permute-start(bf16[64,896]{1,0:T(8,128)(2,1)S(1)} %bitcast.8), channel_id=1, source_target_pairs={{0,1},{1,0},{2,3},{3,2},{4,5},{5,4},{6,7},{7,6},{8,9},{9,8},{10,11... | collective-permute-start | bytes 344072 | tf_op jit(solution)/shard_map/ppermute | solution.py:192
  14.1 0.0 copy-done
  14.1 0.0 copy-done.1
  14.1 0.3 %begin.1.refs_1_ = f32[32,256]{1,0:T(8,128)S(1)} custom-call(bf16[64,896]{1,0:T(8,128)(2,1)S(1)} %bitcast.9, bf16[1,3584,128]{2,1,0:T(8,128)(2,1)S(1)} %copy-done, bf16[1,3584,128]{2,1,0:T(8,128)(2,1)S(1)} %copy-done.1), custom_call_target="tpu_custom_call" | custom-call | tf_op jit(solution)/shard_map/begin/pallas_call | solution.py:194
  14.4 0.7 %collective-permute-done.refs_0_ = bf16[64,896]{1,0:T(8,128)(2,1)S(1)} collective-permute-done((bf16[64,896]{1,0:T(8,128)(2,1)S(1)}, bf16[64,896]{1,0:T(8,128)(2,1)S(1)}, u32[]{:S(2)}, u32[]{:S(2)}) %collective-permute-start) | collective-permute-done | bytes 114720 | tf_op jit(solution)/shard_map/ppermute | solution.py:192
  15.1 0.0 copy-done.2
  15.1 0.0 copy-start.3
  15.1 0.0 copy-start.4
  15.1 0.5 %theirs.1 = (bf16[32,128]{1,0:T(8,128)(2,1)S(1)}, bf16[64,896]{1,0:T(8,128)(2,1)S(1)}) custom-call(bf16[64,896]{1,0:T(8,128)(2,1)S(1)} %collective-permute-done.refs_0_, f32[32,256]{1,0:T(8,128)S(1)} %begin.1.refs_1_, bf16[1,3584,128]{2,1,0:T(8,128)(2,1)S(1)} %copy-done, bf16[1,3584,128]{2,1,0:T(8,128)(2,1)S(1)} %copy-done.1, bf16[1,128,3584]{2,1,0:T(8,128)(2,1)S(1)} %copy-done.2), custom_call_target="tpu_custom_call" | custom-call | tf_op jit(solution)/shard_map/theirs/pallas_call | solution.py:196
  15.6 0.4 %collective-permute-start.1 = (bf16[64,896]{1,0:T(8,128)(2,1)S(1)}, bf16[64,896]{1,0:T(8,128)(2,1)S(1)}, u32[]{:S(2)}, u32[]{:S(2)}) collective-permute-start(bf16[64,896]{1,0:T(8,128)(2,1)S(1)} %get-tuple-element.9.refs_2_), channel_id=1, source_target_pairs={{0,1},{1,0},{2,3},{3,2},{4,5},{5,4},{6,7},{7,6},{8,9},{9,8},{10,11... | collective-permute-start | bytes 344072 | tf_op jit(solution)/shard_map/ppermute | solution.py:199
  16.0 0.0 copy-done.3
  16.0 0.0 copy-done.4
  16.0 0.2 score.1
  16.3 0.2 ours.1.mine_ref
  16.5 0.5 %collective-permute-done.1.other_ref = bf16[64,896]{1,0:T(8,128)(2,1)S(1)} collective-permute-done((bf16[64,896]{1,0:T(8,128)(2,1)S(1)}, bf16[64,896]{1,0:T(8,128)(2,1)S(1)}, u32[]{:S(2)}, u32[]{:S(2)}) %collective-permute-start.1) | collective-permute-done | bytes 114720 | tf_op jit(solution)/shard_map/ppermute | solution.py:199
  17.0 8.5 %all_to_all.23 = bf16[8,8,896]{2,1,0:T(8,128)(2,1)S(1)} all-to-all(bf16[8,8,896]{2,1,0:T(8,128)(2,1)S(1)} %bitcast.7), channel_id=1, replica_groups={{8,4,0,12,15,3,11,7},{9,5,1,13,14,2,10,6},{24,20,16,28,31,19,27,23},{25..., dimensions={0} | all-to-all | bytes 229376 | tf_op jit(solution)/shard_map/all_to_all | solution.py:174
  25.5 0.9 %combine.1 = bf16[128,896]{1,0:T(8,128)(2,1)} custom-call(bf16[128,64]{1,0:T(8,128)(2,1)S(1)} %get-tuple-element.10.match_ref, f32[128,1]{1,0:T(8,128)S(1)} %get-tuple-element.11._.weight_ref, bf16[64,896]{1,0:T(8,128)(2,1)S(1)} %bitcast.6), custom_call_target="tpu_custom_call" | custom-call | tf_op jit(solution)/shard_map/combine/pallas_call | solution.py:212
  (1 shorter events, 0.0 us)
Async XLA Ops:
  0.0 14.1 %copy-start = (bf16[1,3584,128]{2,1,0:T(8,128)(2,1)S(1)}, bf16[1,3584,128]{2,1,0:T(8,128)(2,1)}, u32[]{:S(2)}) copy-start(bf16[1,3584,128]{2,1,0:T(8,128)(2,1)} %refs_2_.3) | copy-start | bytes 2752516
  0.0 14.1 %copy-start.1 = (bf16[1,3584,128]{2,1,0:T(8,128)(2,1)S(1)}, bf16[1,3584,128]{2,1,0:T(8,128)(2,1)}, u32[]{:S(2)}) copy-start(bf16[1,3584,128]{2,1,0:T(8,128)(2,1)} %refs_3_.1) | copy-start | bytes 2752516
  13.4 1.7 %copy-start.2 = (bf16[1,128,3584]{2,1,0:T(8,128)(2,1)S(1)}, bf16[1,128,3584]{2,1,0:T(8,128)(2,1)}, u32[]{:S(2)}) copy-start(bf16[1,128,3584]{2,1,0:T(8,128)(2,1)} %refs_1_.5) | copy-start | bytes 2752516
  13.4 1.7 %collective-permute-start = (bf16[64,896]{1,0:T(8,128)(2,1)S(1)}, bf16[64,896]{1,0:T(8,128)(2,1)S(1)}, u32[]{:S(2)}, u32[]{:S(2)}) collective-permute-start(bf16[64,896]{1,0:T(8,128)(2,1)S(1)} %bitcast.8), channel_id=1, source_target_pairs={{0,1},{1,0},{2,3},{3,2},{4,5},{5,4},{6,7},{7,6},{8,9},{9,8},{10,11... | collective-permute-start | bytes 344072 | tf_op jit(solution)/shard_map/ppermute | solution.py:192
  15.1 0.9 %copy-start.3 = (s32[128,8]{0,1:T(8,128)S(1)}, s32[128,8]{0,1:T(8,128)}, u32[]{:S(2)}) copy-start(s32[128,8]{0,1:T(8,128)} %param.7) | copy-start | bytes 12292
  15.1 0.9 %copy-start.4 = (f32[128,8]{0,1:T(8,128)S(1)}, f32[128,8]{0,1:T(8,128)}, u32[]{:S(2)}) copy-start(f32[128,8]{0,1:T(8,128)} %param.8) | copy-start | bytes 12292
  15.6 1.4 %collective-permute-start.1 = (bf16[64,896]{1,0:T(8,128)(2,1)S(1)}, bf16[64,896]{1,0:T(8,128)(2,1)S(1)}, u32[]{:S(2)}, u32[]{:S(2)}) collective-permute-start(bf16[64,896]{1,0:T(8,128)(2,1)S(1)} %get-tuple-element.9.refs_2_), channel_id=1, source_target_pairs={{0,1},{1,0},{2,3},{3,2},{4,5},{5,4},{6,7},{7,6},{8,9},{9,8},{10,11... | collective-permute-start | bytes 344072 | tf_op jit(solution)/shard_map/ppermute | solution.py:199

commit v19 on v18

--- a/solution.py
+++ b/solution.py
@@ -34,7 +34,7 @@
 
 
 def first_order(ep_count, chip):
-    listed = ((1, 0, 2, 3), (3, 1, 2, 0))[chip % 2]
+    listed = ((2, 3, 0, 1), (3, 2, 1, 0))[chip % 2]
     return [z // 4 * 4 + listed[z % 4] for z in range(ep_count)]
 
 

time: 26.8 us -> 25.6 us (0.955)
  blocking collectives: 20.6 us -> 19.8 us
  starting transfers between devices: 1.17 us -> 0.83 us
    all_to_all x2, blocking collectives: 20.6 us -> 19.8 us  [exchange(): return lax.all_to_all(rows, FAR, 0, 0, axis_index_groups=groups, tiled=True)]
    ppermute x1, starting transfers between devices: 0.74 us -> 0.4 us  [shards(): across = lax.ppermute(incoming, 'core', SWAP)]
where the time goes in v19:
time: 25.6 us; the launch traced here: 25.2 us
  blocking collectives  19.8 us (77%)
  Pallas kernels  3.34 us (13%)
  waiting for transfers between devices  1.19 us (5%)
  starting transfers between devices  0.83 us (3%)
    all_to_all x2, blocking collectives, exchange(): return lax.all_to_all(rows, FAR, 0, 0, axis_index_groups=groups, tiled=True)  19.8 us
    pallas_call x1, Pallas kernels, shards(): call(lambda *refs: route(ep_count, chips, *refs), 'route', half, in_specs...  1.27 us
    pallas_call x1, Pallas kernels, shards(): call(combine, 'combine', jax.ShapeDtypeStruct((row_count, features), jnp....  0.87 us
    ppermute x1, waiting for transfers between devices, shards(): across = lax.ppermute(incoming, 'core', SWAP)  0.68 us
  transfers between devices with their start and end apart: 2, of which 2 were waited for; matrix products, arithmetic and copies ran while one was open for 0% of the time, Pallas kernels for 3%

profile of v19, /device:TPU:0, one launch (start us, length us, event | category | flops | bytes accessed | tf_op | source)
XLA Modules:
  0.0 25.2 jit_solution(5068518709915944825)
XLA Ops:
  0.0 0.0 copy-start
  0.0 0.0 copy-start.1
  0.0 1.3 %route.1 = bf16[64,896]{1,0:T(8,128)(2,1)S(1)} custom-call(s32[8,128]{1,0:T(8,128)} %bitcast.11, bf16[128,896]{1,0:T(8,128)(2,1)} %refs_1_.3), custom_call_target="tpu_custom_call" | custom-call | flops 2000000000 | tf_op jit(solution)/shard_map/route/pallas_call | solution.py:179
  1.3 11.7 %all_to_all.22 = bf16[8,8,896]{2,1,0:T(8,128)(2,1)S(1)} all-to-all(bf16[8,8,896]{2,1,0:T(8,128)(2,1)S(1)} %bitcast.10), channel_id=1, replica_groups={{8,12,0,4,15,11,7,3},{9,13,1,5,14,10,6,2},{24,28,16,20,31,27,23,19},{25..., dimensions={0} | all-to-all | bytes 229376 | tf_op jit(solution)/shard_map/all_to_all | solution.py:174
  12.9 0.0 copy-start.2
  12.9 0.4 %collective-permute-start = (bf16[64,896]{1,0:T(8,128)(2,1)S(1)}, bf16[64,896]{1,0:T(8,128)(2,1)S(1)}, u32[]{:S(2)}, u32[]{:S(2)}) collective-permute-start(bf16[64,896]{1,0:T(8,128)(2,1)S(1)} %bitcast.8), channel_id=1, source_target_pairs={{0,1},{1,0},{2,3},{3,2},{4,5},{5,4},{6,7},{7,6},{8,9},{9,8},{10,11... | collective-permute-start | bytes 344072 | tf_op jit(solution)/shard_map/ppermute | solution.py:192
  13.3 0.0 copy-done
  13.3 0.0 copy-done.1
  13.3 0.3 %begin.1.refs_1_ = f32[32,256]{1,0:T(8,128)S(1)} custom-call(bf16[64,896]{1,0:T(8,128)(2,1)S(1)} %bitcast.9, bf16[1,3584,128]{2,1,0:T(8,128)(2,1)S(1)} %copy-done, bf16[1,3584,128]{2,1,0:T(8,128)(2,1)S(1)} %copy-done.1), custom_call_target="tpu_custom_call" | custom-call | tf_op jit(solution)/shard_map/begin/pallas_call | solution.py:194
  13.6 0.7 %collective-permute-done.refs_0_ = bf16[64,896]{1,0:T(8,128)(2,1)S(1)} collective-permute-done((bf16[64,896]{1,0:T(8,128)(2,1)S(1)}, bf16[64,896]{1,0:T(8,128)(2,1)S(1)}, u32[]{:S(2)}, u32[]{:S(2)}) %collective-permute-start) | collective-permute-done | bytes 114720 | tf_op jit(solution)/shard_map/ppermute | solution.py:192
  14.3 0.0 copy-done.2
  14.3 0.0 copy-start.3
  14.3 0.0 copy-start.4
  14.3 0.5 %theirs.1 = (bf16[32,128]{1,0:T(8,128)(2,1)S(1)}, bf16[64,896]{1,0:T(8,128)(2,1)S(1)}) custom-call(bf16[64,896]{1,0:T(8,128)(2,1)S(1)} %collective-permute-done.refs_0_, f32[32,256]{1,0:T(8,128)S(1)} %begin.1.refs_1_, bf16[1,3584,128]{2,1,0:T(8,128)(2,1)S(1)} %copy-done, bf16[1,3584,128]{2,1,0:T(8,128)(2,1)S(1)} %copy-done.1, bf16[1,128,3584]{2,1,0:T(8,128)(2,1)S(1)} %copy-done.2), custom_call_target="tpu_custom_call" | custom-call | tf_op jit(solution)/shard_map/theirs/pallas_call | solution.py:196
  14.8 0.4 %collective-permute-start.1 = (bf16[64,896]{1,0:T(8,128)(2,1)S(1)}, bf16[64,896]{1,0:T(8,128)(2,1)S(1)}, u32[]{:S(2)}, u32[]{:S(2)}) collective-permute-start(bf16[64,896]{1,0:T(8,128)(2,1)S(1)} %get-tuple-element.9.refs_2_), channel_id=1, source_target_pairs={{0,1},{1,0},{2,3},{3,2},{4,5},{5,4},{6,7},{7,6},{8,9},{9,8},{10,11... | collective-permute-start | bytes 344072 | tf_op jit(solution)/shard_map/ppermute | solution.py:199
  15.2 0.0 copy-done.3
  15.2 0.0 copy-done.4
  15.2 0.2 score.1
  15.5 0.2 ours.1.mine_ref
  15.7 0.5 %collective-permute-done.1.other_ref = bf16[64,896]{1,0:T(8,128)(2,1)S(1)} collective-permute-done((bf16[64,896]{1,0:T(8,128)(2,1)S(1)}, bf16[64,896]{1,0:T(8,128)(2,1)S(1)}, u32[]{:S(2)}, u32[]{:S(2)}) %collective-permute-start.1) | collective-permute-done | bytes 114720 | tf_op jit(solution)/shard_map/ppermute | solution.py:199
  16.2 8.1 %all_to_all.23 = bf16[8,8,896]{2,1,0:T(8,128)(2,1)S(1)} all-to-all(bf16[8,8,896]{2,1,0:T(8,128)(2,1)S(1)} %bitcast.7), channel_id=1, replica_groups={{8,4,0,12,15,3,11,7},{9,5,1,13,14,2,10,6},{24,20,16,28,31,19,27,23},{25..., dimensions={0} | all-to-all | bytes 229376 | tf_op jit(solution)/shard_map/all_to_all | solution.py:174
  24.4 0.9 %combine.1 = bf16[128,896]{1,0:T(8,128)(2,1)} custom-call(bf16[128,64]{1,0:T(8,128)(2,1)S(1)} %get-tuple-element.10.match_ref, f32[128,1]{1,0:T(8,128)S(1)} %get-tuple-element.11._.weight_ref, bf16[64,896]{1,0:T(8,128)(2,1)S(1)} %bitcast.6), custom_call_target="tpu_custom_call" | custom-call | tf_op jit(solution)/shard_map/combine/pallas_call | solution.py:212
  (1 shorter events, 0.0 us)
Async XLA Ops:
  0.0 13.3 %copy-start = (bf16[1,3584,128]{2,1,0:T(8,128)(2,1)S(1)}, bf16[1,3584,128]{2,1,0:T(8,128)(2,1)}, u32[]{:S(2)}) copy-start(bf16[1,3584,128]{2,1,0:T(8,128)(2,1)} %refs_2_.3) | copy-start | bytes 2752516
  0.0 13.3 %copy-start.1 = (bf16[1,3584,128]{2,1,0:T(8,128)(2,1)S(1)}, bf16[1,3584,128]{2,1,0:T(8,128)(2,1)}, u32[]{:S(2)}) copy-start(bf16[1,3584,128]{2,1,0:T(8,128)(2,1)} %refs_3_.1) | copy-start | bytes 2752516
  12.9 1.4 %copy-start.2 = (bf16[1,128,3584]{2,1,0:T(8,128)(2,1)S(1)}, bf16[1,128,3584]{2,1,0:T(8,128)(2,1)}, u32[]{:S(2)}) copy-start(bf16[1,128,3584]{2,1,0:T(8,128)(2,1)} %refs_1_.5) | copy-start | bytes 2752516
  12.9 1.4 %collective-permute-start = (bf16[64,896]{1,0:T(8,128)(2,1)S(1)}, bf16[64,896]{1,0:T(8,128)(2,1)S(1)}, u32[]{:S(2)}, u32[]{:S(2)}) collective-permute-start(bf16[64,896]{1,0:T(8,128)(2,1)S(1)} %bitcast.8), channel_id=1, source_target_pairs={{0,1},{1,0},{2,3},{3,2},{4,5},{5,4},{6,7},{7,6},{8,9},{9,8},{10,11... | collective-permute-start | bytes 344072 | tf_op jit(solution)/shard_map/ppermute | solution.py:192
  14.3 0.9 %copy-start.3 = (s32[128,8]{0,1:T(8,128)S(1)}, s32[128,8]{0,1:T(8,128)}, u32[]{:S(2)}) copy-start(s32[128,8]{0,1:T(8,128)} %param.7) | copy-start | bytes 12292
  14.3 0.9 %copy-start.4 = (f32[128,8]{0,1:T(8,128)S(1)}, f32[128,8]{0,1:T(8,128)}, u32[]{:S(2)}) copy-start(f32[128,8]{0,1:T(8,128)} %param.8) | copy-start | bytes 12292
  14.8 1.4 %collective-permute-start.1 = (bf16[64,896]{1,0:T(8,128)(2,1)S(1)}, bf16[64,896]{1,0:T(8,128)(2,1)S(1)}, u32[]{:S(2)}, u32[]{:S(2)}) collective-permute-start(bf16[64,896]{1,0:T(8,128)(2,1)S(1)} %get-tuple-element.9.refs_2_), channel_id=1, source_target_pairs={{0,1},{1,0},{2,3},{3,2},{4,5},{5,4},{6,7},{7,6},{8,9},{9,8},{10,11... | collective-permute-start | bytes 344072 | tf_op jit(solution)/shard_map/ppermute | solution.py:199

commit v20 on v19

--- a/solution.py
+++ b/solution.py
@@ -34,7 +34,7 @@
 
 
 def first_order(ep_count, chip):
-    listed = ((2, 3, 0, 1), (3, 2, 1, 0))[chip % 2]
+    listed = ((2, 1, 0, 3), (3, 0, 2, 1))[chip % 2]
     return [z // 4 * 4 + listed[z % 4] for z in range(ep_count)]
 
 

time: 25.6 us -> 25.9 us (1.012)
  starting transfers between devices: 0.83 us -> 1.62 us
  blocking collectives: 19.8 us -> 19.1 us
    ppermute x1, starting transfers between devices: 0.4 us -> 1.2 us  [shards(): across = lax.ppermute(incoming, 'core', SWAP)]
    all_to_all x2, blocking collectives: 19.8 us -> 19.1 us  [exchange(): return lax.all_to_all(rows, FAR, 0, 0, axis_index_groups=groups, tiled=True)]
where the time goes in v20:
time: 25.9 us; the launch traced here: 25.5 us
  blocking collectives  19.1 us (74%)
  Pallas kernels  3.44 us (13%)
  starting transfers between devices  1.62 us (6%)
  waiting for transfers between devices  1.19 us (5%)
    all_to_all x2, blocking collectives, exchange(): return lax.all_to_all(rows, FAR, 0, 0, axis_index_groups=groups, tiled=True)  19.1 us
    pallas_call x1, Pallas kernels, shards(): call(lambda *refs: route(ep_count, chips, *refs), 'route', half, in_specs...  1.27 us
    ppermute x1, starting transfers between devices, shards(): across = lax.ppermute(incoming, 'core', SWAP)  1.2 us
    pallas_call x1, Pallas kernels, shards(): call(combine, 'combine', jax.ShapeDtypeStruct((row_count, features), jnp....  0.87 us
    ppermute x1, waiting for transfers between devices, shards(): across = lax.ppermute(incoming, 'core', SWAP)  0.69 us
    pallas_call x1, Pallas kernels, shards(): call(lambda *refs: theirs(chips, *refs), 'theirs', (hidden_shape, half))  0.57 us
  transfers between devices with their start and end apart: 2, of which 2 were waited for; matrix products, arithmetic and copies ran while one was open for 0% of the time, Pallas kernels for 3%

profile of v20, /device:TPU:0, one launch (start us, length us, event | category | flops | bytes accessed | tf_op | source)
XLA Modules:
  0.0 25.5 jit_solution(4475268930476615938)
XLA Ops:
  0.0 0.0 copy-start
  0.0 0.0 copy-start.1
  0.0 1.3 %route.1 = bf16[64,896]{1,0:T(8,128)(2,1)S(1)} custom-call(s32[8,128]{1,0:T(8,128)} %bitcast.11, bf16[128,896]{1,0:T(8,128)(2,1)} %refs_1_.3), custom_call_target="tpu_custom_call" | custom-call | flops 2000000000 | tf_op jit(solution)/shard_map/route/pallas_call | solution.py:179
  1.3 11.0 %all_to_all.22 = bf16[8,8,896]{2,1,0:T(8,128)(2,1)S(1)} all-to-all(bf16[8,8,896]{2,1,0:T(8,128)(2,1)S(1)} %bitcast.10), channel_id=1, replica_groups={{8,4,0,12,15,3,11,7},{9,5,1,13,14,2,10,6},{24,20,16,28,31,19,27,23},{25..., dimensions={0} | all-to-all | bytes 229376 | tf_op jit(solution)/shard_map/all_to_all | solution.py:174
  12.3 0.0 copy-start.2
  12.3 1.2 %collective-permute-start = (bf16[64,896]{1,0:T(8,128)(2,1)S(1)}, bf16[64,896]{1,0:T(8,128)(2,1)S(1)}, u32[]{:S(2)}, u32[]{:S(2)}) collective-permute-start(bf16[64,896]{1,0:T(8,128)(2,1)S(1)} %bitcast.8), channel_id=1, source_target_pairs={{0,1},{1,0},{2,3},{3,2},{4,5},{5,4},{6,7},{7,6},{8,9},{9,8},{10,11... | collective-permute-start | bytes 344072 | tf_op jit(solution)/shard_map/ppermute | solution.py:192
  13.5 0.0 copy-done
  13.5 0.0 copy-done.1
  13.5 0.3 %begin.1.refs_1_ = f32[32,256]{1,0:T(8,128)S(1)} custom-call(bf16[64,896]{1,0:T(8,128)(2,1)S(1)} %bitcast.9, bf16[1,3584,128]{2,1,0:T(8,128)(2,1)S(1)} %copy-done, bf16[1,3584,128]{2,1,0:T(8,128)(2,1)S(1)} %copy-done.1), custom_call_target="tpu_custom_call" | custom-call | tf_op jit(solution)/shard_map/begin/pallas_call | solution.py:194
  13.8 0.7 %collective-permute-done.refs_0_ = bf16[64,896]{1,0:T(8,128)(2,1)S(1)} collective-permute-done((bf16[64,896]{1,0:T(8,128)(2,1)S(1)}, bf16[64,896]{1,0:T(8,128)(2,1)S(1)}, u32[]{:S(2)}, u32[]{:S(2)}) %collective-permute-start) | collective-permute-done | bytes 114720 | tf_op jit(solution)/shard_map/ppermute | solution.py:192
  14.5 0.0 copy-done.2
  14.5 0.0 copy-start.3
  14.5 0.0 copy-start.4
  14.5 0.6 %theirs.1 = (bf16[32,128]{1,0:T(8,128)(2,1)S(1)}, bf16[64,896]{1,0:T(8,128)(2,1)S(1)}) custom-call(bf16[64,896]{1,0:T(8,128)(2,1)S(1)} %collective-permute-done.refs_0_, f32[32,256]{1,0:T(8,128)S(1)} %begin.1.refs_1_, bf16[1,3584,128]{2,1,0:T(8,128)(2,1)S(1)} %copy-done, bf16[1,3584,128]{2,1,0:T(8,128)(2,1)S(1)} %copy-done.1, bf16[1,128,3584]{2,1,0:T(8,128)(2,1)S(1)} %copy-done.2), custom_call_target="tpu_custom_call" | custom-call | tf_op jit(solution)/shard_map/theirs/pallas_call | solution.py:196
  15.0 0.4 %collective-permute-start.1 = (bf16[64,896]{1,0:T(8,128)(2,1)S(1)}, bf16[64,896]{1,0:T(8,128)(2,1)S(1)}, u32[]{:S(2)}, u32[]{:S(2)}) collective-permute-start(bf16[64,896]{1,0:T(8,128)(2,1)S(1)} %get-tuple-element.9.refs_2_), channel_id=1, source_target_pairs={{0,1},{1,0},{2,3},{3,2},{4,5},{5,4},{6,7},{7,6},{8,9},{9,8},{10,11... | collective-permute-start | bytes 344072 | tf_op jit(solution)/shard_map/ppermute | solution.py:199
  15.5 0.0 copy-done.3
  15.5 0.0 copy-done.4
  15.5 0.2 score.1
  15.7 0.2 ours.1.mine_ref
  15.9 0.5 %collective-permute-done.1.other_ref = bf16[64,896]{1,0:T(8,128)(2,1)S(1)} collective-permute-done((bf16[64,896]{1,0:T(8,128)(2,1)S(1)}, bf16[64,896]{1,0:T(8,128)(2,1)S(1)}, u32[]{:S(2)}, u32[]{:S(2)}) %collective-permute-start.1) | collective-permute-done | bytes 114720 | tf_op jit(solution)/shard_map/ppermute | solution.py:199
  16.5 8.1 %all_to_all.23 = bf16[8,8,896]{2,1,0:T(8,128)(2,1)S(1)} all-to-all(bf16[8,8,896]{2,1,0:T(8,128)(2,1)S(1)} %bitcast.7), channel_id=1, replica_groups={{8,4,0,12,15,3,11,7},{9,5,1,13,14,2,10,6},{24,20,16,28,31,19,27,23},{25..., dimensions={0} | all-to-all | bytes 229376 | tf_op jit(solution)/shard_map/all_to_all | solution.py:174
  24.6 0.9 %combine.1 = bf16[128,896]{1,0:T(8,128)(2,1)} custom-call(bf16[128,64]{1,0:T(8,128)(2,1)S(1)} %get-tuple-element.10.match_ref, f32[128,1]{1,0:T(8,128)S(1)} %get-tuple-element.11._.weight_ref, bf16[64,896]{1,0:T(8,128)(2,1)S(1)} %bitcast.6), custom_call_target="tpu_custom_call" | custom-call | tf_op jit(solution)/shard_map/combine/pallas_call | solution.py:212
  (1 shorter events, 0.0 us)
Async XLA Ops:
  0.0 13.5 %copy-start = (bf16[1,3584,128]{2,1,0:T(8,128)(2,1)S(1)}, bf16[1,3584,128]{2,1,0:T(8,128)(2,1)}, u32[]{:S(2)}) copy-start(bf16[1,3584,128]{2,1,0:T(8,128)(2,1)} %refs_2_.3) | copy-start | bytes 2752516
  0.0 13.5 %copy-start.1 = (bf16[1,3584,128]{2,1,0:T(8,128)(2,1)S(1)}, bf16[1,3584,128]{2,1,0:T(8,128)(2,1)}, u32[]{:S(2)}) copy-start(bf16[1,3584,128]{2,1,0:T(8,128)(2,1)} %refs_3_.1) | copy-start | bytes 2752516
  12.3 2.2 %copy-start.2 = (bf16[1,128,3584]{2,1,0:T(8,128)(2,1)S(1)}, bf16[1,128,3584]{2,1,0:T(8,128)(2,1)}, u32[]{:S(2)}) copy-start(bf16[1,128,3584]{2,1,0:T(8,128)(2,1)} %refs_1_.5) | copy-start | bytes 2752516
  12.3 2.2 %collective-permute-start = (bf16[64,896]{1,0:T(8,128)(2,1)S(1)}, bf16[64,896]{1,0:T(8,128)(2,1)S(1)}, u32[]{:S(2)}, u32[]{:S(2)}) collective-permute-start(bf16[64,896]{1,0:T(8,128)(2,1)S(1)} %bitcast.8), channel_id=1, source_target_pairs={{0,1},{1,0},{2,3},{3,2},{4,5},{5,4},{6,7},{7,6},{8,9},{9,8},{10,11... | collective-permute-start | bytes 344072 | tf_op jit(solution)/shard_map/ppermute | solution.py:192
  14.5 1.0 %copy-start.3 = (s32[128,8]{0,1:T(8,128)S(1)}, s32[128,8]{0,1:T(8,128)}, u32[]{:S(2)}) copy-start(s32[128,8]{0,1:T(8,128)} %param.7) | copy-start | bytes 12292
  14.5 1.0 %copy-start.4 = (f32[128,8]{0,1:T(8,128)S(1)}, f32[128,8]{0,1:T(8,128)}, u32[]{:S(2)}) copy-start(f32[128,8]{0,1:T(8,128)} %param.8) | copy-start | bytes 12292
  15.0 1.4 %collective-permute-start.1 = (bf16[64,896]{1,0:T(8,128)(2,1)S(1)}, bf16[64,896]{1,0:T(8,128)(2,1)S(1)}, u32[]{:S(2)}, u32[]{:S(2)}) collective-permute-start(bf16[64,896]{1,0:T(8,128)(2,1)S(1)} %get-tuple-element.9.refs_2_), channel_id=1, source_target_pairs={{0,1},{1,0},{2,3},{3,2},{4,5},{5,4},{6,7},{7,6},{8,9},{9,8},{10,11... | collective-permute-start | bytes 344072 | tf_op jit(solution)/shard_map/ppermute | solution.py:199

commit v21 on v19

--- a/solution.py
+++ b/solution.py
@@ -39,7 +39,7 @@
 
 
 def second_order(ep_count, chip):
-    listed = ((2, 1, 0, 3), (3, 0, 2, 1))[chip % 2]
+    listed = ((2, 1, 0, 3), (3, 2, 0, 1))[chip % 2]
     return [z // 4 * 4 + listed[z % 4] for z in range(ep_count)]
 
 

time: 25.6 us -> 25.4 us (level)
  no operation moved by 1% of the time
where the time goes in v21:
time: 25.4 us; the launch traced here: 25.2 us
  blocking collectives  19.8 us (78%)
  Pallas kernels  3.34 us (13%)
  waiting for transfers between devices  1.19 us (5%)
  starting transfers between devices  0.83 us (3%)
    all_to_all x2, blocking collectives, exchange(): return lax.all_to_all(rows, FAR, 0, 0, axis_index_groups=groups, tiled=True)  19.8 us
    pallas_call x1, Pallas kernels, shards(): call(lambda *refs: route(ep_count, chips, *refs), 'route', half, in_specs...  1.27 us
    pallas_call x1, Pallas kernels, shards(): call(combine, 'combine', jax.ShapeDtypeStruct((row_count, features), jnp....  0.87 us
    ppermute x1, waiting for transfers between devices, shards(): across = lax.ppermute(incoming, 'core', SWAP)  0.68 us
  transfers between devices with their start and end apart: 2, of which 2 were waited for; matrix products, arithmetic and copies ran while one was open for 0% of the time, Pallas kernels for 3%

profile of v21, /device:TPU:0, one launch (start us, length us, event | category | flops | bytes accessed | tf_op | source)
XLA Modules:
  0.0 25.2 jit_solution(17517496241171990771)
XLA Ops:
  0.0 0.0 copy-start
  0.0 0.0 copy-start.1
  0.0 1.3 %route.1 = bf16[64,896]{1,0:T(8,128)(2,1)S(1)} custom-call(s32[8,128]{1,0:T(8,128)} %bitcast.11, bf16[128,896]{1,0:T(8,128)(2,1)} %refs_1_.3), custom_call_target="tpu_custom_call" | custom-call | flops 2000000000 | tf_op jit(solution)/shard_map/route/pallas_call | solution.py:179
  1.3 11.7 %all_to_all.22 = bf16[8,8,896]{2,1,0:T(8,128)(2,1)S(1)} all-to-all(bf16[8,8,896]{2,1,0:T(8,128)(2,1)S(1)} %bitcast.10), channel_id=1, replica_groups={{8,12,0,4,15,11,7,3},{9,13,1,5,14,10,6,2},{24,28,16,20,31,27,23,19},{25..., dimensions={0} | all-to-all | bytes 229376 | tf_op jit(solution)/shard_map/all_to_all | solution.py:174
  12.9 0.0 copy-start.2
  12.9 0.4 %collective-permute-start = (bf16[64,896]{1,0:T(8,128)(2,1)S(1)}, bf16[64,896]{1,0:T(8,128)(2,1)S(1)}, u32[]{:S(2)}, u32[]{:S(2)}) collective-permute-start(bf16[64,896]{1,0:T(8,128)(2,1)S(1)} %bitcast.8), channel_id=1, source_target_pairs={{0,1},{1,0},{2,3},{3,2},{4,5},{5,4},{6,7},{7,6},{8,9},{9,8},{10,11... | collective-permute-start | bytes 344072 | tf_op jit(solution)/shard_map/ppermute | solution.py:192
  13.3 0.0 copy-done
  13.3 0.0 copy-done.1
  13.3 0.3 %begin.1.refs_1_ = f32[32,256]{1,0:T(8,128)S(1)} custom-call(bf16[64,896]{1,0:T(8,128)(2,1)S(1)} %bitcast.9, bf16[1,3584,128]{2,1,0:T(8,128)(2,1)S(1)} %copy-done, bf16[1,3584,128]{2,1,0:T(8,128)(2,1)S(1)} %copy-done.1), custom_call_target="tpu_custom_call" | custom-call | tf_op jit(solution)/shard_map/begin/pallas_call | solution.py:194
  13.6 0.7 %collective-permute-done.refs_0_ = bf16[64,896]{1,0:T(8,128)(2,1)S(1)} collective-permute-done((bf16[64,896]{1,0:T(8,128)(2,1)S(1)}, bf16[64,896]{1,0:T(8,128)(2,1)S(1)}, u32[]{:S(2)}, u32[]{:S(2)}) %collective-permute-start) | collective-permute-done | bytes 114720 | tf_op jit(solution)/shard_map/ppermute | solution.py:192
  14.3 0.0 copy-done.2
  14.3 0.0 copy-start.3
  14.3 0.0 copy-start.4
  14.3 0.5 %theirs.1 = (bf16[32,128]{1,0:T(8,128)(2,1)S(1)}, bf16[64,896]{1,0:T(8,128)(2,1)S(1)}) custom-call(bf16[64,896]{1,0:T(8,128)(2,1)S(1)} %collective-permute-done.refs_0_, f32[32,256]{1,0:T(8,128)S(1)} %begin.1.refs_1_, bf16[1,3584,128]{2,1,0:T(8,128)(2,1)S(1)} %copy-done, bf16[1,3584,128]{2,1,0:T(8,128)(2,1)S(1)} %copy-done.1, bf16[1,128,3584]{2,1,0:T(8,128)(2,1)S(1)} %copy-done.2), custom_call_target="tpu_custom_call" | custom-call | tf_op jit(solution)/shard_map/theirs/pallas_call | solution.py:196
  14.8 0.4 %collective-permute-start.1 = (bf16[64,896]{1,0:T(8,128)(2,1)S(1)}, bf16[64,896]{1,0:T(8,128)(2,1)S(1)}, u32[]{:S(2)}, u32[]{:S(2)}) collective-permute-start(bf16[64,896]{1,0:T(8,128)(2,1)S(1)} %get-tuple-element.9.refs_2_), channel_id=1, source_target_pairs={{0,1},{1,0},{2,3},{3,2},{4,5},{5,4},{6,7},{7,6},{8,9},{9,8},{10,11... | collective-permute-start | bytes 344072 | tf_op jit(solution)/shard_map/ppermute | solution.py:199
  15.2 0.0 copy-done.3
  15.2 0.0 copy-done.4
  15.2 0.2 score.1
  15.5 0.2 ours.1.mine_ref
  15.7 0.5 %collective-permute-done.1.other_ref = bf16[64,896]{1,0:T(8,128)(2,1)S(1)} collective-permute-done((bf16[64,896]{1,0:T(8,128)(2,1)S(1)}, bf16[64,896]{1,0:T(8,128)(2,1)S(1)}, u32[]{:S(2)}, u32[]{:S(2)}) %collective-permute-start.1) | collective-permute-done | bytes 114720 | tf_op jit(solution)/shard_map/ppermute | solution.py:199
  16.2 8.1 %all_to_all.23 = bf16[8,8,896]{2,1,0:T(8,128)(2,1)S(1)} all-to-all(bf16[8,8,896]{2,1,0:T(8,128)(2,1)S(1)} %bitcast.7), channel_id=1, replica_groups={{8,4,0,12,15,11,3,7},{9,5,1,13,14,10,2,6},{24,20,16,28,31,27,19,23},{25..., dimensions={0} | all-to-all | bytes 229376 | tf_op jit(solution)/shard_map/all_to_all | solution.py:174
  24.3 0.9 %combine.1 = bf16[128,896]{1,0:T(8,128)(2,1)} custom-call(bf16[128,64]{1,0:T(8,128)(2,1)S(1)} %get-tuple-element.10.match_ref, f32[128,1]{1,0:T(8,128)S(1)} %get-tuple-element.11._.weight_ref, bf16[64,896]{1,0:T(8,128)(2,1)S(1)} %bitcast.6), custom_call_target="tpu_custom_call" | custom-call | tf_op jit(solution)/shard_map/combine/pallas_call | solution.py:212
  (1 shorter events, 0.0 us)
Async XLA Ops:
  0.0 13.3 %copy-start = (bf16[1,3584,128]{2,1,0:T(8,128)(2,1)S(1)}, bf16[1,3584,128]{2,1,0:T(8,128)(2,1)}, u32[]{:S(2)}) copy-start(bf16[1,3584,128]{2,1,0:T(8,128)(2,1)} %refs_2_.3) | copy-start | bytes 2752516
  0.0 13.3 %copy-start.1 = (bf16[1,3584,128]{2,1,0:T(8,128)(2,1)S(1)}, bf16[1,3584,128]{2,1,0:T(8,128)(2,1)}, u32[]{:S(2)}) copy-start(bf16[1,3584,128]{2,1,0:T(8,128)(2,1)} %refs_3_.1) | copy-start | bytes 2752516
  12.9 1.4 %copy-start.2 = (bf16[1,128,3584]{2,1,0:T(8,128)(2,1)S(1)}, bf16[1,128,3584]{2,1,0:T(8,128)(2,1)}, u32[]{:S(2)}) copy-start(bf16[1,128,3584]{2,1,0:T(8,128)(2,1)} %refs_1_.5) | copy-start | bytes 2752516
  12.9 1.4 %collective-permute-start = (bf16[64,896]{1,0:T(8,128)(2,1)S(1)}, bf16[64,896]{1,0:T(8,128)(2,1)S(1)}, u32[]{:S(2)}, u32[]{:S(2)}) collective-permute-start(bf16[64,896]{1,0:T(8,128)(2,1)S(1)} %bitcast.8), channel_id=1, source_target_pairs={{0,1},{1,0},{2,3},{3,2},{4,5},{5,4},{6,7},{7,6},{8,9},{9,8},{10,11... | collective-permute-start | bytes 344072 | tf_op jit(solution)/shard_map/ppermute | solution.py:192
  14.3 0.9 %copy-start.3 = (s32[128,8]{0,1:T(8,128)S(1)}, s32[128,8]{0,1:T(8,128)}, u32[]{:S(2)}) copy-start(s32[128,8]{0,1:T(8,128)} %param.7) | copy-start | bytes 12292
  14.3 0.9 %copy-start.4 = (f32[128,8]{0,1:T(8,128)S(1)}, f32[128,8]{0,1:T(8,128)}, u32[]{:S(2)}) copy-start(f32[128,8]{0,1:T(8,128)} %param.8) | copy-start | bytes 12292
  14.8 1.4 %collective-permute-start.1 = (bf16[64,896]{1,0:T(8,128)(2,1)S(1)}, bf16[64,896]{1,0:T(8,128)(2,1)S(1)}, u32[]{:S(2)}, u32[]{:S(2)}) collective-permute-start(bf16[64,896]{1,0:T(8,128)(2,1)S(1)} %get-tuple-element.9.refs_2_), channel_id=1, source_target_pairs={{0,1},{1,0},{2,3},{3,2},{4,5},{5,4},{6,7},{7,6},{8,9},{9,8},{10,11... | collective-permute-start | bytes 344072 | tf_op jit(solution)/shard_map/ppermute | solution.py:199

commit v22 on v21

--- a/solution.py
+++ b/solution.py
@@ -34,7 +34,7 @@
 
 
 def first_order(ep_count, chip):
-    listed = ((2, 3, 0, 1), (3, 2, 1, 0))[chip % 2]
+    listed = ((2, 3, 0, 1), (3, 1, 2, 0))[chip % 2]
     return [z // 4 * 4 + listed[z % 4] for z in range(ep_count)]
 
 

time: 25.4 us -> 25.5 us (level)
  no operation moved by 1% of the time
where the time goes in v22:
time: 25.5 us; the launch traced here: 25.2 us
  blocking collectives  19.6 us (77%)
  Pallas kernels  3.35 us (13%)
  waiting for transfers between devices  1.19 us (5%)
  starting transfers between devices  0.98 us (4%)
    all_to_all x2, blocking collectives, exchange(): return lax.all_to_all(rows, FAR, 0, 0, axis_index_groups=groups, tiled=True)  19.6 us
    pallas_call x1, Pallas kernels, shards(): call(lambda *refs: route(ep_count, chips, *refs), 'route', half, in_specs...  1.27 us
    pallas_call x1, Pallas kernels, shards(): call(combine, 'combine', jax.ShapeDtypeStruct((row_count, features), jnp....  0.87 us
    ppermute x1, waiting for transfers between devices, shards(): across = lax.ppermute(incoming, 'core', SWAP)  0.68 us
    ppermute x1, starting transfers between devices, shards(): across = lax.ppermute(incoming, 'core', SWAP)  0.55 us
  transfers between devices with their start and end apart: 2, of which 2 were waited for; matrix products, arithmetic and copies ran while one was open for 0% of the time, Pallas kernels for 3%

profile of v22, /device:TPU:0, one launch (start us, length us, event | category | flops | bytes accessed | tf_op | source)
XLA Modules:
  0.0 25.2 jit_solution(12947316404211468791)
XLA Ops:
  0.0 0.0 copy-start
  0.0 0.0 copy-start.1
  0.0 1.3 %route.1 = bf16[64,896]{1,0:T(8,128)(2,1)S(1)} custom-call(s32[8,128]{1,0:T(8,128)} %bitcast.11, bf16[128,896]{1,0:T(8,128)(2,1)} %refs_1_.3), custom_call_target="tpu_custom_call" | custom-call | flops 2000000000 | tf_op jit(solution)/shard_map/route/pallas_call | solution.py:179
  1.3 11.7 %all_to_all.22 = bf16[8,8,896]{2,1,0:T(8,128)(2,1)S(1)} all-to-all(bf16[8,8,896]{2,1,0:T(8,128)(2,1)S(1)} %bitcast.10), channel_id=1, replica_groups={{8,12,0,4,15,7,11,3},{9,13,1,5,14,6,10,2},{24,28,16,20,31,23,27,19},{25..., dimensions={0} | all-to-all | bytes 229376 | tf_op jit(solution)/shard_map/all_to_all | solution.py:174
  12.9 0.0 copy-start.2
  12.9 0.6 %collective-permute-start = (bf16[64,896]{1,0:T(8,128)(2,1)S(1)}, bf16[64,896]{1,0:T(8,128)(2,1)S(1)}, u32[]{:S(2)}, u32[]{:S(2)}) collective-permute-start(bf16[64,896]{1,0:T(8,128)(2,1)S(1)} %bitcast.8), channel_id=1, source_target_pairs={{0,1},{1,0},{2,3},{3,2},{4,5},{5,4},{6,7},{7,6},{8,9},{9,8},{10,11... | collective-permute-start | bytes 344072 | tf_op jit(solution)/shard_map/ppermute | solution.py:192
  13.5 0.0 copy-done
  13.5 0.0 copy-done.1
  13.5 0.3 %begin.1.refs_1_ = f32[32,256]{1,0:T(8,128)S(1)} custom-call(bf16[64,896]{1,0:T(8,128)(2,1)S(1)} %bitcast.9, bf16[1,3584,128]{2,1,0:T(8,128)(2,1)S(1)} %copy-done, bf16[1,3584,128]{2,1,0:T(8,128)(2,1)S(1)} %copy-done.1), custom_call_target="tpu_custom_call" | custom-call | tf_op jit(solution)/shard_map/begin/pallas_call | solution.py:194
  13.8 0.7 %collective-permute-done.refs_0_ = bf16[64,896]{1,0:T(8,128)(2,1)S(1)} collective-permute-done((bf16[64,896]{1,0:T(8,128)(2,1)S(1)}, bf16[64,896]{1,0:T(8,128)(2,1)S(1)}, u32[]{:S(2)}, u32[]{:S(2)}) %collective-permute-start) | collective-permute-done | bytes 114720 | tf_op jit(solution)/shard_map/ppermute | solution.py:192
  14.5 0.0 copy-done.2
  14.5 0.0 copy-start.3
  14.5 0.0 copy-start.4
  14.5 0.5 %theirs.1 = (bf16[32,128]{1,0:T(8,128)(2,1)S(1)}, bf16[64,896]{1,0:T(8,128)(2,1)S(1)}) custom-call(bf16[64,896]{1,0:T(8,128)(2,1)S(1)} %collective-permute-done.refs_0_, f32[32,256]{1,0:T(8,128)S(1)} %begin.1.refs_1_, bf16[1,3584,128]{2,1,0:T(8,128)(2,1)S(1)} %copy-done, bf16[1,3584,128]{2,1,0:T(8,128)(2,1)S(1)} %copy-done.1, bf16[1,128,3584]{2,1,0:T(8,128)(2,1)S(1)} %copy-done.2), custom_call_target="tpu_custom_call" | custom-call | tf_op jit(solution)/shard_map/theirs/pallas_call | solution.py:196
  14.9 0.4 %collective-permute-start.1 = (bf16[64,896]{1,0:T(8,128)(2,1)S(1)}, bf16[64,896]{1,0:T(8,128)(2,1)S(1)}, u32[]{:S(2)}, u32[]{:S(2)}) collective-permute-start(bf16[64,896]{1,0:T(8,128)(2,1)S(1)} %get-tuple-element.9.refs_2_), channel_id=1, source_target_pairs={{0,1},{1,0},{2,3},{3,2},{4,5},{5,4},{6,7},{7,6},{8,9},{9,8},{10,11... | collective-permute-start | bytes 344072 | tf_op jit(solution)/shard_map/ppermute | solution.py:199
  15.4 0.0 copy-done.3
  15.4 0.0 copy-done.4
  15.4 0.2 score.1
  15.6 0.2 ours.1.mine_ref
  15.8 0.5 %collective-permute-done.1.other_ref = bf16[64,896]{1,0:T(8,128)(2,1)S(1)} collective-permute-done((bf16[64,896]{1,0:T(8,128)(2,1)S(1)}, bf16[64,896]{1,0:T(8,128)(2,1)S(1)}, u32[]{:S(2)}, u32[]{:S(2)}) %collective-permute-start.1) | collective-permute-done | bytes 114720 | tf_op jit(solution)/shard_map/ppermute | solution.py:199
  16.4 8.0 %all_to_all.23 = bf16[8,8,896]{2,1,0:T(8,128)(2,1)S(1)} all-to-all(bf16[8,8,896]{2,1,0:T(8,128)(2,1)S(1)} %bitcast.7), channel_id=1, replica_groups={{8,4,0,12,15,11,3,7},{9,5,1,13,14,10,2,6},{24,20,16,28,31,27,19,23},{25..., dimensions={0} | all-to-all | bytes 229376 | tf_op jit(solution)/shard_map/all_to_all | solution.py:174
  24.4 0.9 %combine.1 = bf16[128,896]{1,0:T(8,128)(2,1)} custom-call(bf16[128,64]{1,0:T(8,128)(2,1)S(1)} %get-tuple-element.10.match_ref, f32[128,1]{1,0:T(8,128)S(1)} %get-tuple-element.11._.weight_ref, bf16[64,896]{1,0:T(8,128)(2,1)S(1)} %bitcast.6), custom_call_target="tpu_custom_call" | custom-call | tf_op jit(solution)/shard_map/combine/pallas_call | solution.py:212
  (1 shorter events, 0.0 us)
Async XLA Ops:
  0.0 13.5 %copy-start = (bf16[1,3584,128]{2,1,0:T(8,128)(2,1)S(1)}, bf16[1,3584,128]{2,1,0:T(8,128)(2,1)}, u32[]{:S(2)}) copy-start(bf16[1,3584,128]{2,1,0:T(8,128)(2,1)} %refs_2_.3) | copy-start | bytes 2752516
  0.0 13.5 %copy-start.1 = (bf16[1,3584,128]{2,1,0:T(8,128)(2,1)S(1)}, bf16[1,3584,128]{2,1,0:T(8,128)(2,1)}, u32[]{:S(2)}) copy-start(bf16[1,3584,128]{2,1,0:T(8,128)(2,1)} %refs_3_.1) | copy-start | bytes 2752516
  12.9 1.5 %copy-start.2 = (bf16[1,128,3584]{2,1,0:T(8,128)(2,1)S(1)}, bf16[1,128,3584]{2,1,0:T(8,128)(2,1)}, u32[]{:S(2)}) copy-start(bf16[1,128,3584]{2,1,0:T(8,128)(2,1)} %refs_1_.5) | copy-start | bytes 2752516
  12.9 1.5 %collective-permute-start = (bf16[64,896]{1,0:T(8,128)(2,1)S(1)}, bf16[64,896]{1,0:T(8,128)(2,1)S(1)}, u32[]{:S(2)}, u32[]{:S(2)}) collective-permute-start(bf16[64,896]{1,0:T(8,128)(2,1)S(1)} %bitcast.8), channel_id=1, source_target_pairs={{0,1},{1,0},{2,3},{3,2},{4,5},{5,4},{6,7},{7,6},{8,9},{9,8},{10,11... | collective-permute-start | bytes 344072 | tf_op jit(solution)/shard_map/ppermute | solution.py:192
  14.5 0.9 %copy-start.3 = (s32[128,8]{0,1:T(8,128)S(1)}, s32[128,8]{0,1:T(8,128)}, u32[]{:S(2)}) copy-start(s32[128,8]{0,1:T(8,128)} %param.7) | copy-start | bytes 12292
  14.5 0.9 %copy-start.4 = (f32[128,8]{0,1:T(8,128)S(1)}, f32[128,8]{0,1:T(8,128)}, u32[]{:S(2)}) copy-start(f32[128,8]{0,1:T(8,128)} %param.8) | copy-start | bytes 12292
  14.9 1.4 %collective-permute-start.1 = (bf16[64,896]{1,0:T(8,128)(2,1)S(1)}, bf16[64,896]{1,0:T(8,128)(2,1)S(1)}, u32[]{:S(2)}, u32[]{:S(2)}) collective-permute-start(bf16[64,896]{1,0:T(8,128)(2,1)S(1)} %get-tuple-element.9.refs_2_), channel_id=1, source_target_pairs={{0,1},{1,0},{2,3},{3,2},{4,5},{5,4},{6,7},{7,6},{8,9},{9,8},{10,11... | collective-permute-start | bytes 344072 | tf_op jit(solution)/shard_map/ppermute | solution.py:199

commit v23 on v21

--- a/solution.py
+++ b/solution.py
@@ -7,6 +7,7 @@
 
 CAP = 8
 PIECE = 32
+FETCH = 16
 FAR = ("ep", "chip", "core")
 SWAP = [(0, 1), (1, 0)]
 LIMIT = pltpu.CompilerParams(vmem_limit_bytes=16 * 1024 * 1024)
@@ -51,11 +52,11 @@
 
 def route(ep_count, chips, ids_hbm, tokens_hbm, outgoing_ref, ids_ref, tokens_ref, sems):
     row_count = ids_ref.shape[1]
-    parts = row_count // PIECE
+    parts = row_count // FETCH
     copies = [pltpu.make_async_copy(ids_hbm, ids_ref, sems.at[parts])] + [
         pltpu.make_async_copy(
-            tokens_hbm.at[pl.ds(part * PIECE, PIECE), :],
-            tokens_ref.at[pl.ds(part * PIECE, PIECE), :],
+            tokens_hbm.at[pl.ds(part * FETCH, FETCH), :],
+            tokens_ref.at[pl.ds(part * FETCH, FETCH), :],
             sems.at[part],
         )
         for part in range(parts)
@@ -184,7 +185,7 @@
         scratch_shapes=[
             pltpu.VMEM((top_count, row_count), jnp.int32),
             pltpu.VMEM((row_count, features), jnp.bfloat16),
-            pltpu.SemaphoreType.DMA((row_count // PIECE + 1,)),
+            pltpu.SemaphoreType.DMA((row_count // FETCH + 1,)),
         ],
         cost_estimate=pl.CostEstimate(flops=2 * 10**9, bytes_accessed=0, transcendentals=0),
     )(*(pltpu.with_memory_space_constraint(value, pltpu.HBM) for value in (ids, tokens)))

time: 25.4 us -> 25.4 us (level)
  no operation moved by 1% of the time
where the time goes in v23:
time: 25.4 us; the launch traced here: 25.2 us
  blocking collectives  19.8 us (78%)
  Pallas kernels  3.33 us (13%)
  waiting for transfers between devices  1.19 us (5%)
  starting transfers between devices  0.83 us (3%)
    all_to_all x2, blocking collectives, exchange(): return lax.all_to_all(rows, FAR, 0, 0, axis_index_groups=groups, tiled=True)  19.8 us
    pallas_call x1, Pallas kernels, shards(): call(lambda *refs: route(ep_count, chips, *refs), 'route', half, in_specs...  1.26 us
    pallas_call x1, Pallas kernels, shards(): call(combine, 'combine', jax.ShapeDtypeStruct((row_count, features), jnp....  0.87 us
    ppermute x1, waiting for transfers between devices, shards(): across = lax.ppermute(incoming, 'core', SWAP)  0.68 us
  transfers between devices with their start and end apart: 2, of which 2 were waited for; matrix products, arithmetic and copies ran while one was open for 0% of the time, Pallas kernels for 3%

profile of v23, /device:TPU:0, one launch (start us, length us, event | category | flops | bytes accessed | tf_op | source)
XLA Modules:
  0.0 25.2 jit_solution(12628242900054969866)
XLA Ops:
  0.0 0.0 copy-start
  0.0 0.0 copy-start.1
  0.0 1.3 %route.1 = bf16[64,896]{1,0:T(8,128)(2,1)S(1)} custom-call(s32[8,128]{1,0:T(8,128)} %bitcast.11, bf16[128,896]{1,0:T(8,128)(2,1)} %refs_1_.3), custom_call_target="tpu_custom_call" | custom-call | flops 2000000000 | tf_op jit(solution)/shard_map/route/pallas_call | solution.py:180
  1.3 11.7 %all_to_all.22 = bf16[8,8,896]{2,1,0:T(8,128)(2,1)S(1)} all-to-all(bf16[8,8,896]{2,1,0:T(8,128)(2,1)S(1)} %bitcast.10), channel_id=1, replica_groups={{8,12,0,4,15,11,7,3},{9,13,1,5,14,10,6,2},{24,28,16,20,31,27,23,19},{25..., dimensions={0} | all-to-all | bytes 229376 | tf_op jit(solution)/shard_map/all_to_all | solution.py:175
  12.9 0.0 copy-start.2
  12.9 0.4 %collective-permute-start = (bf16[64,896]{1,0:T(8,128)(2,1)S(1)}, bf16[64,896]{1,0:T(8,128)(2,1)S(1)}, u32[]{:S(2)}, u32[]{:S(2)}) collective-permute-start(bf16[64,896]{1,0:T(8,128)(2,1)S(1)} %bitcast.8), channel_id=1, source_target_pairs={{0,1},{1,0},{2,3},{3,2},{4,5},{5,4},{6,7},{7,6},{8,9},{9,8},{10,11... | collective-permute-start | bytes 344072 | tf_op jit(solution)/shard_map/ppermute | solution.py:193
  13.3 0.0 copy-done
  13.3 0.0 copy-done.1
  13.3 0.3 %begin.1.refs_1_ = f32[32,256]{1,0:T(8,128)S(1)} custom-call(bf16[64,896]{1,0:T(8,128)(2,1)S(1)} %bitcast.9, bf16[1,3584,128]{2,1,0:T(8,128)(2,1)S(1)} %copy-done, bf16[1,3584,128]{2,1,0:T(8,128)(2,1)S(1)} %copy-done.1), custom_call_target="tpu_custom_call" | custom-call | tf_op jit(solution)/shard_map/begin/pallas_call | solution.py:195
  13.6 0.7 %collective-permute-done.refs_0_ = bf16[64,896]{1,0:T(8,128)(2,1)S(1)} collective-permute-done((bf16[64,896]{1,0:T(8,128)(2,1)S(1)}, bf16[64,896]{1,0:T(8,128)(2,1)S(1)}, u32[]{:S(2)}, u32[]{:S(2)}) %collective-permute-start) | collective-permute-done | bytes 114720 | tf_op jit(solution)/shard_map/ppermute | solution.py:193
  14.3 0.0 copy-done.2
  14.3 0.0 copy-start.3
  14.3 0.0 copy-start.4
  14.3 0.5 %theirs.1 = (bf16[32,128]{1,0:T(8,128)(2,1)S(1)}, bf16[64,896]{1,0:T(8,128)(2,1)S(1)}) custom-call(bf16[64,896]{1,0:T(8,128)(2,1)S(1)} %collective-permute-done.refs_0_, f32[32,256]{1,0:T(8,128)S(1)} %begin.1.refs_1_, bf16[1,3584,128]{2,1,0:T(8,128)(2,1)S(1)} %copy-done, bf16[1,3584,128]{2,1,0:T(8,128)(2,1)S(1)} %copy-done.1, bf16[1,128,3584]{2,1,0:T(8,128)(2,1)S(1)} %copy-done.2), custom_call_target="tpu_custom_call" | custom-call | tf_op jit(solution)/shard_map/theirs/pallas_call | solution.py:197
  14.8 0.4 %collective-permute-start.1 = (bf16[64,896]{1,0:T(8,128)(2,1)S(1)}, bf16[64,896]{1,0:T(8,128)(2,1)S(1)}, u32[]{:S(2)}, u32[]{:S(2)}) collective-permute-start(bf16[64,896]{1,0:T(8,128)(2,1)S(1)} %get-tuple-element.9.refs_2_), channel_id=1, source_target_pairs={{0,1},{1,0},{2,3},{3,2},{4,5},{5,4},{6,7},{7,6},{8,9},{9,8},{10,11... | collective-permute-start | bytes 344072 | tf_op jit(solution)/shard_map/ppermute | solution.py:200
  15.2 0.0 copy-done.3
  15.2 0.0 copy-done.4
  15.2 0.2 score.1
  15.4 0.2 ours.1.mine_ref
  15.7 0.5 %collective-permute-done.1.other_ref = bf16[64,896]{1,0:T(8,128)(2,1)S(1)} collective-permute-done((bf16[64,896]{1,0:T(8,128)(2,1)S(1)}, bf16[64,896]{1,0:T(8,128)(2,1)S(1)}, u32[]{:S(2)}, u32[]{:S(2)}) %collective-permute-start.1) | collective-permute-done | bytes 114720 | tf_op jit(solution)/shard_map/ppermute | solution.py:200
  16.2 8.1 %all_to_all.23 = bf16[8,8,896]{2,1,0:T(8,128)(2,1)S(1)} all-to-all(bf16[8,8,896]{2,1,0:T(8,128)(2,1)S(1)} %bitcast.7), channel_id=1, replica_groups={{8,4,0,12,15,11,3,7},{9,5,1,13,14,10,2,6},{24,20,16,28,31,27,19,23},{25..., dimensions={0} | all-to-all | bytes 229376 | tf_op jit(solution)/shard_map/all_to_all | solution.py:175
  24.3 0.9 %combine.1 = bf16[128,896]{1,0:T(8,128)(2,1)} custom-call(bf16[128,64]{1,0:T(8,128)(2,1)S(1)} %get-tuple-element.10.match_ref, f32[128,1]{1,0:T(8,128)S(1)} %get-tuple-element.11._.weight_ref, bf16[64,896]{1,0:T(8,128)(2,1)S(1)} %bitcast.6), custom_call_target="tpu_custom_call" | custom-call | tf_op jit(solution)/shard_map/combine/pallas_call | solution.py:213
  (1 shorter events, 0.0 us)
Async XLA Ops:
  0.0 13.3 %copy-start = (bf16[1,3584,128]{2,1,0:T(8,128)(2,1)S(1)}, bf16[1,3584,128]{2,1,0:T(8,128)(2,1)}, u32[]{:S(2)}) copy-start(bf16[1,3584,128]{2,1,0:T(8,128)(2,1)} %refs_2_.3) | copy-start | bytes 2752516
  0.0 13.3 %copy-start.1 = (bf16[1,3584,128]{2,1,0:T(8,128)(2,1)S(1)}, bf16[1,3584,128]{2,1,0:T(8,128)(2,1)}, u32[]{:S(2)}) copy-start(bf16[1,3584,128]{2,1,0:T(8,128)(2,1)} %refs_3_.1) | copy-start | bytes 2752516
  12.9 1.4 %copy-start.2 = (bf16[1,128,3584]{2,1,0:T(8,128)(2,1)S(1)}, bf16[1,128,3584]{2,1,0:T(8,128)(2,1)}, u32[]{:S(2)}) copy-start(bf16[1,128,3584]{2,1,0:T(8,128)(2,1)} %refs_1_.5) | copy-start | bytes 2752516
  12.9 1.4 %collective-permute-start = (bf16[64,896]{1,0:T(8,128)(2,1)S(1)}, bf16[64,896]{1,0:T(8,128)(2,1)S(1)}, u32[]{:S(2)}, u32[]{:S(2)}) collective-permute-start(bf16[64,896]{1,0:T(8,128)(2,1)S(1)} %bitcast.8), channel_id=1, source_target_pairs={{0,1},{1,0},{2,3},{3,2},{4,5},{5,4},{6,7},{7,6},{8,9},{9,8},{10,11... | collective-permute-start | bytes 344072 | tf_op jit(solution)/shard_map/ppermute | solution.py:193
  14.3 0.9 %copy-start.3 = (s32[128,8]{0,1:T(8,128)S(1)}, s32[128,8]{0,1:T(8,128)}, u32[]{:S(2)}) copy-start(s32[128,8]{0,1:T(8,128)} %param.7) | copy-start | bytes 12292
  14.3 0.9 %copy-start.4 = (f32[128,8]{0,1:T(8,128)S(1)}, f32[128,8]{0,1:T(8,128)}, u32[]{:S(2)}) copy-start(f32[128,8]{0,1:T(8,128)} %param.8) | copy-start | bytes 12292
  14.8 1.4 %collective-permute-start.1 = (bf16[64,896]{1,0:T(8,128)(2,1)S(1)}, bf16[64,896]{1,0:T(8,128)(2,1)S(1)}, u32[]{:S(2)}, u32[]{:S(2)}) collective-permute-start(bf16[64,896]{1,0:T(8,128)(2,1)S(1)} %get-tuple-element.9.refs_2_), channel_id=1, source_target_pairs={{0,1},{1,0},{2,3},{3,2},{4,5},{5,4},{6,7},{7,6},{8,9},{9,8},{10,11... | collective-permute-start | bytes 344072 | tf_op jit(solution)/shard_map/ppermute | solution.py:200

commit v24 on v23

--- a/solution.py
+++ b/solution.py
@@ -35,12 +35,12 @@
 
 
 def first_order(ep_count, chip):
-    listed = ((2, 3, 0, 1), (3, 2, 1, 0))[chip % 2]
+    listed = ((0, 1, 3, 2), (3, 1, 2, 0))[chip % 2]
     return [z // 4 * 4 + listed[z % 4] for z in range(ep_count)]
 
 
 def second_order(ep_count, chip):
-    listed = ((2, 1, 0, 3), (3, 2, 0, 1))[chip % 2]
+    listed = ((2, 1, 0, 3), (3, 1, 2, 0))[chip % 2]
     return [z // 4 * 4 + listed[z % 4] for z in range(ep_count)]
 
 
@@ -150,10 +150,11 @@
 
 def combine(match_ref, weight_ref, returned_ref, out_hbm, out_ref, sems):
     copies = []
+    summed = jnp.dot(match_ref[...], returned_ref[...], preferred_element_type=jnp.float32)
     for part in range(out_ref.shape[0] // PIECE):
         rows = pl.ds(part * PIECE, PIECE)
-        summed = jnp.dot(match_ref[rows, :], returned_ref[...], preferred_element_type=jnp.float32)
-        out_ref[rows, :] = (weight_ref[rows, :] * summed).astype(jnp.bfloat16)
+        piece = summed[part * PIECE : (part + 1) * PIECE, :]
+        out_ref[rows, :] = (weight_ref[rows, :] * piece).astype(jnp.bfloat16)
         copies.append(pltpu.make_async_copy(out_ref.at[rows, :], out_hbm.at[rows, :], sems.at[part]))
         copies[-1].start()
     for copy in copies:

time: 25.4 us -> 27.5 us (1.083)
  blocking collectives: 19.8 us -> 21.3 us
    all_to_all x2, blocking collectives: 19.8 us -> 21.3 us  [exchange(): return lax.all_to_all(rows, FAR, 0, 0, axis_index_groups=groups, tiled=True)]
where the time goes in v24:
time: 27.5 us; the launch traced here: 27 us
  blocking collectives  21.3 us (77%)
  Pallas kernels  3.37 us (12%)
  waiting for transfers between devices  1.19 us (4%)
  starting transfers between devices  1.08 us (4%)
    all_to_all x2, blocking collectives, exchange(): return lax.all_to_all(rows, FAR, 0, 0, axis_index_groups=groups, tiled=True)  21.3 us
    pallas_call x1, Pallas kernels, shards(): call(lambda *refs: route(ep_count, chips, *refs), 'route', half, in_specs...  1.26 us
    pallas_call x1, Pallas kernels, shards(): call(combine, 'combine', jax.ShapeDtypeStruct((row_count, features), jnp....  0.9 us
    ppermute x1, waiting for transfers between devices, shards(): across = lax.ppermute(incoming, 'core', SWAP)  0.68 us
    ppermute x1, starting transfers between devices, shards(): across = lax.ppermute(incoming, 'core', SWAP)  0.65 us
  transfers between devices with their start and end apart: 2, of which 2 were waited for; matrix products, arithmetic and copies ran while one was open for 0% of the time, Pallas kernels for 3%

profile of v24, /device:TPU:0, one launch (start us, length us, event | category | flops | bytes accessed | tf_op | source)
XLA Modules:
  0.0 27.0 jit_solution(7818729777779835334)
XLA Ops:
  0.0 0.0 copy-start
  0.0 0.0 copy-start.1
  0.0 1.3 %route.1 = bf16[64,896]{1,0:T(8,128)(2,1)S(1)} custom-call(s32[8,128]{1,0:T(8,128)} %bitcast.11, bf16[128,896]{1,0:T(8,128)(2,1)} %refs_1_.3), custom_call_target="tpu_custom_call" | custom-call | flops 2000000000 | tf_op jit(solution)/shard_map/route/pallas_call | solution.py:181
  1.3 13.4 %all_to_all.22 = bf16[8,8,896]{2,1,0:T(8,128)(2,1)S(1)} all-to-all(bf16[8,8,896]{2,1,0:T(8,128)(2,1)S(1)} %bitcast.10), channel_id=1, replica_groups={{0,4,12,8,15,7,11,3},{1,5,13,9,14,6,10,2},{16,20,28,24,31,23,27,19},{17..., dimensions={0} | all-to-all | bytes 229376 | tf_op jit(solution)/shard_map/all_to_all | solution.py:176
  14.7 0.0 copy-start.2
  14.7 0.7 %collective-permute-start = (bf16[64,896]{1,0:T(8,128)(2,1)S(1)}, bf16[64,896]{1,0:T(8,128)(2,1)S(1)}, u32[]{:S(2)}, u32[]{:S(2)}) collective-permute-start(bf16[64,896]{1,0:T(8,128)(2,1)S(1)} %bitcast.8), channel_id=1, source_target_pairs={{0,1},{1,0},{2,3},{3,2},{4,5},{5,4},{6,7},{7,6},{8,9},{9,8},{10,11... | collective-permute-start | bytes 344072 | tf_op jit(solution)/shard_map/ppermute | solution.py:194
  15.3 0.0 copy-done
  15.3 0.0 copy-done.1
  15.3 0.3 %begin.1.refs_1_ = f32[32,256]{1,0:T(8,128)S(1)} custom-call(bf16[64,896]{1,0:T(8,128)(2,1)S(1)} %bitcast.9, bf16[1,3584,128]{2,1,0:T(8,128)(2,1)S(1)} %copy-done, bf16[1,3584,128]{2,1,0:T(8,128)(2,1)S(1)} %copy-done.1), custom_call_target="tpu_custom_call" | custom-call | tf_op jit(solution)/shard_map/begin/pallas_call | solution.py:196
  15.6 0.7 %collective-permute-done.refs_0_ = bf16[64,896]{1,0:T(8,128)(2,1)S(1)} collective-permute-done((bf16[64,896]{1,0:T(8,128)(2,1)S(1)}, bf16[64,896]{1,0:T(8,128)(2,1)S(1)}, u32[]{:S(2)}, u32[]{:S(2)}) %collective-permute-start) | collective-permute-done | bytes 114720 | tf_op jit(solution)/shard_map/ppermute | solution.py:194
  16.3 0.0 copy-done.2
  16.3 0.0 copy-start.3
  16.3 0.0 copy-start.4
  16.3 0.5 %theirs.1 = (bf16[32,128]{1,0:T(8,128)(2,1)S(1)}, bf16[64,896]{1,0:T(8,128)(2,1)S(1)}) custom-call(bf16[64,896]{1,0:T(8,128)(2,1)S(1)} %collective-permute-done.refs_0_, f32[32,256]{1,0:T(8,128)S(1)} %begin.1.refs_1_, bf16[1,3584,128]{2,1,0:T(8,128)(2,1)S(1)} %copy-done, bf16[1,3584,128]{2,1,0:T(8,128)(2,1)S(1)} %copy-done.1, bf16[1,128,3584]{2,1,0:T(8,128)(2,1)S(1)} %copy-done.2), custom_call_target="tpu_custom_call" | custom-call | tf_op jit(solution)/shard_map/theirs/pallas_call | solution.py:198
  16.8 0.4 %collective-permute-start.1 = (bf16[64,896]{1,0:T(8,128)(2,1)S(1)}, bf16[64,896]{1,0:T(8,128)(2,1)S(1)}, u32[]{:S(2)}, u32[]{:S(2)}) collective-permute-start(bf16[64,896]{1,0:T(8,128)(2,1)S(1)} %get-tuple-element.9.refs_2_), channel_id=1, source_target_pairs={{0,1},{1,0},{2,3},{3,2},{4,5},{5,4},{6,7},{7,6},{8,9},{9,8},{10,11... | collective-permute-start | bytes 344072 | tf_op jit(solution)/shard_map/ppermute | solution.py:201
  17.2 0.0 copy-done.3
  17.2 0.0 copy-done.4
  17.2 0.2 score.1
  17.4 0.2 ours.1.mine_ref
  17.7 0.5 %collective-permute-done.1.other_ref = bf16[64,896]{1,0:T(8,128)(2,1)S(1)} collective-permute-done((bf16[64,896]{1,0:T(8,128)(2,1)S(1)}, bf16[64,896]{1,0:T(8,128)(2,1)S(1)}, u32[]{:S(2)}, u32[]{:S(2)}) %collective-permute-start.1) | collective-permute-done | bytes 114720 | tf_op jit(solution)/shard_map/ppermute | solution.py:201
  18.2 7.9 %all_to_all.23 = bf16[8,8,896]{2,1,0:T(8,128)(2,1)S(1)} all-to-all(bf16[8,8,896]{2,1,0:T(8,128)(2,1)S(1)} %bitcast.7), channel_id=1, replica_groups={{8,4,0,12,15,7,11,3},{9,5,1,13,14,6,10,2},{24,20,16,28,31,23,27,19},{25..., dimensions={0} | all-to-all | bytes 229376 | tf_op jit(solution)/shard_map/all_to_all | solution.py:176
  26.1 0.9 %combine.1 = bf16[128,896]{1,0:T(8,128)(2,1)} custom-call(bf16[128,64]{1,0:T(8,128)(2,1)S(1)} %get-tuple-element.10.match_ref, f32[128,1]{1,0:T(8,128)S(1)} %get-tuple-element.11._.weight_ref, bf16[64,896]{1,0:T(8,128)(2,1)S(1)} %bitcast.6), custom_call_target="tpu_custom_call" | custom-call | tf_op jit(solution)/shard_map/combine/pallas_call | solution.py:214
  (1 shorter events, 0.0 us)
Async XLA Ops:
  0.0 15.3 %copy-start = (bf16[1,3584,128]{2,1,0:T(8,128)(2,1)S(1)}, bf16[1,3584,128]{2,1,0:T(8,128)(2,1)}, u32[]{:S(2)}) copy-start(bf16[1,3584,128]{2,1,0:T(8,128)(2,1)} %refs_2_.3) | copy-start | bytes 2752516
  0.0 15.3 %copy-start.1 = (bf16[1,3584,128]{2,1,0:T(8,128)(2,1)S(1)}, bf16[1,3584,128]{2,1,0:T(8,128)(2,1)}, u32[]{:S(2)}) copy-start(bf16[1,3584,128]{2,1,0:T(8,128)(2,1)} %refs_3_.1) | copy-start | bytes 2752516
  14.7 1.6 %copy-start.2 = (bf16[1,128,3584]{2,1,0:T(8,128)(2,1)S(1)}, bf16[1,128,3584]{2,1,0:T(8,128)(2,1)}, u32[]{:S(2)}) copy-start(bf16[1,128,3584]{2,1,0:T(8,128)(2,1)} %refs_1_.5) | copy-start | bytes 2752516
  14.7 1.6 %collective-permute-start = (bf16[64,896]{1,0:T(8,128)(2,1)S(1)}, bf16[64,896]{1,0:T(8,128)(2,1)S(1)}, u32[]{:S(2)}, u32[]{:S(2)}) collective-permute-start(bf16[64,896]{1,0:T(8,128)(2,1)S(1)} %bitcast.8), channel_id=1, source_target_pairs={{0,1},{1,0},{2,3},{3,2},{4,5},{5,4},{6,7},{7,6},{8,9},{9,8},{10,11... | collective-permute-start | bytes 344072 | tf_op jit(solution)/shard_map/ppermute | solution.py:194
  16.3 0.9 %copy-start.3 = (s32[128,8]{0,1:T(8,128)S(1)}, s32[128,8]{0,1:T(8,128)}, u32[]{:S(2)}) copy-start(s32[128,8]{0,1:T(8,128)} %param.7) | copy-start | bytes 12292
  16.3 0.9 %copy-start.4 = (f32[128,8]{0,1:T(8,128)S(1)}, f32[128,8]{0,1:T(8,128)}, u32[]{:S(2)}) copy-start(f32[128,8]{0,1:T(8,128)} %param.8) | copy-start | bytes 12292
  16.8 1.4 %collective-permute-start.1 = (bf16[64,896]{1,0:T(8,128)(2,1)S(1)}, bf16[64,896]{1,0:T(8,128)(2,1)S(1)}, u32[]{:S(2)}, u32[]{:S(2)}) collective-permute-start(bf16[64,896]{1,0:T(8,128)(2,1)S(1)} %get-tuple-element.9.refs_2_), channel_id=1, source_target_pairs={{0,1},{1,0},{2,3},{3,2},{4,5},{5,4},{6,7},{7,6},{8,9},{9,8},{10,11... | collective-permute-start | bytes 344072 | tf_op jit(solution)/shard_map/ppermute | solution.py:201

commit v25 on v23

--- a/solution.py
+++ b/solution.py
@@ -35,12 +35,12 @@
 
 
 def first_order(ep_count, chip):
-    listed = ((2, 3, 0, 1), (3, 2, 1, 0))[chip % 2]
+    listed = ((2, 3, 1, 0), (3, 2, 1, 0))[chip % 2]
     return [z // 4 * 4 + listed[z % 4] for z in range(ep_count)]
 
 
 def second_order(ep_count, chip):
-    listed = ((2, 1, 0, 3), (3, 2, 0, 1))[chip % 2]
+    listed = ((3, 1, 2, 0), (3, 0, 2, 1))[chip % 2]
     return [z // 4 * 4 + listed[z % 4] for z in range(ep_count)]
 
 

time: 25.4 us -> 26.7 us (1.051)
  blocking collectives: 19.8 us -> 21 us
    all_to_all x2, blocking collectives: 19.8 us -> 21 us  [exchange(): return lax.all_to_all(rows, FAR, 0, 0, axis_index_groups=groups, tiled=True)]
where the time goes in v25:
time: 26.7 us; the launch traced here: 26.5 us
  blocking collectives  21 us (79%)
  Pallas kernels  3.43 us (13%)
  waiting for transfers between devices  1.3 us (5%)
  starting transfers between devices  0.67 us (3%)
    all_to_all x2, blocking collectives, exchange(): return lax.all_to_all(rows, FAR, 0, 0, axis_index_groups=groups, tiled=True)  21 us
    pallas_call x1, Pallas kernels, shards(): call(lambda *refs: route(ep_count, chips, *refs), 'route', half, in_specs...  1.26 us
    pallas_call x1, Pallas kernels, shards(): call(combine, 'combine', jax.ShapeDtypeStruct((row_count, features), jnp....  0.87 us
    ppermute x1, waiting for transfers between devices, shards(): across = lax.ppermute(incoming, 'core', SWAP)  0.74 us
    pallas_call x1, Pallas kernels, shards(): call(lambda *refs: theirs(chips, *refs), 'theirs', (hidden_shape, half))  0.57 us
    ppermute x1, waiting for transfers between devices, shards(): crossed = lax.ppermute(other, 'core', SWAP)  0.56 us
  transfers between devices with their start and end apart: 2, of which 2 were waited for; matrix products, arithmetic and copies ran while one was open for 0% of the time, Pallas kernels for 3%

profile of v25, /device:TPU:0, one launch (start us, length us, event | category | flops | bytes accessed | tf_op | source)
XLA Modules:
  0.0 26.5 jit_solution(10623204937466259333)
XLA Ops:
  0.0 0.0 copy-start
  0.0 0.0 copy-start.1
  0.0 1.3 %route.1 = bf16[64,896]{1,0:T(8,128)(2,1)S(1)} custom-call(s32[8,128]{1,0:T(8,128)} %bitcast.11, bf16[128,896]{1,0:T(8,128)(2,1)} %refs_1_.3), custom_call_target="tpu_custom_call" | custom-call | flops 2000000000 | tf_op jit(solution)/shard_map/route/pallas_call | solution.py:180
  1.3 11.2 %all_to_all.22 = bf16[8,8,896]{2,1,0:T(8,128)(2,1)S(1)} all-to-all(bf16[8,8,896]{2,1,0:T(8,128)(2,1)S(1)} %bitcast.10), channel_id=1, replica_groups={{8,12,4,0,15,11,7,3},{9,13,5,1,14,10,6,2},{24,28,20,16,31,27,23,19},{25..., dimensions={0} | all-to-all | bytes 229376 | tf_op jit(solution)/shard_map/all_to_all | solution.py:175
  12.4 0.0 copy-start.2
  12.4 0.3 %collective-permute-start = (bf16[64,896]{1,0:T(8,128)(2,1)S(1)}, bf16[64,896]{1,0:T(8,128)(2,1)S(1)}, u32[]{:S(2)}, u32[]{:S(2)}) collective-permute-start(bf16[64,896]{1,0:T(8,128)(2,1)S(1)} %bitcast.8), channel_id=1, source_target_pairs={{0,1},{1,0},{2,3},{3,2},{4,5},{5,4},{6,7},{7,6},{8,9},{9,8},{10,11... | collective-permute-start | bytes 344072 | tf_op jit(solution)/shard_map/ppermute | solution.py:193
  12.8 0.0 copy-done
  12.8 0.0 copy-done.1
  12.8 0.3 %begin.1.refs_1_ = f32[32,256]{1,0:T(8,128)S(1)} custom-call(bf16[64,896]{1,0:T(8,128)(2,1)S(1)} %bitcast.9, bf16[1,3584,128]{2,1,0:T(8,128)(2,1)S(1)} %copy-done, bf16[1,3584,128]{2,1,0:T(8,128)(2,1)S(1)} %copy-done.1), custom_call_target="tpu_custom_call" | custom-call | tf_op jit(solution)/shard_map/begin/pallas_call | solution.py:195
  13.0 0.7 %collective-permute-done.refs_0_ = bf16[64,896]{1,0:T(8,128)(2,1)S(1)} collective-permute-done((bf16[64,896]{1,0:T(8,128)(2,1)S(1)}, bf16[64,896]{1,0:T(8,128)(2,1)S(1)}, u32[]{:S(2)}, u32[]{:S(2)}) %collective-permute-start) | collective-permute-done | bytes 114720 | tf_op jit(solution)/shard_map/ppermute | solution.py:193
  13.8 0.0 copy-done.2
  13.8 0.0 copy-start.3
  13.8 0.0 copy-start.4
  13.8 0.6 %theirs.1 = (bf16[32,128]{1,0:T(8,128)(2,1)S(1)}, bf16[64,896]{1,0:T(8,128)(2,1)S(1)}) custom-call(bf16[64,896]{1,0:T(8,128)(2,1)S(1)} %collective-permute-done.refs_0_, f32[32,256]{1,0:T(8,128)S(1)} %begin.1.refs_1_, bf16[1,3584,128]{2,1,0:T(8,128)(2,1)S(1)} %copy-done, bf16[1,3584,128]{2,1,0:T(8,128)(2,1)S(1)} %copy-done.1, bf16[1,128,3584]{2,1,0:T(8,128)(2,1)S(1)} %copy-done.2), custom_call_target="tpu_custom_call" | custom-call | tf_op jit(solution)/shard_map/theirs/pallas_call | solution.py:197
  14.4 0.4 %collective-permute-start.1 = (bf16[64,896]{1,0:T(8,128)(2,1)S(1)}, bf16[64,896]{1,0:T(8,128)(2,1)S(1)}, u32[]{:S(2)}, u32[]{:S(2)}) collective-permute-start(bf16[64,896]{1,0:T(8,128)(2,1)S(1)} %get-tuple-element.9.refs_2_), channel_id=1, source_target_pairs={{0,1},{1,0},{2,3},{3,2},{4,5},{5,4},{6,7},{7,6},{8,9},{9,8},{10,11... | collective-permute-start | bytes 344072 | tf_op jit(solution)/shard_map/ppermute | solution.py:200
  14.7 0.0 copy-done.3
  14.7 0.0 copy-done.4
  14.7 0.2 score.1
  15.0 0.2 ours.1.mine_ref
  15.2 0.6 %collective-permute-done.1.other_ref = bf16[64,896]{1,0:T(8,128)(2,1)S(1)} collective-permute-done((bf16[64,896]{1,0:T(8,128)(2,1)S(1)}, bf16[64,896]{1,0:T(8,128)(2,1)S(1)}, u32[]{:S(2)}, u32[]{:S(2)}) %collective-permute-start.1) | collective-permute-done | bytes 114720 | tf_op jit(solution)/shard_map/ppermute | solution.py:200
  15.8 9.9 %all_to_all.23 = bf16[8,8,896]{2,1,0:T(8,128)(2,1)S(1)} all-to-all(bf16[8,8,896]{2,1,0:T(8,128)(2,1)S(1)} %bitcast.7), channel_id=1, replica_groups={{12,4,8,0,15,3,11,7},{13,5,9,1,14,2,10,6},{28,20,24,16,31,19,27,23},{29..., dimensions={0} | all-to-all | bytes 229376 | tf_op jit(solution)/shard_map/all_to_all | solution.py:175
  25.6 0.9 %combine.1 = bf16[128,896]{1,0:T(8,128)(2,1)} custom-call(bf16[128,64]{1,0:T(8,128)(2,1)S(1)} %get-tuple-element.10.match_ref, f32[128,1]{1,0:T(8,128)S(1)} %get-tuple-element.11._.weight_ref, bf16[64,896]{1,0:T(8,128)(2,1)S(1)} %bitcast.6), custom_call_target="tpu_custom_call" | custom-call | tf_op jit(solution)/shard_map/combine/pallas_call | solution.py:213
  (1 shorter events, 0.0 us)
Async XLA Ops:
  0.0 12.8 %copy-start = (bf16[1,3584,128]{2,1,0:T(8,128)(2,1)S(1)}, bf16[1,3584,128]{2,1,0:T(8,128)(2,1)}, u32[]{:S(2)}) copy-start(bf16[1,3584,128]{2,1,0:T(8,128)(2,1)} %refs_2_.3) | copy-start | bytes 2752516
  0.0 12.8 %copy-start.1 = (bf16[1,3584,128]{2,1,0:T(8,128)(2,1)S(1)}, bf16[1,3584,128]{2,1,0:T(8,128)(2,1)}, u32[]{:S(2)}) copy-start(bf16[1,3584,128]{2,1,0:T(8,128)(2,1)} %refs_3_.1) | copy-start | bytes 2752516
  12.4 1.3 %copy-start.2 = (bf16[1,128,3584]{2,1,0:T(8,128)(2,1)S(1)}, bf16[1,128,3584]{2,1,0:T(8,128)(2,1)}, u32[]{:S(2)}) copy-start(bf16[1,128,3584]{2,1,0:T(8,128)(2,1)} %refs_1_.5) | copy-start | bytes 2752516
  12.4 1.3 %collective-permute-start = (bf16[64,896]{1,0:T(8,128)(2,1)S(1)}, bf16[64,896]{1,0:T(8,128)(2,1)S(1)}, u32[]{:S(2)}, u32[]{:S(2)}) collective-permute-start(bf16[64,896]{1,0:T(8,128)(2,1)S(1)} %bitcast.8), channel_id=1, source_target_pairs={{0,1},{1,0},{2,3},{3,2},{4,5},{5,4},{6,7},{7,6},{8,9},{9,8},{10,11... | collective-permute-start | bytes 344072 | tf_op jit(solution)/shard_map/ppermute | solution.py:193
  13.8 0.9 %copy-start.3 = (s32[128,8]{0,1:T(8,128)S(1)}, s32[128,8]{0,1:T(8,128)}, u32[]{:S(2)}) copy-start(s32[128,8]{0,1:T(8,128)} %param.7) | copy-start | bytes 12292
  13.8 0.9 %copy-start.4 = (f32[128,8]{0,1:T(8,128)S(1)}, f32[128,8]{0,1:T(8,128)}, u32[]{:S(2)}) copy-start(f32[128,8]{0,1:T(8,128)} %param.8) | copy-start | bytes 12292
  14.4 1.4 %collective-permute-start.1 = (bf16[64,896]{1,0:T(8,128)(2,1)S(1)}, bf16[64,896]{1,0:T(8,128)(2,1)S(1)}, u32[]{:S(2)}, u32[]{:S(2)}) collective-permute-start(bf16[64,896]{1,0:T(8,128)(2,1)S(1)} %get-tuple-element.9.refs_2_), channel_id=1, source_target_pairs={{0,1},{1,0},{2,3},{3,2},{4,5},{5,4},{6,7},{7,6},{8,9},{9,8},{10,11... | collective-permute-start | bytes 344072 | tf_op jit(solution)/shard_map/ppermute | solution.py:200

commit v26 on v25

--- a/solution.py
+++ b/solution.py
@@ -35,12 +35,12 @@
 
 
 def first_order(ep_count, chip):
-    listed = ((2, 3, 1, 0), (3, 2, 1, 0))[chip % 2]
+    listed = ((3, 2, 0, 1), (3, 2, 1, 0))[chip % 2]
     return [z // 4 * 4 + listed[z % 4] for z in range(ep_count)]
 
 
 def second_order(ep_count, chip):
-    listed = ((3, 1, 2, 0), (3, 0, 2, 1))[chip % 2]
+    listed = ((2, 1, 0, 3), (3, 2, 1, 0))[chip % 2]
     return [z // 4 * 4 + listed[z % 4] for z in range(ep_count)]
 
 

time: 26.7 us -> 25.9 us (0.970)
  blocking collectives: 21 us -> 20.2 us
  starting transfers between devices: 0.67 us -> 0.33 us
  waiting for transfers between devices: 1.3 us -> 1.64 us
    all_to_all x2, blocking collectives: 21 us -> 20.2 us  [exchange(): return lax.all_to_all(rows, FAR, 0, 0, axis_index_groups=groups, tiled=True)]
where the time goes in v26:
time: 25.9 us; the launch traced here: 25.7 us
  blocking collectives  20.2 us (78%)
  Pallas kernels  3.43 us (13%)
  waiting for transfers between devices  1.64 us (6%)
  starting transfers between devices  0.33 us (1%)
    all_to_all x2, blocking collectives, exchange(): return lax.all_to_all(rows, FAR, 0, 0, axis_index_groups=groups, tiled=True)  20.2 us
    pallas_call x1, Pallas kernels, shards(): call(lambda *refs: route(ep_count, chips, *refs), 'route', half, in_specs...  1.26 us
    ppermute x1, waiting for transfers between devices, shards(): across = lax.ppermute(incoming, 'core', SWAP)  0.93 us
    pallas_call x1, Pallas kernels, shards(): call(combine, 'combine', jax.ShapeDtypeStruct((row_count, features), jnp....  0.87 us
    ppermute x1, waiting for transfers between devices, shards(): crossed = lax.ppermute(other, 'core', SWAP)  0.72 us
    pallas_call x1, Pallas kernels, shards(): call(lambda *refs: theirs(chips, *refs), 'theirs', (hidden_shape, half))  0.57 us
  transfers between devices with their start and end apart: 2, of which 2 were waited for; matrix products, arithmetic and copies ran while one was open for 0% of the time, Pallas kernels for 3%

profile of v26, /device:TPU:0, one launch (start us, length us, event | category | flops | bytes accessed | tf_op | source)
XLA Modules:
  0.0 25.7 jit_solution(13281949538198846770)
XLA Ops:
  0.0 0.0 copy-start
  0.0 0.0 copy-start.1
  0.0 1.3 %route.1 = bf16[64,896]{1,0:T(8,128)(2,1)S(1)} custom-call(s32[8,128]{1,0:T(8,128)} %bitcast.11, bf16[128,896]{1,0:T(8,128)(2,1)} %refs_1_.3), custom_call_target="tpu_custom_call" | custom-call | flops 2000000000 | tf_op jit(solution)/shard_map/route/pallas_call | solution.py:180
  1.3 12.2 %all_to_all.22 = bf16[8,8,896]{2,1,0:T(8,128)(2,1)S(1)} all-to-all(bf16[8,8,896]{2,1,0:T(8,128)(2,1)S(1)} %bitcast.10), channel_id=1, replica_groups={{12,8,0,4,15,11,7,3},{13,9,1,5,14,10,6,2},{28,24,16,20,31,27,23,19},{29..., dimensions={0} | all-to-all | bytes 229376 | tf_op jit(solution)/shard_map/all_to_all | solution.py:175
  13.4 0.0 copy-start.2
  13.4 0.1 collective-permute-start
  13.6 0.0 copy-done
  13.6 0.0 copy-done.1
  13.6 0.3 %begin.1.refs_1_ = f32[32,256]{1,0:T(8,128)S(1)} custom-call(bf16[64,896]{1,0:T(8,128)(2,1)S(1)} %bitcast.9, bf16[1,3584,128]{2,1,0:T(8,128)(2,1)S(1)} %copy-done, bf16[1,3584,128]{2,1,0:T(8,128)(2,1)S(1)} %copy-done.1), custom_call_target="tpu_custom_call" | custom-call | tf_op jit(solution)/shard_map/begin/pallas_call | solution.py:195
  13.8 0.9 %collective-permute-done.refs_0_ = bf16[64,896]{1,0:T(8,128)(2,1)S(1)} collective-permute-done((bf16[64,896]{1,0:T(8,128)(2,1)S(1)}, bf16[64,896]{1,0:T(8,128)(2,1)S(1)}, u32[]{:S(2)}, u32[]{:S(2)}) %collective-permute-start) | collective-permute-done | bytes 114720 | tf_op jit(solution)/shard_map/ppermute | solution.py:193
  14.8 0.0 copy-done.2
  14.8 0.0 copy-start.3
  14.8 0.0 copy-start.4
  14.8 0.6 %theirs.1 = (bf16[32,128]{1,0:T(8,128)(2,1)S(1)}, bf16[64,896]{1,0:T(8,128)(2,1)S(1)}) custom-call(bf16[64,896]{1,0:T(8,128)(2,1)S(1)} %collective-permute-done.refs_0_, f32[32,256]{1,0:T(8,128)S(1)} %begin.1.refs_1_, bf16[1,3584,128]{2,1,0:T(8,128)(2,1)S(1)} %copy-done, bf16[1,3584,128]{2,1,0:T(8,128)(2,1)S(1)} %copy-done.1, bf16[1,128,3584]{2,1,0:T(8,128)(2,1)S(1)} %copy-done.2), custom_call_target="tpu_custom_call" | custom-call | tf_op jit(solution)/shard_map/theirs/pallas_call | solution.py:197
  15.3 0.2 collective-permute-start.1
  15.6 0.0 copy-done.3
  15.6 0.0 copy-done.4
  15.6 0.2 score.1
  15.8 0.2 ours.1.mine_ref
  16.0 0.7 %collective-permute-done.1.other_ref = bf16[64,896]{1,0:T(8,128)(2,1)S(1)} collective-permute-done((bf16[64,896]{1,0:T(8,128)(2,1)S(1)}, bf16[64,896]{1,0:T(8,128)(2,1)S(1)}, u32[]{:S(2)}, u32[]{:S(2)}) %collective-permute-start.1) | collective-permute-done | bytes 114720 | tf_op jit(solution)/shard_map/ppermute | solution.py:200
  16.8 8.1 %all_to_all.23 = bf16[8,8,896]{2,1,0:T(8,128)(2,1)S(1)} all-to-all(bf16[8,8,896]{2,1,0:T(8,128)(2,1)S(1)} %bitcast.7), channel_id=1, replica_groups={{8,4,0,12,15,11,7,3},{9,5,1,13,14,10,6,2},{24,20,16,28,31,27,23,19},{25..., dimensions={0} | all-to-all | bytes 229376 | tf_op jit(solution)/shard_map/all_to_all | solution.py:175
  24.8 0.9 %combine.1 = bf16[128,896]{1,0:T(8,128)(2,1)} custom-call(bf16[128,64]{1,0:T(8,128)(2,1)S(1)} %get-tuple-element.10.match_ref, f32[128,1]{1,0:T(8,128)S(1)} %get-tuple-element.11._.weight_ref, bf16[64,896]{1,0:T(8,128)(2,1)S(1)} %bitcast.6), custom_call_target="tpu_custom_call" | custom-call | tf_op jit(solution)/shard_map/combine/pallas_call | solution.py:213
  (1 shorter events, 0.0 us)
Async XLA Ops:
  0.0 13.6 %copy-start = (bf16[1,3584,128]{2,1,0:T(8,128)(2,1)S(1)}, bf16[1,3584,128]{2,1,0:T(8,128)(2,1)}, u32[]{:S(2)}) copy-start(bf16[1,3584,128]{2,1,0:T(8,128)(2,1)} %refs_2_.3) | copy-start | bytes 2752516
  0.0 13.6 %copy-start.1 = (bf16[1,3584,128]{2,1,0:T(8,128)(2,1)S(1)}, bf16[1,3584,128]{2,1,0:T(8,128)(2,1)}, u32[]{:S(2)}) copy-start(bf16[1,3584,128]{2,1,0:T(8,128)(2,1)} %refs_3_.1) | copy-start | bytes 2752516
  13.4 1.3 %copy-start.2 = (bf16[1,128,3584]{2,1,0:T(8,128)(2,1)S(1)}, bf16[1,128,3584]{2,1,0:T(8,128)(2,1)}, u32[]{:S(2)}) copy-start(bf16[1,128,3584]{2,1,0:T(8,128)(2,1)} %refs_1_.5) | copy-start | bytes 2752516
  13.4 1.3 %collective-permute-start = (bf16[64,896]{1,0:T(8,128)(2,1)S(1)}, bf16[64,896]{1,0:T(8,128)(2,1)S(1)}, u32[]{:S(2)}, u32[]{:S(2)}) collective-permute-start(bf16[64,896]{1,0:T(8,128)(2,1)S(1)} %bitcast.8), channel_id=1, source_target_pairs={{0,1},{1,0},{2,3},{3,2},{4,5},{5,4},{6,7},{7,6},{8,9},{9,8},{10,11... | collective-permute-start | bytes 344072 | tf_op jit(solution)/shard_map/ppermute | solution.py:193
  14.8 0.8 %copy-start.3 = (s32[128,8]{0,1:T(8,128)S(1)}, s32[128,8]{0,1:T(8,128)}, u32[]{:S(2)}) copy-start(s32[128,8]{0,1:T(8,128)} %param.7) | copy-start | bytes 12292
  14.8 0.8 %copy-start.4 = (f32[128,8]{0,1:T(8,128)S(1)}, f32[128,8]{0,1:T(8,128)}, u32[]{:S(2)}) copy-start(f32[128,8]{0,1:T(8,128)} %param.8) | copy-start | bytes 12292
  15.3 1.4 %collective-permute-start.1 = (bf16[64,896]{1,0:T(8,128)(2,1)S(1)}, bf16[64,896]{1,0:T(8,128)(2,1)S(1)}, u32[]{:S(2)}, u32[]{:S(2)}) collective-permute-start(bf16[64,896]{1,0:T(8,128)(2,1)S(1)} %get-tuple-element.9.refs_2_), channel_id=1, source_target_pairs={{0,1},{1,0},{2,3},{3,2},{4,5},{5,4},{6,7},{7,6},{8,9},{9,8},{10,11... | collective-permute-start | bytes 344072 | tf_op jit(solution)/shard_map/ppermute | solution.py:200

commit v27 on v23

--- a/solution.py
+++ b/solution.py
@@ -35,7 +35,7 @@
 
 
 def first_order(ep_count, chip):
-    listed = ((2, 3, 0, 1), (3, 2, 1, 0))[chip % 2]
+    listed = ((2, 3, 0, 1), (2, 3, 1, 0))[chip % 2]
     return [z // 4 * 4 + listed[z % 4] for z in range(ep_count)]
 
 

time: 25.4 us -> 25.5 us (level)
  no operation moved by 1% of the time
where the time goes in v27:
time: 25.5 us; the launch traced here: 25.3 us
  blocking collectives  19.8 us (78%)
  Pallas kernels  3.44 us (13%)
  waiting for transfers between devices  1.33 us (5%)
  starting transfers between devices  0.64 us (3%)
    all_to_all x2, blocking collectives, exchange(): return lax.all_to_all(rows, FAR, 0, 0, axis_index_groups=groups, tiled=True)  19.8 us
    pallas_call x1, Pallas kernels, shards(): call(lambda *refs: route(ep_count, chips, *refs), 'route', half, in_specs...  1.26 us
    pallas_call x1, Pallas kernels, shards(): call(combine, 'combine', jax.ShapeDtypeStruct((row_count, features), jnp....  0.87 us
    ppermute x1, waiting for transfers between devices, shards(): across = lax.ppermute(incoming, 'core', SWAP)  0.75 us
    ppermute x1, waiting for transfers between devices, shards(): crossed = lax.ppermute(other, 'core', SWAP)  0.58 us
    pallas_call x1, Pallas kernels, shards(): call(lambda *refs: theirs(chips, *refs), 'theirs', (hidden_shape, half))  0.57 us
  transfers between devices with their start and end apart: 2, of which 2 were waited for; matrix products, arithmetic and copies ran while one was open for 0% of the time, Pallas kernels for 3%

profile of v27, /device:TPU:0, one launch (start us, length us, event | category | flops | bytes accessed | tf_op | source)
XLA Modules:
  0.0 25.3 jit_solution(8120256204074278433)
XLA Ops:
  0.0 0.0 copy-start
  0.0 0.0 copy-start.1
  0.0 1.3 %route.1 = bf16[64,896]{1,0:T(8,128)(2,1)S(1)} custom-call(s32[8,128]{1,0:T(8,128)} %bitcast.11, bf16[128,896]{1,0:T(8,128)(2,1)} %refs_1_.3), custom_call_target="tpu_custom_call" | custom-call | flops 2000000000 | tf_op jit(solution)/shard_map/route/pallas_call | solution.py:180
  1.3 11.8 %all_to_all.22 = bf16[8,8,896]{2,1,0:T(8,128)(2,1)S(1)} all-to-all(bf16[8,8,896]{2,1,0:T(8,128)(2,1)S(1)} %bitcast.10), channel_id=1, replica_groups={{8,12,0,4,11,15,7,3},{9,13,1,5,10,14,6,2},{24,28,16,20,27,31,23,19},{25..., dimensions={0} | all-to-all | bytes 229376 | tf_op jit(solution)/shard_map/all_to_all | solution.py:175
  13.1 0.0 copy-start.2
  13.1 0.3 %collective-permute-start = (bf16[64,896]{1,0:T(8,128)(2,1)S(1)}, bf16[64,896]{1,0:T(8,128)(2,1)S(1)}, u32[]{:S(2)}, u32[]{:S(2)}) collective-permute-start(bf16[64,896]{1,0:T(8,128)(2,1)S(1)} %bitcast.8), channel_id=1, source_target_pairs={{0,1},{1,0},{2,3},{3,2},{4,5},{5,4},{6,7},{7,6},{8,9},{9,8},{10,11... | collective-permute-start | bytes 344072 | tf_op jit(solution)/shard_map/ppermute | solution.py:193
  13.4 0.0 copy-done
  13.4 0.0 copy-done.1
  13.4 0.3 %begin.1.refs_1_ = f32[32,256]{1,0:T(8,128)S(1)} custom-call(bf16[64,896]{1,0:T(8,128)(2,1)S(1)} %bitcast.9, bf16[1,3584,128]{2,1,0:T(8,128)(2,1)S(1)} %copy-done, bf16[1,3584,128]{2,1,0:T(8,128)(2,1)S(1)} %copy-done.1), custom_call_target="tpu_custom_call" | custom-call | tf_op jit(solution)/shard_map/begin/pallas_call | solution.py:195
  13.7 0.8 %collective-permute-done.refs_0_ = bf16[64,896]{1,0:T(8,128)(2,1)S(1)} collective-permute-done((bf16[64,896]{1,0:T(8,128)(2,1)S(1)}, bf16[64,896]{1,0:T(8,128)(2,1)S(1)}, u32[]{:S(2)}, u32[]{:S(2)}) %collective-permute-start) | collective-permute-done | bytes 114720 | tf_op jit(solution)/shard_map/ppermute | solution.py:193
  14.4 0.0 copy-done.2
  14.4 0.0 copy-start.3
  14.4 0.0 copy-start.4
  14.4 0.6 %theirs.1 = (bf16[32,128]{1,0:T(8,128)(2,1)S(1)}, bf16[64,896]{1,0:T(8,128)(2,1)S(1)}) custom-call(bf16[64,896]{1,0:T(8,128)(2,1)S(1)} %collective-permute-done.refs_0_, f32[32,256]{1,0:T(8,128)S(1)} %begin.1.refs_1_, bf16[1,3584,128]{2,1,0:T(8,128)(2,1)S(1)} %copy-done, bf16[1,3584,128]{2,1,0:T(8,128)(2,1)S(1)} %copy-done.1, bf16[1,128,3584]{2,1,0:T(8,128)(2,1)S(1)} %copy-done.2), custom_call_target="tpu_custom_call" | custom-call | tf_op jit(solution)/shard_map/theirs/pallas_call | solution.py:197
  15.0 0.4 %collective-permute-start.1 = (bf16[64,896]{1,0:T(8,128)(2,1)S(1)}, bf16[64,896]{1,0:T(8,128)(2,1)S(1)}, u32[]{:S(2)}, u32[]{:S(2)}) collective-permute-start(bf16[64,896]{1,0:T(8,128)(2,1)S(1)} %get-tuple-element.9.refs_2_), channel_id=1, source_target_pairs={{0,1},{1,0},{2,3},{3,2},{4,5},{5,4},{6,7},{7,6},{8,9},{9,8},{10,11... | collective-permute-start | bytes 344072 | tf_op jit(solution)/shard_map/ppermute | solution.py:200
  15.3 0.0 copy-done.3
  15.3 0.0 copy-done.4
  15.3 0.2 score.1
  15.6 0.2 ours.1.mine_ref
  15.8 0.6 %collective-permute-done.1.other_ref = bf16[64,896]{1,0:T(8,128)(2,1)S(1)} collective-permute-done((bf16[64,896]{1,0:T(8,128)(2,1)S(1)}, bf16[64,896]{1,0:T(8,128)(2,1)S(1)}, u32[]{:S(2)}, u32[]{:S(2)}) %collective-permute-start.1) | collective-permute-done | bytes 114720 | tf_op jit(solution)/shard_map/ppermute | solution.py:200
  16.4 8.0 %all_to_all.23 = bf16[8,8,896]{2,1,0:T(8,128)(2,1)S(1)} all-to-all(bf16[8,8,896]{2,1,0:T(8,128)(2,1)S(1)} %bitcast.7), channel_id=1, replica_groups={{8,4,0,12,15,11,3,7},{9,5,1,13,14,10,2,6},{24,20,16,28,31,27,19,23},{25..., dimensions={0} | all-to-all | bytes 229376 | tf_op jit(solution)/shard_map/all_to_all | solution.py:175
  24.4 0.9 %combine.1 = bf16[128,896]{1,0:T(8,128)(2,1)} custom-call(bf16[128,64]{1,0:T(8,128)(2,1)S(1)} %get-tuple-element.10.match_ref, f32[128,1]{1,0:T(8,128)S(1)} %get-tuple-element.11._.weight_ref, bf16[64,896]{1,0:T(8,128)(2,1)S(1)} %bitcast.6), custom_call_target="tpu_custom_call" | custom-call | tf_op jit(solution)/shard_map/combine/pallas_call | solution.py:213
  (1 shorter events, 0.0 us)
Async XLA Ops:
  0.0 13.4 %copy-start = (bf16[1,3584,128]{2,1,0:T(8,128)(2,1)S(1)}, bf16[1,3584,128]{2,1,0:T(8,128)(2,1)}, u32[]{:S(2)}) copy-start(bf16[1,3584,128]{2,1,0:T(8,128)(2,1)} %refs_2_.3) | copy-start | bytes 2752516
  0.0 13.4 %copy-start.1 = (bf16[1,3584,128]{2,1,0:T(8,128)(2,1)S(1)}, bf16[1,3584,128]{2,1,0:T(8,128)(2,1)}, u32[]{:S(2)}) copy-start(bf16[1,3584,128]{2,1,0:T(8,128)(2,1)} %refs_3_.1) | copy-start | bytes 2752516
  13.1 1.3 %copy-start.2 = (bf16[1,128,3584]{2,1,0:T(8,128)(2,1)S(1)}, bf16[1,128,3584]{2,1,0:T(8,128)(2,1)}, u32[]{:S(2)}) copy-start(bf16[1,128,3584]{2,1,0:T(8,128)(2,1)} %refs_1_.5) | copy-start | bytes 2752516
  13.1 1.3 %collective-permute-start = (bf16[64,896]{1,0:T(8,128)(2,1)S(1)}, bf16[64,896]{1,0:T(8,128)(2,1)S(1)}, u32[]{:S(2)}, u32[]{:S(2)}) collective-permute-start(bf16[64,896]{1,0:T(8,128)(2,1)S(1)} %bitcast.8), channel_id=1, source_target_pairs={{0,1},{1,0},{2,3},{3,2},{4,5},{5,4},{6,7},{7,6},{8,9},{9,8},{10,11... | collective-permute-start | bytes 344072 | tf_op jit(solution)/shard_map/ppermute | solution.py:193
  14.4 0.9 %copy-start.3 = (s32[128,8]{0,1:T(8,128)S(1)}, s32[128,8]{0,1:T(8,128)}, u32[]{:S(2)}) copy-start(s32[128,8]{0,1:T(8,128)} %param.7) | copy-start | bytes 12292
  14.4 0.9 %copy-start.4 = (f32[128,8]{0,1:T(8,128)S(1)}, f32[128,8]{0,1:T(8,128)}, u32[]{:S(2)}) copy-start(f32[128,8]{0,1:T(8,128)} %param.8) | copy-start | bytes 12292
  15.0 1.4 %collective-permute-start.1 = (bf16[64,896]{1,0:T(8,128)(2,1)S(1)}, bf16[64,896]{1,0:T(8,128)(2,1)S(1)}, u32[]{:S(2)}, u32[]{:S(2)}) collective-permute-start(bf16[64,896]{1,0:T(8,128)(2,1)S(1)} %get-tuple-element.9.refs_2_), channel_id=1, source_target_pairs={{0,1},{1,0},{2,3},{3,2},{4,5},{5,4},{6,7},{7,6},{8,9},{9,8},{10,11... | collective-permute-start | bytes 344072 | tf_op jit(solution)/shard_map/ppermute | solution.py:200

commit v28 on v23

--- a/solution.py
+++ b/solution.py
@@ -8,6 +8,8 @@
 CAP = 8
 PIECE = 32
 FETCH = 16
+FIRST_MIRRORED = 1
+SECOND_MIRRORED = 0
 FAR = ("ep", "chip", "core")
 SWAP = [(0, 1), (1, 0)]
 LIMIT = pltpu.CompilerParams(vmem_limit_bytes=16 * 1024 * 1024)
@@ -84,15 +86,22 @@
     weight_ref[...] = to_column(2.5 * chosen / jnp.sum(squashed, axis=0, keepdims=True))
 
 
-def far_groups(order, ep_count, chips):
+def far_groups(order, mirrored, ep_count, chips):
     return [
-        [(z * chips + x) * 2 + (side + x) % 2 for x in range(chips) for z in order(ep_count, x)]
+        [
+            (z * chips + x) * 2 + (side + x) % 2
+            for block in range(chips)
+            for x in [(block + side * mirrored) % chips]
+            for z in order(ep_count, block)
+        ]
         for side in range(2)
     ]
 
 
-def columns_of(chip, own, features):
-    core = lax.rem(lax.axis_index("core") + lax.axis_index("chip") + chip + (0 if own else 1), 2)
+def columns_of(block, own, mirrored, features):
+    side = lax.rem(lax.axis_index("core") + lax.axis_index("chip") + (0 if own else 1), 2)
+    chip = lax.rem(block + side * mirrored, lax.axis_size("chip"))
+    core = lax.rem(side + chip, 2)
     return pl.ds(pl.multiple_of((2 * chip + core) * features, features), features)
 
 
@@ -109,7 +118,7 @@
     total = jnp.zeros((part_rows, 2 * gate_ref.shape[2]), jnp.float32)
     for chip in range(chips):
         rows = rows_ref[chip * part_rows : (chip + 1) * part_rows, :]
-        columns = columns_of(chip, own, features)
+        columns = columns_of(chip, own, FIRST_MIRRORED, features)
         both = jnp.concatenate([gate_ref[0, columns, :], up_ref[0, columns, :]], axis=1)
         acts = jnp.dot(rows, both, preferred_element_type=jnp.float32)
         total += in_order(acts, first_order(ep_count, chip), first_order(ep_count, 0))
@@ -120,7 +129,7 @@
     part_rows, features = out_ref.shape[0] // chips, out_ref.shape[1]
     ep_count = part_rows // CAP
     for chip in range(chips):
-        columns = columns_of(chip, own, features)
+        columns = columns_of(chip, own, SECOND_MIRRORED, features)
         values = jnp.dot(hidden, down_ref[0, :, columns], preferred_element_type=jnp.float32)
         values = in_order(values, first_order(ep_count, 0), second_order(ep_count, chip))
         out_ref[chip * part_rows : (chip + 1) * part_rows, :] = values.astype(jnp.bfloat16)
@@ -170,8 +179,8 @@
     hbm, vmem = (pl.BlockSpec(memory_space=space) for space in (pltpu.HBM, pltpu.VMEM))
     anywhere = pl.BlockSpec(memory_space=pl.ANY)
 
-    def exchange(rows, order):
-        groups = far_groups(order, ep_count, chips)
+    def exchange(rows, order, mirrored):
+        groups = far_groups(order, mirrored, ep_count, chips)
         return lax.all_to_all(rows, FAR, 0, 0, axis_index_groups=groups, tiled=True)
 
     def call(kernel, name, out_shape, **rest):
@@ -189,7 +198,7 @@
         ],
         cost_estimate=pl.CostEstimate(flops=2 * 10**9, bytes_accessed=0, transcendentals=0),
     )(*(pltpu.with_memory_space_constraint(value, pltpu.HBM) for value in (ids, tokens)))
-    incoming = exchange(outgoing, first_order)
+    incoming = exchange(outgoing, first_order, FIRST_MIRRORED)
     across = lax.ppermute(incoming, "core", SWAP)
     acts = jax.ShapeDtypeStruct((slot_count, 2 * hidden_count), jnp.float32)
     begun = call(lambda *refs: begin(chips, *refs), "begin", acts)(incoming, w_gate, w_up)
@@ -209,7 +218,7 @@
         in_specs=[vmem] * 2 + [anywhere],
     )(ids, scores, other)
     summed = call(add, "add", half, in_specs=[vmem] * 2 + [anywhere])(mine, crossed, weight)
-    returned = exchange(summed, second_order)
+    returned = exchange(summed, second_order, SECOND_MIRRORED)
     return call(
         combine,
         "combine",

time: 25.4 us -> 25.7 us (1.012)
  starting transfers between devices: 0.83 us -> 0.2 us
  waiting for transfers between devices: 1.19 us -> 1.72 us
  blocking collectives: 19.8 us -> 20.1 us
    ppermute x1, starting transfers between devices: 0.4 us -> 0.01 us  [shards(): across = lax.ppermute(incoming, 'core', SWAP)]
    ppermute x1, waiting for transfers between devices: 0.68 us -> 1 us  [shards(): across = lax.ppermute(incoming, 'core', SWAP)]
    all_to_all x2, blocking collectives: 19.8 us -> 20.1 us  [exchange(): return lax.all_to_all(rows, FAR, 0, 0, axis_index_groups=groups, tiled=True)]
where the time goes in v28:
time: 25.7 us; the launch traced here: 25.4 us
  blocking collectives  20.1 us (78%)
  Pallas kernels  3.37 us (13%)
  waiting for transfers between devices  1.72 us (7%)
    all_to_all x2, blocking collectives, exchange(): return lax.all_to_all(rows, FAR, 0, 0, axis_index_groups=groups, tiled=True)  20.1 us
    pallas_call x1, Pallas kernels, shards(): call(lambda *refs: route(ep_count, chips, *refs), 'route', half, in_specs...  1.26 us
    ppermute x1, waiting for transfers between devices, shards(): across = lax.ppermute(incoming, 'core', SWAP)  1 us
    pallas_call x1, Pallas kernels, shards(): call(combine, 'combine', jax.ShapeDtypeStruct((row_count, features), jnp....  0.87 us
    ppermute x1, waiting for transfers between devices, shards(): crossed = lax.ppermute(other, 'core', SWAP)  0.71 us
  transfers between devices with their start and end apart: 2, of which 2 were waited for; matrix products, arithmetic and copies ran while one was open for 0% of the time, Pallas kernels for 3%

profile of v28, /device:TPU:0, one launch (start us, length us, event | category | flops | bytes accessed | tf_op | source)
XLA Modules:
  0.0 25.4 jit_solution(5145511631004943982)
XLA Ops:
  0.0 0.0 copy-start
  0.0 0.0 copy-start.1
  0.0 1.3 %route.1 = bf16[64,896]{1,0:T(8,128)(2,1)S(1)} custom-call(s32[8,128]{1,0:T(8,128)} %bitcast.11, bf16[128,896]{1,0:T(8,128)(2,1)} %refs_1_.3), custom_call_target="tpu_custom_call" | custom-call | flops 2000000000 | tf_op jit(solution)/shard_map/route/pallas_call | solution.py:189
  1.3 11.8 %all_to_all.22 = bf16[8,8,896]{2,1,0:T(8,128)(2,1)S(1)} all-to-all(bf16[8,8,896]{2,1,0:T(8,128)(2,1)S(1)} %bitcast.10), channel_id=1, replica_groups={{8,12,0,4,15,11,7,3},{10,14,2,6,13,9,5,1},{24,28,16,20,31,27,23,19},{26..., dimensions={0} | all-to-all | bytes 229376 | tf_op jit(solution)/shard_map/all_to_all | solution.py:184
  13.1 0.0 copy-start.2
  13.1 0.0 collective-permute-start
  13.1 0.0 copy-done
  13.1 0.0 copy-done.1
  13.1 0.3 %begin.1.refs_1_ = f32[32,256]{1,0:T(8,128)S(1)} custom-call(bf16[64,896]{1,0:T(8,128)(2,1)S(1)} %bitcast.9, bf16[1,3584,128]{2,1,0:T(8,128)(2,1)S(1)} %copy-done, bf16[1,3584,128]{2,1,0:T(8,128)(2,1)S(1)} %copy-done.1), custom_call_target="tpu_custom_call" | custom-call | tf_op jit(solution)/shard_map/begin/pallas_call | solution.py:204
  13.4 1.0 %collective-permute-done.refs_0_ = bf16[64,896]{1,0:T(8,128)(2,1)S(1)} collective-permute-done((bf16[64,896]{1,0:T(8,128)(2,1)S(1)}, bf16[64,896]{1,0:T(8,128)(2,1)S(1)}, u32[]{:S(2)}, u32[]{:S(2)}) %collective-permute-start) | collective-permute-done | bytes 114720 | tf_op jit(solution)/shard_map/ppermute | solution.py:202
  14.4 0.0 copy-done.2
  14.4 0.0 copy-start.3
  14.4 0.0 copy-start.4
  14.4 0.5 %theirs.1 = (bf16[32,128]{1,0:T(8,128)(2,1)S(1)}, bf16[64,896]{1,0:T(8,128)(2,1)S(1)}) custom-call(bf16[64,896]{1,0:T(8,128)(2,1)S(1)} %collective-permute-done.refs_0_, f32[32,256]{1,0:T(8,128)S(1)} %begin.1.refs_1_, bf16[1,3584,128]{2,1,0:T(8,128)(2,1)S(1)} %copy-done, bf16[1,3584,128]{2,1,0:T(8,128)(2,1)S(1)} %copy-done.1, bf16[1,128,3584]{2,1,0:T(8,128)(2,1)S(1)} %copy-done.2), custom_call_target="tpu_custom_call" | custom-call | tf_op jit(solution)/shard_map/theirs/pallas_call | solution.py:206
  14.9 0.2 collective-permute-start.1
  15.1 0.0 copy-done.3
  15.1 0.0 copy-done.4
  15.1 0.2 score.1
  15.3 0.2 ours.1.mine_ref
  15.6 0.7 %collective-permute-done.1.other_ref = bf16[64,896]{1,0:T(8,128)(2,1)S(1)} collective-permute-done((bf16[64,896]{1,0:T(8,128)(2,1)S(1)}, bf16[64,896]{1,0:T(8,128)(2,1)S(1)}, u32[]{:S(2)}, u32[]{:S(2)}) %collective-permute-start.1) | collective-permute-done | bytes 114720 | tf_op jit(solution)/shard_map/ppermute | solution.py:209
  16.3 8.3 %all_to_all.23 = bf16[8,8,896]{2,1,0:T(8,128)(2,1)S(1)} all-to-all(bf16[8,8,896]{2,1,0:T(8,128)(2,1)S(1)} %bitcast.7), channel_id=1, replica_groups={{8,4,0,12,15,11,3,7},{9,5,1,13,14,10,2,6},{24,20,16,28,31,27,19,23},{25..., dimensions={0} | all-to-all | bytes 229376 | tf_op jit(solution)/shard_map/all_to_all | solution.py:184
  24.6 0.9 %combine.1 = bf16[128,896]{1,0:T(8,128)(2,1)} custom-call(bf16[128,64]{1,0:T(8,128)(2,1)S(1)} %get-tuple-element.10.match_ref, f32[128,1]{1,0:T(8,128)S(1)} %get-tuple-element.11._.weight_ref, bf16[64,896]{1,0:T(8,128)(2,1)S(1)} %bitcast.6), custom_call_target="tpu_custom_call" | custom-call | tf_op jit(solution)/shard_map/combine/pallas_call | solution.py:222
  (1 shorter events, 0.0 us)
Async XLA Ops:
  0.0 13.1 %copy-start = (bf16[1,3584,128]{2,1,0:T(8,128)(2,1)S(1)}, bf16[1,3584,128]{2,1,0:T(8,128)(2,1)}, u32[]{:S(2)}) copy-start(bf16[1,3584,128]{2,1,0:T(8,128)(2,1)} %refs_2_.3) | copy-start | bytes 2752516
  0.0 13.1 %copy-start.1 = (bf16[1,3584,128]{2,1,0:T(8,128)(2,1)S(1)}, bf16[1,3584,128]{2,1,0:T(8,128)(2,1)}, u32[]{:S(2)}) copy-start(bf16[1,3584,128]{2,1,0:T(8,128)(2,1)} %refs_3_.1) | copy-start | bytes 2752516
  13.1 1.3 %copy-start.2 = (bf16[1,128,3584]{2,1,0:T(8,128)(2,1)S(1)}, bf16[1,128,3584]{2,1,0:T(8,128)(2,1)}, u32[]{:S(2)}) copy-start(bf16[1,128,3584]{2,1,0:T(8,128)(2,1)} %refs_1_.5) | copy-start | bytes 2752516
  13.1 1.3 %collective-permute-start = (bf16[64,896]{1,0:T(8,128)(2,1)S(1)}, bf16[64,896]{1,0:T(8,128)(2,1)S(1)}, u32[]{:S(2)}, u32[]{:S(2)}) collective-permute-start(bf16[64,896]{1,0:T(8,128)(2,1)S(1)} %bitcast.8), channel_id=1, source_target_pairs={{0,1},{1,0},{2,3},{3,2},{4,5},{5,4},{6,7},{7,6},{8,9},{9,8},{10,11... | collective-permute-start | bytes 344072 | tf_op jit(solution)/shard_map/ppermute | solution.py:202
  14.4 0.7 %copy-start.3 = (s32[128,8]{0,1:T(8,128)S(1)}, s32[128,8]{0,1:T(8,128)}, u32[]{:S(2)}) copy-start(s32[128,8]{0,1:T(8,128)} %param.7) | copy-start | bytes 12292
  14.4 0.7 %copy-start.4 = (f32[128,8]{0,1:T(8,128)S(1)}, f32[128,8]{0,1:T(8,128)}, u32[]{:S(2)}) copy-start(f32[128,8]{0,1:T(8,128)} %param.8) | copy-start | bytes 12292
  14.9 1.4 %collective-permute-start.1 = (bf16[64,896]{1,0:T(8,128)(2,1)S(1)}, bf16[64,896]{1,0:T(8,128)(2,1)S(1)}, u32[]{:S(2)}, u32[]{:S(2)}) collective-permute-start(bf16[64,896]{1,0:T(8,128)(2,1)S(1)} %get-tuple-element.9.refs_2_), channel_id=1, source_target_pairs={{0,1},{1,0},{2,3},{3,2},{4,5},{5,4},{6,7},{7,6},{8,9},{9,8},{10,11... | collective-permute-start | bytes 344072 | tf_op jit(solution)/shard_map/ppermute | solution.py:209

commit v29 on v26

--- a/solution.py
+++ b/solution.py
@@ -35,7 +35,7 @@
 
 
 def first_order(ep_count, chip):
-    listed = ((3, 2, 0, 1), (3, 2, 1, 0))[chip % 2]
+    listed = ((2, 3, 1, 0), (3, 2, 1, 0))[chip % 2]
     return [z // 4 * 4 + listed[z % 4] for z in range(ep_count)]
 
 

time: 25.9 us -> 25.8 us (level)
  starting transfers between devices: 0.33 us -> 0.67 us
  waiting for transfers between devices: 1.64 us -> 1.3 us
where the time goes in v29:
time: 25.8 us; the launch traced here: 25.6 us
  blocking collectives  20.1 us (78%)
  Pallas kernels  3.44 us (13%)
  waiting for transfers between devices  1.3 us (5%)
  starting transfers between devices  0.67 us (3%)
    all_to_all x2, blocking collectives, exchange(): return lax.all_to_all(rows, FAR, 0, 0, axis_index_groups=groups, tiled=True)  20.1 us
    pallas_call x1, Pallas kernels, shards(): call(lambda *refs: route(ep_count, chips, *refs), 'route', half, in_specs...  1.26 us
    pallas_call x1, Pallas kernels, shards(): call(combine, 'combine', jax.ShapeDtypeStruct((row_count, features), jnp....  0.87 us
    ppermute x1, waiting for transfers between devices, shards(): across = lax.ppermute(incoming, 'core', SWAP)  0.74 us
    pallas_call x1, Pallas kernels, shards(): call(lambda *refs: theirs(chips, *refs), 'theirs', (hidden_shape, half))  0.57 us
    ppermute x1, waiting for transfers between devices, shards(): crossed = lax.ppermute(other, 'core', SWAP)  0.56 us
  transfers between devices with their start and end apart: 2, of which 2 were waited for; matrix products, arithmetic and copies ran while one was open for 0% of the time, Pallas kernels for 3%

profile of v29, /device:TPU:0, one launch (start us, length us, event | category | flops | bytes accessed | tf_op | source)
XLA Modules:
  0.0 25.6 jit_solution(6393122859413445347)
XLA Ops:
  0.0 0.0 copy-start
  0.0 0.0 copy-start.1
  0.0 1.3 %route.1 = bf16[64,896]{1,0:T(8,128)(2,1)S(1)} custom-call(s32[8,128]{1,0:T(8,128)} %bitcast.11, bf16[128,896]{1,0:T(8,128)(2,1)} %refs_1_.3), custom_call_target="tpu_custom_call" | custom-call | flops 2000000000 | tf_op jit(solution)/shard_map/route/pallas_call | solution.py:180
  1.3 11.2 %all_to_all.22 = bf16[8,8,896]{2,1,0:T(8,128)(2,1)S(1)} all-to-all(bf16[8,8,896]{2,1,0:T(8,128)(2,1)S(1)} %bitcast.10), channel_id=1, replica_groups={{8,12,4,0,15,11,7,3},{9,13,5,1,14,10,6,2},{24,28,20,16,31,27,23,19},{25..., dimensions={0} | all-to-all | bytes 229376 | tf_op jit(solution)/shard_map/all_to_all | solution.py:175
  12.4 0.0 copy-start.2
  12.4 0.3 %collective-permute-start = (bf16[64,896]{1,0:T(8,128)(2,1)S(1)}, bf16[64,896]{1,0:T(8,128)(2,1)S(1)}, u32[]{:S(2)}, u32[]{:S(2)}) collective-permute-start(bf16[64,896]{1,0:T(8,128)(2,1)S(1)} %bitcast.8), channel_id=1, source_target_pairs={{0,1},{1,0},{2,3},{3,2},{4,5},{5,4},{6,7},{7,6},{8,9},{9,8},{10,11... | collective-permute-start | bytes 344072 | tf_op jit(solution)/shard_map/ppermute | solution.py:193
  12.8 0.0 copy-done
  12.8 0.0 copy-done.1
  12.8 0.3 %begin.1.refs_1_ = f32[32,256]{1,0:T(8,128)S(1)} custom-call(bf16[64,896]{1,0:T(8,128)(2,1)S(1)} %bitcast.9, bf16[1,3584,128]{2,1,0:T(8,128)(2,1)S(1)} %copy-done, bf16[1,3584,128]{2,1,0:T(8,128)(2,1)S(1)} %copy-done.1), custom_call_target="tpu_custom_call" | custom-call | tf_op jit(solution)/shard_map/begin/pallas_call | solution.py:195
  13.0 0.7 %collective-permute-done.refs_0_ = bf16[64,896]{1,0:T(8,128)(2,1)S(1)} collective-permute-done((bf16[64,896]{1,0:T(8,128)(2,1)S(1)}, bf16[64,896]{1,0:T(8,128)(2,1)S(1)}, u32[]{:S(2)}, u32[]{:S(2)}) %collective-permute-start) | collective-permute-done | bytes 114720 | tf_op jit(solution)/shard_map/ppermute | solution.py:193
  13.8 0.0 copy-done.2
  13.8 0.0 copy-start.3
  13.8 0.0 copy-start.4
  13.8 0.6 %theirs.1 = (bf16[32,128]{1,0:T(8,128)(2,1)S(1)}, bf16[64,896]{1,0:T(8,128)(2,1)S(1)}) custom-call(bf16[64,896]{1,0:T(8,128)(2,1)S(1)} %collective-permute-done.refs_0_, f32[32,256]{1,0:T(8,128)S(1)} %begin.1.refs_1_, bf16[1,3584,128]{2,1,0:T(8,128)(2,1)S(1)} %copy-done, bf16[1,3584,128]{2,1,0:T(8,128)(2,1)S(1)} %copy-done.1, bf16[1,128,3584]{2,1,0:T(8,128)(2,1)S(1)} %copy-done.2), custom_call_target="tpu_custom_call" | custom-call | tf_op jit(solution)/shard_map/theirs/pallas_call | solution.py:197
  14.4 0.4 %collective-permute-start.1 = (bf16[64,896]{1,0:T(8,128)(2,1)S(1)}, bf16[64,896]{1,0:T(8,128)(2,1)S(1)}, u32[]{:S(2)}, u32[]{:S(2)}) collective-permute-start(bf16[64,896]{1,0:T(8,128)(2,1)S(1)} %get-tuple-element.9.refs_2_), channel_id=1, source_target_pairs={{0,1},{1,0},{2,3},{3,2},{4,5},{5,4},{6,7},{7,6},{8,9},{9,8},{10,11... | collective-permute-start | bytes 344072 | tf_op jit(solution)/shard_map/ppermute | solution.py:200
  14.7 0.0 copy-done.3
  14.7 0.0 copy-done.4
  14.7 0.2 score.1
  15.0 0.2 ours.1.mine_ref
  15.2 0.6 %collective-permute-done.1.other_ref = bf16[64,896]{1,0:T(8,128)(2,1)S(1)} collective-permute-done((bf16[64,896]{1,0:T(8,128)(2,1)S(1)}, bf16[64,896]{1,0:T(8,128)(2,1)S(1)}, u32[]{:S(2)}, u32[]{:S(2)}) %collective-permute-start.1) | collective-permute-done | bytes 114720 | tf_op jit(solution)/shard_map/ppermute | solution.py:200
  15.8 9.0 %all_to_all.23 = bf16[8,8,896]{2,1,0:T(8,128)(2,1)S(1)} all-to-all(bf16[8,8,896]{2,1,0:T(8,128)(2,1)S(1)} %bitcast.7), channel_id=1, replica_groups={{8,4,0,12,15,11,7,3},{9,5,1,13,14,10,6,2},{24,20,16,28,31,27,23,19},{25..., dimensions={0} | all-to-all | bytes 229376 | tf_op jit(solution)/shard_map/all_to_all | solution.py:175
  24.7 0.9 %combine.1 = bf16[128,896]{1,0:T(8,128)(2,1)} custom-call(bf16[128,64]{1,0:T(8,128)(2,1)S(1)} %get-tuple-element.10.match_ref, f32[128,1]{1,0:T(8,128)S(1)} %get-tuple-element.11._.weight_ref, bf16[64,896]{1,0:T(8,128)(2,1)S(1)} %bitcast.6), custom_call_target="tpu_custom_call" | custom-call | tf_op jit(solution)/shard_map/combine/pallas_call | solution.py:213
  (1 shorter events, 0.0 us)
Async XLA Ops:
  0.0 12.8 %copy-start = (bf16[1,3584,128]{2,1,0:T(8,128)(2,1)S(1)}, bf16[1,3584,128]{2,1,0:T(8,128)(2,1)}, u32[]{:S(2)}) copy-start(bf16[1,3584,128]{2,1,0:T(8,128)(2,1)} %refs_2_.3) | copy-start | bytes 2752516
  0.0 12.8 %copy-start.1 = (bf16[1,3584,128]{2,1,0:T(8,128)(2,1)S(1)}, bf16[1,3584,128]{2,1,0:T(8,128)(2,1)}, u32[]{:S(2)}) copy-start(bf16[1,3584,128]{2,1,0:T(8,128)(2,1)} %refs_3_.1) | copy-start | bytes 2752516
  12.4 1.3 %copy-start.2 = (bf16[1,128,3584]{2,1,0:T(8,128)(2,1)S(1)}, bf16[1,128,3584]{2,1,0:T(8,128)(2,1)}, u32[]{:S(2)}) copy-start(bf16[1,128,3584]{2,1,0:T(8,128)(2,1)} %refs_1_.5) | copy-start | bytes 2752516
  12.4 1.3 %collective-permute-start = (bf16[64,896]{1,0:T(8,128)(2,1)S(1)}, bf16[64,896]{1,0:T(8,128)(2,1)S(1)}, u32[]{:S(2)}, u32[]{:S(2)}) collective-permute-start(bf16[64,896]{1,0:T(8,128)(2,1)S(1)} %bitcast.8), channel_id=1, source_target_pairs={{0,1},{1,0},{2,3},{3,2},{4,5},{5,4},{6,7},{7,6},{8,9},{9,8},{10,11... | collective-permute-start | bytes 344072 | tf_op jit(solution)/shard_map/ppermute | solution.py:193
  13.8 0.9 %copy-start.3 = (s32[128,8]{0,1:T(8,128)S(1)}, s32[128,8]{0,1:T(8,128)}, u32[]{:S(2)}) copy-start(s32[128,8]{0,1:T(8,128)} %param.7) | copy-start | bytes 12292
  13.8 0.9 %copy-start.4 = (f32[128,8]{0,1:T(8,128)S(1)}, f32[128,8]{0,1:T(8,128)}, u32[]{:S(2)}) copy-start(f32[128,8]{0,1:T(8,128)} %param.8) | copy-start | bytes 12292
  14.4 1.4 %collective-permute-start.1 = (bf16[64,896]{1,0:T(8,128)(2,1)S(1)}, bf16[64,896]{1,0:T(8,128)(2,1)S(1)}, u32[]{:S(2)}, u32[]{:S(2)}) collective-permute-start(bf16[64,896]{1,0:T(8,128)(2,1)S(1)} %get-tuple-element.9.refs_2_), channel_id=1, source_target_pairs={{0,1},{1,0},{2,3},{3,2},{4,5},{5,4},{6,7},{7,6},{8,9},{9,8},{10,11... | collective-permute-start | bytes 344072 | tf_op jit(solution)/shard_map/ppermute | solution.py:200

commit v30 on v27

--- a/solution.py
+++ b/solution.py
@@ -34,9 +34,8 @@
     return expert * CAP + jnp.sum(counts * onehot, axis=0, keepdims=True), expert
 
 
-def first_order(ep_count, chip):
-    listed = ((2, 3, 0, 1), (2, 3, 1, 0))[chip % 2]
-    return [z // 4 * 4 + listed[z % 4] for z in range(ep_count)]
+def first_members(ep_count, chips):
+    return [(x, z) for z in range(ep_count) for x in range(chips)]
 
 
 def second_order(ep_count, chip):
@@ -44,9 +43,13 @@
     return [z // 4 * 4 + listed[z % 4] for z in range(ep_count)]
 
 
-def row_codes(index, order, ep_count, chips):
-    listed = [z for chip in range(chips) for z in order(ep_count, chip)]
-    expert = sum(jnp.where(index // CAP == at, z // 2, 0) for at, z in enumerate(listed))
+def second_members(ep_count, chips):
+    return [(x, z) for x in range(chips) for z in second_order(ep_count, x)]
+
+
+def row_codes(index, members, ep_count, chips):
+    listed = members(ep_count, chips)
+    expert = sum(jnp.where(index // CAP == at, z // 2, 0) for at, (_, z) in enumerate(listed))
     return (expert * CAP + lax.rem(index, CAP)).astype(jnp.float32)
 
 
@@ -63,7 +66,7 @@
     ]
     for copy in copies:
         copy.start()
-    wanted = row_codes(iota((outgoing_ref.shape[0], row_count), 0), first_order, ep_count, chips)
+    wanted = row_codes(iota((outgoing_ref.shape[0], row_count), 0), first_members, ep_count, chips)
     copies[0].wait()
     code, _ = slot_codes(ids_ref[...].astype(jnp.float32), ep_count // 2)
     dispatch = jnp.where(code == wanted, 1.0, 0.0).astype(jnp.bfloat16)
@@ -77,16 +80,16 @@
 def score(ep_count, chips, ids_ref, scores_ref, _, match_ref, weight_ref):
     ids = ids_ref[...].astype(jnp.float32)
     code, expert = slot_codes(ids, ep_count // 2)
-    wanted = row_codes(iota(match_ref.shape, 1), second_order, ep_count, chips)
+    wanted = row_codes(iota(match_ref.shape, 1), second_members, ep_count, chips)
     match_ref[...] = jnp.where(to_column(code) == wanted, 1.0, 0.0).astype(jnp.bfloat16)
     squashed = jax.nn.sigmoid(scores_ref[...])
     chosen = jnp.sum(jnp.where(ids == expert, squashed, 0.0), axis=0, keepdims=True)
     weight_ref[...] = to_column(2.5 * chosen / jnp.sum(squashed, axis=0, keepdims=True))
 
 
-def far_groups(order, ep_count, chips):
+def far_groups(members, ep_count, chips):
     return [
-        [(z * chips + x) * 2 + (side + x) % 2 for x in range(chips) for z in order(ep_count, x)]
+        [(z * chips + x) * 2 + (side + x) % 2 for x, z in members(ep_count, chips)]
         for side in range(2)
     ]
 
@@ -104,15 +107,16 @@
 
 
 def lift(chips, own, rows_ref, gate_ref, up_ref):
-    part_rows, features = rows_ref.shape[0] // chips, rows_ref.shape[1]
-    ep_count = part_rows // CAP
-    total = jnp.zeros((part_rows, 2 * gate_ref.shape[2]), jnp.float32)
+    rows, features = rows_ref[...], rows_ref.shape[1]
+    ep_count = rows_ref.shape[0] // (CAP * chips)
+    members = first_members(ep_count, chips)
+    total = jnp.zeros((ep_count * CAP, 2 * gate_ref.shape[2]), jnp.float32)
     for chip in range(chips):
-        rows = rows_ref[chip * part_rows : (chip + 1) * part_rows, :]
         columns = columns_of(chip, own, features)
         both = jnp.concatenate([gate_ref[0, columns, :], up_ref[0, columns, :]], axis=1)
         acts = jnp.dot(rows, both, preferred_element_type=jnp.float32)
-        total += in_order(acts, first_order(ep_count, chip), first_order(ep_count, 0))
+        places = [members.index((chip, z)) * CAP for z in range(ep_count)]
+        total += jnp.concatenate([acts[at : at + CAP, :] for at in places], axis=0)
     return total
 
 
@@ -122,7 +126,7 @@
     for chip in range(chips):
         columns = columns_of(chip, own, features)
         values = jnp.dot(hidden, down_ref[0, :, columns], preferred_element_type=jnp.float32)
-        values = in_order(values, first_order(ep_count, 0), second_order(ep_count, chip))
+        values = in_order(values, list(range(ep_count)), second_order(ep_count, chip))
         out_ref[chip * part_rows : (chip + 1) * part_rows, :] = values.astype(jnp.bfloat16)
 
 
@@ -170,8 +174,8 @@
     hbm, vmem = (pl.BlockSpec(memory_space=space) for space in (pltpu.HBM, pltpu.VMEM))
     anywhere = pl.BlockSpec(memory_space=pl.ANY)
 
-    def exchange(rows, order):
-        groups = far_groups(order, ep_count, chips)
+    def exchange(rows, members):
+        groups = far_groups(members, ep_count, chips)
         return lax.all_to_all(rows, FAR, 0, 0, axis_index_groups=groups, tiled=True)
 
     def call(kernel, name, out_shape, **rest):
@@ -189,7 +193,7 @@
         ],
         cost_estimate=pl.CostEstimate(flops=2 * 10**9, bytes_accessed=0, transcendentals=0),
     )(*(pltpu.with_memory_space_constraint(value, pltpu.HBM) for value in (ids, tokens)))
-    incoming = exchange(outgoing, first_order)
+    incoming = exchange(outgoing, first_members)
     across = lax.ppermute(incoming, "core", SWAP)
     acts = jax.ShapeDtypeStruct((slot_count, 2 * hidden_count), jnp.float32)
     begun = call(lambda *refs: begin(chips, *refs), "begin", acts)(incoming, w_gate, w_up)
@@ -209,7 +213,7 @@
         in_specs=[vmem] * 2 + [anywhere],
     )(ids, scores, other)
     summed = call(add, "add", half, in_specs=[vmem] * 2 + [anywhere])(mine, crossed, weight)
-    returned = exchange(summed, second_order)
+    returned = exchange(summed, second_members)
     return call(
         combine,
         "combine",

time: 25.5 us -> 27.2 us (1.067)
  blocking collectives: 19.8 us -> 21.3 us
  starting transfers between devices: 0.64 us -> 1.03 us
    all_to_all x2, blocking collectives: 19.8 us -> 21.3 us  [exchange(): return lax.all_to_all(rows, FAR, 0, 0, axis_index_groups=groups, tiled=True)]
    ppermute x1, starting transfers between devices: 0.29 us -> 0.61 us  [shards(): across = lax.ppermute(incoming, 'core', SWAP)]
where the time goes in v30:
time: 27.2 us; the launch traced here: 27 us
  blocking collectives  21.3 us (78%)
  Pallas kernels  3.35 us (12%)
  waiting for transfers between devices  1.18 us (4%)
  starting transfers between devices  1.03 us (4%)
    all_to_all x2, blocking collectives, exchange(): return lax.all_to_all(rows, FAR, 0, 0, axis_index_groups=groups, tiled=True)  21.3 us
    pallas_call x1, Pallas kernels, shards(): call(lambda *refs: route(ep_count, chips, *refs), 'route', half, in_specs...  1.26 us
    pallas_call x1, Pallas kernels, shards(): call(combine, 'combine', jax.ShapeDtypeStruct((row_count, features), jnp....  0.87 us
    ppermute x1, waiting for transfers between devices, shards(): across = lax.ppermute(incoming, 'core', SWAP)  0.67 us
    ppermute x1, starting transfers between devices, shards(): across = lax.ppermute(incoming, 'core', SWAP)  0.61 us
  transfers between devices with their start and end apart: 2, of which 2 were waited for; matrix products, arithmetic and copies ran while one was open for 0% of the time, Pallas kernels for 3%

profile of v30, /device:TPU:0, one launch (start us, length us, event | category | flops | bytes accessed | tf_op | source)
XLA Modules:
  0.0 27.0 jit_solution(9326941143953956772)
XLA Ops:
  0.0 0.0 copy-start
  0.0 0.0 copy-start.1
  0.0 1.3 %route.1 = bf16[64,896]{1,0:T(8,128)(2,1)S(1)} custom-call(s32[8,128]{1,0:T(8,128)} %bitcast.11, bf16[128,896]{1,0:T(8,128)(2,1)} %refs_1_.3), custom_call_target="tpu_custom_call" | custom-call | flops 2000000000 | tf_op jit(solution)/shard_map/route/pallas_call | solution.py:184
  1.3 13.3 %all_to_all.22 = bf16[8,8,896]{2,1,0:T(8,128)(2,1)S(1)} all-to-all(bf16[8,8,896]{2,1,0:T(8,128)(2,1)S(1)} %bitcast.10), channel_id=1, replica_groups={{0,3,4,7,8,11,12,15},{1,2,5,6,9,10,13,14},{16,19,20,23,24,27,28,31},{17..., dimensions={0} | all-to-all | bytes 229376 | tf_op jit(solution)/shard_map/all_to_all | solution.py:179
  14.6 0.0 copy-start.2
  14.6 0.6 %collective-permute-start = (bf16[64,896]{1,0:T(8,128)(2,1)S(1)}, bf16[64,896]{1,0:T(8,128)(2,1)S(1)}, u32[]{:S(2)}, u32[]{:S(2)}) collective-permute-start(bf16[64,896]{1,0:T(8,128)(2,1)S(1)} %bitcast.8), channel_id=1, source_target_pairs={{0,1},{1,0},{2,3},{3,2},{4,5},{5,4},{6,7},{7,6},{8,9},{9,8},{10,11... | collective-permute-start | bytes 344072 | tf_op jit(solution)/shard_map/ppermute | solution.py:197
  15.2 0.0 copy-done
  15.2 0.0 copy-done.1
  15.2 0.3 %begin.1.refs_1_ = f32[32,256]{1,0:T(8,128)S(1)} custom-call(bf16[64,896]{1,0:T(8,128)(2,1)S(1)} %bitcast.9, bf16[1,3584,128]{2,1,0:T(8,128)(2,1)S(1)} %copy-done, bf16[1,3584,128]{2,1,0:T(8,128)(2,1)S(1)} %copy-done.1), custom_call_target="tpu_custom_call" | custom-call | tf_op jit(solution)/shard_map/begin/pallas_call | solution.py:199
  15.5 0.7 %collective-permute-done.refs_0_ = bf16[64,896]{1,0:T(8,128)(2,1)S(1)} collective-permute-done((bf16[64,896]{1,0:T(8,128)(2,1)S(1)}, bf16[64,896]{1,0:T(8,128)(2,1)S(1)}, u32[]{:S(2)}, u32[]{:S(2)}) %collective-permute-start) | collective-permute-done | bytes 114720 | tf_op jit(solution)/shard_map/ppermute | solution.py:197
  16.1 0.0 copy-done.2
  16.1 0.0 copy-start.3
  16.1 0.0 copy-start.4
  16.1 0.5 %theirs.1 = (bf16[32,128]{1,0:T(8,128)(2,1)S(1)}, bf16[64,896]{1,0:T(8,128)(2,1)S(1)}) custom-call(bf16[64,896]{1,0:T(8,128)(2,1)S(1)} %collective-permute-done.refs_0_, f32[32,256]{1,0:T(8,128)S(1)} %begin.1.refs_1_, bf16[1,3584,128]{2,1,0:T(8,128)(2,1)S(1)} %copy-done, bf16[1,3584,128]{2,1,0:T(8,128)(2,1)S(1)} %copy-done.1, bf16[1,128,3584]{2,1,0:T(8,128)(2,1)S(1)} %copy-done.2), custom_call_target="tpu_custom_call" | custom-call | tf_op jit(solution)/shard_map/theirs/pallas_call | solution.py:201
  16.6 0.4 %collective-permute-start.1 = (bf16[64,896]{1,0:T(8,128)(2,1)S(1)}, bf16[64,896]{1,0:T(8,128)(2,1)S(1)}, u32[]{:S(2)}, u32[]{:S(2)}) collective-permute-start(bf16[64,896]{1,0:T(8,128)(2,1)S(1)} %get-tuple-element.9.refs_2_), channel_id=1, source_target_pairs={{0,1},{1,0},{2,3},{3,2},{4,5},{5,4},{6,7},{7,6},{8,9},{9,8},{10,11... | collective-permute-start | bytes 344072 | tf_op jit(solution)/shard_map/ppermute | solution.py:204
  17.0 0.0 copy-done.3
  17.0 0.0 copy-done.4
  17.0 0.2 score.1
  17.3 0.2 ours.1.mine_ref
  17.5 0.5 %collective-permute-done.1.other_ref = bf16[64,896]{1,0:T(8,128)(2,1)S(1)} collective-permute-done((bf16[64,896]{1,0:T(8,128)(2,1)S(1)}, bf16[64,896]{1,0:T(8,128)(2,1)S(1)}, u32[]{:S(2)}, u32[]{:S(2)}) %collective-permute-start.1) | collective-permute-done | bytes 114720 | tf_op jit(solution)/shard_map/ppermute | solution.py:204
  18.0 8.0 %all_to_all.23 = bf16[8,8,896]{2,1,0:T(8,128)(2,1)S(1)} all-to-all(bf16[8,8,896]{2,1,0:T(8,128)(2,1)S(1)} %bitcast.7), channel_id=1, replica_groups={{8,4,0,12,15,11,3,7},{9,5,1,13,14,10,2,6},{24,20,16,28,31,27,19,23},{25..., dimensions={0} | all-to-all | bytes 229376 | tf_op jit(solution)/shard_map/all_to_all | solution.py:179
  26.1 0.9 %combine.1 = bf16[128,896]{1,0:T(8,128)(2,1)} custom-call(bf16[128,64]{1,0:T(8,128)(2,1)S(1)} %get-tuple-element.10.match_ref, f32[128,1]{1,0:T(8,128)S(1)} %get-tuple-element.11._.weight_ref, bf16[64,896]{1,0:T(8,128)(2,1)S(1)} %bitcast.6), custom_call_target="tpu_custom_call" | custom-call | tf_op jit(solution)/shard_map/combine/pallas_call | solution.py:217
  (1 shorter events, 0.0 us)
Async XLA Ops:
  0.0 15.2 %copy-start = (bf16[1,3584,128]{2,1,0:T(8,128)(2,1)S(1)}, bf16[1,3584,128]{2,1,0:T(8,128)(2,1)}, u32[]{:S(2)}) copy-start(bf16[1,3584,128]{2,1,0:T(8,128)(2,1)} %refs_2_.3) | copy-start | bytes 2752516
  0.0 15.2 %copy-start.1 = (bf16[1,3584,128]{2,1,0:T(8,128)(2,1)S(1)}, bf16[1,3584,128]{2,1,0:T(8,128)(2,1)}, u32[]{:S(2)}) copy-start(bf16[1,3584,128]{2,1,0:T(8,128)(2,1)} %refs_3_.1) | copy-start | bytes 2752516
  14.6 1.6 %copy-start.2 = (bf16[1,128,3584]{2,1,0:T(8,128)(2,1)S(1)}, bf16[1,128,3584]{2,1,0:T(8,128)(2,1)}, u32[]{:S(2)}) copy-start(bf16[1,128,3584]{2,1,0:T(8,128)(2,1)} %refs_1_.5) | copy-start | bytes 2752516
  14.6 1.6 %collective-permute-start = (bf16[64,896]{1,0:T(8,128)(2,1)S(1)}, bf16[64,896]{1,0:T(8,128)(2,1)S(1)}, u32[]{:S(2)}, u32[]{:S(2)}) collective-permute-start(bf16[64,896]{1,0:T(8,128)(2,1)S(1)} %bitcast.8), channel_id=1, source_target_pairs={{0,1},{1,0},{2,3},{3,2},{4,5},{5,4},{6,7},{7,6},{8,9},{9,8},{10,11... | collective-permute-start | bytes 344072 | tf_op jit(solution)/shard_map/ppermute | solution.py:197
  16.1 0.9 %copy-start.3 = (s32[128,8]{0,1:T(8,128)S(1)}, s32[128,8]{0,1:T(8,128)}, u32[]{:S(2)}) copy-start(s32[128,8]{0,1:T(8,128)} %param.7) | copy-start | bytes 12292
  16.1 0.9 %copy-start.4 = (f32[128,8]{0,1:T(8,128)S(1)}, f32[128,8]{0,1:T(8,128)}, u32[]{:S(2)}) copy-start(f32[128,8]{0,1:T(8,128)} %param.8) | copy-start | bytes 12292
  16.6 1.4 %collective-permute-start.1 = (bf16[64,896]{1,0:T(8,128)(2,1)S(1)}, bf16[64,896]{1,0:T(8,128)(2,1)S(1)}, u32[]{:S(2)}, u32[]{:S(2)}) collective-permute-start(bf16[64,896]{1,0:T(8,128)(2,1)S(1)} %get-tuple-element.9.refs_2_), channel_id=1, source_target_pairs={{0,1},{1,0},{2,3},{3,2},{4,5},{5,4},{6,7},{7,6},{8,9},{9,8},{10,11... | collective-permute-start | bytes 344072 | tf_op jit(solution)/shard_map/ppermute | solution.py:204

commit v31 on v27

--- a/solution.py
+++ b/solution.py
@@ -35,7 +35,7 @@
 
 
 def first_order(ep_count, chip):
-    listed = ((2, 3, 0, 1), (2, 3, 1, 0))[chip % 2]
+    listed = ((2, 3, 0, 1), (1, 0, 3, 2))[chip % 2]
     return [z // 4 * 4 + listed[z % 4] for z in range(ep_count)]
 
 

time: 25.5 us -> 25.7 us (level)
  starting transfers between devices: 0.64 us -> 1.03 us
    ppermute x1, starting transfers between devices: 0.29 us -> 0.6 us  [shards(): across = lax.ppermute(incoming, 'core', SWAP)]
where the time goes in v31:
time: 25.7 us; the launch traced here: 25.5 us
  blocking collectives  19.9 us (77%)
  Pallas kernels  3.33 us (13%)
  waiting for transfers between devices  1.19 us (5%)
  starting transfers between devices  1.03 us (4%)
    all_to_all x2, blocking collectives, exchange(): return lax.all_to_all(rows, FAR, 0, 0, axis_index_groups=groups, tiled=True)  19.9 us
    pallas_call x1, Pallas kernels, shards(): call(lambda *refs: route(ep_count, chips, *refs), 'route', half, in_specs...  1.26 us
    pallas_call x1, Pallas kernels, shards(): call(combine, 'combine', jax.ShapeDtypeStruct((row_count, features), jnp....  0.87 us
    ppermute x1, waiting for transfers between devices, shards(): across = lax.ppermute(incoming, 'core', SWAP)  0.68 us
    ppermute x1, starting transfers between devices, shards(): across = lax.ppermute(incoming, 'core', SWAP)  0.6 us
  transfers between devices with their start and end apart: 2, of which 2 were waited for; matrix products, arithmetic and copies ran while one was open for 0% of the time, Pallas kernels for 3%

profile of v31, /device:TPU:0, one launch (start us, length us, event | category | flops | bytes accessed | tf_op | source)
XLA Modules:
  0.0 25.5 jit_solution(13050196559377390689)
XLA Ops:
  0.0 0.0 copy-start
  0.0 0.0 copy-start.1
  0.0 1.3 %route.1 = bf16[64,896]{1,0:T(8,128)(2,1)S(1)} custom-call(s32[8,128]{1,0:T(8,128)} %bitcast.11, bf16[128,896]{1,0:T(8,128)(2,1)} %refs_1_.3), custom_call_target="tpu_custom_call" | custom-call | flops 2000000000 | tf_op jit(solution)/shard_map/route/pallas_call | solution.py:180
  1.3 11.7 %all_to_all.22 = bf16[8,8,896]{2,1,0:T(8,128)(2,1)S(1)} all-to-all(bf16[8,8,896]{2,1,0:T(8,128)(2,1)S(1)} %bitcast.10), channel_id=1, replica_groups={{8,12,0,4,7,3,15,11},{9,13,1,5,6,2,14,10},{24,28,16,20,23,19,31,27},{25..., dimensions={0} | all-to-all | bytes 229376 | tf_op jit(solution)/shard_map/all_to_all | solution.py:175
  12.9 0.0 copy-start.2
  12.9 0.6 %collective-permute-start = (bf16[64,896]{1,0:T(8,128)(2,1)S(1)}, bf16[64,896]{1,0:T(8,128)(2,1)S(1)}, u32[]{:S(2)}, u32[]{:S(2)}) collective-permute-start(bf16[64,896]{1,0:T(8,128)(2,1)S(1)} %bitcast.8), channel_id=1, source_target_pairs={{0,1},{1,0},{2,3},{3,2},{4,5},{5,4},{6,7},{7,6},{8,9},{9,8},{10,11... | collective-permute-start | bytes 344072 | tf_op jit(solution)/shard_map/ppermute | solution.py:193
  13.5 0.0 copy-done
  13.5 0.0 copy-done.1
  13.5 0.3 %begin.1.refs_1_ = f32[32,256]{1,0:T(8,128)S(1)} custom-call(bf16[64,896]{1,0:T(8,128)(2,1)S(1)} %bitcast.9, bf16[1,3584,128]{2,1,0:T(8,128)(2,1)S(1)} %copy-done, bf16[1,3584,128]{2,1,0:T(8,128)(2,1)S(1)} %copy-done.1), custom_call_target="tpu_custom_call" | custom-call | tf_op jit(solution)/shard_map/begin/pallas_call | solution.py:195
  13.8 0.7 %collective-permute-done.refs_0_ = bf16[64,896]{1,0:T(8,128)(2,1)S(1)} collective-permute-done((bf16[64,896]{1,0:T(8,128)(2,1)S(1)}, bf16[64,896]{1,0:T(8,128)(2,1)S(1)}, u32[]{:S(2)}, u32[]{:S(2)}) %collective-permute-start) | collective-permute-done | bytes 114720 | tf_op jit(solution)/shard_map/ppermute | solution.py:193
  14.5 0.0 copy-done.2
  14.5 0.0 copy-start.3
  14.5 0.0 copy-start.4
  14.5 0.5 %theirs.1 = (bf16[32,128]{1,0:T(8,128)(2,1)S(1)}, bf16[64,896]{1,0:T(8,128)(2,1)S(1)}) custom-call(bf16[64,896]{1,0:T(8,128)(2,1)S(1)} %collective-permute-done.refs_0_, f32[32,256]{1,0:T(8,128)S(1)} %begin.1.refs_1_, bf16[1,3584,128]{2,1,0:T(8,128)(2,1)S(1)} %copy-done, bf16[1,3584,128]{2,1,0:T(8,128)(2,1)S(1)} %copy-done.1, bf16[1,128,3584]{2,1,0:T(8,128)(2,1)S(1)} %copy-done.2), custom_call_target="tpu_custom_call" | custom-call | tf_op jit(solution)/shard_map/theirs/pallas_call | solution.py:197
  15.0 0.4 %collective-permute-start.1 = (bf16[64,896]{1,0:T(8,128)(2,1)S(1)}, bf16[64,896]{1,0:T(8,128)(2,1)S(1)}, u32[]{:S(2)}, u32[]{:S(2)}) collective-permute-start(bf16[64,896]{1,0:T(8,128)(2,1)S(1)} %get-tuple-element.9.refs_2_), channel_id=1, source_target_pairs={{0,1},{1,0},{2,3},{3,2},{4,5},{5,4},{6,7},{7,6},{8,9},{9,8},{10,11... | collective-permute-start | bytes 344072 | tf_op jit(solution)/shard_map/ppermute | solution.py:200
  15.4 0.0 copy-done.3
  15.4 0.0 copy-done.4
  15.4 0.2 score.1
  15.6 0.2 ours.1.mine_ref
  15.9 0.5 %collective-permute-done.1.other_ref = bf16[64,896]{1,0:T(8,128)(2,1)S(1)} collective-permute-done((bf16[64,896]{1,0:T(8,128)(2,1)S(1)}, bf16[64,896]{1,0:T(8,128)(2,1)S(1)}, u32[]{:S(2)}, u32[]{:S(2)}) %collective-permute-start.1) | collective-permute-done | bytes 114720 | tf_op jit(solution)/shard_map/ppermute | solution.py:200
  16.4 8.2 %all_to_all.23 = bf16[8,8,896]{2,1,0:T(8,128)(2,1)S(1)} all-to-all(bf16[8,8,896]{2,1,0:T(8,128)(2,1)S(1)} %bitcast.7), channel_id=1, replica_groups={{8,4,0,12,15,11,3,7},{9,5,1,13,14,10,2,6},{24,20,16,28,31,27,19,23},{25..., dimensions={0} | all-to-all | bytes 229376 | tf_op jit(solution)/shard_map/all_to_all | solution.py:175
  24.6 0.9 %combine.1 = bf16[128,896]{1,0:T(8,128)(2,1)} custom-call(bf16[128,64]{1,0:T(8,128)(2,1)S(1)} %get-tuple-element.10.match_ref, f32[128,1]{1,0:T(8,128)S(1)} %get-tuple-element.11._.weight_ref, bf16[64,896]{1,0:T(8,128)(2,1)S(1)} %bitcast.6), custom_call_target="tpu_custom_call" | custom-call | tf_op jit(solution)/shard_map/combine/pallas_call | solution.py:213
  (1 shorter events, 0.0 us)
Async XLA Ops:
  0.0 13.5 %copy-start = (bf16[1,3584,128]{2,1,0:T(8,128)(2,1)S(1)}, bf16[1,3584,128]{2,1,0:T(8,128)(2,1)}, u32[]{:S(2)}) copy-start(bf16[1,3584,128]{2,1,0:T(8,128)(2,1)} %refs_2_.3) | copy-start | bytes 2752516
  0.0 13.5 %copy-start.1 = (bf16[1,3584,128]{2,1,0:T(8,128)(2,1)S(1)}, bf16[1,3584,128]{2,1,0:T(8,128)(2,1)}, u32[]{:S(2)}) copy-start(bf16[1,3584,128]{2,1,0:T(8,128)(2,1)} %refs_3_.1) | copy-start | bytes 2752516
  12.9 1.6 %copy-start.2 = (bf16[1,128,3584]{2,1,0:T(8,128)(2,1)S(1)}, bf16[1,128,3584]{2,1,0:T(8,128)(2,1)}, u32[]{:S(2)}) copy-start(bf16[1,128,3584]{2,1,0:T(8,128)(2,1)} %refs_1_.5) | copy-start | bytes 2752516
  12.9 1.6 %collective-permute-start = (bf16[64,896]{1,0:T(8,128)(2,1)S(1)}, bf16[64,896]{1,0:T(8,128)(2,1)S(1)}, u32[]{:S(2)}, u32[]{:S(2)}) collective-permute-start(bf16[64,896]{1,0:T(8,128)(2,1)S(1)} %bitcast.8), channel_id=1, source_target_pairs={{0,1},{1,0},{2,3},{3,2},{4,5},{5,4},{6,7},{7,6},{8,9},{9,8},{10,11... | collective-permute-start | bytes 344072 | tf_op jit(solution)/shard_map/ppermute | solution.py:193
  14.5 0.9 %copy-start.3 = (s32[128,8]{0,1:T(8,128)S(1)}, s32[128,8]{0,1:T(8,128)}, u32[]{:S(2)}) copy-start(s32[128,8]{0,1:T(8,128)} %param.7) | copy-start | bytes 12292
  14.5 0.9 %copy-start.4 = (f32[128,8]{0,1:T(8,128)S(1)}, f32[128,8]{0,1:T(8,128)}, u32[]{:S(2)}) copy-start(f32[128,8]{0,1:T(8,128)} %param.8) | copy-start | bytes 12292
  15.0 1.4 %collective-permute-start.1 = (bf16[64,896]{1,0:T(8,128)(2,1)S(1)}, bf16[64,896]{1,0:T(8,128)(2,1)S(1)}, u32[]{:S(2)}, u32[]{:S(2)}) collective-permute-start(bf16[64,896]{1,0:T(8,128)(2,1)S(1)} %get-tuple-element.9.refs_2_), channel_id=1, source_target_pairs={{0,1},{1,0},{2,3},{3,2},{4,5},{5,4},{6,7},{7,6},{8,9},{9,8},{10,11... | collective-permute-start | bytes 344072 | tf_op jit(solution)/shard_map/ppermute | solution.py:200

commit v32 on v31

--- a/solution.py
+++ b/solution.py
@@ -35,7 +35,7 @@
 
 
 def first_order(ep_count, chip):
-    listed = ((2, 3, 0, 1), (1, 0, 3, 2))[chip % 2]
+    listed = ((2, 3, 0, 1), (2, 3, 0, 1))[chip % 2]
     return [z // 4 * 4 + listed[z % 4] for z in range(ep_count)]
 
 

time: 25.7 us -> 25.8 us (level)
  starting transfers between devices: 1.03 us -> 0.64 us
    ppermute x1, starting transfers between devices: 0.6 us -> 0.29 us  [shards(): across = lax.ppermute(incoming, 'core', SWAP)]
where the time goes in v32:
time: 25.8 us; the launch traced here: 25.6 us
  blocking collectives  20.1 us (78%)
  Pallas kernels  3.42 us (13%)
  waiting for transfers between devices  1.34 us (5%)
  starting transfers between devices  0.64 us (2%)
    all_to_all x2, blocking collectives, exchange(): return lax.all_to_all(rows, FAR, 0, 0, axis_index_groups=groups, tiled=True)  20.1 us
    pallas_call x1, Pallas kernels, shards(): call(lambda *refs: route(ep_count, chips, *refs), 'route', half, in_specs...  1.26 us
    pallas_call x1, Pallas kernels, shards(): call(combine, 'combine', jax.ShapeDtypeStruct((row_count, features), jnp....  0.87 us
    ppermute x1, waiting for transfers between devices, shards(): across = lax.ppermute(incoming, 'core', SWAP)  0.76 us
    ppermute x1, waiting for transfers between devices, shards(): crossed = lax.ppermute(other, 'core', SWAP)  0.58 us
    pallas_call x1, Pallas kernels, shards(): call(lambda *refs: theirs(chips, *refs), 'theirs', (hidden_shape, half))  0.57 us
  transfers between devices with their start and end apart: 2, of which 2 were waited for; matrix products, arithmetic and copies ran while one was open for 0% of the time, Pallas kernels for 3%

profile of v32, /device:TPU:0, one launch (start us, length us, event | category | flops | bytes accessed | tf_op | source)
XLA Modules:
  0.0 25.6 jit_solution(10611563530566728493)
XLA Ops:
  0.0 0.0 copy-start
  0.0 0.0 copy-start.1
  0.0 1.3 %route.1 = bf16[64,896]{1,0:T(8,128)(2,1)S(1)} custom-call(s32[8,128]{1,0:T(8,128)} %bitcast.11, bf16[128,896]{1,0:T(8,128)(2,1)} %refs_1_.3), custom_call_target="tpu_custom_call" | custom-call | flops 2000000000 | tf_op jit(solution)/shard_map/route/pallas_call | solution.py:180
  1.3 11.8 %all_to_all.22 = bf16[8,8,896]{2,1,0:T(8,128)(2,1)S(1)} all-to-all(bf16[8,8,896]{2,1,0:T(8,128)(2,1)S(1)} %bitcast.10), channel_id=1, replica_groups={{8,12,0,4,11,15,3,7},{9,13,1,5,10,14,2,6},{24,28,16,20,27,31,19,23},{25..., dimensions={0} | all-to-all | bytes 229376 | tf_op jit(solution)/shard_map/all_to_all | solution.py:175
  13.1 0.0 copy-start.2
  13.1 0.3 %collective-permute-start = (bf16[64,896]{1,0:T(8,128)(2,1)S(1)}, bf16[64,896]{1,0:T(8,128)(2,1)S(1)}, u32[]{:S(2)}, u32[]{:S(2)}) collective-permute-start(bf16[64,896]{1,0:T(8,128)(2,1)S(1)} %bitcast.8), channel_id=1, source_target_pairs={{0,1},{1,0},{2,3},{3,2},{4,5},{5,4},{6,7},{7,6},{8,9},{9,8},{10,11... | collective-permute-start | bytes 344072 | tf_op jit(solution)/shard_map/ppermute | solution.py:193
  13.4 0.0 copy-done
  13.4 0.0 copy-done.1
  13.4 0.3 begin.1.refs_1_
  13.6 0.8 %collective-permute-done.refs_0_ = bf16[64,896]{1,0:T(8,128)(2,1)S(1)} collective-permute-done((bf16[64,896]{1,0:T(8,128)(2,1)S(1)}, bf16[64,896]{1,0:T(8,128)(2,1)S(1)}, u32[]{:S(2)}, u32[]{:S(2)}) %collective-permute-start) | collective-permute-done | bytes 114720 | tf_op jit(solution)/shard_map/ppermute | solution.py:193
  14.4 0.0 copy-done.2
  14.4 0.0 copy-start.3
  14.4 0.0 copy-start.4
  14.4 0.6 %theirs.1 = (bf16[32,128]{1,0:T(8,128)(2,1)S(1)}, bf16[64,896]{1,0:T(8,128)(2,1)S(1)}) custom-call(bf16[64,896]{1,0:T(8,128)(2,1)S(1)} %collective-permute-done.refs_0_, f32[32,256]{1,0:T(8,128)S(1)} %begin.1.refs_1_, bf16[1,3584,128]{2,1,0:T(8,128)(2,1)S(1)} %copy-done, bf16[1,3584,128]{2,1,0:T(8,128)(2,1)S(1)} %copy-done.1, bf16[1,128,3584]{2,1,0:T(8,128)(2,1)S(1)} %copy-done.2), custom_call_target="tpu_custom_call" | custom-call | tf_op jit(solution)/shard_map/theirs/pallas_call | solution.py:197
  15.0 0.4 %collective-permute-start.1 = (bf16[64,896]{1,0:T(8,128)(2,1)S(1)}, bf16[64,896]{1,0:T(8,128)(2,1)S(1)}, u32[]{:S(2)}, u32[]{:S(2)}) collective-permute-start(bf16[64,896]{1,0:T(8,128)(2,1)S(1)} %get-tuple-element.9.refs_2_), channel_id=1, source_target_pairs={{0,1},{1,0},{2,3},{3,2},{4,5},{5,4},{6,7},{7,6},{8,9},{9,8},{10,11... | collective-permute-start | bytes 344072 | tf_op jit(solution)/shard_map/ppermute | solution.py:200
  15.3 0.0 copy-done.3
  15.3 0.0 copy-done.4
  15.3 0.2 score.1
  15.6 0.2 ours.1.mine_ref
  15.8 0.6 %collective-permute-done.1.other_ref = bf16[64,896]{1,0:T(8,128)(2,1)S(1)} collective-permute-done((bf16[64,896]{1,0:T(8,128)(2,1)S(1)}, bf16[64,896]{1,0:T(8,128)(2,1)S(1)}, u32[]{:S(2)}, u32[]{:S(2)}) %collective-permute-start.1) | collective-permute-done | bytes 114720 | tf_op jit(solution)/shard_map/ppermute | solution.py:200
  16.4 8.3 %all_to_all.23 = bf16[8,8,896]{2,1,0:T(8,128)(2,1)S(1)} all-to-all(bf16[8,8,896]{2,1,0:T(8,128)(2,1)S(1)} %bitcast.7), channel_id=1, replica_groups={{8,4,0,12,15,11,3,7},{9,5,1,13,14,10,2,6},{24,20,16,28,31,27,19,23},{25..., dimensions={0} | all-to-all | bytes 229376 | tf_op jit(solution)/shard_map/all_to_all | solution.py:175
  24.7 0.9 %combine.1 = bf16[128,896]{1,0:T(8,128)(2,1)} custom-call(bf16[128,64]{1,0:T(8,128)(2,1)S(1)} %get-tuple-element.10.match_ref, f32[128,1]{1,0:T(8,128)S(1)} %get-tuple-element.11._.weight_ref, bf16[64,896]{1,0:T(8,128)(2,1)S(1)} %bitcast.6), custom_call_target="tpu_custom_call" | custom-call | tf_op jit(solution)/shard_map/combine/pallas_call | solution.py:213
  (1 shorter events, 0.0 us)
Async XLA Ops:
  0.0 13.4 %copy-start = (bf16[1,3584,128]{2,1,0:T(8,128)(2,1)S(1)}, bf16[1,3584,128]{2,1,0:T(8,128)(2,1)}, u32[]{:S(2)}) copy-start(bf16[1,3584,128]{2,1,0:T(8,128)(2,1)} %refs_2_.3) | copy-start | bytes 2752516
  0.0 13.4 %copy-start.1 = (bf16[1,3584,128]{2,1,0:T(8,128)(2,1)S(1)}, bf16[1,3584,128]{2,1,0:T(8,128)(2,1)}, u32[]{:S(2)}) copy-start(bf16[1,3584,128]{2,1,0:T(8,128)(2,1)} %refs_3_.1) | copy-start | bytes 2752516
  13.1 1.3 %copy-start.2 = (bf16[1,128,3584]{2,1,0:T(8,128)(2,1)S(1)}, bf16[1,128,3584]{2,1,0:T(8,128)(2,1)}, u32[]{:S(2)}) copy-start(bf16[1,128,3584]{2,1,0:T(8,128)(2,1)} %refs_1_.5) | copy-start | bytes 2752516
  13.1 1.3 %collective-permute-start = (bf16[64,896]{1,0:T(8,128)(2,1)S(1)}, bf16[64,896]{1,0:T(8,128)(2,1)S(1)}, u32[]{:S(2)}, u32[]{:S(2)}) collective-permute-start(bf16[64,896]{1,0:T(8,128)(2,1)S(1)} %bitcast.8), channel_id=1, source_target_pairs={{0,1},{1,0},{2,3},{3,2},{4,5},{5,4},{6,7},{7,6},{8,9},{9,8},{10,11... | collective-permute-start | bytes 344072 | tf_op jit(solution)/shard_map/ppermute | solution.py:193
  14.4 0.9 %copy-start.3 = (s32[128,8]{0,1:T(8,128)S(1)}, s32[128,8]{0,1:T(8,128)}, u32[]{:S(2)}) copy-start(s32[128,8]{0,1:T(8,128)} %param.7) | copy-start | bytes 12292
  14.4 0.9 %copy-start.4 = (f32[128,8]{0,1:T(8,128)S(1)}, f32[128,8]{0,1:T(8,128)}, u32[]{:S(2)}) copy-start(f32[128,8]{0,1:T(8,128)} %param.8) | copy-start | bytes 12292
  15.0 1.4 %collective-permute-start.1 = (bf16[64,896]{1,0:T(8,128)(2,1)S(1)}, bf16[64,896]{1,0:T(8,128)(2,1)S(1)}, u32[]{:S(2)}, u32[]{:S(2)}) collective-permute-start(bf16[64,896]{1,0:T(8,128)(2,1)S(1)} %get-tuple-element.9.refs_2_), channel_id=1, source_target_pairs={{0,1},{1,0},{2,3},{3,2},{4,5},{5,4},{6,7},{7,6},{8,9},{9,8},{10,11... | collective-permute-start | bytes 344072 | tf_op jit(solution)/shard_map/ppermute | solution.py:200

commit v33 on v21

--- a/solution.py
+++ b/solution.py
@@ -39,7 +39,7 @@
 
 
 def second_order(ep_count, chip):
-    listed = ((2, 1, 0, 3), (3, 2, 0, 1))[chip % 2]
+    listed = ((2, 1, 0, 3), (3, 2, 1, 0))[chip % 2]
     return [z // 4 * 4 + listed[z % 4] for z in range(ep_count)]
 
 

time: 25.4 us -> 25.4 us (level)
  no operation moved by 1% of the time
where the time goes in v33:
time: 25.4 us; the launch traced here: 25.2 us
  blocking collectives  19.8 us (78%)
  Pallas kernels  3.34 us (13%)
  waiting for transfers between devices  1.19 us (5%)
  starting transfers between devices  0.83 us (3%)
    all_to_all x2, blocking collectives, exchange(): return lax.all_to_all(rows, FAR, 0, 0, axis_index_groups=groups, tiled=True)  19.8 us
    pallas_call x1, Pallas kernels, shards(): call(lambda *refs: route(ep_count, chips, *refs), 'route', half, in_specs...  1.27 us
    pallas_call x1, Pallas kernels, shards(): call(combine, 'combine', jax.ShapeDtypeStruct((row_count, features), jnp....  0.87 us
    ppermute x1, waiting for transfers between devices, shards(): across = lax.ppermute(incoming, 'core', SWAP)  0.68 us
  transfers between devices with their start and end apart: 2, of which 2 were waited for; matrix products, arithmetic and copies ran while one was open for 0% of the time, Pallas kernels for 3%

profile of v33, /device:TPU:0, one launch (start us, length us, event | category | flops | bytes accessed | tf_op | source)
XLA Modules:
  0.0 25.2 jit_solution(17213901318551171009)
XLA Ops:
  0.0 0.0 copy-start
  0.0 0.0 copy-start.1
  0.0 1.3 %route.1 = bf16[64,896]{1,0:T(8,128)(2,1)S(1)} custom-call(s32[8,128]{1,0:T(8,128)} %bitcast.11, bf16[128,896]{1,0:T(8,128)(2,1)} %refs_1_.3), custom_call_target="tpu_custom_call" | custom-call | flops 2000000000 | tf_op jit(solution)/shard_map/route/pallas_call | solution.py:179
  1.3 11.7 %all_to_all.22 = bf16[8,8,896]{2,1,0:T(8,128)(2,1)S(1)} all-to-all(bf16[8,8,896]{2,1,0:T(8,128)(2,1)S(1)} %bitcast.10), channel_id=1, replica_groups={{8,12,0,4,15,11,7,3},{9,13,1,5,14,10,6,2},{24,28,16,20,31,27,23,19},{25..., dimensions={0} | all-to-all | bytes 229376 | tf_op jit(solution)/shard_map/all_to_all | solution.py:174
  12.9 0.0 copy-start.2
  12.9 0.4 %collective-permute-start = (bf16[64,896]{1,0:T(8,128)(2,1)S(1)}, bf16[64,896]{1,0:T(8,128)(2,1)S(1)}, u32[]{:S(2)}, u32[]{:S(2)}) collective-permute-start(bf16[64,896]{1,0:T(8,128)(2,1)S(1)} %bitcast.8), channel_id=1, source_target_pairs={{0,1},{1,0},{2,3},{3,2},{4,5},{5,4},{6,7},{7,6},{8,9},{9,8},{10,11... | collective-permute-start | bytes 344072 | tf_op jit(solution)/shard_map/ppermute | solution.py:192
  13.3 0.0 copy-done
  13.3 0.0 copy-done.1
  13.3 0.3 %begin.1.refs_1_ = f32[32,256]{1,0:T(8,128)S(1)} custom-call(bf16[64,896]{1,0:T(8,128)(2,1)S(1)} %bitcast.9, bf16[1,3584,128]{2,1,0:T(8,128)(2,1)S(1)} %copy-done, bf16[1,3584,128]{2,1,0:T(8,128)(2,1)S(1)} %copy-done.1), custom_call_target="tpu_custom_call" | custom-call | tf_op jit(solution)/shard_map/begin/pallas_call | solution.py:194
  13.6 0.7 %collective-permute-done.refs_0_ = bf16[64,896]{1,0:T(8,128)(2,1)S(1)} collective-permute-done((bf16[64,896]{1,0:T(8,128)(2,1)S(1)}, bf16[64,896]{1,0:T(8,128)(2,1)S(1)}, u32[]{:S(2)}, u32[]{:S(2)}) %collective-permute-start) | collective-permute-done | bytes 114720 | tf_op jit(solution)/shard_map/ppermute | solution.py:192
  14.3 0.0 copy-done.2
  14.3 0.0 copy-start.3
  14.3 0.0 copy-start.4
  14.3 0.5 %theirs.1 = (bf16[32,128]{1,0:T(8,128)(2,1)S(1)}, bf16[64,896]{1,0:T(8,128)(2,1)S(1)}) custom-call(bf16[64,896]{1,0:T(8,128)(2,1)S(1)} %collective-permute-done.refs_0_, f32[32,256]{1,0:T(8,128)S(1)} %begin.1.refs_1_, bf16[1,3584,128]{2,1,0:T(8,128)(2,1)S(1)} %copy-done, bf16[1,3584,128]{2,1,0:T(8,128)(2,1)S(1)} %copy-done.1, bf16[1,128,3584]{2,1,0:T(8,128)(2,1)S(1)} %copy-done.2), custom_call_target="tpu_custom_call" | custom-call | tf_op jit(solution)/shard_map/theirs/pallas_call | solution.py:196
  14.8 0.4 %collective-permute-start.1 = (bf16[64,896]{1,0:T(8,128)(2,1)S(1)}, bf16[64,896]{1,0:T(8,128)(2,1)S(1)}, u32[]{:S(2)}, u32[]{:S(2)}) collective-permute-start(bf16[64,896]{1,0:T(8,128)(2,1)S(1)} %get-tuple-element.9.refs_2_), channel_id=1, source_target_pairs={{0,1},{1,0},{2,3},{3,2},{4,5},{5,4},{6,7},{7,6},{8,9},{9,8},{10,11... | collective-permute-start | bytes 344072 | tf_op jit(solution)/shard_map/ppermute | solution.py:199
  15.2 0.0 copy-done.3
  15.2 0.0 copy-done.4
  15.2 0.2 score.1
  15.5 0.2 ours.1.mine_ref
  15.7 0.5 %collective-permute-done.1.other_ref = bf16[64,896]{1,0:T(8,128)(2,1)S(1)} collective-permute-done((bf16[64,896]{1,0:T(8,128)(2,1)S(1)}, bf16[64,896]{1,0:T(8,128)(2,1)S(1)}, u32[]{:S(2)}, u32[]{:S(2)}) %collective-permute-start.1) | collective-permute-done | bytes 114720 | tf_op jit(solution)/shard_map/ppermute | solution.py:199
  16.2 8.2 %all_to_all.23 = bf16[8,8,896]{2,1,0:T(8,128)(2,1)S(1)} all-to-all(bf16[8,8,896]{2,1,0:T(8,128)(2,1)S(1)} %bitcast.7), channel_id=1, replica_groups={{8,4,0,12,15,11,7,3},{9,5,1,13,14,10,6,2},{24,20,16,28,31,27,23,19},{25..., dimensions={0} | all-to-all | bytes 229376 | tf_op jit(solution)/shard_map/all_to_all | solution.py:174
  24.4 0.9 %combine.1 = bf16[128,896]{1,0:T(8,128)(2,1)} custom-call(bf16[128,64]{1,0:T(8,128)(2,1)S(1)} %get-tuple-element.10.match_ref, f32[128,1]{1,0:T(8,128)S(1)} %get-tuple-element.11._.weight_ref, bf16[64,896]{1,0:T(8,128)(2,1)S(1)} %bitcast.6), custom_call_target="tpu_custom_call" | custom-call | tf_op jit(solution)/shard_map/combine/pallas_call | solution.py:212
  (1 shorter events, 0.0 us)
Async XLA Ops:
  0.0 13.3 %copy-start = (bf16[1,3584,128]{2,1,0:T(8,128)(2,1)S(1)}, bf16[1,3584,128]{2,1,0:T(8,128)(2,1)}, u32[]{:S(2)}) copy-start(bf16[1,3584,128]{2,1,0:T(8,128)(2,1)} %refs_2_.3) | copy-start | bytes 2752516
  0.0 13.3 %copy-start.1 = (bf16[1,3584,128]{2,1,0:T(8,128)(2,1)S(1)}, bf16[1,3584,128]{2,1,0:T(8,128)(2,1)}, u32[]{:S(2)}) copy-start(bf16[1,3584,128]{2,1,0:T(8,128)(2,1)} %refs_3_.1) | copy-start | bytes 2752516
  12.9 1.4 %copy-start.2 = (bf16[1,128,3584]{2,1,0:T(8,128)(2,1)S(1)}, bf16[1,128,3584]{2,1,0:T(8,128)(2,1)}, u32[]{:S(2)}) copy-start(bf16[1,128,3584]{2,1,0:T(8,128)(2,1)} %refs_1_.5) | copy-start | bytes 2752516
  12.9 1.4 %collective-permute-start = (bf16[64,896]{1,0:T(8,128)(2,1)S(1)}, bf16[64,896]{1,0:T(8,128)(2,1)S(1)}, u32[]{:S(2)}, u32[]{:S(2)}) collective-permute-start(bf16[64,896]{1,0:T(8,128)(2,1)S(1)} %bitcast.8), channel_id=1, source_target_pairs={{0,1},{1,0},{2,3},{3,2},{4,5},{5,4},{6,7},{7,6},{8,9},{9,8},{10,11... | collective-permute-start | bytes 344072 | tf_op jit(solution)/shard_map/ppermute | solution.py:192
  14.3 0.9 %copy-start.3 = (s32[128,8]{0,1:T(8,128)S(1)}, s32[128,8]{0,1:T(8,128)}, u32[]{:S(2)}) copy-start(s32[128,8]{0,1:T(8,128)} %param.7) | copy-start | bytes 12292
  14.3 0.9 %copy-start.4 = (f32[128,8]{0,1:T(8,128)S(1)}, f32[128,8]{0,1:T(8,128)}, u32[]{:S(2)}) copy-start(f32[128,8]{0,1:T(8,128)} %param.8) | copy-start | bytes 12292
  14.8 1.4 %collective-permute-start.1 = (bf16[64,896]{1,0:T(8,128)(2,1)S(1)}, bf16[64,896]{1,0:T(8,128)(2,1)S(1)}, u32[]{:S(2)}, u32[]{:S(2)}) collective-permute-start(bf16[64,896]{1,0:T(8,128)(2,1)S(1)} %get-tuple-element.9.refs_2_), channel_id=1, source_target_pairs={{0,1},{1,0},{2,3},{3,2},{4,5},{5,4},{6,7},{7,6},{8,9},{9,8},{10,11... | collective-permute-start | bytes 344072 | tf_op jit(solution)/shard_map/ppermute | solution.py:199

commit v34 on v21

--- a/solution.py
+++ b/solution.py
@@ -7,6 +7,7 @@
 
 CAP = 8
 PIECE = 32
+WRITE = 64
 FAR = ("ep", "chip", "core")
 SWAP = [(0, 1), (1, 0)]
 LIMIT = pltpu.CompilerParams(vmem_limit_bytes=16 * 1024 * 1024)
@@ -149,8 +150,8 @@
 
 def combine(match_ref, weight_ref, returned_ref, out_hbm, out_ref, sems):
     copies = []
-    for part in range(out_ref.shape[0] // PIECE):
-        rows = pl.ds(part * PIECE, PIECE)
+    for part in range(out_ref.shape[0] // WRITE):
+        rows = pl.ds(part * WRITE, WRITE)
         summed = jnp.dot(match_ref[rows, :], returned_ref[...], preferred_element_type=jnp.float32)
         out_ref[rows, :] = (weight_ref[rows, :] * summed).astype(jnp.bfloat16)
         copies.append(pltpu.make_async_copy(out_ref.at[rows, :], out_hbm.at[rows, :], sems.at[part]))
@@ -216,7 +217,7 @@
         out_specs=hbm,
         scratch_shapes=[
             pltpu.VMEM((row_count, features), jnp.bfloat16),
-            pltpu.SemaphoreType.DMA((row_count // PIECE,)),
+            pltpu.SemaphoreType.DMA((row_count // WRITE,)),
         ],
     )(match, weight, returned)
 

time: 25.4 us -> 25.5 us (level)
  no operation moved by 1% of the time
where the time goes in v34:
time: 25.5 us; the launch traced here: 25.2 us
  blocking collectives  19.8 us (78%)
  Pallas kernels  3.35 us (13%)
  waiting for transfers between devices  1.19 us (5%)
  starting transfers between devices  0.83 us (3%)
    all_to_all x2, blocking collectives, exchange(): return lax.all_to_all(rows, FAR, 0, 0, axis_index_groups=groups, tiled=True)  19.8 us
    pallas_call x1, Pallas kernels, shards(): call(lambda *refs: route(ep_count, chips, *refs), 'route', half, in_specs...  1.27 us
    pallas_call x1, Pallas kernels, shards(): call(combine, 'combine', jax.ShapeDtypeStruct((row_count, features), jnp....  0.88 us
    ppermute x1, waiting for transfers between devices, shards(): across = lax.ppermute(incoming, 'core', SWAP)  0.68 us
  transfers between devices with their start and end apart: 2, of which 2 were waited for; matrix products, arithmetic and copies ran while one was open for 0% of the time, Pallas kernels for 3%

profile of v34, /device:TPU:0, one launch (start us, length us, event | category | flops | bytes accessed | tf_op | source)
XLA Modules:
  0.0 25.2 jit_solution(6246481660552058701)
XLA Ops:
  0.0 0.0 copy-start
  0.0 0.0 copy-start.1
  0.0 1.3 %route.1 = bf16[64,896]{1,0:T(8,128)(2,1)S(1)} custom-call(s32[8,128]{1,0:T(8,128)} %bitcast.11, bf16[128,896]{1,0:T(8,128)(2,1)} %refs_1_.3), custom_call_target="tpu_custom_call" | custom-call | flops 2000000000 | tf_op jit(solution)/shard_map/route/pallas_call | solution.py:180
  1.3 11.7 %all_to_all.22 = bf16[8,8,896]{2,1,0:T(8,128)(2,1)S(1)} all-to-all(bf16[8,8,896]{2,1,0:T(8,128)(2,1)S(1)} %bitcast.10), channel_id=1, replica_groups={{8,12,0,4,15,11,7,3},{9,13,1,5,14,10,6,2},{24,28,16,20,31,27,23,19},{25..., dimensions={0} | all-to-all | bytes 229376 | tf_op jit(solution)/shard_map/all_to_all | solution.py:175
  12.9 0.0 copy-start.2
  12.9 0.4 %collective-permute-start = (bf16[64,896]{1,0:T(8,128)(2,1)S(1)}, bf16[64,896]{1,0:T(8,128)(2,1)S(1)}, u32[]{:S(2)}, u32[]{:S(2)}) collective-permute-start(bf16[64,896]{1,0:T(8,128)(2,1)S(1)} %bitcast.8), channel_id=1, source_target_pairs={{0,1},{1,0},{2,3},{3,2},{4,5},{5,4},{6,7},{7,6},{8,9},{9,8},{10,11... | collective-permute-start | bytes 344072 | tf_op jit(solution)/shard_map/ppermute | solution.py:193
  13.3 0.0 copy-done
  13.3 0.0 copy-done.1
  13.3 0.3 %begin.1.refs_1_ = f32[32,256]{1,0:T(8,128)S(1)} custom-call(bf16[64,896]{1,0:T(8,128)(2,1)S(1)} %bitcast.9, bf16[1,3584,128]{2,1,0:T(8,128)(2,1)S(1)} %copy-done, bf16[1,3584,128]{2,1,0:T(8,128)(2,1)S(1)} %copy-done.1), custom_call_target="tpu_custom_call" | custom-call | tf_op jit(solution)/shard_map/begin/pallas_call | solution.py:195
  13.6 0.7 %collective-permute-done.refs_0_ = bf16[64,896]{1,0:T(8,128)(2,1)S(1)} collective-permute-done((bf16[64,896]{1,0:T(8,128)(2,1)S(1)}, bf16[64,896]{1,0:T(8,128)(2,1)S(1)}, u32[]{:S(2)}, u32[]{:S(2)}) %collective-permute-start) | collective-permute-done | bytes 114720 | tf_op jit(solution)/shard_map/ppermute | solution.py:193
  14.3 0.0 copy-done.2
  14.3 0.0 copy-start.3
  14.3 0.0 copy-start.4
  14.3 0.5 %theirs.1 = (bf16[32,128]{1,0:T(8,128)(2,1)S(1)}, bf16[64,896]{1,0:T(8,128)(2,1)S(1)}) custom-call(bf16[64,896]{1,0:T(8,128)(2,1)S(1)} %collective-permute-done.refs_0_, f32[32,256]{1,0:T(8,128)S(1)} %begin.1.refs_1_, bf16[1,3584,128]{2,1,0:T(8,128)(2,1)S(1)} %copy-done, bf16[1,3584,128]{2,1,0:T(8,128)(2,1)S(1)} %copy-done.1, bf16[1,128,3584]{2,1,0:T(8,128)(2,1)S(1)} %copy-done.2), custom_call_target="tpu_custom_call" | custom-call | tf_op jit(solution)/shard_map/theirs/pallas_call | solution.py:197
  14.8 0.4 %collective-permute-start.1 = (bf16[64,896]{1,0:T(8,128)(2,1)S(1)}, bf16[64,896]{1,0:T(8,128)(2,1)S(1)}, u32[]{:S(2)}, u32[]{:S(2)}) collective-permute-start(bf16[64,896]{1,0:T(8,128)(2,1)S(1)} %get-tuple-element.9.refs_2_), channel_id=1, source_target_pairs={{0,1},{1,0},{2,3},{3,2},{4,5},{5,4},{6,7},{7,6},{8,9},{9,8},{10,11... | collective-permute-start | bytes 344072 | tf_op jit(solution)/shard_map/ppermute | solution.py:200
  15.2 0.0 copy-done.3
  15.2 0.0 copy-done.4
  15.2 0.2 score.1
  15.5 0.2 ours.1.mine_ref
  15.7 0.5 %collective-permute-done.1.other_ref = bf16[64,896]{1,0:T(8,128)(2,1)S(1)} collective-permute-done((bf16[64,896]{1,0:T(8,128)(2,1)S(1)}, bf16[64,896]{1,0:T(8,128)(2,1)S(1)}, u32[]{:S(2)}, u32[]{:S(2)}) %collective-permute-start.1) | collective-permute-done | bytes 114720 | tf_op jit(solution)/shard_map/ppermute | solution.py:200
  16.2 8.1 %all_to_all.23 = bf16[8,8,896]{2,1,0:T(8,128)(2,1)S(1)} all-to-all(bf16[8,8,896]{2,1,0:T(8,128)(2,1)S(1)} %bitcast.7), channel_id=1, replica_groups={{8,4,0,12,15,11,3,7},{9,5,1,13,14,10,2,6},{24,20,16,28,31,27,19,23},{25..., dimensions={0} | all-to-all | bytes 229376 | tf_op jit(solution)/shard_map/all_to_all | solution.py:175
  24.3 0.9 %combine.1 = bf16[128,896]{1,0:T(8,128)(2,1)} custom-call(bf16[128,64]{1,0:T(8,128)(2,1)S(1)} %get-tuple-element.10.match_ref, f32[128,1]{1,0:T(8,128)S(1)} %get-tuple-element.11._.weight_ref, bf16[64,896]{1,0:T(8,128)(2,1)S(1)} %bitcast.6), custom_call_target="tpu_custom_call" | custom-call | tf_op jit(solution)/shard_map/combine/pallas_call | solution.py:213
  (1 shorter events, 0.0 us)
Async XLA Ops:
  0.0 13.3 %copy-start = (bf16[1,3584,128]{2,1,0:T(8,128)(2,1)S(1)}, bf16[1,3584,128]{2,1,0:T(8,128)(2,1)}, u32[]{:S(2)}) copy-start(bf16[1,3584,128]{2,1,0:T(8,128)(2,1)} %refs_2_.3) | copy-start | bytes 2752516
  0.0 13.3 %copy-start.1 = (bf16[1,3584,128]{2,1,0:T(8,128)(2,1)S(1)}, bf16[1,3584,128]{2,1,0:T(8,128)(2,1)}, u32[]{:S(2)}) copy-start(bf16[1,3584,128]{2,1,0:T(8,128)(2,1)} %refs_3_.1) | copy-start | bytes 2752516
  12.9 1.4 %copy-start.2 = (bf16[1,128,3584]{2,1,0:T(8,128)(2,1)S(1)}, bf16[1,128,3584]{2,1,0:T(8,128)(2,1)}, u32[]{:S(2)}) copy-start(bf16[1,128,3584]{2,1,0:T(8,128)(2,1)} %refs_1_.5) | copy-start | bytes 2752516
  12.9 1.4 %collective-permute-start = (bf16[64,896]{1,0:T(8,128)(2,1)S(1)}, bf16[64,896]{1,0:T(8,128)(2,1)S(1)}, u32[]{:S(2)}, u32[]{:S(2)}) collective-permute-start(bf16[64,896]{1,0:T(8,128)(2,1)S(1)} %bitcast.8), channel_id=1, source_target_pairs={{0,1},{1,0},{2,3},{3,2},{4,5},{5,4},{6,7},{7,6},{8,9},{9,8},{10,11... | collective-permute-start | bytes 344072 | tf_op jit(solution)/shard_map/ppermute | solution.py:193
  14.3 0.9 %copy-start.3 = (s32[128,8]{0,1:T(8,128)S(1)}, s32[128,8]{0,1:T(8,128)}, u32[]{:S(2)}) copy-start(s32[128,8]{0,1:T(8,128)} %param.7) | copy-start | bytes 12292
  14.3 0.9 %copy-start.4 = (f32[128,8]{0,1:T(8,128)S(1)}, f32[128,8]{0,1:T(8,128)}, u32[]{:S(2)}) copy-start(f32[128,8]{0,1:T(8,128)} %param.8) | copy-start | bytes 12292
  14.8 1.4 %collective-permute-start.1 = (bf16[64,896]{1,0:T(8,128)(2,1)S(1)}, bf16[64,896]{1,0:T(8,128)(2,1)S(1)}, u32[]{:S(2)}, u32[]{:S(2)}) collective-permute-start(bf16[64,896]{1,0:T(8,128)(2,1)S(1)} %get-tuple-element.9.refs_2_), channel_id=1, source_target_pairs={{0,1},{1,0},{2,3},{3,2},{4,5},{5,4},{6,7},{7,6},{8,9},{9,8},{10,11... | collective-permute-start | bytes 344072 | tf_op jit(solution)/shard_map/ppermute | solution.py:200
